TPU v7x, 32 devices: a whole 2x2x4 slice. The times are simulated.
32 devices in a mesh: dp: 8 (over y, x, core), tensor: 4 (over z).
Axes of the slice: x: 2, y: 2, z: 4, core: 2. Of those that a mesh axis runs over, the one named last changes fastest.
Arguments:
- tokens: bfloat16 [32768, 768], P(('dp', 'tensor')), may hold values from -6 to 6
- prior_logits: bfloat16 [32768, 12], P(('dp', 'tensor')), may hold values from -6 to 6
- expert_ids: int32 [32768, 2], P('dp'), may hold values from 0 to 11, as said below
- expert_ranks: int32 [32768, 2], P('dp'), may hold values from 0 to 768, as said below
- piece_starts: int32 [32, 2], P('dp'), may hold values from 0 to 768, as said below
- norm_attn: bfloat16 [768], replicated, may hold values from 0.5 to 1.5
- qkv_weight: bfloat16 [3, 768, 768], P(None, 'dp', 'tensor'), may hold values from -0.21875 to 0.21875
- out_weight: bfloat16 [768, 768], P('tensor', 'dp'), may hold values from -0.625 to 0.625
- norm_moe: bfloat16 [768], replicated, may hold values from 0.5 to 1.5
- router_weight: bfloat16 [768, 12], replicated, may hold values from -0.109375 to 0.109375
- residual_weight: bfloat16 [12, 12], replicated, may hold values from -0.875 to 0.875
- const_vectors: bfloat16 [2, 768], replicated, may hold values from -6 to 6
- const_gates: bfloat16 [2, 2, 768], replicated, may hold values from -0.21875 to 0.21875
- w_gate_up: bfloat16 [2, 8, 768, 2048], P(None, None, 'dp', 'tensor'), may hold values from -0.21875 to 0.21875
- w_down: bfloat16 [8, 2048, 768], P(None, 'tensor', 'dp'), may hold values from -1 to 1
- out_grad: bfloat16 [32768, 768], P(('dp', 'tensor')), may hold values from -6 to 6
Outputs:
- layer_out: bfloat16 [32768, 768], P(('dp', 'tensor'))
- input_grad: float32 [32768, 768], P(('dp', 'tensor'))
- prior_grad: float32 [32768, 12], P(('dp', 'tensor'))
- norm_attn_grad: float32 [768], replicated
- qkv_grad: float32 [3, 768, 768], P(None, 'dp', 'tensor')
- out_weight_grad: float32 [768, 768], P('tensor', 'dp')
- norm_moe_grad: float32 [768], replicated
- router_grad: float32 [768, 12], replicated
- residual_grad: float32 [12, 12], replicated
- const_vector_grad: float32 [2, 768], replicated
- const_gate_grad: float32 [2, 2, 768], replicated
- gate_up_grad: float32 [2, 8, 768, 2048], P(None, None, 'dp', 'tensor')
- down_grad: float32 [8, 2048, 768], P(None, 'tensor', 'dp')
Inputs may be any that keep to these rules, and one draw needn't show every extreme that they name: `expert_ids`: each token names two different experts: ids below 8 are feed-forward experts, 8 the zero expert, 9 the copy expert, 10 and 11 the constant experts. In the tokens of each index of dp some feed-forward expert is named 2 * 768 times or more. `expert_ranks`: within the tokens of one index of dp, the choices that name one expert carry the ranks 0, 1, and so on, each once, up to 767; choices past the first 768 of an expert carry 768. `piece_starts`: each row gives the first positions of the 2 picture pieces of one sequence in rising order; the pieces do not intersect and do not pass the sequence's end.
All inputs are finite; a program needn't handle non-finite values.
Results may differ from a plain program's by a relative error of at most 0.018.
Values may be sent and summed in bfloat16 or wider, within the bound.
A program may use at most 320 MiB of HBM per device.

v0:
```python
import jax
import jax.numpy as jnp
from jax import lax
from jax.sharding import PartitionSpec as P

HD = 64
NF = 8
SEQ = 1024
PIECE = 256
CAP = 768


eps = 1e-06


def rms_factor(values):
    return lax.rsqrt(jnp.mean(values * values, axis=-1, keepdims=True) + eps)


def norm_back(grad, values, factor, gain):
    scaled = grad * gain
    inner = jnp.mean(scaled * values, axis=-1, keepdims=True)
    return factor * scaled - values * factor * factor * factor * inner


def rotary(positions, width):
    place = (jnp.arange(positions) % SEQ).astype(jnp.float32)
    freqs = jnp.power(10000.0, jnp.arange(width // 2).astype(jnp.float32) * (-2.0 / width))
    angles = place[:, None] * freqs[None, :]
    return (jnp.cos(angles)[:, None, :], jnp.sin(angles)[:, None, :])


def rotate(values, cosine, sine):
    half = values.shape[-1] // 2
    front = values[..., :half]
    behind = values[..., half:]
    return jnp.concatenate(
        [front * cosine - behind * sine, behind * cosine + front * sine], axis=-1
    )


def visible(starts):
    position = jnp.arange(SEQ)
    piece_of = jnp.zeros((SEQ,), jnp.int32)
    for index in range(starts.shape[0]):
        inside = (position >= starts[index]) & (position < starts[index] + PIECE)
        piece_of = jnp.where(inside, index + 1, piece_of)
    causal = position[None, :] <= position[:, None]
    same_piece = (piece_of[:, None] > 0) & (piece_of[:, None] == piece_of[None, :])
    return causal | same_piece


def dispatch(route_ids, route_ranks):
    group_rows = route_ids.shape[0]
    retained = (route_ids < NF) & (route_ranks < CAP)
    target = jnp.where(retained, route_ids * CAP + route_ranks, NF * CAP)
    token_index = jnp.broadcast_to(
        jnp.arange(group_rows, dtype=jnp.int32)[:, None], route_ids.shape
    )
    slot_token = (
        jnp.zeros((NF * CAP + 1,), jnp.int32)
        .at[target.reshape(-1)]
        .set(token_index.reshape(-1))[: NF * CAP]
    )
    filled = jnp.zeros((NF * CAP + 1,), jnp.float32).at[target.reshape(-1)].set(1.0)[: NF * CAP]
    return (retained, target, slot_token, filled)


def masked_scores(query, keys, starts):
    scores = jnp.einsum("qhd,khd->hqk", query, keys, preferred_element_type=jnp.float32) * HD ** (
        -0.5
    )
    return jnp.where(visible(starts)[None], scores, -1e30)


def attend_block(parts):
    query, keys, values, starts = parts
    scores = masked_scores(query, keys, starts)
    row_max = jnp.max(scores, axis=-1, keepdims=True)
    denominator = jnp.sum(jnp.exp(scores - row_max), axis=-1, keepdims=True)
    log_total = row_max + jnp.log(denominator)
    shares = jnp.exp(scores - log_total).astype(jnp.bfloat16)
    mixed = jnp.einsum("hqk,khd->qhd", shares, values, preferred_element_type=jnp.float32)
    return (mixed.astype(jnp.bfloat16), log_total)


def attend_back(parts):
    query, keys, values, starts, log_total, grad_out = parts
    shares = jnp.exp(masked_scores(query, keys, starts) - log_total)
    grad_shares = jnp.einsum("qhd,khd->hqk", grad_out, values, preferred_element_type=jnp.float32)
    centre = jnp.sum(shares * grad_shares, axis=-1, keepdims=True)
    grad_scores = (shares * (grad_shares - centre)).astype(jnp.bfloat16)
    factor = HD ** (-0.5)
    grad_query = (
        jnp.einsum("hqk,khd->qhd", grad_scores, keys, preferred_element_type=jnp.float32) * factor
    )
    grad_keys = (
        jnp.einsum("hqk,qhd->khd", grad_scores, query, preferred_element_type=jnp.float32) * factor
    )
    grad_values = jnp.einsum(
        "hqk,qhd->khd", shares.astype(jnp.bfloat16), grad_out, preferred_element_type=jnp.float32
    )
    return (grad_query, grad_keys, grad_values)


def on_device(
    tokens,
    prior_logits,
    expert_ids,
    expert_ranks,
    piece_starts,
    norm_attn,
    qkv_weight,
    out_weight,
    norm_moe,
    router_weight,
    residual_weight,
    const_vectors,
    const_gates,
    w_gate_up,
    w_down,
    out_grad,
):
    highest = lax.Precision.HIGHEST
    local_rows = tokens.shape[0]
    group_rows = expert_ids.shape[0]
    sequences = group_rows // SEQ
    head_count = qkv_weight.shape[2] // HD
    row_start = lax.axis_index("tensor") * local_rows
    seq_shape = (sequences, SEQ, head_count, HD)
    gain_attn = norm_attn.astype(jnp.float32)
    gain_moe = norm_moe.astype(jnp.float32)
    tok_vals = tokens.astype(jnp.float32)
    factor_attn = rms_factor(tok_vals)
    normed_attn = (tok_vals * factor_attn * gain_attn).astype(jnp.bfloat16)
    attn_rows = lax.all_gather(normed_attn, "tensor", axis=0, tiled=True)
    qkv_full, out_full = (
        lax.all_gather(qkv_weight, "dp", axis=1, tiled=True),
        lax.all_gather(out_weight, "dp", axis=1, tiled=True),
    )
    projected = jnp.einsum("gd,cde->cge", attn_rows, qkv_full, preferred_element_type=jnp.float32)
    cosine, sine = rotary(group_rows, HD)
    query = (
        rotate(projected[0].reshape(group_rows, head_count, HD), cosine, sine)
        .astype(jnp.bfloat16)
        .reshape(seq_shape)
    )
    keys = (
        rotate(projected[1].reshape(group_rows, head_count, HD), cosine, sine)
        .astype(jnp.bfloat16)
        .reshape(seq_shape)
    )
    values = projected[2].astype(jnp.bfloat16).reshape(seq_shape)
    mixed, log_total = lax.map(attend_block, (query, keys, values, piece_starts))
    mixed_rows = mixed.reshape(group_rows, head_count * HD)
    attn_part = jnp.dot(mixed_rows, out_full, preferred_element_type=jnp.float32)
    attn_out = lax.psum_scatter(attn_part, "tensor", scatter_dimension=0, tiled=True)
    resid = tok_vals + attn_out
    factor_moe = rms_factor(resid)
    normed_moe = (resid * factor_moe * gain_moe).astype(jnp.bfloat16)
    moe_rows, prior_rows = (
        lax.all_gather(normed_moe, "tensor", axis=0, tiled=True),
        lax.all_gather(prior_logits, "tensor", axis=0, tiled=True),
    )
    logits = jnp.dot(moe_rows, router_weight, preferred_element_type=jnp.float32) + jnp.dot(
        prior_rows, residual_weight, preferred_element_type=jnp.float32
    )
    shares = jax.nn.softmax(logits, axis=-1)
    gates = jnp.take_along_axis(shares, expert_ids, axis=1)
    retained, target, slot_token, filled = dispatch(expert_ids, expert_ranks)
    picker = jnp.minimum(target, NF * CAP - 1)
    slot_gate = (
        jnp.zeros((NF * CAP + 1,), jnp.float32)
        .at[target.reshape(-1)]
        .set(gates.reshape(-1))[: NF * CAP]
        * filled
    )
    expert_rows = (moe_rows[slot_token] * filled[:, None].astype(jnp.bfloat16)).reshape(NF, CAP, -1)
    gate_full, down_full = (
        lax.all_gather(w_gate_up, "dp", axis=2, tiled=True),
        lax.all_gather(w_down, "dp", axis=2, tiled=True),
    )
    gate_up = jnp.einsum(
        "ecd,sedf->secf", expert_rows, gate_full, preferred_element_type=jnp.float32
    )
    sigmoid_vals = jax.nn.sigmoid(gate_up[0])
    activated = gate_up[0] * sigmoid_vals
    hidden = (activated * gate_up[1]).astype(jnp.bfloat16)
    expert_out = jnp.einsum(
        "ecf,efd->ecd", hidden, down_full, preferred_element_type=jnp.float32
    ).reshape(NF * CAP, -1)
    retained_gates = jnp.where(retained, gates, 0.0)
    combined = jnp.sum(retained_gates[:, :, None] * expert_out[picker], axis=1)
    ffn_out = lax.psum_scatter(
        combined.astype(jnp.bfloat16), "tensor", scatter_dimension=0, tiled=True
    ).astype(jnp.float32)
    local_ids = lax.dynamic_slice_in_dim(expert_ids, row_start, local_rows, 0)
    local_shares = lax.dynamic_slice_in_dim(shares, row_start, local_rows, 0)
    local_gates = lax.dynamic_slice_in_dim(gates, row_start, local_rows, 0)
    normed_vals = normed_moe.astype(jnp.float32)
    vectors = const_vectors.astype(jnp.float32)
    gate_mats = const_gates.astype(jnp.float32)
    const_count = vectors.shape[0]
    copy_share = jnp.sum(jnp.where(local_ids == NF + 1, local_gates, 0.0), axis=1)
    const_share = jnp.stack(
        [
            jnp.sum(jnp.where(local_ids == NF + 2 + index, local_gates, 0.0), axis=1)
            for index in range(const_count)
        ],
        axis=1,
    )
    mixing = jax.nn.softmax(
        jnp.einsum("gd,cjd->gcj", normed_vals, gate_mats, precision=highest), axis=-1
    )
    const_out = (
        mixing[:, :, 0:1] * normed_vals[:, None, :] + mixing[:, :, 1:2] * vectors[None, :, :]
    )
    others = copy_share[:, None] * normed_vals + jnp.sum(
        const_share[:, :, None] * const_out, axis=1
    )
    layer_out = (resid + ffn_out + others).astype(jnp.bfloat16)
    grad_out = out_grad.astype(jnp.float32)
    grad_moe_rows = lax.all_gather(out_grad, "tensor", axis=0, tiled=True)
    gate_back, down_back = (
        lax.all_gather(w_gate_up, "dp", axis=2, tiled=True),
        lax.all_gather(w_down, "dp", axis=2, tiled=True),
    )
    slot_grads = grad_moe_rows[slot_token].astype(jnp.float32)
    grad_expert = (slot_gate[:, None] * slot_grads).astype(jnp.bfloat16).reshape(NF, CAP, -1)
    slot_inner = jnp.sum(slot_grads * expert_out, axis=-1)
    gate_grad_ffn = jnp.where(retained, slot_inner[picker], 0.0)
    down_grad = jnp.einsum("ecf,ecd->efd", hidden, grad_expert, preferred_element_type=jnp.float32)
    grad_hidden = jnp.einsum(
        "ecd,efd->ecf", grad_expert, down_back, preferred_element_type=jnp.float32
    )
    slope = sigmoid_vals * (1.0 + gate_up[0] * (1.0 - sigmoid_vals))
    grad_gate_up = jnp.stack([grad_hidden * gate_up[1] * slope, grad_hidden * activated]).astype(
        jnp.bfloat16
    )
    gate_up_grad = jnp.einsum(
        "ecd,secf->sedf", expert_rows, grad_gate_up, preferred_element_type=jnp.float32
    )
    slot_input_grad = jnp.einsum(
        "secf,sedf->ecd", grad_gate_up, gate_back, preferred_element_type=jnp.float32
    ).reshape(NF * CAP, -1)
    grad_ffn_in = jnp.sum(jnp.where(retained[:, :, None], slot_input_grad[picker], 0.0), axis=1)
    gate_up_grad, down_grad = (
        lax.psum_scatter(gate_up_grad, "dp", scatter_dimension=2, tiled=True),
        lax.psum_scatter(down_grad, "dp", scatter_dimension=2, tiled=True),
    )
    grad_ffn_in, gate_grad_ffn = (
        lax.psum_scatter(grad_ffn_in, "tensor", scatter_dimension=0, tiled=True),
        lax.psum_scatter(gate_grad_ffn, "tensor", scatter_dimension=0, tiled=True),
    )
    copy_inner = jnp.sum(grad_out * normed_vals, axis=-1)
    const_inner = jnp.sum(grad_out[:, None, :] * const_out, axis=-1)
    choice_inner = jnp.where(local_ids == NF + 1, copy_inner[:, None], 0.0)
    for index in range(const_count):
        choice_inner = choice_inner + jnp.where(
            local_ids == NF + 2 + index, const_inner[:, index : index + 1], 0.0
        )
    gate_grad = gate_grad_ffn + choice_inner
    expert_range = jnp.arange(shares.shape[1])
    onehot = (local_ids[:, :, None] == expert_range[None, None, :]).astype(jnp.float32)
    grad_router = jnp.sum(onehot * gate_grad[:, :, None], axis=1)
    grad_logits = local_shares * (
        grad_router - jnp.sum(local_shares * grad_router, axis=-1, keepdims=True)
    )
    prior_vals = prior_logits.astype(jnp.float32)
    router_grad = jnp.dot(normed_vals.T, grad_logits, precision=highest)
    residual_grad = jnp.dot(prior_vals.T, grad_logits, precision=highest)
    prior_grad = jnp.dot(grad_logits, residual_weight.astype(jnp.float32).T, precision=highest)
    vector_inner = jnp.dot(grad_out, vectors.T, precision=highest)
    grad_mixing = const_share[:, :, None] * jnp.stack(
        [jnp.broadcast_to(copy_inner[:, None], vector_inner.shape), vector_inner], axis=-1
    )
    grad_blend = mixing * (grad_mixing - jnp.sum(mixing * grad_mixing, axis=-1, keepdims=True))
    const_gate_grad = jnp.einsum("gcj,gd->cjd", grad_blend, normed_vals, precision=highest)
    const_vector_grad = jnp.einsum(
        "gc,gd->cd", const_share * mixing[:, :, 1], grad_out, precision=highest
    )
    direct_share = copy_share + jnp.sum(const_share * mixing[:, :, 0], axis=1)
    grad_moe_in = (
        grad_ffn_in
        + jnp.dot(grad_logits, router_weight.astype(jnp.float32).T, precision=highest)
        + direct_share[:, None] * grad_out
        + jnp.einsum("gcj,cjd->gd", grad_blend, gate_mats, precision=highest)
    )
    norm_moe_grad = jnp.sum(grad_moe_in * resid * factor_moe, axis=0)
    grad_resid = grad_out + norm_back(grad_moe_in, resid, factor_moe, gain_moe)
    grad_mixed_out = grad_resid.astype(jnp.bfloat16)
    grad_attn_rows = lax.all_gather(grad_mixed_out, "tensor", axis=0, tiled=True)
    out_weight_grad = jnp.dot(mixed_rows.T, grad_attn_rows, preferred_element_type=jnp.float32)
    grad_mixed = jnp.dot(grad_attn_rows, out_full.T, preferred_element_type=jnp.float32).astype(
        jnp.bfloat16
    )
    grad_query, grad_keys, grad_values = lax.map(
        attend_back, (query, keys, values, piece_starts, log_total, grad_mixed.reshape(seq_shape))
    )
    grad_query = rotate(grad_query.reshape(group_rows, head_count, HD), cosine, -sine).reshape(
        group_rows, -1
    )
    grad_keys = rotate(grad_keys.reshape(group_rows, head_count, HD), cosine, -sine).reshape(
        group_rows, -1
    )
    grad_proj = jnp.stack([grad_query, grad_keys, grad_values.reshape(group_rows, -1)]).astype(
        jnp.bfloat16
    )
    qkv_grad = jnp.einsum("gd,cge->cde", attn_rows, grad_proj, preferred_element_type=jnp.float32)
    qkv_grad, out_weight_grad = (
        lax.psum_scatter(qkv_grad, "dp", scatter_dimension=1, tiled=True),
        lax.psum_scatter(out_weight_grad, "dp", scatter_dimension=1, tiled=True),
    )
    grad_attn_part = jnp.einsum(
        "cge,cde->gd", grad_proj, qkv_full, preferred_element_type=jnp.float32
    )
    grad_attn_in = lax.psum_scatter(
        grad_attn_part.astype(jnp.bfloat16), "tensor", scatter_dimension=0, tiled=True
    ).astype(jnp.float32)
    norm_attn_grad = jnp.sum(grad_attn_in * tok_vals * factor_attn, axis=0)
    input_grad = grad_resid + norm_back(grad_attn_in, tok_vals, factor_attn, gain_attn)
    summed = lax.psum(
        (
            norm_attn_grad,
            norm_moe_grad,
            router_grad,
            residual_grad,
            const_vector_grad,
            const_gate_grad,
        ),
        ("dp", "tensor"),
    )
    return (
        layer_out,
        input_grad,
        prior_grad,
        summed[0],
        qkv_grad,
        out_weight_grad,
        summed[1],
        summed[2],
        summed[3],
        summed[4],
        summed[5],
        gate_up_grad,
        down_grad,
    )


def solution(mesh):
    return jax.shard_map(
        on_device,
        mesh=mesh,
        in_specs=(
            P(("dp", "tensor"), None),
            P(("dp", "tensor"), None),
            P("dp", None),
            P("dp", None),
            P("dp", None),
            P(),
            P(None, "dp", "tensor"),
            P("tensor", "dp"),
            P(),
            P(),
            P(),
            P(),
            P(),
            P(None, None, "dp", "tensor"),
            P(None, "tensor", "dp"),
            P(("dp", "tensor"), None),
        ),
        out_specs=(
            P(("dp", "tensor"), None),
            P(("dp", "tensor"), None),
            P(("dp", "tensor"), None),
            P(),
            P(None, "dp", "tensor"),
            P("tensor", "dp"),
            P(),
            P(),
            P(),
            P(),
            P(),
            P(None, None, "dp", "tensor"),
            P(None, "tensor", "dp"),
        ),
        check_vma=False,
    )
```

profile of v0, /device:TPU:0, one launch (start us, length us, event | category | flops | bytes accessed | tf_op | source)
XLA Modules:
  0.0 2311.5 jit_solution(15294237833634498149)
XLA Ops:
  13.6 14.6 all_gather.30
  30.4 9.7 all_gather.31
  43.3 88.3 %all-gather.7.cloned.1.call-done = bf16[4096,768]{1,0:T(8,128)(2,1)} async-done(((bf16[1024,768]{1,0:T(8,128)(2,1)}), bf16[4096,768]{1,0:T(8,128)(2,1)}) %all-gather.7.cloned.1.call-update) | async-done | bytes 6291472 | tf_op jit(solution)/shard_map/all_gather | solution.py:136
  162.3 78.4 %while.26 = (s32[]{:T(128)}, bf16[4,1024,3,64]{1,3,2,0:T(8,128)(2,1)}, f32[4,3,1024,1]{2,1,3,0:T(4,128)}, bf16[4,1024,3,64]{1,3,2,0:T(8,128)(2,1)}, s32[4,2]{0,1...) while((s32[]{:T(128)}, ...), condition=%wide.region_4.5_spmd, body=%wide.region_1.4_spmd.sunk | while | flops 844314624 | bytes 47825620 | solution.py:154
  252.3 209.6 %reduce-scatter.16.cloned.1.call-done = f32[1024,768]{1,0:T(8,128)} async-done(((f32[4096,768]{1,0:T(8,128)}), f32[1024,768]{1,0:T(8,128)}) %reduce-scatter.16.cloned.1.call-update) | async-done | bytes 3145744 | tf_op jit(solution)/shard_map/reduce_scatter | solution.py:157
  474.1 20.2 all_gather.33
  494.3 90.6 %all-gather.9.cloned.1.call-done = bf16[4096,768]{1,0:T(8,128)(2,1)} async-done(((bf16[1024,768]{1,0:T(8,128)(2,1)}), bf16[4096,768]{1,0:T(8,128)(2,1)}) %all-gather.9.cloned.1.call-update) | async-done | bytes 6291472 | tf_op jit(solution)/shard_map/all_gather | solution.py:162
  589.8 65.5 %gather_fusion.5 = f32[8192]{0:T(1024)S(1)} fusion(f32[4096,12]{0,1:T(8,128)S(1)} %fusion.110, s32[8192]{0:T(1024)S(1)} %reshape.523), kind=kCustom, calls=%fused_computation.5 | custom fusion | bytes 131072 | tf_op jit(solution)/shard_map/jit(take_along_axis)/gather | solution.py:169
  664.3 30.5 %scatter_custom_fusion.2 = f32[6145]{0:T(1024)S(1)} fusion(s32[8192]{0:T(1024)S(1)} %bitcast.295, f32[8192]{0:T(1024)S(1)} %reshape.549, f32[]{:T(128)} %constant.72.clone.1), kind=kCustom, calls=%fused_computation.211 | custom fusion | bytes 24584 | tf_op jit(solution)/shard_map/scatter | solution.py:175
  694.9 30.5 %scatter_custom_fusion.1 = f32[6145]{0:T(1024)S(1)} fusion(s32[8192]{0:T(1024)S(1)} %bitcast.296, f32[8192]{0:T(1024)S(1)} %broadcast.468, f32[]{:T(128)} %constant.72.clone.1), kind=kCustom, calls=%fused_computation.213 | custom fusion | bytes 24584 | tf_op jit(solution)/shard_map/scatter | solution.py:65
  725.4 30.9 %scatter_custom_fusion = s32[6145]{0:T(1024)S(1)} fusion(s32[8192]{0:T(1024)S(1)} %bitcast.297, s32[8192]{0:T(1024)} %reshape.533, s32[]{:T(128)} %constant.70.clone.1), kind=kCustom, calls=%fused_computation.215 | custom fusion | bytes 25092 | tf_op jit(solution)/shard_map/scatter | solution.py:63
  756.3 32.4 %gather_fusion = bf16[6144,768]{1,0:T(8,128)(2,1)} fusion(bf16[4096,768]{1,0:T(8,128)(2,1)} %all-gather.9.cloned.1.call-done, s32[6144]{0:T(1024)S(1)} %fusion.114), kind=kCustom, calls=%fused_computation | custom fusion | bytes 18898944 | tf_op jit(solution)/shard_map/gather | solution.py:178
  788.8 31.8 %gather_fusion.2 = bf16[6144,768]{1,0:T(8,128)(2,1)} fusion(bf16[4096,768]{1,0:T(8,128)(2,1)} %all-gather.15.cloned.1.call-done, s32[6144]{0:T(1024)S(1)} %fusion.114), kind=kCustom, calls=%fused_computation.2 | custom fusion | bytes 18898944 | tf_op jit(solution)/shard_map/gather | solution.py:228
  820.5 12.2 fusion.81
  832.7 20.8 fusion.69
  853.5 22.3 fusion.86
  875.8 14.5 fusion.60
  892.2 45.5 %gather_fusion.4 = f32[8192]{0:T(1024)S(1)} fusion(f32[6144]{0:T(1024)S(1)} %reduce_sum.220, s32[8192]{0:T(1024)S(1)} %broadcast_clamp_fusion), kind=kCustom, calls=%fused_computation.4 | custom fusion | bytes 98304 | tf_op jit(solution)/shard_map/gather | solution.py:231
  942.6 18.5 fusion.63
  961.0 45.9 %gather_fusion.3 = f32[8192,768]{1,0:T(8,128)} fusion(f32[6144,768]{1,0:T(8,128)} %bitcast.268, s32[8192]{0:T(1024)S(1)} %broadcast_clamp_fusion), kind=kCustom, calls=%fused_computation.3 | custom fusion | bytes 50364416 | tf_op jit(solution)/shard_map/gather | solution.py:246
  1006.9 29.1 %reshape.508 = f32[4096,2,768]{2,1,0:T(2,128)} reshape(f32[8192,768]{1,0:T(8,128)} %gather_fusion.3) | data formatting | bytes 50331648 | tf_op jit(solution)/shard_map/gather | solution.py:246
  1036.0 43.5 %select_reduce_fusion = f32[4096,768]{1,0:T(8,128)} fusion(f32[4096,2,768]{2,1,0:T(2,128)} %reshape.508, pred[4096,2]{1,0:T(8,128)(4,1)S(1)} %copy-done.22), kind=kLoop, calls=%fused_computation.90 | loop fusion | flops 9437184 | bytes 37756928 | tf_op jit(solution)/shard_map/reduce_sum | solution.py:246
  1096.2 194.3 %reduce-scatter.20.cloned.1.call-done = f32[1024,768]{1,0:T(8,128)} async-done(((f32[4096,768]{1,0:T(8,128)}), f32[1024,768]{1,0:T(8,128)}) %reduce-scatter.20.cloned.1.call-update) | async-done | bytes 3145744 | tf_op jit(solution)/shard_map/reduce_scatter | solution.py:252
  1301.3 116.5 %all-gather.17.cloned.1.call-done = bf16[4096,768]{1,0:T(8,128)(2,1)} async-done(((bf16[1024,768]{1,0:T(8,128)(2,1)}), bf16[4096,768]{1,0:T(8,128)(2,1)}) %all-gather.17.cloned.1.call-update) | async-done | bytes 6291472 | tf_op jit(solution)/shard_map/all_gather | solution.py:292
  1425.6 292.8 %while.27 = (s32[]{:T(128)}, f32[4,1024,3,64]{1,0,3,2:T(4,128)}, f32[4,1024,3,64]{1,0,3,2:T(4,128)}, bf16[4,1024,3,64]{1,3,2,0:T(8,128)(2,1)}, bf16[4,1024,3,64]...) while((s32[]{:T(128)}, f32[4,1024,3,64]{1,0,3,2:T(4,128)}, ...), condition=%wide.region_33.34_spmd, body=%wide.region_31.33_spmd.sunk | while | flops 2065053696 | bytes 164595984 | solution.py:297
  1454.5 15.3 dynamic_update_slice.30
  1474.7 15.3 dynamic_update_slice.29
  1490.0 8.9 fusion.215
  1527.6 15.3 dynamic_update_slice.30
  1547.8 15.3 dynamic_update_slice.29
  1563.1 8.9 fusion.215
  1600.7 15.3 dynamic_update_slice.30
  1620.9 15.3 dynamic_update_slice.29
  1636.2 8.9 fusion.215
  1673.8 15.3 dynamic_update_slice.30
  1694.0 15.3 dynamic_update_slice.29
  1709.3 8.9 fusion.215
  1761.2 22.7 fusion.72
  1783.9 25.4 %copy.255 = f32[2,8,768,512]{3,1,0,2:T(8,128)} copy(f32[2,8,768,512]{2,3,0,1:T(8,128)} %fusion.72) | data formatting | bytes 50331648 | tf_op jit(solution)/shard_map/ecd,secf->sedf/transpose | solution.py:240
  1820.6 45.8 %gather_fusion.1 = f32[8192,768]{1,0:T(8,128)} fusion(f32[6144,768]{1,0:T(8,128)} %bitcast.267, s32[8192]{0:T(1024)S(1)} %copy-done.5), kind=kCustom, calls=%fused_computation.1 | custom fusion | bytes 50364416 | tf_op jit(solution)/shard_map/gather | solution.py:193
  1866.4 30.0 %reshape.492 = f32[4096,2,768]{2,1,0:T(2,128)} reshape(f32[8192,768]{1,0:T(8,128)} %gather_fusion.1) | data formatting | bytes 50331648 | tf_op jit(solution)/shard_map/gather | solution.py:193
  1897.0 37.9 %multiply_reduce_fusion.1 = bf16[4096,768]{1,0:T(8,128)(2,1)} fusion(f32[4096,2,768]{2,1,0:T(2,128)} %reshape.492, f32[4096,2]{1,0:T(8,128)S(1)} %copy.236), kind=kLoop, calls=%fused_computation.91 | loop fusion | flops 9437184 | bytes 31490048 | tf_op jit(solution)/shard_map/reduce_sum | solution.py:193
  1935.7 11.9 fusion.79
  1957.6 22.8 reduce-scatter.24.cloned.1.call-done
  1985.7 107.7 %reduce-scatter.22.cloned.1.call-done = bf16[1024,768]{1,0:T(8,128)(2,1)} async-done(((bf16[4096,768]{1,0:T(8,128)(2,1)}), bf16[1024,768]{1,0:T(8,128)(2,1)}) %reduce-scatter.22.cloned.1.call-update) | async-done | bytes 1572880 | tf_op jit(solution)/shard_map/reduce_scatter | solution.py:317
  2096.7 50.8 %all-reduce = (f32[768]{0:T(1024)}, f32[768]{0:T(1024)}, f32[768,12]{0,1:T(8,128)}, f32[12,12]{0,1:T(8,128)S(1)}, f32[2,768]{1,0:T(2,128)}, /*index=5*/f32[2,2,768]{2,1,0:T(2,128)}) all-reduce(f32[768]{0:T(1024)S(1)} %get-tuple-element.294, f32[768]{0:T(1024)S(1)} %copy-done.80, ...), channel_id=1, replica_groups=mesh['dp'=8,'tensor'=4] {'dp','tensor'}, use_global_device_ids=true, to_apply=%region_37.38 | all-reduce | flops 15504 | bytes 124032 | tf_op jit(solution)/shard_map/psum | solution.py:322
  2148.2 59.7 %reduce-scatter.18.cloned.1.call-done = bf16[1024,768]{1,0:T(8,128)(2,1)} async-done(((bf16[4096,768]{1,0:T(8,128)(2,1)}), bf16[1024,768]{1,0:T(8,128)(2,1)}) %reduce-scatter.18.cloned.1.call-update) | async-done | bytes 1572880 | tf_op jit(solution)/shard_map/reduce_scatter | solution.py:194
  2215.8 89.0 %reduce-scatter.26.cloned.1.call-done = f32[8,512,96]{1,2,0:T(8,128)} async-done(((f32[8,512,768]{1,2,0:T(8,128)}), f32[8,512,96]{1,2,0:T(8,128)}) %reduce-scatter.26.cloned.1.call-update) | async-done | bytes 1572880 | tf_op jit(solution)/shard_map/reduce_scatter | solution.py:249
  (437 shorter events, 406.3 us)
Async XLA Ops:
  7.2 577.7 %copy-start = (bf16[768,12]{0,1:T(8,128)(2,1)S(1)}, bf16[768,12]{0,1:T(8,128)(2,1)}, u32[]{:S(2)}) copy-start(bf16[768,12]{0,1:T(8,128)(2,1)} %param.29) | copy-start | bytes 55300
  7.2 124.4 %all-gather.7.cloned.1.call-start = ((), (), s32[]{:S(2)}) async-start(), calls=%async_computation.9 | async-start | bytes 7864320 | tf_op jit(solution)/shard_map/all_gather | solution.py:136
  13.4 17.0 copy-start.69
  13.4 448.5 %reduce-scatter.16.cloned.1.call-start = ((), (), s32[]{:S(2)}) async-start(), calls=%async_computation.10 | async-start | bytes 15728640 | tf_op jit(solution)/shard_map/reduce_scatter | solution.py:157
  43.3 95.4 %copy-start.19 = (f32[4096,32]{0,1:T(8,128)}, f32[4096,32]{0,1:T(8,128)S(1)}, u32[]{:S(2)}) copy-start(f32[4096,32]{0,1:T(8,128)S(1)} %get-tuple-element.382) | copy-start | bytes 1572868
  251.6 210.3 %copy-start.15 = (bf16[1024,768]{1,0:T(8,128)(2,1)S(1)}, bf16[1024,768]{1,0:T(8,128)(2,1)}, u32[]{:S(2)}) copy-start(bf16[1024,768]{1,0:T(8,128)(2,1)} %param.20) | copy-start | bytes 4718596
  251.6 333.2 %all-gather.9.cloned.1.call-start = ((), (), s32[]{:S(2)}) async-start(), calls=%async_computation.11 | async-start | bytes 7864320 | tf_op jit(solution)/shard_map/all_gather | solution.py:162
  252.3 212.0 %copy-start.49 = (f32[768]{0:T(1024)}, f32[768]{0:T(1024)S(1)}, u32[]{:S(2)}) copy-start(f32[768]{0:T(1024)S(1)} %convert_element_type.179) | copy-start | bytes 9220
  252.3 212.0 %copy-start.8 = (bf16[1024,768]{1,0:T(8,128)(2,1)S(1)}, bf16[1024,768]{1,0:T(8,128)(2,1)}, u32[]{:S(2)}) copy-start(bf16[1024,768]{1,0:T(8,128)(2,1)} %param.35) | copy-start | bytes 4718596
  467.1 321.7 %all-gather.15.cloned.1.call-start = ((), (), s32[]{:S(2)}) async-start(), calls=%async_computation.15 | async-start | bytes 7864320 | tf_op jit(solution)/shard_map/all_gather | solution.py:223
  467.7 352.9 %all-gather.13.cloned.1.call-start = ((), (), s32[]{:S(2)}) async-start(), calls=%async_computation.13 | async-start | bytes 7077888 | tf_op jit(solution)/shard_map/all_gather | solution.py:181
  468.2 364.5 %all-gather.11.cloned.1.call-start = ((), (), s32[]{:S(2)}) async-start(), calls=%async_computation.12 | async-start | bytes 14155776 | tf_op jit(solution)/shard_map/all_gather | solution.py:180
  469.8 621.2 %reduce-scatter.28.cloned.1.call-start = ((), (), s32[]{:S(2)}) async-start(), calls=%async_computation.21 | async-start | bytes 2621440
  494.3 95.1 %copy-start.78 = (bf16[12,12]{1,0:T(8,128)(2,1)S(1)}, bf16[12,12]{1,0:T(8,128)(2,1)}, u32[]{:S(2)}) copy-start(bf16[12,12]{1,0:T(8,128)(2,1)} %param.30) | copy-start | bytes 868
  589.8 65.6 %copy-start.1 = (f32[4096,12]{0,1:T(8,128)}, f32[4096,12]{0,1:T(8,128)S(1)}, u32[]{:S(2)}) copy-start(f32[4096,12]{0,1:T(8,128)S(1)} %fusion.110) | copy-start | bytes 589828
  725.4 95.1 %copy-start.76 = (f32[8,768]{1,0:T(8,128)}, f32[8,768]{1,0:T(8,128)S(1)}, u32[]{:S(2)}) copy-start(f32[8,768]{1,0:T(8,128)S(1)} %mul.648) | copy-start | bytes 73732
  756.3 76.4 %copy-start.81 = (bf16[8,768]{1,0:T(8,128)(2,1)}, bf16[8,768]{1,0:T(8,128)(2,1)S(1)}, u32[]{:S(2)}) copy-start(bf16[8,768]{1,0:T(8,128)(2,1)S(1)} %convert_element_type.182) | copy-start | bytes 36868
  892.2 68.8 %copy-start.4 = (s32[8192]{0:T(1024)}, s32[8192]{0:T(1024)S(1)}, u32[]{:S(2)}) copy-start(s32[8192]{0:T(1024)S(1)} %broadcast_clamp_fusion) | copy-start | bytes 98308
  942.5 348.0 %reduce-scatter.20.cloned.1.call-start = ((), (), s32[]{:S(2)}) async-start(), calls=%async_computation.16 | async-start | bytes 15728640 | tf_op jit(solution)/shard_map/reduce_scatter | solution.py:252
  1006.9 29.1 %copy-start.22 = (pred[4096,2]{1,0:T(8,128)(4,1)S(1)}, pred[4096,2]{1,0:T(8,128)(4,1)}, u32[]{:S(2)}) copy-start(pred[4096,2]{1,0:T(8,128)(4,1)} %copy.242) | copy-start | bytes 24580
  1079.6 338.2 %all-gather.17.cloned.1.call-start = ((), (), s32[]{:S(2)}) async-start(), calls=%async_computation.17 | async-start | bytes 7864320 | tf_op jit(solution)/shard_map/all_gather | solution.py:292
  1083.3 207.2 %copy-start.41 = (f32[1024,2,1]{0,2,1:T(1,128)}, f32[1024,2,1]{0,2,1:T(1,128)S(1)}, u32[]{:S(2)}) copy-start(f32[1024,2,1]{0,2,1:T(1,128)S(1)} %stack.37) | copy-start | bytes 24580
  1085.9 204.6 %copy-start.37 = (f32[1024,2]{0,1:T(2,128)}, f32[1024,2]{0,1:T(2,128)S(1)}, u32[]{:S(2)}) copy-start(f32[1024,2]{0,1:T(2,128)S(1)} %pad_maximum_fusion.10) | copy-start | bytes 24580
  1086.0 204.6 %copy-start.43 = (f32[1024,2,1]{0,2,1:T(1,128)}, f32[1024,2,1]{0,2,1:T(1,128)S(1)}, u32[]{:S(2)}) copy-start(f32[1024,2,1]{0,2,1:T(1,128)S(1)} %stack_broadcast_in_dim.2) | copy-start | bytes 24580
  1086.0 204.5 %copy-start.33 = (f32[1024,2,2]{0,2,1:T(2,128)}, f32[1024,2,2]{0,2,1:T(2,128)S(1)}, u32[]{:S(2)}) copy-start(f32[1024,2,2]{0,2,1:T(2,128)S(1)} %get-tuple-element.342) | copy-start | bytes 49156
  1086.0 204.5 %copy-start.57 = (f32[1024,2]{0,1:T(2,128)}, f32[1024,2]{0,1:T(2,128)S(1)}, u32[]{:S(2)}) copy-start(f32[1024,2]{0,1:T(2,128)S(1)} %get-tuple-element.341) | copy-start | bytes 24580
  1091.0 199.6 %copy-start.50 = (f32[768]{0:T(1024)S(1)}, f32[768]{0:T(1024)}, u32[]{:S(2)}) copy-start(f32[768]{0:T(1024)} %copy-done.49) | copy-start | bytes 9220
  1091.0 199.6 %copy-start.53 = (f32[1024]{0:T(1024)S(1)}, f32[1024]{0:T(1024)}, u32[]{:S(2)}) copy-start(f32[1024]{0:T(1024)} %copy-done.52) | copy-start | bytes 12292
  1290.6 8.4 copy-start.12
  1298.9 118.9 %copy-start.21 = (bf16[192,768]{0,1:T(8,128)(2,1)S(1)}, bf16[192,768]{0,1:T(8,128)(2,1)}, u32[]{:S(2)}) copy-start(bf16[192,768]{0,1:T(8,128)(2,1)} %all_gather.31) | copy-start | bytes 884740
  1301.2 651.0 %reduce-scatter.32.cloned.1.call-start = ((), (), s32[]{:S(2)}) async-start(), calls=%async_computation.23 | async-start | bytes 884736
  1473.9 16.1 copy-start.6
  1547.0 16.1 copy-start.6
  1620.1 16.1 copy-start.6
  1693.2 16.1 copy-start.6
  1741.9 212.0 %reduce-scatter.30.cloned.1.call-start = ((), (), s32[]{:S(2)}) async-start(), calls=%async_computation.22 | async-start | bytes 2211840
  1761.2 219.2 %reduce-scatter.24.cloned.1.call-start = ((), (), s32[]{:S(2)}) async-start(), calls=%async_computation.19 | async-start | bytes 28311552 | tf_op jit(solution)/shard_map/reduce_scatter | solution.py:248
  1809.4 284.0 %reduce-scatter.22.cloned.1.call-start = ((), (), s32[]{:S(2)}) async-start(), calls=%async_computation.18 | async-start | bytes 7864320 | tf_op jit(solution)/shard_map/reduce_scatter | solution.py:317
  1819.9 388.0 %reduce-scatter.18.cloned.1.call-start = ((), (), s32[]{:S(2)}) async-start(), calls=%async_computation.14 | async-start | bytes 7864320 | tf_op jit(solution)/shard_map/reduce_scatter | solution.py:194
  1866.4 30.0 %copy-start.45 = (f32[4096,2]{0,1:T(2,128)S(1)}, f32[4096,2]{0,1:T(2,128)}, u32[]{:S(2)}) copy-start(f32[4096,2]{0,1:T(2,128)} %get-tuple-element.345) | copy-start | bytes 98308
  1935.0 369.8 %reduce-scatter.26.cloned.1.call-start = ((), (), s32[]{:S(2)}) async-start(), calls=%async_computation.20 | async-start | bytes 14155776 | tf_op jit(solution)/shard_map/reduce_scatter | solution.py:249
  1957.5 135.9 %copy-start.62 = (f32[1024]{0:T(1024)S(1)}, f32[1024]{0:T(1024)}, u32[]{:S(2)}) copy-start(f32[1024]{0:T(1024)} %copy-done.61) | copy-start | bytes 12292
  1957.6 135.9 %copy-start.64 = (f32[768]{0:T(1024)S(1)}, f32[768]{0:T(1024)}, u32[]{:S(2)}) copy-start(f32[768]{0:T(1024)} %copy-done.63) | copy-start | bytes 9220
  1985.7 111.0 %copy-start.80 = (f32[768]{0:T(1024)S(1)}, f32[768]{0:T(1024)}, u32[]{:S(2)}) copy-start(f32[768]{0:T(1024)} %get-tuple-element.290) | copy-start | bytes 9220
  1985.7 222.2 %copy-start.51 = (f32[768]{0:T(1024)S(1)}, f32[768]{0:T(1024)}, u32[]{:S(2)}) copy-start(f32[768]{0:T(1024)} %copy-done.49) | copy-start | bytes 9220
  1985.7 222.2 %copy-start.54 = (f32[1024]{0:T(1024)S(1)}, f32[1024]{0:T(1024)}, u32[]{:S(2)}) copy-start(f32[1024]{0:T(1024)} %copy-done.52) | copy-start | bytes 12292
  1985.7 222.2 %copy-start.71 = (f32[1024]{0:T(1024)S(1)}, f32[1024]{0:T(1024)}, u32[]{:S(2)}) copy-start(f32[1024]{0:T(1024)} %copy-done.70) | copy-start | bytes 12292
  1985.7 222.2 %copy-start.73 = (f32[1024]{0:T(1024)S(1)}, f32[1024]{0:T(1024)}, u32[]{:S(2)}) copy-start(f32[1024]{0:T(1024)} %copy-done.72) | copy-start | bytes 12292
  (61 other events, 172.7 us)
Sparse Core Ops, SparseCore 0:
  13.5 118.0 all-gather.6
  251.8 210.0 reduce-scatter.15
  467.2 117.6 all-gather.8
  586.3 114.2 all-gather.14
  702.3 43.7 all-gather.12
  748.4 72.1 all-gather.10
  942.6 42.8 reduce-scatter.27
  1079.7 210.8 reduce-scatter.19
  1301.4 116.3 all-gather.16
  1742.0 33.1 reduce-scatter.31
  1779.6 40.2 reduce-scatter.29
  1823.4 156.8 reduce-scatter.23
  1982.6 110.7 reduce-scatter.21
  2095.6 112.2 reduce-scatter.17
  2211.8 92.8 reduce-scatter.25
where the time goes:
time: 2320 us; the launch traced here: 2310 us
  waiting for transfers between devices  980 us (42%)
  local copies, waits for them, and re-layouts  674 us (29%)
  matrix products  310 us (13%)
  other arithmetic  226 us (10%)
  blocking collectives  95.2 us (4%)
    reduce_scatter x1, waiting for transfers between devices, on_device(): lax.psum_scatter(attn_part, 'tensor', scatter_dimension=0, tiled=True)  210 us
    reduce_scatter x1, waiting for transfers between devices, on_device(): lax.psum_scatter(grad_ffn_in, 'tensor', scatter_dimension=0, tiled=True)  194 us
    dynamic_update_slice x16, local copies, waits for them, and re-layouts, on_device(): lax.map(attend_back, (query, keys, values, piece_starts, log_total, grad_...  129 us
    all_gather x1, waiting for transfers between devices, on_device(): lax.all_gather(grad_mixed_out, 'tensor', axis=0, tiled=True)  116 us
    reduce_scatter x1, waiting for transfers between devices, on_device(): lax.psum_scatter(grad_attn_part.astype(jnp.bfloat16), 'tensor', scatter_d...  108 us
    all_gather x1, waiting for transfers between devices, on_device(): lax.all_gather(normed_moe, 'tensor', axis=0, tiled=True)  90.6 us
    reduce_scatter x1, waiting for transfers between devices, on_device(): lax.psum_scatter(down_grad, 'dp', scatter_dimension=2, tiled=True)  89 us
    all_gather x1, waiting for transfers between devices, on_device(): attn_rows = lax.all_gather(normed_attn, 'tensor', axis=0, tiled=True)  88.3 us
  transfers between devices with their start and end apart: 15, of which 9 were waited for; matrix products, arithmetic and copies ran while one was open for 27% of the time, Pallas kernels for 0%

commit v1 on v0

v1 whole, which is shorter than its diff:
```python
import functools

import jax
import jax.numpy as jnp
import numpy as np
from jax import lax
from jax.experimental import pallas as pl
from jax.experimental.pallas import tpu as pltpu
from jax.sharding import PartitionSpec as P

HD = 64
NF = 8
NC = 2
SEQ = 1024
PIECE = 256
PIECES = 2
CAP = 768
EPS = 1e-06
QT = 256
LANES = 128
TM = 256
WIN = 256
Z0 = 16

bf16 = jnp.bfloat16
f32 = jnp.float32
i32 = jnp.int32

VM = pl.BlockSpec(memory_space=pltpu.VMEM)
SM = pl.BlockSpec(memory_space=pltpu.SMEM)
ANY = pl.BlockSpec(memory_space=pl.ANY)


def nn(a, b):
    return lax.dot_general(a, b, (((1,), (0,)), ((), ())), preferred_element_type=f32)


def nt(a, b):
    return lax.dot_general(a, b, (((1,), (1,)), ((), ())), preferred_element_type=f32)


def tn(a, b):
    return lax.dot_general(a, b, (((0,), (0,)), ((), ())), preferred_element_type=f32)


def split(x):
    hi = x.astype(bf16)
    return hi, (x - hi.astype(f32)).astype(bf16)


def lanes(rows):
    return lax.broadcasted_iota(i32, (rows, LANES), 1)


def rot(x, cosine, sine):
    first = lanes(x.shape[0]) % HD < HD // 2
    other = jnp.where(first, pltpu.roll(x, LANES - HD // 2, 1), pltpu.roll(x, HD // 2, 1))
    return x * cosine + other * sine


def head_masks():
    low = lax.broadcasted_iota(i32, (1, LANES), 1) < HD
    a = jnp.where(low, 1.0, 0.0)
    return a, 1.0 - a


def rotary_tables():
    place = np.arange(SEQ, dtype=np.float32)
    half = HD // 2
    freqs = np.power(np.float32(10000.0), np.arange(half, dtype=np.float32) * np.float32(-2.0 / HD)).astype(np.float32)
    angles = (place[:, None] * freqs[None, :]).astype(np.float32).astype(np.float64)
    c, s = np.cos(angles).astype(np.float32), np.sin(angles).astype(np.float32)
    return np.concatenate([c, c, c, c], 1), np.concatenate([-s, s, -s, s], 1)


def window_bias(starts_ref, tile, width, transposed):
    shape = (width, QT) if transposed else (QT, width)
    qpos = lax.broadcasted_iota(i32, shape, 1 if transposed else 0) + tile * QT
    kpos = lax.broadcasted_iota(i32, shape, 0 if transposed else 1) + tile * QT
    seen = jnp.where(kpos <= qpos, 1, 0)
    for piece in range(PIECES):
        s = starts_ref[0, piece]
        both = jnp.where(qpos >= s, 1, 0) * jnp.where(qpos < s + PIECE, 1, 0)
        both = both * jnp.where(kpos >= s, 1, 0) * jnp.where(kpos < s + PIECE, 1, 0)
        seen = jnp.maximum(seen, both)
    return jnp.where(seen > 0, 0.0, -1e30)


def fwd_kernel(
    starts_ref, tok_ref, prior_ref, ids_ref, ranks_ref, ga_ref, gm_ref, cos_ref, sin_ref, wqkv_ref, wo_ref, wr_ref,
    wres_ref, cv_ref,
    q_ref, k_ref, v_ref, mixed_ref, lse_ref, nattn_ref, resid_ref, nmoe_ref, base_ref, aux_ref, pay_ref,
    bias_ref,
):
    d = tok_ref.shape[1]
    pairs = d // LANES
    ntile = SEQ // QT
    ga, gm = ga_ref[...], gm_ref[...]
    mask_a, mask_b = head_masks()
    mask16 = (mask_a.astype(bf16), mask_b.astype(bf16))

    def project(i, carry):
        rows = pl.ds(pl.multiple_of(i * QT, QT), QT)
        x = tok_ref[rows, :].astype(f32)
        r1 = lax.rsqrt(jnp.mean(x * x, axis=-1, keepdims=True) + EPS)
        n = (x * r1 * ga).astype(bf16)
        nattn_ref[rows, :] = n
        cosine, sine = cos_ref[rows, :], sin_ref[rows, :]
        for c, out in ((0, q_ref), (1, k_ref), (2, v_ref)):
            proj = nn(n, wqkv_ref[c])
            for p in range(pairs):
                part = proj[:, p * LANES : (p + 1) * LANES]
                if c < 2:
                    part = rot(part, cosine, sine)
                part = part.astype(bf16)
                if c == 0:
                    part = part * jnp.array(HD**-0.5, bf16)
                out[rows, p * LANES : (p + 1) * LANES] = part
        return carry

    lax.fori_loop(0, ntile, project, 0)

    taken = jnp.zeros((1, LANES), f32)
    lower = jnp.where(
        lax.broadcasted_iota(i32, (QT, QT), 1) < lax.broadcasted_iota(i32, (QT, QT), 0), 1.0, 0.0
    ).astype(bf16)
    lane = lanes(QT)
    for i in range(ntile):
        lo = i * QT
        width = min(SEQ, lo + 2 * QT) - lo
        rows = pl.ds(lo, QT)
        bias_ref[:, :width] = window_bias(starts_ref, i, width, False)

        def pair(p, lse):
            cols = pl.ds(pl.multiple_of(p * LANES, LANES), LANES)
            q2 = q_ref[rows, cols]
            outs = []
            for h in range(2):
                qh = q2 * mask16[h]
                sb = nt(qh, k_ref[lo : lo + width, cols]) + bias_ref[:, :width]
                m = jnp.max(sb, axis=-1, keepdims=True)
                if lo:
                    sa = nt(qh, k_ref[0:lo, cols])
                    m = jnp.maximum(m, jnp.max(sa, axis=-1, keepdims=True))
                pb = jnp.exp(sb - m)
                total = jnp.sum(pb, axis=-1, keepdims=True)
                acc = nn(pb.astype(bf16), v_ref[lo : lo + width, cols])
                if lo:
                    pa = jnp.exp(sa - m)
                    total = total + jnp.sum(pa, axis=-1, keepdims=True)
                    acc = acc + nn(pa.astype(bf16), v_ref[0:lo, cols])
                outs.append(acc / total)
                lse = jnp.where(lane == 2 * p + h, m + jnp.log(total), lse)
            mixed_ref[rows, cols] = (outs[0] * mask_a + outs[1] * mask_b).astype(bf16)
            return lse

        lse = lax.fori_loop(0, pairs, pair, jnp.zeros((QT, LANES), f32))
        lse_ref[:, rows] = lse.T[0 : lse_ref.shape[0], :]

        x = tok_ref[rows, :].astype(f32)
        resid = x + nn(mixed_ref[rows, :], wo_ref[...])
        resid_ref[rows, :] = resid
        r2 = lax.rsqrt(jnp.mean(resid * resid, axis=-1, keepdims=True) + EPS)
        nm = (resid * r2 * gm).astype(bf16)
        nmoe_ref[rows, :] = nm
        raw = nn(nm, wr_ref[...])
        logits = raw + nn(prior_ref[rows, :], wres_ref[...])
        logits = jnp.where(lane < NF + 2 + NC, logits, -1e30)
        e = jnp.exp(logits - jnp.max(logits, axis=-1, keepdims=True))
        shares = e / jnp.sum(e, axis=-1, keepdims=True)
        id0, id1 = ids_ref[rows, 0:1], ids_ref[rows, 1:2]
        rk0, rk1 = ranks_ref[rows, 0:1], ranks_ref[rows, 1:2]
        hit0, hit1 = jnp.where(lane == id0, 1.0, 0.0), jnp.where(lane == id1, 1.0, 0.0)
        gates = shares * (hit0 + hit1)
        keep0, keep1 = jnp.where(rk0 < CAP, 1.0, 0.0), jnp.where(rk1 < CAP, 1.0, 0.0)
        kept = (hit0 * keep0 + hit1 * keep1) * jnp.where(lane < NF, 1.0, 0.0)
        pos = nn(lower, kept.astype(bf16)) + taken
        taken = taken + jnp.sum(kept, axis=0, keepdims=True)
        pay_ref[0:NF, rows] = jnp.where(kept > 0, shares, -1.0).T[0:NF, :]
        pay_ref[NF : 2 * NF, rows] = jnp.where(kept > 0, pos, -1.0).T[0:NF, :]
        nv = nm.astype(f32)
        aux = jnp.where(lane < NF + 2 + NC, shares, 0.0)
        direct = gates[:, NF + 1 : NF + 2]
        others = None
        for c in range(NC):
            z0, z1 = raw[:, Z0 + 2 * c : Z0 + 2 * c + 1], raw[:, Z0 + 2 * c + 1 : Z0 + 2 * c + 2]
            m0, m1 = 1.0 / (1.0 + jnp.exp(z1 - z0)), 1.0 / (1.0 + jnp.exp(z0 - z1))
            aux = jnp.where(lane == Z0 + 2 * c, m0, aux)
            aux = jnp.where(lane == Z0 + 2 * c + 1, m1, aux)
            w = gates[:, NF + 2 + c : NF + 3 + c]
            direct = direct + w * m0
            term = (w * m1) * cv_ref[c : c + 1, :]
            others = term if others is None else others + term
        aux_ref[rows, :] = aux
        base_ref[rows, :] = resid + direct * nv + others


def mid_kernel(
    dx_ref, gg_ref, og_ref, nmoe_ref, resid_ref, ids_ref, aux_ref, prior_ref, wr_ref, wres_ref, cv_ref, gm_ref,
    gmo_ref, gres_ref, pgrad_ref, nmg_ref, wrg_ref, resg_ref, cvg_ref,
):
    gm = gm_ref[...]
    lane = lanes(QT)
    nmg_ref[...] = jnp.zeros_like(nmg_ref)
    wrg_ref[...] = jnp.zeros_like(wrg_ref)
    resg_ref[...] = jnp.zeros_like(resg_ref)
    cvg_ref[...] = jnp.zeros_like(cvg_ref)

    def tile(i, carry):
        rows = pl.ds(pl.multiple_of(i * QT, QT), QT)
        g16, n16 = og_ref[rows, :], nmoe_ref[rows, :]
        g, nv = g16.astype(f32), n16.astype(f32)
        x = resid_ref[rows, :]
        r2 = lax.rsqrt(jnp.mean(x * x, axis=-1, keepdims=True) + EPS)
        aux = aux_ref[rows, :]
        shares = jnp.where(lane < NF + 2 + NC, aux, 0.0)
        id0, id1 = ids_ref[rows, 0:1], ids_ref[rows, 1:2]
        chosen = jnp.where(lane == id0, 1.0, 0.0) + jnp.where(lane == id1, 1.0, 0.0)
        gates = shares * chosen
        copy_inner = jnp.sum(g * nv, axis=-1, keepdims=True)
        inner = jnp.where(lane < NF, gg_ref[rows, :], 0.0)
        inner = jnp.where(lane == NF + 1, copy_inner, inner)
        direct = gates[:, NF + 1 : NF + 2]
        blend = jnp.zeros((QT, LANES), f32)
        cvw = jnp.zeros((QT, LANES), f32)
        for c in range(NC):
            m0, m1 = aux[:, Z0 + 2 * c : Z0 + 2 * c + 1], aux[:, Z0 + 2 * c + 1 : Z0 + 2 * c + 2]
            v_inner = jnp.sum(g * cv_ref[c : c + 1, :], axis=-1, keepdims=True)
            mean = m0 * copy_inner + m1 * v_inner
            inner = jnp.where(lane == NF + 2 + c, mean, inner)
            w = gates[:, NF + 2 + c : NF + 3 + c]
            direct = direct + w * m0
            blend = jnp.where(lane == Z0 + 2 * c, m0 * (w * copy_inner - w * mean), blend)
            blend = jnp.where(lane == Z0 + 2 * c + 1, m1 * (w * v_inner - w * mean), blend)
            cvw = jnp.where(lane == c, w * m1, cvw)
        grad_router = inner * chosen
        glog = shares * (grad_router - jnp.sum(shares * grad_router, axis=-1, keepdims=True))
        both_hi, both_lo = split(glog + blend)
        log_hi, log_lo = split(glog)
        cv_hi, cv_lo = split(cvw)
        pgrad_ref[rows, :] = nt(log_hi, wres_ref[...]) + nt(log_lo, wres_ref[...])
        wrg_ref[...] += tn(n16, both_hi) + tn(n16, both_lo)
        resg_ref[...] += tn(prior_ref[rows, :], log_hi) + tn(prior_ref[rows, :], log_lo)
        cvg_ref[...] += tn(g16, cv_hi) + tn(g16, cv_lo)
        gmi = dx_ref[rows, :].astype(f32) + direct * g + nt(both_hi, wr_ref[...]) + nt(both_lo, wr_ref[...])
        nmg_ref[...] += jnp.sum(gmi * x * r2, axis=0, keepdims=True)
        scaled = gmi * gm
        avg = jnp.mean(scaled * x, axis=-1, keepdims=True)
        gres = g + r2 * scaled - x * (r2 * r2 * r2 * avg)
        gres_ref[rows, :] = gres
        gmo_ref[rows, :] = gres.astype(bf16)
        return carry

    lax.fori_loop(0, SEQ // QT, tile, 0)


def bwd_kernel(
    starts_ref, gmo_ref, gres_ref, mixed_ref, q_ref, k_ref, v_ref, lse_ref, nattn_ref, tok_ref, ga_ref, cos_ref,
    sin_ref, wqkv_ref, wo_ref,
    igrad_ref, qkvg_ref, wog_ref, nag_ref,
    do_ref, delta_ref, bias_ref, gp_ref, dk_ref, dv_ref, dq_ref,
):
    d = tok_ref.shape[1]
    pairs = d // LANES
    ntile = SEQ // QT
    ga = ga_ref[...]
    mask_a, mask_b = head_masks()
    mask16 = (mask_a.astype(bf16), mask_b.astype(bf16))
    maskf = (mask_a, mask_b)
    heads = delta_ref.shape[0]
    pick = jnp.where(
        lax.broadcasted_iota(i32, (heads, d), 1) // HD == lax.broadcasted_iota(i32, (heads, d), 0), 1.0, 0.0
    ).astype(bf16)

    def start(i, carry):
        rows = pl.ds(pl.multiple_of(i * QT, QT), QT)
        do = nt(gmo_ref[rows, :], wo_ref[...]).astype(bf16)
        do_ref[rows, :] = do
        hi, lo = split(do.astype(f32) * mixed_ref[rows, :].astype(f32))
        delta_ref[:, rows] = nt(pick, hi) + nt(pick, lo)
        return carry

    lax.fori_loop(0, ntile, start, 0)
    wog_ref[...] = tn(mixed_ref[...], gmo_ref[...]).astype(wog_ref.dtype)
    for i in range(ntile):
        width = min(SEQ, (i + 2) * QT) - i * QT
        bias_ref[i, 0:width, :] = window_bias(starts_ref, i, width, True)

    def pair(p, carry):
        cols = pl.ds(pl.multiple_of(p * LANES, LANES), LANES)
        dk_ref[...] = jnp.zeros_like(dk_ref)
        dv_ref[...] = jnp.zeros_like(dv_ref)
        for i in range(ntile):
            lo = i * QT
            width = min(SEQ, lo + 2 * QT) - lo
            rows = pl.ds(lo, QT)
            q2, do2 = q_ref[rows, cols], do_ref[rows, cols]
            dq = jnp.zeros((QT, LANES), f32)
            for h in range(2):
                qh, doh = q2 * mask16[h], do2 * mask16[h]
                lse, delta = lse_ref[pl.ds(2 * p + h, 1), rows], delta_ref[pl.ds(2 * p + h, 1), rows]
                spans = [(lo, width, True)] + ([(0, lo, False)] if lo else [])
                for at, size, masked in spans:
                    k2 = k_ref[at : at + size, cols]
                    s = nt(k2, qh)
                    if masked:
                        s = s + bias_ref[i, 0:size, :]
                    prob = jnp.exp(s - lse)
                    ds = (prob * (nt(v_ref[at : at + size, cols], doh) - delta)).astype(bf16)
                    dv_ref[at : at + size, :] += nn(prob.astype(bf16), doh)
                    dk_ref[at : at + size, :] += nn(ds, qh)
                    dq = dq + tn(ds, k2) * maskf[h]
            dq_ref[rows, :] = dq * HD**-0.5
        cosine, sine = cos_ref[...], -sin_ref[...]
        gp_ref[0, :, cols] = rot(dq_ref[...], cosine, sine).astype(bf16)
        gp_ref[1, :, cols] = rot(dk_ref[...], cosine, sine).astype(bf16)
        gp_ref[2, :, cols] = dv_ref[...].astype(bf16)
        return carry

    lax.fori_loop(0, pairs, pair, 0)
    for c in range(3):
        qkvg_ref[c] = tn(nattn_ref[...], gp_ref[c]).astype(qkvg_ref.dtype)
    nag_ref[...] = jnp.zeros_like(nag_ref)

    def finish(i, carry):
        rows = pl.ds(pl.multiple_of(i * QT, QT), QT)
        gai = nt(gp_ref[0, rows, :], wqkv_ref[0]) + nt(gp_ref[1, rows, :], wqkv_ref[1])
        gai = gai + nt(gp_ref[2, rows, :], wqkv_ref[2])
        x = tok_ref[rows, :].astype(f32)
        r1 = lax.rsqrt(jnp.mean(x * x, axis=-1, keepdims=True) + EPS)
        nag_ref[...] += jnp.sum(gai * x * r1, axis=0, keepdims=True)
        scaled = gai * ga
        avg = jnp.mean(scaled * x, axis=-1, keepdims=True)
        igrad_ref[rows, :] = gres_ref[rows, :] + r1 * scaled - x * (r1 * r1 * r1 * avg)
        return carry

    lax.fori_loop(0, ntile, finish, 0)


def pack_kernel(
    meta_ref, pos_ref, gate_ref, x_ref, y_ref, xc_ref, yc_ref, gc_ref, xs, ys, gs, sems,
):
    g = pl.program_id(0)
    off, count = meta_ref[g], meta_ref[NF + 1 + g]
    pos, gate = pos_ref[0], gate_ref[0]
    group = pos.shape[1]

    def window(j, carry):
        at = pl.multiple_of(off + j * WIN, 16)
        slot = (lax.broadcasted_iota(i32, (WIN, group), 0) + j * WIN).astype(f32)
        hot = jnp.where(slot == pos, 1.0, 0.0)
        h16 = hot.astype(bf16)
        xs[pl.ds(at, WIN), :] = nn(h16, x_ref[0]).astype(bf16)
        ys[pl.ds(at, WIN), :] = nn(h16, y_ref[0]).astype(bf16)
        gs[pl.ds(at, WIN), :] = jnp.broadcast_to(jnp.sum(hot * gate, axis=1, keepdims=True), (WIN, LANES))
        return carry

    lax.fori_loop(0, (count + WIN - 1) // WIN, window, 0)

    @pl.when(g == NF - 1)
    def _():
        at = pl.multiple_of(meta_ref[NF], 16)
        for k in range(TM // WIN):
            xs[pl.ds(at + k * WIN, WIN), :] = jnp.zeros((WIN, xs.shape[1]), bf16)
            ys[pl.ds(at + k * WIN, WIN), :] = jnp.zeros((WIN, ys.shape[1]), bf16)
            gs[pl.ds(at + k * WIN, WIN), :] = jnp.zeros((WIN, LANES), f32)
        tiles = meta_ref[2 * NF + 1]

        def copies(t):
            rows = pl.ds(pl.multiple_of(t * TM, TM), TM)
            return [
                pltpu.make_async_copy(src.at[rows, :], dst.at[rows, :], sems.at[n, t])
                for n, (src, dst) in enumerate(((xs, xc_ref), (ys, yc_ref), (gs, gc_ref)))
            ]

        def begin(t, carry):
            for c in copies(t):
                c.start()
            return carry

        def end(t, carry):
            for c in copies(t):
                c.wait()
            return carry

        lax.fori_loop(0, tiles, begin, 0)
        lax.fori_loop(0, tiles, end, 0)


def ffn_kernel(meta_ref, x_ref, y_ref, gc_ref, w_ref, out_ref, dx_ref, gg_ref, dw_ref, acc):
    i = pl.program_id(0)

    @pl.when(i == 0)
    def _():
        acc[...] = jnp.zeros_like(acc)

    @pl.when(i < meta_ref[2 * NF + 1])
    def _():
        x = x_ref[...]
        gate = gc_ref[:, 0:1]
        dy = y_ref[...].astype(f32)
        ge = (gate * dy).astype(bf16)
        rows, d = x.shape
        x_t, ge_t = x.T, ge.T

        def chunk(c, carry):
            eo, dx = carry
            wg, wu, wd = w_ref[c, 0], w_ref[c, 1], w_ref[c, 2]
            gv, uv = nn(x, wg), nn(x, wu)
            gh = nn(ge, wd)
            sig = 1.0 / (1.0 + jnp.exp(-gv))
            act = gv * sig
            hid = (act * uv).astype(bf16)
            eo = eo + nt(hid, wd)
            gg = (gh * uv * (sig * (1.0 + gv * (1.0 - sig)))).astype(bf16)
            gu = (gh * act).astype(bf16)
            dx = dx + nt(gg, wg) + nt(gu, wu)
            acc[c, 0] += nn(x_t, gg)
            acc[c, 1] += nn(x_t, gu)
            acc[c, 2] += nn(ge_t, hid)
            return eo, dx

        zero = jnp.zeros((rows, d), f32)
        eo, dx = lax.fori_loop(0, w_ref.shape[0], chunk, (zero, zero))
        out_ref[...] = (gate * eo).astype(bf16)
        dx_ref[...] = dx.astype(bf16)
        gg_ref[...] = jnp.broadcast_to(jnp.sum(dy * eo, axis=1, keepdims=True), gg_ref.shape)

    @pl.when(i == pl.num_programs(0) - 1)
    def _():
        dw_ref[...] = acc[...].astype(bf16)


def unpack_kernel(
    meta_ref, pos_ref, yc_ref, dxc_ref, ggc_ref, out_ref, dx_ref, gg_ref, ys, xs, gs, sems,
):
    g = pl.program_id(0)
    off, count = meta_ref[g], meta_ref[NF + 1 + g]

    @pl.when(g == 0)
    def _():
        tiles = meta_ref[2 * NF + 1]

        def copies(t):
            rows = pl.ds(pl.multiple_of(t * TM, TM), TM)
            return [
                pltpu.make_async_copy(src.at[rows, :], dst.at[rows, :], sems.at[n, t])
                for n, (src, dst) in enumerate(((yc_ref, ys), (dxc_ref, xs), (ggc_ref, gs)))
            ]

        def begin(t, carry):
            for c in copies(t):
                c.start()
            return carry

        def end(t, carry):
            for c in copies(t):
                c.wait()
            return carry

        lax.fori_loop(0, tiles, begin, 0)
        lax.fori_loop(0, tiles, end, 0)

    pos = pos_ref[0]
    group = pos.shape[1]
    d = ys.shape[1]

    def window(j, first):
        at = pl.multiple_of(off + j * WIN, 16)
        index = lax.broadcasted_iota(i32, (WIN, group), 0) + j * WIN
        hot = jnp.where(index.astype(f32) == pos, 1.0, 0.0)
        h16 = hot.astype(bf16)
        live = lax.broadcasted_iota(i32, (WIN, d), 0) + j * WIN < count
        yv = jnp.where(live, ys[pl.ds(at, WIN), :].astype(f32), 0.0).astype(bf16)
        xv = jnp.where(live, xs[pl.ds(at, WIN), :].astype(f32), 0.0).astype(bf16)
        gv = jnp.where(live[:, 0:1], gs[pl.ds(at, WIN), 0:1], 0.0)
        py, px = tn(h16, yv).astype(bf16), tn(h16, xv).astype(bf16)
        pg = jnp.sum(hot * gv, axis=0, keepdims=True)
        if first:
            out_ref[0], dx_ref[0], gg_ref[0] = py, px, pg
        else:
            out_ref[0] += py
            dx_ref[0] += px
            gg_ref[0] += pg

    window(0, True)

    def more(j, carry):
        window(j, False)
        return carry

    lax.fori_loop(1, (count + WIN - 1) // WIN, more, 0)


def shape(dims, dtype):
    return jax.ShapeDtypeStruct(dims, dtype)


def cost(gflop, mbytes, mexp=0):
    return pl.CostEstimate(flops=int(gflop * 1e9), bytes_accessed=int(mbytes * 1e6), transcendentals=int(mexp * 1e6))


def experts(x_all, y_all, pos, gate, w_all):
    groups, group, d = x_all.shape
    count = (jnp.max(pos, axis=1) + 1.0).astype(i32)
    padded = (count + 15) // 16 * 16
    order = jnp.arange(NF)
    ends = jnp.sum(jnp.where(order[None, :] <= order[:, None], padded[None, :], 0), axis=1)
    tiles = jnp.maximum((ends[-1:] + TM - 1) // TM, 1)
    meta = jnp.concatenate([jnp.zeros((1,), i32), ends, count, tiles])
    room = NF * min(CAP, group) + TM + WIN
    room = (room + TM - 1) // TM * TM
    most = room // TM
    pos3, gate3 = pos.reshape(groups, 1, group), gate.reshape(groups, 1, group)
    params = pltpu.CompilerParams(vmem_limit_bytes=60 << 20, dimension_semantics=("arbitrary",))
    row_spec = pl.BlockSpec((1, 1, group), lambda g, *_: (g, 0, 0))
    tok_spec = pl.BlockSpec((1, group, d), lambda g, *_: (g, 0, 0))
    scratch = [
        pltpu.VMEM((room, d), bf16),
        pltpu.VMEM((room, d), bf16),
        pltpu.VMEM((room, LANES), f32),
        pltpu.SemaphoreType.DMA((3, most)),
    ]
    xc, yc, gc = pl.pallas_call(
        pack_kernel,
        out_shape=(shape((room, d), bf16), shape((room, d), bf16), shape((room, LANES), f32)),
        grid_spec=pltpu.PrefetchScalarGridSpec(
            num_scalar_prefetch=1,
            grid=(groups,),
            in_specs=[row_spec, row_spec, tok_spec, tok_spec],
            out_specs=(ANY, ANY, ANY),
            scratch_shapes=scratch,
        ),
        compiler_params=params,
        cost_estimate=cost(8, 30),
    )(meta, pos3, gate3, x_all, y_all)
    tile = lambda i, m: (jnp.minimum(i, m[2 * NF + 1] - 1), 0)
    zero4 = lambda i, m: (0, 0, 0, 0)
    out_c, dx_c, gg_c, dw = pl.pallas_call(
        ffn_kernel,
        out_shape=(
            shape((room, d), bf16), shape((room, d), bf16), shape((room, LANES), f32), shape(w_all.shape, bf16),
        ),
        grid_spec=pltpu.PrefetchScalarGridSpec(
            num_scalar_prefetch=1,
            grid=(most,),
            in_specs=[
                pl.BlockSpec((TM, d), tile),
                pl.BlockSpec((TM, d), tile),
                pl.BlockSpec((TM, LANES), tile),
                pl.BlockSpec(w_all.shape, zero4, pipeline_mode=pl.Buffered(1)),
            ],
            out_specs=(
                pl.BlockSpec((TM, d), tile),
                pl.BlockSpec((TM, d), tile),
                pl.BlockSpec((TM, LANES), tile),
                pl.BlockSpec(w_all.shape, zero4, pipeline_mode=pl.Buffered(1)),
            ),
            scratch_shapes=[pltpu.VMEM(w_all.shape, f32)],
        ),
        compiler_params=params,
        cost_estimate=cost(44, 30),
    )(meta, xc, yc, gc, w_all)
    out, dx, gg = pl.pallas_call(
        unpack_kernel,
        out_shape=(
            shape((groups, group, d), bf16), shape((groups, group, d), bf16), shape((groups, 1, group), f32),
        ),
        grid_spec=pltpu.PrefetchScalarGridSpec(
            num_scalar_prefetch=1,
            grid=(groups,),
            in_specs=[row_spec, ANY, ANY, ANY],
            out_specs=(tok_spec, tok_spec, row_spec),
            scratch_shapes=scratch,
        ),
        compiler_params=params,
        cost_estimate=cost(8, 30),
    )(meta, pos3, out_c, dx_c, gg_c)
    return out, dx, gg, dw


def on_device(
    dp,
    tensor,
    tokens,
    prior_logits,
    expert_ids,
    expert_ranks,
    piece_starts,
    norm_attn,
    qkv_weight,
    out_weight,
    norm_moe,
    router_weight,
    residual_weight,
    const_vectors,
    const_gates,
    w_gate_up,
    w_down,
    out_grad,
):
    rows, d = tokens.shape
    ne = router_weight.shape[1]
    packs = dp // NF
    groups = None if packs == 1 else [list(range(NF * r, NF * (r + 1))) for r in range(packs)]
    across = None if packs == 1 else [list(range(j, dp, NF)) for j in range(NF)]
    here = lax.axis_index("tensor")
    ids = lax.dynamic_slice_in_dim(expert_ids, here * rows, rows, 0)
    ranks = lax.dynamic_slice_in_dim(expert_ranks, here * rows, rows, 0)
    starts = lax.dynamic_slice_in_dim(piece_starts, here, 1, 0)
    ga, gm = norm_attn.astype(f32).reshape(1, d), norm_moe.astype(f32).reshape(1, d)
    cosine, sine = (jnp.asarray(t) for t in rotary_tables())
    prior = jnp.pad(prior_logits, ((0, 0), (0, LANES - ne)))
    wr = jnp.concatenate(
        [router_weight, jnp.zeros((d, Z0 - ne), bf16), const_gates.reshape(2 * NC, d).T,
         jnp.zeros((d, LANES - Z0 - 2 * NC), bf16)], axis=1)
    wres = jnp.pad(residual_weight, ((0, LANES - ne), (0, LANES - ne)))
    cv = const_vectors.astype(f32)

    wqkv = lax.all_gather(lax.all_gather(qkv_weight, "tensor", axis=2, tiled=True), "dp", axis=1, tiled=True)
    wo = lax.all_gather(lax.all_gather(out_weight, "tensor", axis=0, tiled=True), "dp", axis=1, tiled=True)

    shard = w_down.shape[1]
    w_local = jnp.concatenate([w_gate_up, w_down.transpose(0, 2, 1)[None]], axis=0)
    w_mine = lax.all_to_all(w_local, "dp", 1, 2, tiled=True, axis_index_groups=groups)
    w_mine = w_mine.reshape(3, w_local.shape[2] * NF, shard)
    if packs > 1:
        w_mine = lax.all_gather(w_mine, "dp", axis=1, tiled=True, axis_index_groups=across)
    w_all = lax.all_gather(w_mine, "tensor", axis=0, tiled=False)

    y_all = lax.all_gather(out_grad, "dp", axis=0, tiled=False, axis_index_groups=groups)

    heads = 16
    q, k, v, mixed, lse, nattn, resid, nmoe, base, aux, pay = pl.pallas_call(
        fwd_kernel,
        in_specs=[SM] + [VM] * 13,
        out_specs=[VM] * 11,
        out_shape=(
            shape((rows, d), bf16), shape((rows, d), bf16), shape((rows, d), bf16), shape((rows, d), bf16),
            shape((heads, rows), f32), shape((rows, d), bf16), shape((rows, d), f32), shape((rows, d), bf16),
            shape((rows, d), f32), shape((rows, LANES), f32), shape((2 * NF, rows), f32),
        ),
        scratch_shapes=[pltpu.VMEM((QT, 2 * QT), f32)],
        compiler_params=pltpu.CompilerParams(vmem_limit_bytes=60 << 20),
        cost_estimate=cost(40, 30, 10),
    )(starts, tokens, prior, ids, ranks, ga, gm, cosine, sine, wqkv, wo, wr, wres, cv)

    x_all = lax.all_gather(nmoe, "dp", axis=0, tiled=False, axis_index_groups=groups)
    payload = pay.reshape(2, NF, rows).transpose(1, 0, 2)
    payload = lax.all_to_all(payload, "dp", 0, 0, tiled=True, axis_index_groups=groups)
    out_p, dx_p, gg_p, dw = experts(x_all, y_all, payload[:, 1], payload[:, 0], w_all)
    gg = lax.all_to_all(gg_p.reshape(NF, rows), "dp", 0, 0, tiled=True, axis_index_groups=groups)
    gg = jnp.pad(gg, ((0, LANES - NF), (0, 0))).T
    scatter = functools.partial(
        lax.psum_scatter, axis_name="dp", scatter_dimension=0, tiled=True, axis_index_groups=groups
    )
    dx = scatter(dx_p.reshape(NF * rows, d))
    ffn = scatter(out_p.reshape(NF * rows, d))
    layer_out = (base + ffn.astype(f32)).astype(bf16)

    dw_mine = lax.psum_scatter(dw, "tensor", scatter_dimension=0, tiled=False)
    if packs > 1:
        dw_mine = lax.psum_scatter(dw_mine, "dp", scatter_dimension=1, tiled=True, axis_index_groups=across)
    dw_mine = dw_mine.reshape(3, NF, -1, shard)
    dw_mine = lax.all_to_all(dw_mine, "dp", 1, 1, tiled=True, axis_index_groups=groups).astype(f32)
    gate_up_grad, down_grad = dw_mine[0:2], dw_mine[2].transpose(0, 2, 1)

    gmo, gres, pgrad, nmg, wrg, resg, cvg = pl.pallas_call(
        mid_kernel,
        in_specs=[VM] * 12,
        out_specs=[VM] * 7,
        out_shape=(
            shape((rows, d), bf16), shape((rows, d), f32), shape((rows, LANES), f32), shape((1, d), f32),
            shape((d, LANES), f32), shape((LANES, LANES), f32), shape((d, LANES), f32),
        ),
        compiler_params=pltpu.CompilerParams(vmem_limit_bytes=60 << 20),
        cost_estimate=cost(2, 20),
    )(dx, gg, out_grad, nmoe, resid, ids, aux, prior, wr, wres, cv, gm)
    igrad, qkvg, wog, nag = pl.pallas_call(
        bwd_kernel,
        in_specs=[SM] + [VM] * 14,
        out_specs=[VM] * 4,
        out_shape=(
            shape((rows, d), f32), shape((3, d, d), bf16), shape((d, d), bf16), shape((1, d), f32),
        ),
        scratch_shapes=[
            pltpu.VMEM((rows, d), bf16),
            pltpu.VMEM((heads, rows), f32),
            pltpu.VMEM((rows // QT, 2 * QT, QT), f32),
            pltpu.VMEM((3, rows, d), bf16),
            pltpu.VMEM((rows, LANES), f32),
            pltpu.VMEM((rows, LANES), f32),
            pltpu.VMEM((rows, LANES), f32),
        ],
        compiler_params=pltpu.CompilerParams(vmem_limit_bytes=60 << 20),
        cost_estimate=cost(80, 40, 10),
    )(starts, gmo, gres, mixed, q, k, v, lse, nattn, tokens, ga, cosine, sine, wqkv, wo)

    qkvg = lax.psum_scatter(qkvg, "dp", scatter_dimension=1, tiled=True)
    qkvg = lax.psum_scatter(qkvg, "tensor", scatter_dimension=2, tiled=True).astype(f32)
    wog = lax.psum_scatter(wog, "dp", scatter_dimension=1, tiled=True)
    wog = lax.psum_scatter(wog, "tensor", scatter_dimension=0, tiled=True).astype(f32)
    small = lax.psum(
        (nag.reshape(d), nmg.reshape(d), wrg[:, 0 : Z0 + 2 * NC], resg[0:ne, 0:ne], cvg[:, 0:NC]), ("dp", "tensor")
    )
    return (
        layer_out,
        igrad,
        pgrad[:, 0:ne],
        small[0],
        qkvg,
        wog,
        small[1],
        small[2][:, 0:ne],
        small[3],
        small[4].T,
        small[2][:, Z0 : Z0 + 2 * NC].T.reshape(NC, 2, d),
        gate_up_grad,
        down_grad,
    )


def solution(mesh):
    body = functools.partial(on_device, mesh.shape["dp"], mesh.shape["tensor"])
    rows = P(("dp", "tensor"), None)
    return jax.shard_map(
        body,
        mesh=mesh,
        in_specs=(
            rows, rows, P("dp", None), P("dp", None), P("dp", None), P(), P(None, "dp", "tensor"), P("tensor", "dp"),
            P(), P(), P(), P(), P(), P(None, None, "dp", "tensor"), P(None, "tensor", "dp"), rows,
        ),
        out_specs=(
            rows, rows, rows, P(), P(None, "dp", "tensor"), P("tensor", "dp"), P(), P(), P(), P(), P(),
            P(None, None, "dp", "tensor"), P(None, "tensor", "dp"),
        ),
        check_vma=False,
    )
```

time: 2320 us -> 1170 us (0.50)
  local copies, waits for them, and re-layouts: 674 us -> 42.7 us
  matrix products: 310 us -> 0 us
  Pallas kernels: 0 us -> 232 us
  waiting for transfers between devices: 980 us -> 759 us
  other arithmetic: 226 us -> 10.8 us
    reduce_scatter x6 -> x5, waiting for transfers between devices: 683 us -> 321 us  [the longest x1 93.4 us: on_device(): ffn = scatter(out_p.reshape(NF * rows, d))]
    gather x14 -> x0, local copies, waits for them, and re-layouts: 333 us -> none  [the longest x2 75.8 us: on_device(): combined = jnp.sum(retained_gates[:, :, None] * expert_out[picker], axis=1)]
    dot_general x49 -> x0, matrix products: 297 us -> none  [the longest x4 35.6 us: attend_back(): jnp.einsum('hqk,qhd->khd', shares.astype(jnp.bfloat16), grad_out, preferr...]
    pallas_call x0 -> x6, Pallas kernels: none -> 232 us  [the longest x1 73.8 us: experts(): pl.pallas_call(ffn_kernel, out_shape=(shape((room, d), bf16), shape((room...]
    psum x0 -> x1, waiting for transfers between devices: none -> 134 us  [on_device(): lax.psum((nag.reshape(d), nmg.reshape(d), wrg[:, 0:Z0 + 2 * NC], resg[0:n...]
    dynamic_update_slice x16 -> x0, local copies, waits for them, and re-layouts: 129 us -> none  [on_device(): lax.map(attend_back, (query, keys, values, piece_starts, log_total, grad_...]
    reduce_sum x17 -> x1, other arithmetic: 114 us -> 0.12 us  [experts(): jnp.sum(jnp.where(order[None, :] <= order[:, None], padded[None, :], 0),...]
    scatter x3 -> x0, local copies, waits for them, and re-layouts: 91.8 us -> none  [the longest x1 30.9 us: dispatch(): slot_token = jnp.zeros((NF * CAP + 1,), jnp.int32).at[target.reshape(-1)]...]
  transfers between devices with their start and end apart: 15 -> 14, of which waited for: 9 -> 11; matrix products, arithmetic and copies ran while one was open for 27% -> 4% of each run, Pallas kernels for 0% -> 12%
where the time goes in v1:
time: 1170 us; the launch traced here: 1160 us
  waiting for transfers between devices  759 us (65%)
  Pallas kernels  232 us (20%)
  blocking collectives  96.4 us (8%)
  local copies, waits for them, and re-layouts  42.7 us (4%)
  between operations  15.3 us (1%)
    all_gather x1, waiting for transfers between devices, on_device(): w_all = lax.all_gather(w_mine, 'tensor', axis=0, tiled=False)  151 us
    psum x1, waiting for transfers between devices, on_device(): lax.psum((nag.reshape(d), nmg.reshape(d), wrg[:, 0:Z0 + 2 * NC], resg[0:n...  134 us
    reduce_scatter x1, waiting for transfers between devices, on_device(): ffn = scatter(out_p.reshape(NF * rows, d))  93.4 us
    reduce_scatter x1, waiting for transfers between devices, on_device(): dw_mine = lax.psum_scatter(dw, 'tensor', scatter_dimension=0, tiled=False)  84.5 us
    reduce_scatter x1, waiting for transfers between devices, on_device(): dx = scatter(dx_p.reshape(NF * rows, d))  80.4 us
    pallas_call x1, Pallas kernels, experts(): pl.pallas_call(ffn_kernel, out_shape=(shape((room, d), bf16), shape((room...  73.8 us
    all_gather x1, waiting for transfers between devices, on_device(): lax.all_gather(nmoe, 'dp', axis=0, tiled=False, axis_index_groups=groups)  62.7 us
    unnamed x15, waiting for transfers between devices  60.2 us
  transfers between devices with their start and end apart: 14, of which 11 were waited for; matrix products, arithmetic and copies ran while one was open for 4% of the time, Pallas kernels for 12%

profile of v1, /device:TPU:0, one launch (start us, length us, event | category | flops | bytes accessed | tf_op | source)
XLA Modules:
  0.0 1161.0 jit_solution(13585606222625077739)
XLA Ops:
  7.2 15.7 %all_gather.29 = bf16[768,96]{1,0:T(8,128)(2,1)S(1)} all-gather(bf16[192,96]{1,0:T(8,128)(2,1)} %param.25), channel_id=1, replica_groups=mesh['dp'=8,'tensor'=4] {'tensor'}, dimensions={0}, use_global_device_ids=true | all-gather | bytes 184320 | tf_op jit(solution)/shard_map/all_gather | solution.py:621
  22.9 0.8 copy.122
  23.8 1.1 copy.120
  24.9 18.0 %all_gather.27 = bf16[3,96,768]{1,0,2:T(4,128)(2,1)S(1)} all-gather(bf16[3,96,192]{1,0,2:T(4,128)(2,1)S(1)} %copy.120), channel_id=1, replica_groups=mesh['dp'=8,'tensor'=4] {'tensor'}, dimensions={2}, use_global_device_ids=true | all-gather | bytes 552960 | tf_op jit(solution)/shard_map/all_gather | solution.py:620
  42.9 1.2 copy.121
  50.2 1.0 copy.143.ranks_ref
  51.3 1.1 copy.142.ids_ref
  52.3 0.8 maximum_maximum_fusion.wr_ref
  53.2 2.4 copy.125.wo_ref
  55.5 30.2 %all-gather.8.cloned.1.call-done.wqkv_ref = bf16[3,768,768]{2,1,0:T(8,128)(2,1)} async-done(((bf16[3,96,768]{2,1,0:T(8,128)(2,1)}), bf16[3,768,768]{2,1,0:T(8,128)(2,1)}) %all-gather.8.cloned.1.call-update) | async-done | bytes 3538960 | tf_op jit(solution)/shard_map/all_gather | solution.py:620
  85.7 48.6 %shard_map.273 = (bf16[1024,768]{1,0:T(8,128)(2,1)}, bf16[1024,768]{1,0:T(8,128)(2,1)}, bf16[1024,768]{1,0:T(8,128)(2,1)}, bf16[1024,768]{1,0:T(8,128)(2,1)}, f3...) custom-call(s32[1,2]{1,0:T(1,128)} %copy.141.starts_ref, ...), custom_call_target="tpu_custom_call" | custom-call | flops 40000000000 | bytes 30000000 | tf_op jit(solution)/shard_map/pallas_call | solution.py:634
  134.4 1.3 copy-done.2
  135.9 47.8 %all_to_all.28 = bf16[3,8,96,512]{3,2,0,1:T(8,128)(2,1)S(1)} all-to-all(bf16[3,8,96,512]{3,2,0,1:T(8,128)(2,1)S(1)} %pad_maximum_fusion), channel_id=1, replica_groups=mesh['dp'=8,'tensor'=4] {'dp'}, dimensions={1} | all-to-all | bytes 4718592 | tf_op jit(solution)/shard_map/all_to_all | solution.py:625
  183.7 1.6 copy.128
  186.1 7.4 all_to_all.29
  196.2 62.7 %all-gather.14.cloned.1.call-done = bf16[8192,768]{1,0:T(8,128)(2,1)} async-done(((bf16[1024,768]{1,0:T(8,128)(2,1)}), bf16[8192,768]{1,0:T(8,128)(2,1)}) %all-gather.14.cloned.1.call-update) | async-done | bytes 12582928 | tf_op jit(solution)/shard_map/all_gather | solution.py:648
  259.0 17.9 %shard_map.274 = (bf16[6656,768]{1,0:T(8,128)(2,1)}, bf16[6656,768]{1,0:T(8,128)(2,1)}, f32[6656,128]{1,0:T(8,128)}) custom-call(s32[18]{0:T(128)} %pad_add_fusion.meta_ref, f32[8,1,1024]{2,1,0:T(1,128)} %get-tuple-element.162.pos_ref, f32[8,1,1024]{2,1,0:T(1,128)} %get-tuple-element.160.gate_ref, bf16[8,1024,768]{2,1,0:T(8,128)(2,1)} %bitcast.49, ...), custom_call_target="tpu_custom_call" | custom-call | flops 8000000000 | bytes 30000000 | tf_op jit(solution)/shard_map/pallas_call | solution.py:524
  276.9 150.9 %all-gather.12.cloned.1.call-done.w_ref = bf16[4,3,768,512]{3,2,1,0:T(8,128)(2,1)} async-done(((bf16[1,3,768,512]{3,2,1,0:T(8,128)(2,1)}), bf16[4,3,768,512]{3,2,1,0:T(8,128)(2,1)}) %all-gather.12.cloned.1.call-update) | async-done | bytes 9437200 | tf_op jit(solution)/shard_map/all_gather | solution.py:629
  427.8 73.8 %shard_map.275 = (bf16[6656,768]{1,0:T(8,128)(2,1)}, bf16[6656,768]{1,0:T(8,128)(2,1)}, f32[6656,128]{1,0:T(8,128)}, bf16[4,3,768,512]{3,2,1,0:T(8,128)(2,1)}) custom-call(s32[18]{0:T(128)} %pad_add_fusion.meta_ref, bf16[6656,768]{1,0:T(8,128)(2,1)} %get-tuple-element.48.x_ref, bf16[6656,768]{1,0:T(8,128)(2,1)} %get-tuple-element.49.y_ref, ...), custom_call_target="tpu_custom_call" | custom-call | flops 44000002048 | bytes 30000000 | tf_op jit(solution)/shard_map/pallas_call | solution.py:539
  501.6 16.5 %shard_map.276 = (bf16[8,1024,768]{2,1,0:T(8,128)(2,1)}, bf16[8,1024,768]{2,1,0:T(8,128)(2,1)}, f32[8,1,1024]{2,1,0:T(1,128)}) custom-call(s32[18]{0:T(128)} %pad_add_fusion.meta_ref, f32[8,1,1024]{2,1,0:T(1,128)} %get-tuple-element.162.pos_ref, bf16[6656,768]{1,0:T(8,128)(2,1)} %get-tuple-element.51.yc_ref, bf16[6656,768]{1,0:T(8,128)(2,1)} %get-tuple-element.52.dxc_ref, ...), custom_call_target="tpu_custom_call" | custom-call | flops 8000000000 | bytes 30000000 | tf_op jit(solution)/shard_map/pallas_call | solution.py:564
  518.9 7.6 all_to_all.30
  526.7 0.8 pad_bitcast_fusion.gg_ref
  527.6 80.4 %reduce-scatter.14.cloned.1.call-done.dx_ref = bf16[1024,768]{1,0:T(8,128)(2,1)} async-done(((bf16[8192,768]{1,0:T(8,128)(2,1)}), bf16[1024,768]{1,0:T(8,128)(2,1)}) %reduce-scatter.14.cloned.1.call-update) | async-done | bytes 1572880 | tf_op jit(solution)/shard_map/reduce_scatter | solution.py:657
  607.9 17.4 %shard_map.277 = (bf16[1024,768]{1,0:T(8,128)(2,1)}, f32[1024,768]{1,0:T(8,128)}, f32[1024,128]{1,0:T(8,128)}, f32[1,768]{1,0:T(1,128)}, f32[768,128]{1,0:T(8,12...) custom-call(bf16[1024,768]{1,0:T(8,128)(2,1)} %reduce-scatter.14.cloned.1.call-done.dx_ref, ...), custom_call_target="tpu_custom_call" | custom-call | flops 2000000000 | bytes 20000000 | tf_op jit(solution)/shard_map/pallas_call | solution.py:668
  625.3 58.1 %shard_map.278 = (f32[1024,768]{1,0:T(8,128)}, bf16[3,768,768]{2,1,0:T(8,128)(2,1)}, bf16[768,768]{1,0:T(8,128)(2,1)}, f32[1,768]{1,0:T(1,128)}) custom-call(s32[1,2]{1,0:T(1,128)} %copy.141.starts_ref, bf16[1024,768]{1,0:T(8,128)(2,1)} %get-tuple-element.59.gmo_ref, f32[1024,768]{1,0:T(8,128)} %get-tuple-element.60.gres_ref, ...), custom_call_target="tpu_custom_call" | custom-call | flops 80000000000 | bytes 40000000 | tf_op jit(solution)/shard_map/pallas_call | solution.py:679
  683.4 2.4 copy.139
  687.1 84.5 %reduce-scatter.20.cloned.1.call-done = bf16[1,3,768,512]{3,2,1,0:T(8,128)(2,1)} async-done(((bf16[4,3,768,512]{3,2,1,0:T(8,128)(2,1)}), bf16[1,3,768,512]{3,2,1,0:T(8,128)(2,1)}) %reduce-scatter.20.cloned.1.call-update) | async-done | bytes 2359312 | tf_op jit(solution)/shard_map/reduce_scatter | solution.py:661
  771.6 3.3 copy.132
  774.9 3.8 all-to-all-start.3
  780.0 1.3 slice.39
  782.1 36.4 %reduce-scatter.24.cloned.1.call-done = bf16[96,768]{1,0:T(8,128)(2,1)} async-done(((bf16[768,768]{1,0:T(8,128)(2,1)}), bf16[96,768]{1,0:T(8,128)(2,1)}) %reduce-scatter.24.cloned.1.call-update) | async-done | bytes 147472
  818.5 1.7 copy.140
  820.3 0.8 copy.133
  821.1 49.4 %reduce-scatter.16.cloned.1.call-done = bf16[3,96,768]{2,1,0:T(8,128)(2,1)} async-done(((bf16[3,768,768]{2,1,0:T(8,128)(2,1)}), bf16[3,96,768]{2,1,0:T(8,128)(2,1)}) %reduce-scatter.16.cloned.1.call-update) | async-done | bytes 442384 | tf_op jit(solution)/shard_map/reduce_scatter | solution.py:699
  870.5 1.4 copy.137
  872.0 1.2 reshape.107
  873.2 93.4 %reduce-scatter.12.cloned.1.call-done = bf16[1024,768]{1,0:T(8,128)(2,1)} async-done(((bf16[8192,768]{1,0:T(8,128)(2,1)}), bf16[1024,768]{1,0:T(8,128)(2,1)}) %reduce-scatter.12.cloned.1.call-update) | async-done | bytes 1572880 | tf_op jit(solution)/shard_map/reduce_scatter | solution.py:658
  966.7 3.8 add_convert_fusion
  970.5 134.2 %all-reduce.6.cloned.1.call-done = (f32[768]{0:T(1024)}, f32[768]{0:T(1024)}, f32[768,20]{1,0:T(8,128)}, f32[12,12]{1,0:T(8,128)}, f32[2,768]{0,1:T(8,128)}) async-done(((f32[768]{0:T(1024)}, f32[768]{0:T(1024)}, f32[768,20]{1,0:T(8,128)}, f32[12,12]{1,0:T(8,128)}, f32[2,768]{0,1:T(8,128)}), (f32[768]{0:T(1024)}, f32[768]{0:T(1024)}, f32[768,20]{1,0:T(8,128)}, f32[12,12]{1,0:T(8,128)}, ...) | async-done | bytes 74320 | tf_op jit(solution)/shard_map/psum | solution.py:703
  1104.7 1.7 copy.135
  1106.5 1.8 copy.134
  1108.3 1.2 slice_bitcast_fusion.1
  1110.6 2.0 copy.136
  1113.3 1.3 slice_bitcast_fusion
  1114.6 13.1 %reduce-scatter.18.cloned.1.call-done = bf16[192,96]{1,0:T(8,128)(2,1)} async-done(((bf16[768,96]{1,0:T(8,128)(2,1)}), bf16[192,96]{1,0:T(8,128)(2,1)}) %reduce-scatter.18.cloned.1.call-update) | async-done | bytes 36880 | tf_op jit(solution)/shard_map/reduce_scatter | solution.py:702
  1127.7 1.4 convert_element_type.38
  1129.1 21.1 %reduce-scatter.22.cloned.1.call-done = bf16[192,288]{1,0:T(8,128)(2,1)} async-done(((bf16[768,288]{1,0:T(8,128)(2,1)}), bf16[192,288]{1,0:T(8,128)(2,1)}) %reduce-scatter.22.cloned.1.call-update) | async-done | bytes 110608
  1150.2 1.0 reshape.108
  (105 shorter events, 18.3 us)
Async XLA Ops:
  7.2 37.7 %copy-start = (s32[4,2]{0,1:T(2,128)S(1)}, s32[4,2]{0,1:T(2,128)}, u32[]{:S(2)}) copy-start(s32[4,2]{0,1:T(2,128)} %param.22) | copy-start | bytes 100
  7.2 46.0 %all-gather.10.cloned.1.call-start = ((), (), s32[]{:S(2)}) async-start(), calls=%async_computation.12 | async-start | bytes 1327104 | tf_op jit(solution)/shard_map/all_gather | solution.py:621
  23.7 22.0 %copy-start.18 = (bf16[768]{0:T(1024)(128)(2,1)S(1)}, bf16[768]{0:T(1024)(128)(2,1)}, u32[]{:S(2)}) copy-start(bf16[768]{0:T(1024)(128)(2,1)} %param.23) | copy-start | bytes 4612
  23.7 22.6 %copy-start.19 = (bf16[768]{0:T(1024)(128)(2,1)S(1)}, bf16[768]{0:T(1024)(128)(2,1)}, u32[]{:S(2)}) copy-start(bf16[768]{0:T(1024)(128)(2,1)} %param.26) | copy-start | bytes 4612
  23.7 23.2 %copy-start.15 = (bf16[2,768]{1,0:T(2,128)(2,1)S(1)}, bf16[2,768]{1,0:T(2,128)(2,1)}, u32[]{:S(2)}) copy-start(bf16[2,768]{1,0:T(2,128)(2,1)} %param.29) | copy-start | bytes 9220
  23.7 23.8 %copy-start.11 = (bf16[2,2,768]{2,1,0:T(2,128)(2,1)S(1)}, bf16[2,2,768]{2,1,0:T(2,128)(2,1)}, u32[]{:S(2)}) copy-start(bf16[2,2,768]{2,1,0:T(2,128)(2,1)} %param.30) | copy-start | bytes 18436
  23.7 23.8 %copy-start.12 = (bf16[12,12]{1,0:T(8,128)(2,1)S(1)}, bf16[12,12]{1,0:T(8,128)(2,1)}, u32[]{:S(2)}) copy-start(bf16[12,12]{1,0:T(8,128)(2,1)} %param.28) | copy-start | bytes 868
  23.8 24.6 %copy-start.9 = (bf16[768,12]{0,1:T(8,128)(2,1)S(1)}, bf16[768,12]{0,1:T(8,128)(2,1)}, u32[]{:S(2)}) copy-start(bf16[768,12]{0,1:T(8,128)(2,1)} %param.27) | copy-start | bytes 55300
  23.8 62.0 %all-gather.8.cloned.1.call-start = ((), (), s32[]{:S(2)}) async-start(), calls=%async_computation.11 | async-start | bytes 3981312 | tf_op jit(solution)/shard_map/all_gather | solution.py:620
  24.9 23.6 %copy-start.7 = (bf16[1024,12]{0,1:T(8,128)(2,1)S(1)}, bf16[1024,12]{0,1:T(8,128)(2,1)}, u32[]{:S(2)}) copy-start(bf16[1024,12]{0,1:T(8,128)(2,1)} %param.19) | copy-start | bytes 73732
  44.1 152.1 %all-gather.16.cloned.1.call-start = ((), (), s32[]{:S(2)}) async-start(), calls=%async_computation.20 | async-start | bytes 14155776 | tf_op jit(solution)/shard_map/all_gather | solution.py:631
  44.9 214.1 %all-gather.14.cloned.1.call-start = ((), (), s32[]{:S(2)}) async-start(), calls=%async_computation.19 | async-start | bytes 14155776 | tf_op jit(solution)/shard_map/all_gather | solution.py:648
  55.5 78.9 %copy-start.3 = (bf16[8,512,96]{1,2,0:T(8,128)(2,1)S(1)}, bf16[8,512,96]{1,2,0:T(8,128)(2,1)}, u32[]{:S(2)}) copy-start(bf16[8,512,96]{1,2,0:T(8,128)(2,1)} %param.32) | copy-start | bytes 2359300
  134.3 1.4 copy-start.2
  134.4 293.4 %all-gather.12.cloned.1.call-start = ((), (), s32[]{:S(2)}) async-start(), calls=%async_computation.13 | async-start | bytes 11796480 | tf_op jit(solution)/shard_map/all_gather | solution.py:629
  185.2 0.8 copy-start.6
  185.3 422.7 %reduce-scatter.14.cloned.1.call-start = ((), (), s32[]{:S(2)}) async-start(), calls=%async_computation.15 | async-start | bytes 14155776 | tf_op jit(solution)/shard_map/reduce_scatter | solution.py:657
  518.1 253.5 %reduce-scatter.20.cloned.1.call-start = ((), (), s32[]{:S(2)}) async-start(), calls=%async_computation.18 | async-start | bytes 11796480 | tf_op jit(solution)/shard_map/reduce_scatter | solution.py:661
  518.2 0.8 copy-start.8
  518.9 299.6 %reduce-scatter.24.cloned.1.call-start = ((), (), s32[]{:S(2)}) async-start(), calls=%async_computation.22 | async-start | bytes 1327104
  685.8 184.7 %reduce-scatter.16.cloned.1.call-start = ((), (), s32[]{:S(2)}) async-start(), calls=%async_computation.16 | async-start | bytes 3981312 | tf_op jit(solution)/shard_map/reduce_scatter | solution.py:699
  686.5 280.2 %reduce-scatter.12.cloned.1.call-start = ((), (), s32[]{:S(2)}) async-start(), calls=%async_computation.14 | async-start | bytes 14155776 | tf_op jit(solution)/shard_map/reduce_scatter | solution.py:658
  774.9 3.9 copy-start.17
  774.9 4.5 copy-start.16
  774.9 6.4 copy-start.5
  774.9 45.4 %copy-start.4 = (f32[1024,128]{1,0:T(8,128)S(1)}, f32[1024,128]{1,0:T(8,128)}, u32[]{:S(2)}) copy-start(f32[1024,128]{1,0:T(8,128)} %get-tuple-element.68) | copy-start | bytes 1572868
  774.9 335.3 %all-to-all-start.3 = ((bf16[3,8,96,512]{3,2,0,1:T(8,128)(2,1)}), bf16[3,8,96,512]{3,2,0,1:T(8,128)(2,1)S(1)}, u32[]{:S(2)}, u32[]{:S(2)}) async-start(bf16[3,8,96,512]{3,2,0,1:T(8,128)(2,1)} %copy.132), calls=%async_computation.8 | async-start | bytes 4718592 | tf_op jit(solution)/shard_map/all_to_all | solution.py:665
  778.7 326.0 %all-reduce.6.cloned.1.call-start = ((), (), s32[]{:S(2)}) async-start(), calls=%async_computation.23 | async-start | bytes 1605632 | tf_op jit(solution)/shard_map/psum | solution.py:703
  782.1 345.6 %reduce-scatter.18.cloned.1.call-start = ((), (), s32[]{:S(2)}) async-start(), calls=%async_computation.17 | async-start | bytes 245760 | tf_op jit(solution)/shard_map/reduce_scatter | solution.py:702
  820.2 330.0 %reduce-scatter.22.cloned.1.call-start = ((), (), s32[]{:S(2)}) async-start(), calls=%async_computation.21 | async-start | bytes 737280
  1112.6 41.4 %copy-start.1 = (s32[4,2]{0,1:T(2,128)S(1)}, s32[4,2]{0,1:T(2,128)}, u32[]{:S(2)}) copy-start(s32[4,2]{0,1:T(2,128)} %param.22) | copy-start | bytes 100
  1113.3 38.9 %copy-start.14 = (f32[768]{0:T(1024)S(1)}, f32[768]{0:T(1024)}, u32[]{:S(2)}) copy-start(f32[768]{0:T(1024)} %get-tuple-element.168) | copy-start | bytes 9220
  1113.3 39.5 %copy-start.13 = (f32[768]{0:T(1024)S(1)}, f32[768]{0:T(1024)}, u32[]{:S(2)}) copy-start(f32[768]{0:T(1024)} %get-tuple-element.171) | copy-start | bytes 9220
  1113.3 40.1 %copy-start.10 = (f32[12,12]{1,0:T(8,128)S(1)}, f32[12,12]{1,0:T(8,128)}, u32[]{:S(2)}) copy-start(f32[12,12]{1,0:T(8,128)} %get-tuple-element.173) | copy-start | bytes 1732
Sparse Core Ops, SparseCore 0:
  23.9 25.3 all-gather.9
  51.7 33.9 all-gather.7
  87.6 95.9 all-gather.15
  185.4 73.5 all-gather.13
  261.0 166.7 all-gather.11
  518.2 89.6 reduce-scatter.13
  610.3 161.2 reduce-scatter.19
  775.4 43.0 reduce-scatter.23
  822.4 48.0 reduce-scatter.15
  874.3 92.3 reduce-scatter.11
  975.0 129.7 all-reduce.5
  1107.5 20.1 reduce-scatter.17
  1130.0 20.2 reduce-scatter.21

commit v2 on v1

--- a/solution.py
+++ b/solution.py
@@ -86,12 +86,439 @@
     return jnp.where(seen > 0, 0.0, -1e30)
 
 
+MESH = pl.DeviceIdType.MESH
+GATHER_COPIES = 13
+REDUCE_COPIES = 10
+
+
+def flip(index, m):
+    for bit in (1, 2, 4):
+        if m & bit:
+            index = index + bit - 2 * bit * (index // bit % 2)
+    return index
+
+
+def remote(src, dst, sems, n, axis, peer):
+    return pltpu.make_async_remote_copy(
+        src_ref=src,
+        dst_ref=dst,
+        send_sem=sems.at[0, n],
+        recv_sem=sems.at[1, n],
+        device_id={axis: peer},
+        device_id_type=MESH,
+    )
+
+
+def greet(peers):
+    barrier = pltpu.get_barrier_semaphore()
+    for axis, peer in peers:
+        pl.semaphore_signal(barrier, inc=1, device_id={axis: peer}, device_id_type=MESH)
+    pl.semaphore_wait(barrier, len(peers))
+
+
+def near_peers():
+    me = lax.axis_index("dp")
+    return [("dp", flip(me, m)) for m in (1, 2, 4)]
+
+
+def far_peers(tensor):
+    me = lax.axis_index("tensor")
+    return [("tensor", (me + k) % tensor) for k in range(1, tensor)]
+
+
+class Gather8:
+    def __init__(self, src, dst, sems, own_sem):
+        me = lax.axis_index("dp")
+        slot = me % NF
+        nx, ny, nc = flip(me, 2), flip(me, 4), flip(me, 1)
+        sx, sy, sd = flip(slot, 2), flip(slot, 4), flip(slot, 6)
+        self.own = pltpu.make_async_copy(src(None), dst(slot, None), own_sem)
+        go = lambda n, s, d, peer: remote(s, d, sems, n, "dp", peer)
+        on = lambda n, s, h, peer: go(n, dst(s, h), dst(s, h), peer)
+        self.c = [
+            go(0, src(0), dst(slot, 0), nx),
+            go(1, src(1), dst(slot, 1), ny),
+            go(2, src(1), dst(slot, 1), nx),
+            go(3, src(0), dst(slot, 0), ny),
+            go(4, src(None), dst(slot, None), nc),
+            on(5, sx, 0, ny),
+            on(6, sy, 1, nx),
+            on(7, sx, 0, nc),
+            on(8, sy, 1, nc),
+            on(9, sx, 1, nc),
+            on(10, sy, 0, nc),
+            on(11, sd, 0, nc),
+            on(12, sd, 1, nc),
+        ]
+
+    def begin(self):
+        self.own.start()
+        for n in range(5):
+            self.c[n].start()
+
+    def forward(self):
+        for got, out in ((0, (5, 7)), (1, (6, 8))):
+            self.c[got].wait_recv()
+            for n in out:
+                self.c[n].start()
+
+    def share(self):
+        for got, out in ((2, 9), (3, 10)):
+            self.c[got].wait_recv()
+            self.c[out].start()
+
+    def last(self):
+        for got, out in ((5, 11), (6, 12)):
+            self.c[got].wait_recv()
+            self.c[out].start()
+
+    def end(self):
+        for n in (4, 7, 8, 9, 10, 11, 12):
+            self.c[n].wait_recv()
+        for c in self.c:
+            c.wait_send()
+        self.own.wait()
+
+
+def halves(ref, index, rows):
+    half = rows // 2
+    return lambda s, h: ref.at[s] if h is None else ref.at[s, pl.ds(h * half, half)]
+
+
+def gather_kernel(src, dst, sems, own_sem):
+    greet(near_peers())
+    half = src.shape[0] // 2
+    g = Gather8(
+        lambda h: src if h is None else src.at[pl.ds(h * half, half)], halves(dst, 0, src.shape[0]), sems, own_sem
+    )
+    g.begin()
+    g.forward()
+    g.share()
+    g.last()
+    g.end()
+
+
+def gather8(x, cid):
+    return pl.pallas_call(
+        gather_kernel,
+        in_specs=[ANY],
+        out_specs=ANY,
+        out_shape=shape((NF, *x.shape), x.dtype),
+        scratch_shapes=[pltpu.SemaphoreType.DMA((2, GATHER_COPIES)), pltpu.SemaphoreType.DMA],
+        compiler_params=pltpu.CompilerParams(collective_id=cid, has_side_effects=True),
+        cost_estimate=cost(50, 30),
+    )(x)
+
+
+def weights_kernel(tensor, w_ref, out_ref, zbuf, slab, sems, zsems, own_sem):
+    here = lax.axis_index("tensor")
+    k, r, f = w_ref.shape
+    greet(near_peers() + far_peers(tensor))
+    copies = [
+        remote(w_ref, zbuf.at[here], zsems, n, axis, peer) for n, (axis, peer) in enumerate(far_peers(tensor))
+    ]
+    for c in copies:
+        c.start()
+    zbuf[here] = w_ref[...]
+    for c in copies:
+        c.wait_recv()
+    for c in range(k):
+        for t in range(0, tensor, 2):
+            both = jnp.concatenate([zbuf[t, c].astype(f32), zbuf[t + 1, c].astype(f32)], axis=-1)
+            slab[c, :, t * f : (t + 2) * f] = both.astype(bf16)
+    part = lambda h: pl.ds(0, k) if h is None else pl.ds(h * (k // 2), k // 2)
+    g = Gather8(
+        lambda h: slab.at[part(h)],
+        lambda s, h: out_ref.at[part(h), pl.ds(pl.multiple_of(s * r, r), r), :],
+        sems,
+        own_sem,
+    )
+    g.begin()
+    g.forward()
+    g.share()
+    g.last()
+    g.end()
+    for c in copies:
+        c.wait_send()
+
+
+def gather_weights(w, tensor, cid):
+    k, r, f = w.shape
+    return pl.pallas_call(
+        functools.partial(weights_kernel, tensor),
+        in_specs=[VM],
+        out_specs=ANY,
+        out_shape=shape((k, NF * r, tensor * f), w.dtype),
+        scratch_shapes=[
+            pltpu.VMEM((tensor, k, r, f), bf16),
+            pltpu.VMEM((k, r, tensor * f), bf16),
+            pltpu.SemaphoreType.DMA((2, GATHER_COPIES)),
+            pltpu.SemaphoreType.DMA((2, tensor - 1)),
+            pltpu.SemaphoreType.DMA,
+        ],
+        compiler_params=pltpu.CompilerParams(collective_id=cid, has_side_effects=True),
+        cost_estimate=cost(30, 10),
+    )(w)
+
+
+class Reduce8:
+    def __init__(self, view, bufs, sems, lsems):
+        self.own, self.away, self.qd, self.qx, self.qy, self.ind, self.inx, self.iny = bufs
+        me = lax.axis_index("dp")
+        slot = me % NF
+        half = self.qd.shape[0] // 2
+        a, b = pl.ds(0, half), pl.ds(half, half)
+        self.a, self.b = a, b
+        nx, ny, nc = flip(me, 2), flip(me, 4), flip(me, 1)
+        mine = [flip(slot, m) for m in (6, 2, 4)] + [slot]
+        self.loads = [pltpu.make_async_copy(view(s), self.own.at[n], lsems.at[n]) for n, s in enumerate(mine)]
+        self.over = [remote(view(flip(s, 1)), self.away.at[n], sems, n, "dp", nc) for n, s in enumerate(mine)]
+        go = lambda n, q, i, part, peer: remote(q.at[part], i.at[part], sems, n, "dp", peer)
+        self.da, self.db = go(4, self.qd, self.ind, a, nx), go(5, self.qd, self.ind, b, ny)
+        self.xa, self.yb = go(6, self.qx, self.inx, a, nx), go(7, self.qy, self.iny, b, ny)
+        self.ya, self.xb = go(8, self.qy, self.iny, a, ny), go(9, self.qx, self.inx, b, nx)
+
+    def load(self):
+        for c in self.loads:
+            c.start()
+
+    def begin(self):
+        for c in self.over:
+            c.start()
+
+    def add(self, out, n, part, more=None):
+        total = self.own[n, part].astype(f32) + self.away[n, part].astype(f32)
+        if more is not None:
+            total = total + more[part].astype(f32)
+        out[part] = total.astype(bf16)
+
+    def ready(self, n):
+        self.loads[n].wait()
+        self.over[n].wait_recv()
+
+    def first(self):
+        self.ready(0)
+        self.add(self.qd, 0, self.a)
+        self.da.start()
+        self.add(self.qd, 0, self.b)
+        self.db.start()
+
+    def second(self):
+        self.ready(1)
+        self.add(self.qx, 1, self.a)
+        self.xa.start()
+        self.ready(2)
+        self.add(self.qy, 2, self.b)
+        self.yb.start()
+
+    def third(self):
+        self.ready(3)
+        self.da.wait_recv()
+        self.add(self.qy, 2, self.a, self.ind)
+        self.ya.start()
+        self.db.wait_recv()
+        self.add(self.qx, 1, self.b, self.ind)
+        self.xb.start()
+
+    def end(self, write):
+        for part, first, second in ((self.a, self.xa, self.ya), (self.b, self.yb, self.xb)):
+            first.wait_recv()
+            second.wait_recv()
+            total = self.own[3, part].astype(f32) + self.away[3, part].astype(f32)
+            write(part, total + self.inx[part].astype(f32) + self.iny[part].astype(f32))
+
+    def close(self):
+        for c in self.over + [self.da, self.db, self.xa, self.yb, self.ya, self.xb]:
+            c.wait_send()
+
+
+def reduce_scratch(block):
+    return [pltpu.VMEM((4, *block), bf16)] * 2 + [pltpu.VMEM(block, bf16)] * 6 + [
+        pltpu.SemaphoreType.DMA((2, REDUCE_COPIES)),
+        pltpu.SemaphoreType.DMA((4,)),
+    ]
+
+
+def reduce_kernel(p_ref, out_ref, *scratch):
+    r = Reduce8(lambda s: p_ref.at[s], scratch[:8], *scratch[8:10])
+    r.load()
+    greet(near_peers())
+    r.begin()
+    r.first()
+    r.second()
+    r.third()
+
+    def write(part, total):
+        out_ref[part] = total.astype(out_ref.dtype)
+
+    r.end(write)
+    r.close()
+
+
+def reduce8(p, cid):
+    groups, rows, columns = p.shape
+    block = (2, rows // 2, columns)
+    out = pl.pallas_call(
+        reduce_kernel,
+        in_specs=[ANY],
+        out_specs=VM,
+        out_shape=shape(block, bf16),
+        scratch_shapes=reduce_scratch(block),
+        compiler_params=pltpu.CompilerParams(collective_id=cid, has_side_effects=True, vmem_limit_bytes=60 << 20),
+        cost_estimate=cost(50, 30),
+    )(p.reshape(groups, *block))
+    return out.reshape(rows, columns)
+
+
+def exchange_kernel(n, *refs):
+    srcs, dst, sems, own_sems = refs[:n], refs[n], refs[n + 1], refs[n + 2]
+    me = lax.axis_index("dp")
+    slot = me % NF
+    at, pieces = 0, []
+    for src in srcs:
+        pieces.append((src, pl.ds(at, src.shape[0])))
+        at += src.shape[0]
+    own = [
+        pltpu.make_async_copy(src.at[:, slot], dst.at[part, slot], own_sems.at[i])
+        for i, (src, part) in enumerate(pieces)
+    ]
+    for c in own:
+        c.start()
+    greet([("dp", flip(me, m)) for m in range(1, NF)])
+    copies = []
+    for m in (6, 7, 2, 3, 4, 5, 1):
+        for i, (src, part) in enumerate(pieces):
+            at = (m - 1) * n + i
+            copies.append(remote(src.at[:, flip(slot, m)], dst.at[part, slot], sems, at, "dp", flip(me, m)))
+    for c in copies:
+        c.start()
+    for c in copies:
+        c.wait_recv()
+    for c in copies:
+        c.wait_send()
+    for c in own:
+        c.wait()
+
+
+def exchange8(xs, cid):
+    total = sum(x.shape[0] for x in xs)
+    return pl.pallas_call(
+        functools.partial(exchange_kernel, len(xs)),
+        in_specs=[ANY] * len(xs),
+        out_specs=ANY,
+        out_shape=shape((total, *xs[0].shape[1:]), xs[0].dtype),
+        scratch_shapes=[
+            pltpu.SemaphoreType.DMA((2, (NF - 1) * len(xs))),
+            pltpu.SemaphoreType.DMA((len(xs),)),
+        ],
+        compiler_params=pltpu.CompilerParams(collective_id=cid, has_side_effects=True),
+        cost_estimate=cost(25, 10),
+    )(*xs)
+
+
+def final_kernel(
+    tensor, g_ref, wrg_ref, cvg_ref, resg_ref, nmg_ref, nag_ref, out_ref, small_ref, zf, zs, zr, sbuf, srecv, *scratch
+):
+    here = lax.axis_index("tensor")
+    me = lax.axis_index("dp")
+    k, d, _ = g_ref.shape
+    r, f = out_ref.shape[1:]
+    zsems, ssems = scratch[10], scratch[11]
+    red = Reduce8(lambda s: g_ref.at[:, pl.ds(pl.multiple_of(s * r, r), r), :], scratch[:8], *scratch[8:10])
+    red.load()
+    sbuf[0] = jnp.zeros_like(sbuf[0])
+    sbuf[0, 0:24, :] = wrg_ref[0:24, :]
+    sbuf[0, 24:32, :] = cvg_ref[0:8, :]
+    sbuf[0, 32:33, :] = nmg_ref[...]
+    sbuf[0, 33:34, :] = nag_ref[...]
+    sbuf[0, 40:56, 0:LANES] = resg_ref[0:16, :]
+    greet(near_peers() + far_peers(tensor))
+    red.begin()
+    rounds = [remote(sbuf.at[n], srecv.at[n], ssems, n, "dp", flip(me, m)) for n, m in enumerate((1, 2, 4))]
+    rounds[0].start()
+    red.first()
+    rounds[0].wait_recv()
+    sbuf[1] = sbuf[0] + srecv[0]
+    rounds[1].start()
+    red.second()
+    rounds[1].wait_recv()
+    sbuf[2] = sbuf[1] + srecv[1]
+    rounds[2].start()
+    red.third()
+    rounds[2].wait_recv()
+    sbuf[3] = sbuf[2] + srecv[2]
+    far = [
+        remote(sbuf.at[3], srecv.at[3 + here], ssems, 3 + n, axis, peer)
+        for n, (axis, peer) in enumerate(far_peers(tensor))
+    ]
+    for c in far:
+        c.start()
+
+    def write(part, total):
+        for t in range(tensor):
+            zf[t, part] = total[:, :, t * f : (t + 1) * f]
+            zs[t, part] = total[:, :, t * f : (t + 1) * f].astype(bf16)
+
+    red.end(write)
+    out_copies = [
+        remote(zs.at[peer], zr.at[here], zsems, n, axis, peer) for n, (axis, peer) in enumerate(far_peers(tensor))
+    ]
+    for c in out_copies:
+        c.start()
+    srecv[3 + here] = sbuf[3]
+    for c in far:
+        c.wait_recv()
+    total = srecv[3]
+    for t in range(1, tensor):
+        total = total + srecv[3 + t]
+    small_ref[...] = total
+    zr[here] = jnp.zeros(zr.shape[1:], bf16)
+    for c in out_copies:
+        c.wait_recv()
+    total = zf[here]
+    for t in range(tensor):
+        total = total + zr[t].astype(f32)
+    out_ref[...] = total
+    red.close()
+    for c in rounds + far + out_copies:
+        c.wait_send()
+
+
+def finish(g, wrg, cvg, resg, nmg, nag, tensor, cid):
+    k, d, columns = g.shape
+    r, f = d // NF, columns // tensor
+    return pl.pallas_call(
+        functools.partial(final_kernel, tensor),
+        in_specs=[ANY] + [VM] * 5,
+        out_specs=[VM] * 2,
+        out_shape=(shape((k, r, f), f32), shape((56, d), f32)),
+        scratch_shapes=[
+            pltpu.VMEM((tensor, k, r, f), f32),
+            pltpu.VMEM((tensor, k, r, f), bf16),
+            pltpu.VMEM((tensor, k, r, f), bf16),
+            pltpu.VMEM((4, 56, d), f32),
+            pltpu.VMEM((3 + tensor, 56, d), f32),
+            *reduce_scratch((k, r, columns)),
+            pltpu.SemaphoreType.DMA((2, tensor - 1)),
+            pltpu.SemaphoreType.DMA((2, 2 + tensor)),
+        ],
+        compiler_params=pltpu.CompilerParams(collective_id=cid, has_side_effects=True, vmem_limit_bytes=60 << 20),
+        cost_estimate=cost(30, 10),
+    )(g, wrg, cvg, resg, nmg, nag)
+
+
 def fwd_kernel(
-    starts_ref, tok_ref, prior_ref, ids_ref, ranks_ref, ga_ref, gm_ref, cos_ref, sin_ref, wqkv_ref, wo_ref, wr_ref,
-    wres_ref, cv_ref,
-    q_ref, k_ref, v_ref, mixed_ref, lse_ref, nattn_ref, resid_ref, nmoe_ref, base_ref, aux_ref, pay_ref,
-    bias_ref,
+    starts_ref, tok_ref, prior_ref, ids_ref, ranks_ref, ga_ref, gm_ref, cos_ref, sin_ref, w_ref, wr_ref, wres_ref, cv_ref,
+    og_ref,
+    q_ref, k_ref, v_ref, mixed_ref, lse_ref, nattn_ref, resid_ref, nmoe_ref, base_ref, aux_ref, pay_ref, yall_ref,
+    bias_ref, sems, own_sem,
 ):
+    greet(near_peers())
+    half = og_ref.shape[0] // 2
+    spread = Gather8(
+        lambda h: og_ref if h is None else og_ref.at[pl.ds(h * half, half)], halves(yall_ref, 0, og_ref.shape[0]), sems, own_sem
+    )
+    spread.begin()
     d = tok_ref.shape[1]
     pairs = d // LANES
     ntile = SEQ // QT
@@ -107,7 +534,7 @@
         nattn_ref[rows, :] = n
         cosine, sine = cos_ref[rows, :], sin_ref[rows, :]
         for c, out in ((0, q_ref), (1, k_ref), (2, v_ref)):
-            proj = nn(n, wqkv_ref[c])
+            proj = nn(n, w_ref[c])
             for p in range(pairs):
                 part = proj[:, p * LANES : (p + 1) * LANES]
                 if c < 2:
@@ -158,7 +585,7 @@
         lse_ref[:, rows] = lse.T[0 : lse_ref.shape[0], :]
 
         x = tok_ref[rows, :].astype(f32)
-        resid = x + nn(mixed_ref[rows, :], wo_ref[...])
+        resid = x + nt(mixed_ref[rows, :], w_ref[3])
         resid_ref[rows, :] = resid
         r2 = lax.rsqrt(jnp.mean(resid * resid, axis=-1, keepdims=True) + EPS)
         nm = (resid * r2 * gm).astype(bf16)
@@ -193,6 +620,12 @@
             others = term if others is None else others + term
         aux_ref[rows, :] = aux
         base_ref[rows, :] = resid + direct * nv + others
+        stages = (spread.forward, spread.share, spread.last, spread.end)
+        if ntile == len(stages):
+            stages[i]()
+        elif i == ntile - 1:
+            for stage in stages:
+                stage()
 
 
 def mid_kernel(
@@ -239,9 +672,9 @@
         log_hi, log_lo = split(glog)
         cv_hi, cv_lo = split(cvw)
         pgrad_ref[rows, :] = nt(log_hi, wres_ref[...]) + nt(log_lo, wres_ref[...])
-        wrg_ref[...] += tn(n16, both_hi) + tn(n16, both_lo)
+        wrg_ref[...] += tn(both_hi, n16) + tn(both_lo, n16)
         resg_ref[...] += tn(prior_ref[rows, :], log_hi) + tn(prior_ref[rows, :], log_lo)
-        cvg_ref[...] += tn(g16, cv_hi) + tn(g16, cv_lo)
+        cvg_ref[...] += tn(cv_hi, g16) + tn(cv_lo, g16)
         gmi = dx_ref[rows, :].astype(f32) + direct * g + nt(both_hi, wr_ref[...]) + nt(both_lo, wr_ref[...])
         nmg_ref[...] += jnp.sum(gmi * x * r2, axis=0, keepdims=True)
         scaled = gmi * gm
@@ -256,8 +689,8 @@
 
 def bwd_kernel(
     starts_ref, gmo_ref, gres_ref, mixed_ref, q_ref, k_ref, v_ref, lse_ref, nattn_ref, tok_ref, ga_ref, cos_ref,
-    sin_ref, wqkv_ref, wo_ref,
-    igrad_ref, qkvg_ref, wog_ref, nag_ref,
+    sin_ref, w_ref,
+    igrad_ref, wg_ref, nag_ref,
     do_ref, delta_ref, bias_ref, gp_ref, dk_ref, dv_ref, dq_ref,
 ):
     d = tok_ref.shape[1]
@@ -274,14 +707,14 @@
 
     def start(i, carry):
         rows = pl.ds(pl.multiple_of(i * QT, QT), QT)
-        do = nt(gmo_ref[rows, :], wo_ref[...]).astype(bf16)
+        do = nn(gmo_ref[rows, :], w_ref[3]).astype(bf16)
         do_ref[rows, :] = do
         hi, lo = split(do.astype(f32) * mixed_ref[rows, :].astype(f32))
         delta_ref[:, rows] = nt(pick, hi) + nt(pick, lo)
         return carry
 
     lax.fori_loop(0, ntile, start, 0)
-    wog_ref[...] = tn(mixed_ref[...], gmo_ref[...]).astype(wog_ref.dtype)
+    wg_ref[3] = tn(gmo_ref[...], mixed_ref[...]).astype(wg_ref.dtype)
     for i in range(ntile):
         width = min(SEQ, (i + 2) * QT) - i * QT
         bias_ref[i, 0:width, :] = window_bias(starts_ref, i, width, True)
@@ -319,13 +752,13 @@
 
     lax.fori_loop(0, pairs, pair, 0)
     for c in range(3):
-        qkvg_ref[c] = tn(nattn_ref[...], gp_ref[c]).astype(qkvg_ref.dtype)
+        wg_ref[c] = tn(nattn_ref[...], gp_ref[c]).astype(wg_ref.dtype)
     nag_ref[...] = jnp.zeros_like(nag_ref)
 
     def finish(i, carry):
         rows = pl.ds(pl.multiple_of(i * QT, QT), QT)
-        gai = nt(gp_ref[0, rows, :], wqkv_ref[0]) + nt(gp_ref[1, rows, :], wqkv_ref[1])
-        gai = gai + nt(gp_ref[2, rows, :], wqkv_ref[2])
+        gai = nt(gp_ref[0, rows, :], w_ref[0]) + nt(gp_ref[1, rows, :], w_ref[1])
+        gai = gai + nt(gp_ref[2, rows, :], w_ref[2])
         x = tok_ref[rows, :].astype(f32)
         r1 = lax.rsqrt(jnp.mean(x * x, axis=-1, keepdims=True) + EPS)
         nag_ref[...] += jnp.sum(gai * x * r1, axis=0, keepdims=True)
@@ -617,35 +1050,40 @@
     wres = jnp.pad(residual_weight, ((0, LANES - ne), (0, LANES - ne)))
     cv = const_vectors.astype(f32)
 
-    wqkv = lax.all_gather(lax.all_gather(qkv_weight, "tensor", axis=2, tiled=True), "dp", axis=1, tiled=True)
-    wo = lax.all_gather(lax.all_gather(out_weight, "tensor", axis=0, tiled=True), "dp", axis=1, tiled=True)
-
+    w_attn = jnp.concatenate([qkv_weight, out_weight.T[None]], axis=0)
+    w_down_t = w_down.transpose(0, 2, 1)[None]
     shard = w_down.shape[1]
-    w_local = jnp.concatenate([w_gate_up, w_down.transpose(0, 2, 1)[None]], axis=0)
-    w_mine = lax.all_to_all(w_local, "dp", 1, 2, tiled=True, axis_index_groups=groups)
-    w_mine = w_mine.reshape(3, w_local.shape[2] * NF, shard)
+    w_mine = exchange8([w_gate_up, w_down_t], 1)
+    w_mine = w_mine.reshape(3, -1, shard)
     if packs > 1:
         w_mine = lax.all_gather(w_mine, "dp", axis=1, tiled=True, axis_index_groups=across)
     w_all = lax.all_gather(w_mine, "tensor", axis=0, tiled=False)
-
-    y_all = lax.all_gather(out_grad, "dp", axis=0, tiled=False, axis_index_groups=groups)
+    if packs > 1:
+        w_attn = lax.all_gather(w_attn, "tensor", axis=2, tiled=True)
+        w_attn = lax.all_gather(w_attn, "dp", axis=1, tiled=True)
+    else:
+        w_attn = gather_weights(w_attn, tensor, 2)
 
     heads = 16
-    q, k, v, mixed, lse, nattn, resid, nmoe, base, aux, pay = pl.pallas_call(
+    q, k, v, mixed, lse, nattn, resid, nmoe, base, aux, pay, y_all = pl.pallas_call(
         fwd_kernel,
-        in_specs=[SM] + [VM] * 13,
-        out_specs=[VM] * 11,
+        in_specs=[SM] + [VM] * 12 + [ANY],
+        out_specs=[VM] * 11 + [ANY],
         out_shape=(
             shape((rows, d), bf16), shape((rows, d), bf16), shape((rows, d), bf16), shape((rows, d), bf16),
             shape((heads, rows), f32), shape((rows, d), bf16), shape((rows, d), f32), shape((rows, d), bf16),
-            shape((rows, d), f32), shape((rows, LANES), f32), shape((2 * NF, rows), f32),
+            shape((rows, d), f32), shape((rows, LANES), f32), shape((2 * NF, rows), f32), shape((NF, rows, d), bf16),
         ),
-        scratch_shapes=[pltpu.VMEM((QT, 2 * QT), f32)],
-        compiler_params=pltpu.CompilerParams(vmem_limit_bytes=60 << 20),
+        scratch_shapes=[
+            pltpu.VMEM((QT, 2 * QT), f32),
+            pltpu.SemaphoreType.DMA((2, GATHER_COPIES)),
+            pltpu.SemaphoreType.DMA,
+        ],
+        compiler_params=pltpu.CompilerParams(collective_id=3, has_side_effects=True, vmem_limit_bytes=60 << 20),
         cost_estimate=cost(40, 30, 10),
-    )(starts, tokens, prior, ids, ranks, ga, gm, cosine, sine, wqkv, wo, wr, wres, cv)
-
-    x_all = lax.all_gather(nmoe, "dp", axis=0, tiled=False, axis_index_groups=groups)
+    )(starts, tokens, prior, ids, ranks, ga, gm, cosine, sine, w_attn, wr, wres, cv, out_grad)
+
+    x_all = gather8(nmoe, 4)
     payload = pay.reshape(2, NF, rows).transpose(1, 0, 2)
     payload = lax.all_to_all(payload, "dp", 0, 0, tiled=True, axis_index_groups=groups)
     out_p, dx_p, gg_p, dw = experts(x_all, y_all, payload[:, 1], payload[:, 0], w_all)
@@ -654,7 +1092,7 @@
     scatter = functools.partial(
         lax.psum_scatter, axis_name="dp", scatter_dimension=0, tiled=True, axis_index_groups=groups
     )
-    dx = scatter(dx_p.reshape(NF * rows, d))
+    dx = reduce8(dx_p, 5)
     ffn = scatter(out_p.reshape(NF * rows, d))
     layer_out = (base + ffn.astype(f32)).astype(bf16)
 
@@ -662,7 +1100,7 @@
     if packs > 1:
         dw_mine = lax.psum_scatter(dw_mine, "dp", scatter_dimension=1, tiled=True, axis_index_groups=across)
     dw_mine = dw_mine.reshape(3, NF, -1, shard)
-    dw_mine = lax.all_to_all(dw_mine, "dp", 1, 1, tiled=True, axis_index_groups=groups).astype(f32)
+    dw_mine = exchange8([dw_mine], 6).astype(f32)
     gate_up_grad, down_grad = dw_mine[0:2], dw_mine[2].transpose(0, 2, 1)
 
     gmo, gres, pgrad, nmg, wrg, resg, cvg = pl.pallas_call(
@@ -671,18 +1109,16 @@
         out_specs=[VM] * 7,
         out_shape=(
             shape((rows, d), bf16), shape((rows, d), f32), shape((rows, LANES), f32), shape((1, d), f32),
-            shape((d, LANES), f32), shape((LANES, LANES), f32), shape((d, LANES), f32),
+            shape((LANES, d), f32), shape((LANES, LANES), f32), shape((LANES, d), f32),
         ),
         compiler_params=pltpu.CompilerParams(vmem_limit_bytes=60 << 20),
         cost_estimate=cost(2, 20),
     )(dx, gg, out_grad, nmoe, resid, ids, aux, prior, wr, wres, cv, gm)
-    igrad, qkvg, wog, nag = pl.pallas_call(
+    igrad, wg, nag = pl.pallas_call(
         bwd_kernel,
-        in_specs=[SM] + [VM] * 14,
-        out_specs=[VM] * 4,
-        out_shape=(
-            shape((rows, d), f32), shape((3, d, d), bf16), shape((d, d), bf16), shape((1, d), f32),
-        ),
+        in_specs=[SM] + [VM] * 13,
+        out_specs=[VM] * 3,
+        out_shape=(shape((rows, d), f32), shape((4, d, d), bf16), shape((1, d), f32)),
         scratch_shapes=[
             pltpu.VMEM((rows, d), bf16),
             pltpu.VMEM((heads, rows), f32),
@@ -694,27 +1130,27 @@
         ],
         compiler_params=pltpu.CompilerParams(vmem_limit_bytes=60 << 20),
         cost_estimate=cost(80, 40, 10),
-    )(starts, gmo, gres, mixed, q, k, v, lse, nattn, tokens, ga, cosine, sine, wqkv, wo)
-
-    qkvg = lax.psum_scatter(qkvg, "dp", scatter_dimension=1, tiled=True)
-    qkvg = lax.psum_scatter(qkvg, "tensor", scatter_dimension=2, tiled=True).astype(f32)
-    wog = lax.psum_scatter(wog, "dp", scatter_dimension=1, tiled=True)
-    wog = lax.psum_scatter(wog, "tensor", scatter_dimension=0, tiled=True).astype(f32)
-    small = lax.psum(
-        (nag.reshape(d), nmg.reshape(d), wrg[:, 0 : Z0 + 2 * NC], resg[0:ne, 0:ne], cvg[:, 0:NC]), ("dp", "tensor")
-    )
+    )(starts, gmo, gres, mixed, q, k, v, lse, nattn, tokens, ga, cosine, sine, w_attn)
+
+    if packs > 1:
+        wg = lax.psum_scatter(wg, "dp", scatter_dimension=1, tiled=True)
+        wg = lax.psum_scatter(wg, "tensor", scatter_dimension=2, tiled=True).astype(f32)
+        wrg, cvg, resg, nmg, nag = lax.psum((wrg, cvg, resg, nmg, nag), ("dp", "tensor"))
+    else:
+        wg, small = finish(wg, wrg, cvg, resg, nmg, nag, tensor, 7)
+        wrg, cvg, resg, nmg, nag = small[0:24], small[24:32], small[40:56, 0:LANES], small[32], small[33]
     return (
         layer_out,
         igrad,
         pgrad[:, 0:ne],
-        small[0],
-        qkvg,
-        wog,
-        small[1],
-        small[2][:, 0:ne],
-        small[3],
-        small[4].T,
-        small[2][:, Z0 : Z0 + 2 * NC].T.reshape(NC, 2, d),
+        nag.reshape(d),
+        wg[0:3],
+        wg[3].T,
+        nmg.reshape(d),
+        wrg[0:ne].T,
+        resg[0:ne, 0:ne],
+        cvg[0:NC],
+        wrg[Z0 : Z0 + 2 * NC].reshape(NC, 2, d),
         gate_up_grad,
         down_grad,
     )

time: 1170 us -> 638 us (0.55)
  waiting for transfers between devices: 759 us -> 11.3 us
  Pallas kernels: 232 us -> 551 us
  blocking collectives: 96.4 us -> 0 us
  local copies, waits for them, and re-layouts: 42.7 us -> 26 us
  starting transfers between devices: 4.32 us -> 16.6 us
    pallas_call x2 -> x8, Pallas kernels: 107 us -> 438 us  [the longest x1 73.5 us: on_device(): pl.pallas_call(fwd_kernel, in_specs=[SM] + [VM] * 12 + [ANY], out_specs=[...]
    all_gather x1, waiting for transfers between devices: 151 us -> 0.02 us  [on_device(): w_all = lax.all_gather(w_mine, 'tensor', axis=0, tiled=False)]
    reduce_scatter x3 -> x0, waiting for transfers between devices: 143 us -> none  [the longest x1 80.4 us: on_device(): dx = scatter(dx_p.reshape(NF * rows, d))]
    psum x1 -> x0, waiting for transfers between devices: 134 us -> none  [on_device(): lax.psum((nag.reshape(d), nmg.reshape(d), wrg[:, 0:Z0 + 2 * NC], resg[0:n...]
    all_gather x4 -> x0, waiting for transfers between devices: 93 us -> none  [the longest x1 62.7 us: on_device(): lax.all_gather(nmoe, 'dp', axis=0, tiled=False, axis_index_groups=groups)]
    reduce_scatter x1, waiting for transfers between devices: 84.5 us -> 0.01 us  [on_device(): dw_mine = lax.psum_scatter(dw, 'tensor', scatter_dimension=0, tiled=False)]
    reduce_scatter x1, waiting for transfers between devices: 93.4 us -> 11.2 us  [on_device(): ffn = scatter(out_p.reshape(NF * rows, d))]
    all_to_all x3 -> x0, blocking collectives: 62.8 us -> none  [the longest x1 47.8 us: on_device(): lax.all_to_all(w_local, 'dp', 1, 2, tiled=True, axis_index_groups=groups)]
  transfers between devices with their start and end apart: 14 -> 5, of which waited for: 11 -> 1; matrix products, arithmetic and copies ran while one was open for 4% -> 5% of each run, Pallas kernels for 12% -> 73%
where the time goes in v2:
time: 638 us; the launch traced here: 627 us
  Pallas kernels  551 us (86%)
  local copies, waits for them, and re-layouts  26 us (4%)
  starting transfers between devices  16.6 us (3%)
  between operations  14.9 us (2%)
  waiting for transfers between devices  11.3 us (2%)
  other arithmetic  7.13 us (1%)
    pallas_call x1, Pallas kernels, on_device(): pl.pallas_call(fwd_kernel, in_specs=[SM] + [VM] * 12 + [ANY], out_specs=[...  73.5 us
    pallas_call x1, Pallas kernels, finish(): pl.pallas_call(functools.partial(final_kernel, tensor), in_specs=[ANY] +...  68.5 us
    pallas_call x2, Pallas kernels, exchange8(): pl.pallas_call(functools.partial(exchange_kernel, len(xs)), in_specs=[ANY...  65 us
    pallas_call x1, Pallas kernels, experts(): pl.pallas_call(ffn_kernel, out_shape=(shape((room, d), bf16), shape((room...  63.8 us
    pallas_call x1, Pallas kernels, reduce8(): pl.pallas_call(reduce_kernel, in_specs=[ANY], out_specs=VM, out_shape=sha...  61.1 us
    pallas_call x1, Pallas kernels, gather8(): pl.pallas_call(gather_kernel, in_specs=[ANY], out_specs=ANY, out_shape=sh...  58.8 us
    pallas_call x1, Pallas kernels, on_device(): pl.pallas_call(bwd_kernel, in_specs=[SM] + [VM] * 13, out_specs=[VM] * 3,...  58 us
    pallas_call x1, Pallas kernels, gather_weights(): pl.pallas_call(functools.partial(weights_kernel, tensor), in_specs=[VM],...  52.9 us
  transfers between devices with their start and end apart: 5, of which 1 were waited for; matrix products, arithmetic and copies ran while one was open for 5% of the time, Pallas kernels for 73%

profile of v2, /device:TPU:0, one launch (start us, length us, event | category | flops | bytes accessed | tf_op | source)
XLA Modules:
  0.0 627.3 jit_solution(12828866014173591030)
XLA Ops:
  7.3 31.4 %shard_map.277 = bf16[3,8,96,512]{3,2,1,0:T(8,128)(2,1)} custom-call(bf16[2,8,96,512]{3,2,1,0:T(8,128)(2,1)} %refs_0_.1, bf16[1,8,96,512]{3,2,1,0:T(8,128)(2,1)} %bitcast.39), custom_call_target="tpu_custom_call" | custom-call | flops 24999999488 | bytes 10000000 | tf_op jit(solution)/shard_map/pallas_call | solution.py:405
  38.8 0.6 copy.74.starts_ref
  39.6 0.6 reshape.94.ga_ref
  40.2 0.6 reshape.96.gm_ref
  40.7 0.6 convert_element_type.27.cv_ref
  41.4 0.6 pad.13.wres_ref
  42.1 0.2 copy.68
  42.5 0.2 copy.64
  42.7 0.8 pad.12.prior_ref
  43.4 0.7 constant_dynamic-slice_fusion
  44.2 1.0 copy.76.ranks_ref
  45.2 1.0 copy.75.ids_ref
  46.2 0.7 pad_maximum_fusion.w_ref
  46.9 0.8 maximum_maximum_fusion.wr_ref
  47.7 52.9 %shard_map.273.w_ref = bf16[4,768,768]{2,1,0:T(8,128)(2,1)} custom-call(bf16[4,96,192]{2,1,0:T(8,128)(2,1)} %pad_maximum_fusion.w_ref), custom_call_target="tpu_custom_call" | custom-call | flops 30000001024 | bytes 10000000 | tf_op jit(solution)/shard_map/pallas_call | solution.py:247
  100.6 73.5 %shard_map.274 = (bf16[1024,768]{1,0:T(8,128)(2,1)}, bf16[1024,768]{1,0:T(8,128)(2,1)}, bf16[1024,768]{1,0:T(8,128)(2,1)}, bf16[1024,768]{1,0:T(8,128)(2,1)}, f3...) custom-call(s32[1,2]{1,0:T(1,128)} %copy.74.starts_ref, ...), custom_call_target="tpu_custom_call" | custom-call | flops 40000000000 | bytes 30000000 | tf_op jit(solution)/shard_map/pallas_call | solution.py:1068
  174.1 1.5 copy.78
  175.6 3.4 all-to-all-start
  179.0 58.8 %shard_map.275.x_ref = bf16[8,1024,768]{2,1,0:T(8,128)(2,1)} custom-call(bf16[1024,768]{1,0:T(8,128)(2,1)} %get-tuple-element.49.src.nmoe_ref), custom_call_target="tpu_custom_call" | custom-call | flops 49999998976 | bytes 30000000 | tf_op jit(solution)/shard_map/pallas_call | solution.py:202
  237.8 0.7 fusion.1
  238.7 0.6 slice.50
  239.9 0.6 pad_add_fusion.meta_ref
  240.5 16.9 %shard_map.276 = (bf16[6656,768]{1,0:T(8,128)(2,1)}, bf16[6656,768]{1,0:T(8,128)(2,1)}, f32[6656,128]{1,0:T(8,128)}) custom-call(s32[18]{0:T(128)} %pad_add_fusion.meta_ref, f32[8,1,1024]{2,1,0:T(1,128)} %get-tuple-element.137.pos_ref, f32[8,1,1024]{2,1,0:T(1,128)} %get-tuple-element.135.gate_ref, bf16[8,1024,768]{2,1,0:T(8,128)(2,1)} %shard_map.275.x_ref, ...), custom_call_target="tpu_custom_call" | custom-call | flops 8000000000 | bytes 30000000 | tf_op jit(solution)/shard_map/pallas_call | solution.py:957
  257.5 63.8 %shard_map.278 = (bf16[6656,768]{1,0:T(8,128)(2,1)}, bf16[6656,768]{1,0:T(8,128)(2,1)}, f32[6656,128]{1,0:T(8,128)}, bf16[4,3,768,512]{3,2,1,0:T(8,128)(2,1)}) custom-call(s32[18]{0:T(128)} %pad_add_fusion.meta_ref, bf16[6656,768]{1,0:T(8,128)(2,1)} %get-tuple-element.51.x_ref, bf16[6656,768]{1,0:T(8,128)(2,1)} %get-tuple-element.52.y_ref, ...), custom_call_target="tpu_custom_call" | custom-call | flops 44000002048 | bytes 30000000 | tf_op jit(solution)/shard_map/pallas_call | solution.py:972
  321.4 16.0 %shard_map.279 = (bf16[8,1024,768]{2,1,0:T(8,128)(2,1)}, bf16[8,1024,768]{2,1,0:T(8,128)(2,1)}, f32[8,1,1024]{2,1,0:T(1,128)}) custom-call(s32[18]{0:T(128)} %pad_add_fusion.meta_ref, f32[8,1,1024]{2,1,0:T(1,128)} %get-tuple-element.137.pos_ref, bf16[6656,768]{1,0:T(8,128)(2,1)} %get-tuple-element.54.yc_ref, bf16[6656,768]{1,0:T(8,128)(2,1)} %get-tuple-element.55.dxc_ref, ...), custom_call_target="tpu_custom_call" | custom-call | flops 8000000000 | bytes 30000000 | tf_op jit(solution)/shard_map/pallas_call | solution.py:997
  337.5 13.1 %all-to-all-start.1 = ((f32[8,1,1024]{2,1,0:T(1,128)}), f32[8,1,1024]{2,1,0:T(1,128)S(1)}, u32[]{:S(2)}, u32[]{:S(2)}) async-start(f32[8,1,1024]{2,1,0:T(1,128)} %get-tuple-element.59), calls=%async_computation.2 | async-start | bytes 65536 | tf_op jit(solution)/shard_map/all_to_all | solution.py:1090
  350.6 61.1 %shard_map.280 = bf16[2,512,768]{2,1,0:T(8,128)(2,1)} custom-call(bf16[8,2,512,768]{3,2,1,0:T(8,128)(2,1)} %bitcast.40), custom_call_target="tpu_custom_call" | custom-call | flops 49999998976 | bytes 30000000 | tf_op jit(solution)/shard_map/pallas_call | solution.py:361
  411.7 0.2 copy.71
  411.9 0.8 pad_bitcast_fusion.gg_ref
  412.8 16.7 %shard_map.281 = (bf16[1024,768]{1,0:T(8,128)(2,1)}, f32[1024,768]{1,0:T(8,128)}, f32[1024,128]{1,0:T(8,128)}, f32[1,768]{1,0:T(1,128)}, f32[128,768]{1,0:T(8,12...) custom-call(bf16[1024,768]{1,0:T(8,128)(2,1)} %bitcast.33, f32[1024,128]{1,0:T(8,128)} %pad_bitcast_fusion.gg_ref, ...), custom_call_target="tpu_custom_call" | custom-call | flops 2000000000 | bytes 20000000 | tf_op jit(solution)/shard_map/pallas_call | solution.py:1106
  429.4 58.0 %shard_map.282 = (f32[1024,768]{1,0:T(8,128)}, bf16[4,768,768]{2,1,0:T(8,128)(2,1)}, f32[1,768]{1,0:T(1,128)}) custom-call(s32[1,2]{1,0:T(1,128)} %copy.74.starts_ref, bf16[1024,768]{1,0:T(8,128)(2,1)} %get-tuple-element.62.gmo_ref, f32[1024,768]{1,0:T(8,128)} %get-tuple-element.63.gres_ref, bf16[1024,768]{1,0:T(8,128)(2,1)} %get-tuple-element.64.mixed_ref, ...), custom_call_target="tpu_custom_call" | custom-call | flops 80000000000 | bytes 40000000 | tf_op jit(solution)/shard_map/pallas_call | solution.py:1117
  487.4 68.5 %shard_map.283 = (f32[4,96,192]{2,1,0:T(8,128)}, f32[56,768]{1,0:T(8,128)}) custom-call(bf16[4,768,768]{2,1,0:T(8,128)(2,1)} %get-tuple-element.72.g_ref, f32[128,768]{1,0:T(8,128)} %get-tuple-element.73.wrg_ref, f32[128,768]{1,0:T(8,128)} %get-tuple-element.74.cvg_ref, f32[128,128]{1,0:T(8,128)} %get-tuple-element.75.resg_ref, ...), custom_call_target="tpu_custom_call" | custom-call | flops 30000001024 | bytes 10000000 | tf_op jit(solution)/shard_map/pallas_call | solution.py:490
  556.0 1.3 slice.59
  557.3 1.3 slice.58
  558.6 0.7 slice.60
  559.4 0.6 reshape.92
  560.0 0.8 copy.72
  560.8 1.7 slice.54
  562.5 0.9 slice_bitcast_fusion.1
  563.4 0.7 copy.73
  564.1 1.4 slice_reduce_fusion
  565.6 1.4 slice_bitcast_fusion.2
  567.0 33.7 %shard_map.284 = bf16[3,8,96,512]{3,2,1,0:T(8,128)(2,1)} custom-call(bf16[3,8,96,512]{3,2,1,0:T(8,128)(2,1)} %bitcast.38), custom_call_target="tpu_custom_call" | custom-call | flops 24999999488 | bytes 10000000 | tf_op jit(solution)/shard_map/pallas_call | solution.py:405
  600.7 3.6 slice.65
  604.3 0.6 convert_element_type.31
  605.0 1.3 slice_bitcast_fusion
  606.3 11.2 %reduce-scatter.3.cloned.1.call-done = bf16[1024,768]{1,0:T(8,128)(2,1)} async-done(((bf16[8192,768]{1,0:T(8,128)(2,1)}), bf16[1024,768]{1,0:T(8,128)(2,1)}) %reduce-scatter.3.cloned.1.call-update) | async-done | bytes 1572880 | tf_op jit(solution)/shard_map/reduce_scatter | solution.py:1096
  617.5 3.0 add_convert_fusion
  (49 shorter events, 0.9 us)
Async XLA Ops:
  7.2 31.5 %copy-start = (s32[4,2]{0,1:T(2,128)S(1)}, s32[4,2]{0,1:T(2,128)}, u32[]{:S(2)}) copy-start(s32[4,2]{0,1:T(2,128)} %param.22) | copy-start | bytes 100
  7.2 250.3 %all-gather.2.cloned.1.call-start = ((), (), s32[]{:S(2)}) async-start(), calls=%async_computation.4 | async-start | bytes 11796480 | tf_op jit(solution)/shard_map/all_gather | solution.py:1060
  7.2 32.3 %copy-start.12 = (bf16[768]{0:T(1024)(128)(2,1)S(1)}, bf16[768]{0:T(1024)(128)(2,1)}, u32[]{:S(2)}) copy-start(bf16[768]{0:T(1024)(128)(2,1)} %param.23) | copy-start | bytes 4612
  7.3 32.9 %copy-start.13 = (bf16[768]{0:T(1024)(128)(2,1)S(1)}, bf16[768]{0:T(1024)(128)(2,1)}, u32[]{:S(2)}) copy-start(bf16[768]{0:T(1024)(128)(2,1)} %param.26) | copy-start | bytes 4612
  7.3 33.5 %copy-start.11 = (bf16[2,768]{1,0:T(2,128)(2,1)S(1)}, bf16[2,768]{1,0:T(2,128)(2,1)}, u32[]{:S(2)}) copy-start(bf16[2,768]{1,0:T(2,128)(2,1)} %param.29) | copy-start | bytes 9220
  7.3 34.1 %copy-start.9 = (bf16[2,2,768]{2,1,0:T(2,128)(2,1)S(1)}, bf16[2,2,768]{2,1,0:T(2,128)(2,1)}, u32[]{:S(2)}) copy-start(bf16[2,2,768]{2,1,0:T(2,128)(2,1)} %param.30) | copy-start | bytes 18436
  7.3 34.1 %copy-start.10 = (bf16[12,12]{1,0:T(8,128)(2,1)S(1)}, bf16[12,12]{1,0:T(8,128)(2,1)}, u32[]{:S(2)}) copy-start(bf16[12,12]{1,0:T(8,128)(2,1)} %param.28) | copy-start | bytes 868
  7.3 34.7 %copy-start.6 = (bf16[192,96]{1,0:T(8,128)(2,1)S(1)}, bf16[192,96]{1,0:T(8,128)(2,1)}, u32[]{:S(2)}) copy-start(bf16[192,96]{1,0:T(8,128)(2,1)} %param.25) | copy-start | bytes 110596
  7.3 35.0 %copy-start.8 = (bf16[768,12]{0,1:T(8,128)(2,1)S(1)}, bf16[768,12]{0,1:T(8,128)(2,1)}, u32[]{:S(2)}) copy-start(bf16[768,12]{0,1:T(8,128)(2,1)} %param.27) | copy-start | bytes 55300
  7.3 35.2 %copy-start.7 = (bf16[1024,12]{0,1:T(8,128)(2,1)S(1)}, bf16[1024,12]{0,1:T(8,128)(2,1)}, u32[]{:S(2)}) copy-start(bf16[1024,12]{0,1:T(8,128)(2,1)} %param.19) | copy-start | bytes 73732
  38.7 7.5 %copy-start.5 = (bf16[3,96,192]{2,1,0:T(8,128)(2,1)S(1)}, bf16[3,96,192]{2,1,0:T(8,128)(2,1)}, u32[]{:S(2)}) copy-start(bf16[3,96,192]{2,1,0:T(8,128)(2,1)} %param.24) | copy-start | bytes 331780
  175.6 62.2 %all-to-all-start = ((f32[8,2,1024]{2,1,0:T(2,128)}), f32[8,2,1024]{2,1,0:T(2,128)S(1)}, u32[]{:S(2)}, u32[]{:S(2)}) async-start(f32[8,2,1024]{2,1,0:T(2,128)} %bitcast.28), calls=%async_computation | async-start | bytes 131072 | tf_op jit(solution)/shard_map/all_to_all | solution.py:1088
  179.0 388.0 %reduce-scatter.5.cloned.1.call-start = ((), (), s32[]{:S(2)}) async-start(), calls=%async_computation.6 | async-start | bytes 11796480 | tf_op jit(solution)/shard_map/reduce_scatter | solution.py:1099
  321.3 296.2 %reduce-scatter.3.cloned.1.call-start = ((), (), s32[]{:S(2)}) async-start(), calls=%async_computation.5 | async-start | bytes 14155776 | tf_op jit(solution)/shard_map/reduce_scatter | solution.py:1096
  337.5 74.2 %all-to-all-start.1 = ((f32[8,1,1024]{2,1,0:T(1,128)}), f32[8,1,1024]{2,1,0:T(1,128)S(1)}, u32[]{:S(2)}, u32[]{:S(2)}) async-start(f32[8,1,1024]{2,1,0:T(1,128)} %get-tuple-element.59), calls=%async_computation.2 | async-start | bytes 65536 | tf_op jit(solution)/shard_map/all_to_all | solution.py:1090
  487.4 72.5 %copy-start.4 = (f32[1024,128]{1,0:T(8,128)S(1)}, f32[1024,128]{1,0:T(8,128)}, u32[]{:S(2)}) copy-start(f32[1024,128]{1,0:T(8,128)} %get-tuple-element.71) | copy-start | bytes 1572868
  600.7 3.7 copy-start.2
  605.0 12.6 %copy-start.3 = (f32[1024,768]{1,0:T(8,128)S(1)}, f32[1024,768]{1,0:T(8,128)}, u32[]{:S(2)}) copy-start(f32[1024,768]{1,0:T(8,128)} %get-tuple-element.47) | copy-start | bytes 9437188
  617.5 3.0 copy-start.1
Sparse Core Ops, SparseCore 0:
  38.8 183.8 all-gather.1
  321.5 183.1 reduce-scatter.4
  508.2 109.3 reduce-scatter.2

commit v3 on v0

--- a/solution.py
+++ b/solution.py
@@ -1,20 +1,1059 @@
+import functools
+
 import jax
 import jax.numpy as jnp
+import numpy as np
 from jax import lax
+from jax.experimental import pallas as pl
+from jax.experimental.pallas import tpu as pltpu
 from jax.sharding import PartitionSpec as P
 
 HD = 64
 NF = 8
+NC = 2
 SEQ = 1024
 PIECE = 256
+PIECES = 2
 CAP = 768
-
-
-eps = 1e-06
+EPS = 1e-06
+QT = 256
+LANES = 128
+TM = 256
+ROOM = 256
+Z0 = 16
+
+bf16 = jnp.bfloat16
+f32 = jnp.float32
+i32 = jnp.int32
+
+VM = pl.BlockSpec(memory_space=pltpu.VMEM)
+SM = pl.BlockSpec(memory_space=pltpu.SMEM)
+ANY = pl.BlockSpec(memory_space=pl.ANY)
+
+
+def nn(a, b):
+    return lax.dot_general(a, b, (((1,), (0,)), ((), ())), preferred_element_type=f32)
+
+
+def nt(a, b):
+    return lax.dot_general(a, b, (((1,), (1,)), ((), ())), preferred_element_type=f32)
+
+
+def tn(a, b):
+    return lax.dot_general(a, b, (((0,), (0,)), ((), ())), preferred_element_type=f32)
+
+
+def split(x):
+    hi = x.astype(bf16)
+    return hi, (x - hi.astype(f32)).astype(bf16)
+
+
+def lanes(rows):
+    return lax.broadcasted_iota(i32, (rows, LANES), 1)
+
+
+def rot(x, cosine, sine):
+    first = lanes(x.shape[0]) % HD < HD // 2
+    other = jnp.where(first, pltpu.roll(x, LANES - HD // 2, 1), pltpu.roll(x, HD // 2, 1))
+    return x * cosine + other * sine
+
+
+def head_masks():
+    low = lax.broadcasted_iota(i32, (1, LANES), 1) < HD
+    a = jnp.where(low, 1.0, 0.0)
+    return a, 1.0 - a
+
+
+def rotary_tables():
+    place = np.arange(SEQ, dtype=np.float32)
+    half = HD // 2
+    freqs = np.power(np.float32(10000.0), np.arange(half, dtype=np.float32) * np.float32(-2.0 / HD)).astype(np.float32)
+    angles = (place[:, None] * freqs[None, :]).astype(np.float32).astype(np.float64)
+    c, s = np.cos(angles).astype(np.float32), np.sin(angles).astype(np.float32)
+    return np.concatenate([c, c, c, c], 1), np.concatenate([-s, s, -s, s], 1)
+
+
+def window_bias(starts_ref, tile, width, transposed):
+    shape = (width, QT) if transposed else (QT, width)
+    qpos = lax.broadcasted_iota(i32, shape, 1 if transposed else 0) + tile * QT
+    kpos = lax.broadcasted_iota(i32, shape, 0 if transposed else 1) + tile * QT
+    seen = jnp.where(kpos <= qpos, 1, 0)
+    for piece in range(PIECES):
+        s = starts_ref[0, piece]
+        both = jnp.where(qpos >= s, 1, 0) * jnp.where(qpos < s + PIECE, 1, 0)
+        both = both * jnp.where(kpos >= s, 1, 0) * jnp.where(kpos < s + PIECE, 1, 0)
+        seen = jnp.maximum(seen, both)
+    return jnp.where(seen > 0, 0.0, -1e30)
+
+
+MESH = pl.DeviceIdType.MESH
+GATHER_COPIES = 13
+REDUCE_COPIES = 10
+
+
+def flip(index, m):
+    for bit in (1, 2, 4):
+        if m & bit:
+            index = index + bit - 2 * bit * (index // bit % 2)
+    return index
+
+
+def remote(src, dst, sems, n, axis, peer):
+    return pltpu.make_async_remote_copy(
+        src_ref=src,
+        dst_ref=dst,
+        send_sem=sems.at[0, n],
+        recv_sem=sems.at[1, n],
+        device_id={axis: peer},
+        device_id_type=MESH,
+    )
+
+
+def greet(peers):
+    barrier = pltpu.get_barrier_semaphore()
+    for axis, peer in peers:
+        pl.semaphore_signal(barrier, inc=1, device_id={axis: peer}, device_id_type=MESH)
+    pl.semaphore_wait(barrier, len(peers))
+
+
+def near_peers():
+    me = lax.axis_index("dp")
+    return [("dp", flip(me, m)) for m in (1, 2, 4)]
+
+
+def far_peers(tensor):
+    me = lax.axis_index("tensor")
+    return [("tensor", (me + k) % tensor) for k in range(1, tensor)]
+
+
+class Gather8:
+    def __init__(self, src, dst, sems, own_sem):
+        me = lax.axis_index("dp")
+        slot = me % NF
+        nx, ny, nc = flip(me, 2), flip(me, 4), flip(me, 1)
+        sx, sy, sd = flip(slot, 2), flip(slot, 4), flip(slot, 6)
+        self.own = pltpu.make_async_copy(src(None), dst(slot, None), own_sem)
+        go = lambda n, s, d, peer: remote(s, d, sems, n, "dp", peer)
+        on = lambda n, s, h, peer: go(n, dst(s, h), dst(s, h), peer)
+        self.c = [
+            go(0, src(0), dst(slot, 0), nx),
+            go(1, src(1), dst(slot, 1), ny),
+            go(2, src(1), dst(slot, 1), nx),
+            go(3, src(0), dst(slot, 0), ny),
+            go(4, src(None), dst(slot, None), nc),
+            on(5, sx, 0, ny),
+            on(6, sy, 1, nx),
+            on(7, sx, 0, nc),
+            on(8, sy, 1, nc),
+            on(9, sx, 1, nc),
+            on(10, sy, 0, nc),
+            on(11, sd, 0, nc),
+            on(12, sd, 1, nc),
+        ]
+
+    def begin(self):
+        self.own.start()
+        for n in range(5):
+            self.c[n].start()
+
+    def forward(self):
+        for got, out in ((0, (5, 7)), (1, (6, 8))):
+            self.c[got].wait_recv()
+            for n in out:
+                self.c[n].start()
+
+    def share(self):
+        for got, out in ((2, 9), (3, 10)):
+            self.c[got].wait_recv()
+            self.c[out].start()
+
+    def last(self):
+        for got, out in ((5, 11), (6, 12)):
+            self.c[got].wait_recv()
+            self.c[out].start()
+
+    def end(self):
+        for n in (4, 7, 8, 9, 10, 11, 12):
+            self.c[n].wait_recv()
+        for c in self.c:
+            c.wait_send()
+        self.own.wait()
+
+
+def halves(ref, index, rows):
+    half = rows // 2
+    return lambda s, h: ref.at[s] if h is None else ref.at[s, pl.ds(h * half, half)]
+
+
+def all_peers():
+    me = lax.axis_index("dp")
+    return [("dp", flip(me, m)) for m in range(1, NF)]
+
+
+class Swap8:
+    def __init__(self, src, dst, sems, own_sems):
+        me = lax.axis_index("dp")
+        slot = me % NF
+        count = src.shape[0] // NF
+        self.own = [
+            pltpu.make_async_copy(src.at[NF * i + slot], dst.at[NF * i + slot], own_sems.at[i]) for i in range(count)
+        ]
+        self.c = [
+            remote(
+                src.at[NF * i + flip(slot, m)], dst.at[NF * i + slot], sems, (m - 1) * count + i, "dp", flip(me, m)
+            )
+            for m in range(1, NF)
+            for i in range(count)
+        ]
+
+    def begin(self):
+        for c in self.own + self.c:
+            c.start()
+
+    def end(self):
+        for c in self.c:
+            c.wait_recv()
+        for c in self.c:
+            c.wait_send()
+        for c in self.own:
+            c.wait()
+
+
+def weights_kernel(slab, gu_ref, dn_ref, out_ref, wx_ref, sems, own_sem, *scratch):
+    k, r, _ = slab.shape
+    greet(all_peers())
+    part = lambda h: pl.ds(0, k) if h is None else pl.ds(h * (k // 2), k // 2)
+    g = Gather8(
+        lambda h: slab.at[part(h)],
+        lambda s, h: out_ref.at[part(h), pl.ds(pl.multiple_of(s * r, r), r), :],
+        sems,
+        own_sem,
+    )
+    swap = Exchange8([gu_ref, dn_ref], wx_ref, 1, *scratch)
+    g.begin()
+    swap.begin()
+    g.forward()
+    g.share()
+    g.last()
+    g.end()
+    swap.end()
+
+
+def gather_weights(w, gate_up, down, cid):
+    k, r, f = w.shape
+    return pl.pallas_call(
+        weights_kernel,
+        in_specs=[ANY] * 3,
+        out_specs=[ANY] * 2,
+        out_shape=(shape((k, NF * r, f), w.dtype), half_shape(gate_up)),
+        scratch_shapes=[
+            pltpu.SemaphoreType.DMA((2, GATHER_COPIES)),
+            pltpu.SemaphoreType.DMA,
+            *exchange_scratch(2),
+        ],
+        compiler_params=pltpu.CompilerParams(collective_id=cid, has_side_effects=True),
+        cost_estimate=cost(35, 10),
+    )(w, gate_up, down)
+
+
+def half_kernel(gu_ref, dn_ref, wx_ref, *scratch):
+    greet(all_peers())
+    swap = Exchange8([gu_ref, dn_ref], wx_ref, 1, *scratch)
+    swap.begin()
+    swap.end()
+
+
+def exchange_half(gate_up, down, cid):
+    return pl.pallas_call(
+        half_kernel,
+        in_specs=[ANY] * 2,
+        out_specs=ANY,
+        out_shape=half_shape(gate_up),
+        scratch_shapes=exchange_scratch(2),
+        compiler_params=pltpu.CompilerParams(collective_id=cid, has_side_effects=True),
+        cost_estimate=cost(25, 10),
+    )(gate_up, down)
+
+
+class Reduce8:
+    def __init__(self, view, bufs, sems, lsems):
+        self.own, self.away, self.ind, self.inx, self.iny = bufs
+        me = lax.axis_index("dp")
+        slot = me % NF
+        half = self.ind.shape[0] // 2
+        a, b = pl.ds(0, half), pl.ds(half, half)
+        self.a, self.b = a, b
+        nx, ny, nc = flip(me, 2), flip(me, 4), flip(me, 1)
+        mine = [flip(slot, m) for m in (6, 2, 4)] + [slot]
+        self.loads = [pltpu.make_async_copy(view(s), self.own.at[n % 2], lsems.at[n]) for n, s in enumerate(mine)]
+        self.over = [remote(view(flip(s, 1)), self.away.at[n], sems, n, "dp", nc) for n, s in enumerate(mine)]
+        go = lambda n, k, i, part, peer: remote(self.away.at[k, part], i.at[part], sems, n, "dp", peer)
+        self.da, self.db = go(4, 0, self.ind, a, nx), go(5, 0, self.ind, b, ny)
+        self.xa, self.yb = go(6, 1, self.inx, a, nx), go(7, 2, self.iny, b, ny)
+        self.ya, self.xb = go(8, 2, self.iny, a, ny), go(9, 1, self.inx, b, nx)
+
+    def load(self):
+        self.loads[0].start()
+        self.loads[1].start()
+
+    def begin(self):
+        for c in self.over:
+            c.start()
+
+    def add(self, n, part):
+        self.away[n, part] = (self.own[n % 2, part].astype(f32) + self.away[n, part].astype(f32)).astype(bf16)
+
+    def more(self, n, part):
+        self.away[n, part] = (self.away[n, part].astype(f32) + self.ind[part].astype(f32)).astype(bf16)
+
+    def ready(self, n):
+        self.loads[n].wait()
+        self.over[n].wait_recv()
+
+    def first(self):
+        self.ready(0)
+        self.add(0, self.a)
+        self.da.start()
+        self.add(0, self.b)
+        self.db.start()
+        self.loads[2].start()
+
+    def second(self):
+        self.ready(1)
+        self.add(1, self.a)
+        self.xa.start()
+        self.add(1, self.b)
+        self.loads[3].start()
+        self.ready(2)
+        self.add(2, self.b)
+        self.yb.start()
+        self.add(2, self.a)
+
+    def third(self):
+        self.da.wait_recv()
+        self.more(2, self.a)
+        self.ya.start()
+        self.db.wait_recv()
+        self.more(1, self.b)
+        self.xb.start()
+
+    def end(self, write):
+        self.ready(3)
+        for part, first, second in ((self.a, self.xa, self.ya), (self.b, self.yb, self.xb)):
+            first.wait_recv()
+            second.wait_recv()
+            total = self.own[1, part].astype(f32) + self.away[3, part].astype(f32)
+            write(part, total + self.inx[part].astype(f32) + self.iny[part].astype(f32))
+
+    def close(self):
+        for c in self.over + [self.da, self.db, self.xa, self.yb, self.ya, self.xb]:
+            c.wait_send()
+
+
+def reduce_scratch(block):
+    return [pltpu.VMEM((2, *block), bf16), pltpu.VMEM((4, *block), bf16)] + [pltpu.VMEM(block, bf16)] * 3 + [
+        pltpu.SemaphoreType.DMA((2, REDUCE_COPIES)),
+        pltpu.SemaphoreType.DMA((4,)),
+    ]
+
+
+class Exchange8:
+    def __init__(self, srcs, dst, part, sems, own_sems):
+        me = lax.axis_index("dp")
+        slot = me % NF
+        width = dst.shape[-1]
+
+        def piece(src, e):
+            return src.at[:, e] if part is None else src.at[:, e, :, pl.ds(part * width, width)]
+
+        at, pieces = 0, []
+        for src in srcs:
+            pieces.append((src, pl.ds(at, src.shape[0])))
+            at += src.shape[0]
+        self.own = [
+            pltpu.make_async_copy(piece(src, slot), dst.at[rows, slot], own_sems.at[i])
+            for i, (src, rows) in enumerate(pieces)
+        ]
+        self.c = [
+            remote(
+                piece(src, flip(slot, m)), dst.at[rows, slot], sems, (m - 1) * len(srcs) + i, "dp", flip(me, m)
+            )
+            for m in (6, 7, 2, 3, 4, 5, 1)
+            for i, (src, rows) in enumerate(pieces)
+        ]
+
+    def begin(self):
+        for c in self.c + self.own:
+            c.start()
+
+    def end(self):
+        for c in self.c:
+            c.wait_recv()
+        for c in self.c:
+            c.wait_send()
+        for c in self.own:
+            c.wait()
+
+
+class Send8:
+    order = (6, 7, 2, 3, 4, 5, 1)
+
+    def __init__(self, src, dst, sems, own_sem, packed):
+        me = lax.axis_index("dp")
+        slot = me % NF
+        at = lambda m: src.at[m] if packed else src.at[flip(slot, m)]
+        self.slot = slot
+        self.own = pltpu.make_async_copy(at(0), dst.at[slot], own_sem)
+        self.c = {m: remote(at(m), dst.at[slot], sems, m - 1, "dp", flip(me, m)) for m in self.order}
+
+    def start(self, m):
+        (self.c[m] if m else self.own).start()
+
+    def begin(self):
+        for m in (*self.order, 0):
+            self.start(m)
+
+    def got(self, m):
+        if m:
+            self.c[m].wait_recv()
+        else:
+            self.own.wait()
+
+    def close(self):
+        for c in self.c.values():
+            c.wait_send()
+
+
+def send_scratch():
+    return [pltpu.SemaphoreType.DMA((2, NF - 1)), pltpu.SemaphoreType.DMA]
+
+
+def half_shape(gate_up):
+    _, groups, r, f = gate_up.shape
+    return shape((3, groups, r, f // 2), bf16)
+
+
+def exchange_scratch(n):
+    return [pltpu.SemaphoreType.DMA((2, (NF - 1) * n)), pltpu.SemaphoreType.DMA((n,))]
+
+
+def prologue_kernel(tensor, gu_ref, dn_ref, w_ref, out_ref, slab_ref, zbuf, zsems, *scratch):
+    here = lax.axis_index("tensor")
+    k, _, f = w_ref.shape
+    greet(all_peers() + far_peers(tensor))
+    copies = [
+        remote(w_ref, zbuf.at[here], zsems, n, axis, peer) for n, (axis, peer) in enumerate(far_peers(tensor))
+    ]
+    for c in copies:
+        c.start()
+    swap = Exchange8([gu_ref, dn_ref], out_ref, 0, *scratch)
+    swap.begin()
+    zbuf[here] = w_ref[...]
+    for c in copies:
+        c.wait_recv()
+    for c in range(k):
+        for t in range(0, tensor, 2):
+            both = jnp.concatenate([zbuf[t, c].astype(f32), zbuf[t + 1, c].astype(f32)], axis=-1)
+            slab_ref[c, :, t * f : (t + 2) * f] = both.astype(bf16)
+    swap.end()
+    for c in copies:
+        c.wait_send()
+
+
+def prologue(gate_up, down, w, tensor, cid):
+    k, r, f = w.shape
+    return pl.pallas_call(
+        functools.partial(prologue_kernel, tensor),
+        in_specs=[ANY, ANY, VM],
+        out_specs=[ANY, VM],
+        out_shape=(half_shape(gate_up), shape((k, r, tensor * f), bf16)),
+        scratch_shapes=[
+            pltpu.VMEM((tensor, k, r, f), bf16),
+            pltpu.SemaphoreType.DMA((2, tensor - 1)),
+            *exchange_scratch(2),
+        ],
+        compiler_params=pltpu.CompilerParams(collective_id=cid, has_side_effects=True),
+        cost_estimate=cost(25, 10),
+    )(gate_up, down, w)
+
+
+def exchange_kernel(a_ref, b_ref, a_out, b_out, *scratch):
+    greet(all_peers())
+    swaps = [Exchange8([a_ref], a_out, None, *scratch[0:2]), Exchange8([b_ref], b_out, None, *scratch[2:4])]
+    for swap in swaps:
+        swap.begin()
+    for swap in swaps:
+        swap.end()
+
+
+def exchange8(a, b, cid):
+    return pl.pallas_call(
+        exchange_kernel,
+        in_specs=[ANY] * 2,
+        out_specs=[ANY] * 2,
+        out_shape=(shape(a.shape, a.dtype), shape(b.shape, b.dtype)),
+        scratch_shapes=exchange_scratch(1) + exchange_scratch(1),
+        compiler_params=pltpu.CompilerParams(collective_id=cid, has_side_effects=True),
+        cost_estimate=cost(25, 10),
+    )(a, b)
+
+
+def final_kernel(
+    tensor, g_ref, dwa_ref, dwb_ref, wrg_ref, cvg_ref, resg_ref, nmg_ref, nag_ref, count_ref, out_ref, small_ref, dwax_ref,
+    dwbx_ref, zf, zs, zr, sbuf, srecv, *scratch,
+):
+    here = lax.axis_index("tensor")
+    me = lax.axis_index("dp")
+    k, d, _ = g_ref.shape
+    r, f = out_ref.shape[1:]
+    zsems, ssems = scratch[7], scratch[8]
+    red = Reduce8(lambda s: g_ref.at[:, pl.ds(pl.multiple_of(s * r, r), r), :], scratch[:5], *scratch[5:7])
+    swaps = [
+        Exchange8([dwa_ref], dwax_ref, None, *scratch[9:11]), Exchange8([dwb_ref], dwbx_ref, None, *scratch[11:13])
+    ]
+    red.load()
+    sbuf[0] = jnp.zeros_like(sbuf[0])
+    sbuf[0, 0:24, :] = wrg_ref[0:24, :]
+    sbuf[0, 24:26, :] = cvg_ref[0:2, :]
+    sbuf[0, 26:27, :] = nmg_ref[...]
+    sbuf[0, 27:28, :] = nag_ref[...]
+    sbuf[0, 28:29, 0:LANES] = jnp.where(count_ref[...] > ROOM, 1.0, 0.0)
+    sbuf[0, 32:48, 0:LANES] = resg_ref[0:16, :]
+    greet(all_peers() + far_peers(tensor))
+    red.begin()
+    rounds = [remote(sbuf.at[n], srecv.at[n], ssems, n, "dp", flip(me, m)) for n, m in enumerate((1, 2, 4))]
+    rounds[0].start()
+    red.first()
+    for swap in swaps:
+        swap.begin()
+    rounds[0].wait_recv()
+    sbuf[1] = sbuf[0] + srecv[0]
+    rounds[1].start()
+    red.second()
+    rounds[1].wait_recv()
+    sbuf[2] = sbuf[1] + srecv[1]
+    rounds[2].start()
+    red.third()
+    rounds[2].wait_recv()
+    sbuf[3] = sbuf[2] + srecv[2]
+    far = [
+        remote(sbuf.at[3], srecv.at[3 + here], ssems, 3 + n, axis, peer)
+        for n, (axis, peer) in enumerate(far_peers(tensor))
+    ]
+    for c in far:
+        c.start()
+
+    def write(part, total):
+        for t in range(tensor):
+            zf[t, part] = total[:, :, t * f : (t + 1) * f]
+            zs[t, part] = total[:, :, t * f : (t + 1) * f].astype(bf16)
+
+    red.end(write)
+    out_copies = [
+        remote(zs.at[peer], zr.at[here], zsems, n, axis, peer) for n, (axis, peer) in enumerate(far_peers(tensor))
+    ]
+    for c in out_copies:
+        c.start()
+    srecv[3 + here] = sbuf[3]
+    for c in far:
+        c.wait_recv()
+    total = srecv[3]
+    for t in range(1, tensor):
+        total = total + srecv[3 + t]
+    small_ref[...] = total
+    zr[here] = jnp.zeros(zr.shape[1:], bf16)
+    for c in out_copies:
+        c.wait_recv()
+    total = zf[here]
+    for t in range(tensor):
+        total = total + zr[t].astype(f32)
+    out_ref[...] = total
+    red.close()
+    for c in rounds + far + out_copies:
+        c.wait_send()
+    for swap in swaps:
+        swap.end()
+
+
+def finish(g, dwa, dwb, wrg, cvg, resg, nmg, nag, count, tensor, cid):
+    k, d, columns = g.shape
+    r, f = d // NF, columns // tensor
+    return pl.pallas_call(
+        functools.partial(final_kernel, tensor),
+        in_specs=[ANY] * 3 + [VM] * 6,
+        out_specs=[VM] * 2 + [ANY] * 2,
+        out_shape=(shape((k, r, f), f32), shape((48, d), f32), shape(dwa.shape, bf16), shape(dwb.shape, bf16)),
+        scratch_shapes=[
+            pltpu.VMEM((tensor, k, r, f), f32),
+            pltpu.VMEM((tensor, k, r, f), bf16),
+            pltpu.VMEM((tensor, k, r, f), bf16),
+            pltpu.VMEM((4, 48, d), f32),
+            pltpu.VMEM((3 + tensor, 48, d), f32),
+            *reduce_scratch((k, r, columns)),
+            pltpu.SemaphoreType.DMA((2, tensor - 1)),
+            pltpu.SemaphoreType.DMA((2, 2 + tensor)),
+            *exchange_scratch(1),
+            *exchange_scratch(1),
+        ],
+        compiler_params=pltpu.CompilerParams(collective_id=cid, has_side_effects=True, vmem_limit_bytes=60 << 20),
+        cost_estimate=cost(30, 10),
+    )(g, dwa, dwb, wrg, cvg, resg, nmg, nag, count)
+
+
+def fwd_kernel(
+    starts_ref, tok_ref, prior_ref, ids_ref, ranks_ref, ga_ref, gm_ref, cos_ref, sin_ref, w_ref, wr_ref, wres_ref, cv_ref,
+    og_ref,
+    q_ref, k_ref, v_ref, mixed_ref, lse_ref, nattn_ref, resid_ref, nmoe_ref, base_ref, aux_ref, pos_ref, count_ref, xr_ref,
+    yr_ref, payr_ref,
+    bias_ref, gate_ref, xs, ys, pay, *scratch,
+):
+    greet(all_peers())
+    send_x, send_y = Send8(xs, xr_ref, *scratch[0:2], True), Send8(ys, yr_ref, *scratch[2:4], True)
+    swap = Swap8(pay, payr_ref, *scratch[4:6])
+    lane = lanes(QT)
+    lower = jnp.where(
+        lax.broadcasted_iota(i32, (QT, QT), 1) < lax.broadcasted_iota(i32, (QT, QT), 0), 1.0, 0.0
+    ).astype(bf16)
+
+    def hits(rows):
+        id0, id1 = ids_ref[rows, 0:1], ids_ref[rows, 1:2]
+        rk0, rk1 = ranks_ref[rows, 0:1], ranks_ref[rows, 1:2]
+        hit0, hit1 = jnp.where(lane == id0, 1.0, 0.0), jnp.where(lane == id1, 1.0, 0.0)
+        keep0, keep1 = jnp.where(rk0 < CAP, 1.0, 0.0), jnp.where(rk1 < CAP, 1.0, 0.0)
+        return hit0 + hit1, (hit0 * keep0 + hit1 * keep1) * jnp.where(lane < NF, 1.0, 0.0)
+
+    def places(i, taken):
+        rows = pl.ds(pl.multiple_of(i * QT, QT), QT)
+        _, kept = hits(rows)
+        pos = nn(lower, kept.astype(bf16)) + taken
+        pos_ref[:, 0, rows] = jnp.where(kept > 0, pos, -1.0).T[0:NF, :]
+        return taken + jnp.sum(kept, axis=0, keepdims=True)
+
+    count_ref[...] = lax.fori_loop(0, SEQ // QT, places, jnp.zeros((1, LANES), f32))
+    for m in (*Send8.order, 0):
+        ys[m] = nn(hot_rows(pos_ref[flip(send_y.slot, m)]), og_ref[...]).astype(bf16)
+        send_y.start(m)
+    d = tok_ref.shape[1]
+    pairs = d // LANES
+    ntile = SEQ // QT
+    ga, gm = ga_ref[...], gm_ref[...]
+    mask_a, mask_b = head_masks()
+    mask16 = (mask_a.astype(bf16), mask_b.astype(bf16))
+
+    def project(i, carry):
+        rows = pl.ds(pl.multiple_of(i * QT, QT), QT)
+        x = tok_ref[rows, :].astype(f32)
+        r1 = lax.rsqrt(jnp.mean(x * x, axis=-1, keepdims=True) + EPS)
+        n = (x * r1 * ga).astype(bf16)
+        nattn_ref[rows, :] = n
+        cosine, sine = cos_ref[rows, :], sin_ref[rows, :]
+        for c, out in ((0, q_ref), (1, k_ref), (2, v_ref)):
+            proj = nn(n, w_ref[c])
+            for p in range(pairs):
+                part = proj[:, p * LANES : (p + 1) * LANES]
+                if c < 2:
+                    part = rot(part, cosine, sine)
+                part = part.astype(bf16)
+                if c == 0:
+                    part = part * jnp.array(HD**-0.5, bf16)
+                out[rows, p * LANES : (p + 1) * LANES] = part
+        return carry
+
+    lax.fori_loop(0, ntile, project, 0)
+
+    for i in range(ntile):
+        lo = i * QT
+        width = min(SEQ, lo + 2 * QT) - lo
+        rows = pl.ds(lo, QT)
+        bias_ref[:, :width] = window_bias(starts_ref, i, width, False)
+
+        def pair(p, lse):
+            cols = pl.ds(pl.multiple_of(p * LANES, LANES), LANES)
+            q2 = q_ref[rows, cols]
+            outs = []
+            for h in range(2):
+                qh = q2 * mask16[h]
+                sb = nt(qh, k_ref[lo : lo + width, cols]) + bias_ref[:, :width]
+                m = jnp.max(sb, axis=-1, keepdims=True)
+                if lo:
+                    sa = nt(qh, k_ref[0:lo, cols])
+                    m = jnp.maximum(m, jnp.max(sa, axis=-1, keepdims=True))
+                pb = jnp.exp(sb - m)
+                total = jnp.sum(pb, axis=-1, keepdims=True)
+                acc = nn(pb.astype(bf16), v_ref[lo : lo + width, cols])
+                if lo:
+                    pa = jnp.exp(sa - m)
+                    total = total + jnp.sum(pa, axis=-1, keepdims=True)
+                    acc = acc + nn(pa.astype(bf16), v_ref[0:lo, cols])
+                outs.append(acc / total)
+                lse = jnp.where(lane == 2 * p + h, m + jnp.log(total), lse)
+            mixed_ref[rows, cols] = (outs[0] * mask_a + outs[1] * mask_b).astype(bf16)
+            return lse
+
+        lse = lax.fori_loop(0, pairs, pair, jnp.zeros((QT, LANES), f32))
+        lse_ref[:, rows] = lse.T[0 : lse_ref.shape[0], :]
+
+        x = tok_ref[rows, :].astype(f32)
+        resid = x + nt(mixed_ref[rows, :], w_ref[3])
+        resid_ref[rows, :] = resid
+        r2 = lax.rsqrt(jnp.mean(resid * resid, axis=-1, keepdims=True) + EPS)
+        nm = (resid * r2 * gm).astype(bf16)
+        nmoe_ref[rows, :] = nm
+        raw = nn(nm, wr_ref[...])
+        logits = raw + nn(prior_ref[rows, :], wres_ref[...])
+        logits = jnp.where(lane < NF + 2 + NC, logits, -1e30)
+        e = jnp.exp(logits - jnp.max(logits, axis=-1, keepdims=True))
+        shares = e / jnp.sum(e, axis=-1, keepdims=True)
+        chosen, kept = hits(rows)
+        gates = shares * chosen
+        gate_ref[:, 0, rows] = (shares * kept).T[0:NF, :]
+        nv = nm.astype(f32)
+        aux = jnp.where(lane < NF + 2 + NC, shares, 0.0)
+        direct = gates[:, NF + 1 : NF + 2]
+        others = None
+        for c in range(NC):
+            z0, z1 = raw[:, Z0 + 2 * c : Z0 + 2 * c + 1], raw[:, Z0 + 2 * c + 1 : Z0 + 2 * c + 2]
+            m0, m1 = 1.0 / (1.0 + jnp.exp(z1 - z0)), 1.0 / (1.0 + jnp.exp(z0 - z1))
+            aux = jnp.where(lane == Z0 + 2 * c, m0, aux)
+            aux = jnp.where(lane == Z0 + 2 * c + 1, m1, aux)
+            w = gates[:, NF + 2 + c : NF + 3 + c]
+            direct = direct + w * m0
+            term = (w * m1) * cv_ref[c : c + 1, :]
+            others = term if others is None else others + term
+        aux_ref[rows, :] = aux
+        base_ref[rows, :] = resid + direct * nv + others
+
+    for m in (*Send8.order, 0):
+        e = flip(send_x.slot, m)
+        place = pos_ref[e]
+        hot = hot_rows(place)
+        xs[m] = nn(hot, nmoe_ref[...]).astype(bf16)
+        send_x.start(m)
+        pay[e] = jnp.sum(nt(split_rows(gate_ref[e]), hot), axis=0, keepdims=True)
+        filled = jnp.minimum(jnp.max(place, axis=1, keepdims=True) + 1.0, float(ROOM))
+        pay[NF + e] = jnp.broadcast_to(filled, (1, ROOM))
+    swap.begin()
+    for send in (send_y, send_x):
+        for m in (*Send8.order, 0):
+            send.got(m)
+        send.close()
+    swap.end()
+
+
+def mid_kernel(
+    dxb_ref, ggb_ref, pos_ref, og_ref, nmoe_ref, resid_ref, ids_ref, aux_ref, prior_ref, wr_ref, wres_ref, cv_ref, gm_ref,
+    gmo_ref, gres_ref, pgrad_ref, nmg_ref, wrg_ref, resg_ref, cvg_ref,
+    dxr, ggr, dx_ref, gg_ref, *scratch,
+):
+    greet(all_peers())
+    send, swap = Send8(dxb_ref, dxr, *scratch[0:2], False), Swap8(ggb_ref, ggr, *scratch[2:4])
+    swap.begin()
+    send.begin()
+    swap.end()
+    for n, m in enumerate((0, 1, 2, 3, 4, 5, 6, 7)):
+        send.got(m)
+        e = flip(send.slot, m)
+        hot = hot_rows(pos_ref[e])
+        gg_ref[pl.ds(e, 1), :] = jnp.sum(nn(split_rows(ggr[e]), hot), axis=0, keepdims=True)
+        part = tn(hot, dxr[e])
+        if n:
+            dx_ref[...] += part
+        else:
+            dx_ref[...] = part
+    send.close()
+    gm = gm_ref[...]
+    lane = lanes(QT)
+    nmg_ref[...] = jnp.zeros_like(nmg_ref)
+    wrg_ref[...] = jnp.zeros_like(wrg_ref)
+    resg_ref[...] = jnp.zeros_like(resg_ref)
+    cvg_ref[...] = jnp.zeros_like(cvg_ref)
+
+    def tile(i, carry):
+        rows = pl.ds(pl.multiple_of(i * QT, QT), QT)
+        g16, n16 = og_ref[rows, :], nmoe_ref[rows, :]
+        g, nv = g16.astype(f32), n16.astype(f32)
+        x = resid_ref[rows, :]
+        r2 = lax.rsqrt(jnp.mean(x * x, axis=-1, keepdims=True) + EPS)
+        aux = aux_ref[rows, :]
+        shares = jnp.where(lane < NF + 2 + NC, aux, 0.0)
+        id0, id1 = ids_ref[rows, 0:1], ids_ref[rows, 1:2]
+        chosen = jnp.where(lane == id0, 1.0, 0.0) + jnp.where(lane == id1, 1.0, 0.0)
+        gates = shares * chosen
+        copy_inner = jnp.sum(g * nv, axis=-1, keepdims=True)
+        inner = jnp.concatenate([gg_ref[:, rows], jnp.zeros((LANES - NF, QT), f32)], axis=0).T
+        inner = jnp.where(lane == NF + 1, copy_inner, inner)
+        direct = gates[:, NF + 1 : NF + 2]
+        blend = jnp.zeros((QT, LANES), f32)
+        cvw = jnp.zeros((QT, LANES), f32)
+        for c in range(NC):
+            m0, m1 = aux[:, Z0 + 2 * c : Z0 + 2 * c + 1], aux[:, Z0 + 2 * c + 1 : Z0 + 2 * c + 2]
+            v_inner = jnp.sum(g * cv_ref[c : c + 1, :], axis=-1, keepdims=True)
+            mean = m0 * copy_inner + m1 * v_inner
+            inner = jnp.where(lane == NF + 2 + c, mean, inner)
+            w = gates[:, NF + 2 + c : NF + 3 + c]
+            direct = direct + w * m0
+            blend = jnp.where(lane == Z0 + 2 * c, m0 * (w * copy_inner - w * mean), blend)
+            blend = jnp.where(lane == Z0 + 2 * c + 1, m1 * (w * v_inner - w * mean), blend)
+            cvw = jnp.where(lane == c, w * m1, cvw)
+        grad_router = inner * chosen
+        glog = shares * (grad_router - jnp.sum(shares * grad_router, axis=-1, keepdims=True))
+        both_hi, both_lo = split(glog + blend)
+        log_hi, log_lo = split(glog)
+        cv_hi, cv_lo = split(cvw)
+        pgrad_ref[rows, :] = nt(log_hi, wres_ref[...]) + nt(log_lo, wres_ref[...])
+        wrg_ref[...] += tn(both_hi, n16) + tn(both_lo, n16)
+        resg_ref[...] += tn(prior_ref[rows, :], log_hi) + tn(prior_ref[rows, :], log_lo)
+        cvg_ref[...] += tn(cv_hi, g16) + tn(cv_lo, g16)
+        gmi = dx_ref[rows, :] + direct * g + nt(both_hi, wr_ref[...]) + nt(both_lo, wr_ref[...])
+        nmg_ref[...] += jnp.sum(gmi * x * r2, axis=0, keepdims=True)
+        scaled = gmi * gm
+        avg = jnp.mean(scaled * x, axis=-1, keepdims=True)
+        gres = g + r2 * scaled - x * (r2 * r2 * r2 * avg)
+        gres_ref[rows, :] = gres
+        gmo_ref[rows, :] = gres.astype(bf16)
+        return carry
+
+    lax.fori_loop(0, SEQ // QT, tile, 0)
+
+
+def bwd_kernel(
+    starts_ref, gmo_ref, gres_ref, mixed_ref, q_ref, k_ref, v_ref, lse_ref, nattn_ref, tok_ref, ga_ref, cos_ref,
+    sin_ref, w_ref, outb_ref, pos_ref, base_ref,
+    igrad_ref, wg_ref, nag_ref, layer_ref,
+    do_ref, delta_ref, bias_ref, gp_ref, dk_ref, dv_ref, dq_ref, outr, *scratch,
+):
+    greet(all_peers())
+    send = Send8(outb_ref, outr, *scratch, False)
+    send.begin()
+    d = tok_ref.shape[1]
+    pairs = d // LANES
+    ntile = SEQ // QT
+    ga = ga_ref[...]
+    mask_a, mask_b = head_masks()
+    mask16 = (mask_a.astype(bf16), mask_b.astype(bf16))
+    maskf = (mask_a, mask_b)
+    heads = delta_ref.shape[0]
+    pick = jnp.where(
+        lax.broadcasted_iota(i32, (heads, d), 1) // HD == lax.broadcasted_iota(i32, (heads, d), 0), 1.0, 0.0
+    ).astype(bf16)
+
+    def start(i, carry):
+        rows = pl.ds(pl.multiple_of(i * QT, QT), QT)
+        do = nn(gmo_ref[rows, :], w_ref[3]).astype(bf16)
+        do_ref[rows, :] = do
+        hi, lo = split(do.astype(f32) * mixed_ref[rows, :].astype(f32))
+        delta_ref[:, rows] = nt(pick, hi) + nt(pick, lo)
+        return carry
+
+    lax.fori_loop(0, ntile, start, 0)
+    wg_ref[3] = tn(gmo_ref[...], mixed_ref[...]).astype(wg_ref.dtype)
+    for i in range(ntile):
+        width = min(SEQ, (i + 2) * QT) - i * QT
+        bias_ref[i, 0:width, :] = window_bias(starts_ref, i, width, True)
+
+    def pair(p, carry):
+        cols = pl.ds(pl.multiple_of(p * LANES, LANES), LANES)
+        dk_ref[...] = jnp.zeros_like(dk_ref)
+        dv_ref[...] = jnp.zeros_like(dv_ref)
+        for i in range(ntile):
+            lo = i * QT
+            width = min(SEQ, lo + 2 * QT) - lo
+            rows = pl.ds(lo, QT)
+            q2, do2 = q_ref[rows, cols], do_ref[rows, cols]
+            dq = jnp.zeros((QT, LANES), f32)
+            for h in range(2):
+                qh, doh = q2 * mask16[h], do2 * mask16[h]
+                lse, delta = lse_ref[pl.ds(2 * p + h, 1), rows], delta_ref[pl.ds(2 * p + h, 1), rows]
+                spans = [(lo, width, True)] + ([(0, lo, False)] if lo else [])
+                for at, size, masked in spans:
+                    k2 = k_ref[at : at + size, cols]
+                    s = nt(k2, qh)
+                    if masked:
+                        s = s + bias_ref[i, 0:size, :]
+                    prob = jnp.exp(s - lse)
+                    ds = (prob * (nt(v_ref[at : at + size, cols], doh) - delta)).astype(bf16)
+                    dv_ref[at : at + size, :] += nn(prob.astype(bf16), doh)
+                    dk_ref[at : at + size, :] += nn(ds, qh)
+                    dq = dq + tn(ds, k2) * maskf[h]
+            dq_ref[rows, :] = dq * HD**-0.5
+        cosine, sine = cos_ref[...], -sin_ref[...]
+        gp_ref[0, :, cols] = rot(dq_ref[...], cosine, sine).astype(bf16)
+        gp_ref[1, :, cols] = rot(dk_ref[...], cosine, sine).astype(bf16)
+        gp_ref[2, :, cols] = dv_ref[...].astype(bf16)
+        return carry
+
+    lax.fori_loop(0, pairs, pair, 0)
+    for c in range(3):
+        wg_ref[c] = tn(nattn_ref[...], gp_ref[c]).astype(wg_ref.dtype)
+    nag_ref[...] = jnp.zeros_like(nag_ref)
+    for m in range(NF):
+        send.got(m)
+
+    def finish(i, carry):
+        rows = pl.ds(pl.multiple_of(i * QT, QT), QT)
+        layer = base_ref[rows, :]
+        for e in range(NF):
+            layer = layer + tn(hot_rows(pos_ref[e, :, rows]), outr[e])
+        layer_ref[rows, :] = layer.astype(bf16)
+        gai = nt(gp_ref[0, rows, :], w_ref[0]) + nt(gp_ref[1, rows, :], w_ref[1])
+        gai = gai + nt(gp_ref[2, rows, :], w_ref[2])
+        x = tok_ref[rows, :].astype(f32)
+        r1 = lax.rsqrt(jnp.mean(x * x, axis=-1, keepdims=True) + EPS)
+        nag_ref[...] += jnp.sum(gai * x * r1, axis=0, keepdims=True)
+        scaled = gai * ga
+        avg = jnp.mean(scaled * x, axis=-1, keepdims=True)
+        igrad_ref[rows, :] = gres_ref[rows, :] + r1 * scaled - x * (r1 * r1 * r1 * avg)
+        return carry
+
+    lax.fori_loop(0, ntile, finish, 0)
+    send.close()
+
+
+def ffn_tile(x, gate, y, w_ref, acc, eo, dx):
+    dy = y.astype(f32)
+    ge = (gate * dy).astype(bf16)
+    x_t, ge_t = x.T, ge.T
+    for c in range(w_ref.shape[0]):
+        wg, wu, wd = w_ref[c, 0], w_ref[c, 1], w_ref[c, 2]
+        gv, uv = nn(x, wg), nn(x, wu)
+        gh = nn(ge, wd)
+        sig = 1.0 / (1.0 + jnp.exp(-gv))
+        act = gv * sig
+        hid = (act * uv).astype(bf16)
+        eo = eo + nt(hid, wd)
+        gg = (gh * uv * (sig * (1.0 + gv * (1.0 - sig)))).astype(bf16)
+        gu = (gh * act).astype(bf16)
+        dx = dx + nt(gg, wg) + nt(gu, wu)
+        acc[c, 0] += nn(x_t, gg)
+        acc[c, 1] += nn(x_t, gu)
+        acc[c, 2] += nn(ge_t, hid)
+    return eo, dx
+
+
+def first_kernel(pay_ref, x_ref, y_ref, w_ref, xc_ref, yc_ref, gc_ref, eo_ref, dx_ref, dw_ref, meta_ref, acc):
+    d = x_ref.shape[2]
+    gates = [pay_ref[g] for g in range(NF)] + [jnp.zeros((LANES - NF, ROOM), f32)]
+    columns = jnp.concatenate(gates, axis=0).T
+    off = jnp.int32(0)
+    for g in range(NF):
+        rows = pl.ds(pl.multiple_of(off, 16), ROOM)
+        xc_ref[rows, :] = x_ref[g]
+        yc_ref[rows, :] = y_ref[g]
+        gc_ref[rows, :] = jnp.broadcast_to(columns[:, g : g + 1], (ROOM, LANES))
+        meta_ref[g] = off
+        off = off + (jnp.max(pay_ref[NF + g]).astype(i32) + 15) // 16 * 16
+    rows = pl.ds(pl.multiple_of(off, 16), TM)
+    xc_ref[rows, :] = jnp.zeros((TM, d), bf16)
+    yc_ref[rows, :] = jnp.zeros((TM, d), bf16)
+    gc_ref[rows, :] = jnp.zeros((TM, LANES), f32)
+    tiles = jnp.maximum((off + TM - 1) // TM, 1)
+    meta_ref[NF] = tiles
+    acc[...] = jnp.zeros_like(acc)
+    zero = jnp.zeros((TM, d), f32)
+
+    def tile(t, carry):
+        rows = pl.ds(pl.multiple_of(t * TM, TM), TM)
+        eo_ref[rows, :], dx_ref[rows, :] = ffn_tile(
+            xc_ref[rows, :], gc_ref[rows, 0:1], yc_ref[rows, :], w_ref, acc, zero, zero
+        )
+        return carry
+
+    lax.fori_loop(0, tiles, tile, 0)
+    dw_ref[...] = acc[...].astype(bf16)
+
+
+def second_kernel(
+    meta_ref, xc_ref, yc_ref, gc_ref, eo_ref, dx_ref, w_ref, outb_ref, dxb_ref, ggb_ref, dw_ref, outs, dxs, ggs, acc
+):
+    d = xc_ref.shape[1]
+    tiles = meta_ref[NF]
+    acc[...] = jnp.zeros_like(acc)
+    rows = pl.ds(pl.multiple_of(tiles * TM, TM), ROOM)
+    outs[rows, :] = jnp.zeros((ROOM, d), bf16)
+    dxs[rows, :] = jnp.zeros((ROOM, d), bf16)
+    ggs[rows, :] = jnp.zeros((ROOM, LANES), f32)
+
+    def tile(t, carry):
+        rows = pl.ds(pl.multiple_of(t * TM, TM), TM)
+        gate, y = gc_ref[rows, 0:1], yc_ref[rows, :]
+        eo, dx = ffn_tile(xc_ref[rows, :], gate, y, w_ref, acc, eo_ref[rows, :], dx_ref[rows, :])
+        outs[rows, :] = (gate * eo).astype(bf16)
+        dxs[rows, :] = dx.astype(bf16)
+        ggs[rows, :] = jnp.broadcast_to(jnp.sum(y.astype(f32) * eo, axis=1, keepdims=True), (TM, LANES))
+        return carry
+
+    lax.fori_loop(0, tiles, tile, 0)
+    lane = lanes(ROOM)
+    columns = jnp.zeros((ROOM, LANES), f32)
+    for g in range(NF):
+        rows = pl.ds(pl.multiple_of(meta_ref[g], 16), ROOM)
+        outb_ref[g] = outs[rows, :]
+        dxb_ref[g] = dxs[rows, :]
+        columns = jnp.where(lane == g, ggs[rows, :], columns)
+    ggb_ref[:, 0, :] = columns.T[0:NF, :]
+    dw_ref[...] = acc[...].astype(bf16)
+
+
+def experts_first(pay, x, y, w):
+    groups, _, d = x.shape
+    total = groups * ROOM + TM
+    return pl.pallas_call(
+        first_kernel,
+        in_specs=[VM] * 4,
+        out_specs=[VM] * 6 + [SM],
+        out_shape=(
+            shape((total, d), bf16), shape((total, d), bf16), shape((total, LANES), f32), shape((total, d), f32),
+            shape((total, d), f32), shape(w.shape, bf16), shape((NF + 1,), i32),
+        ),
+        scratch_shapes=[pltpu.VMEM(w.shape, f32)],
+        compiler_params=pltpu.CompilerParams(vmem_limit_bytes=60 << 20),
+        cost_estimate=cost(22, 25),
+    )(pay, x, y, w)
+
+
+def experts_second(meta, xc, yc, gc, eo, dx, w):
+    total, d = xc.shape
+    blocks = shape((NF, ROOM, d), bf16)
+    room = total + ROOM
+    return pl.pallas_call(
+        second_kernel,
+        in_specs=[SM] + [VM] * 6,
+        out_specs=[VM] * 4,
+        out_shape=(blocks, blocks, shape((NF, 1, ROOM), f32), shape(w.shape, bf16)),
+        scratch_shapes=[
+            pltpu.VMEM((room, d), bf16),
+            pltpu.VMEM((room, d), bf16),
+            pltpu.VMEM((room, LANES), f32),
+            pltpu.VMEM(w.shape, f32),
+        ],
+        compiler_params=pltpu.CompilerParams(vmem_limit_bytes=60 << 20),
+        cost_estimate=cost(22, 25),
+    )(meta, xc, yc, gc, eo, dx, w)
+
+
+def hot_rows(pos):
+    slot = lax.broadcasted_iota(i32, (ROOM, pos.shape[1]), 0).astype(f32)
+    return jnp.where(slot == pos, 1.0, 0.0).astype(bf16)
+
+
+def split_rows(row):
+    hi = row.astype(bf16).astype(f32)
+    mid = (row - hi).astype(bf16).astype(f32)
+    at = lax.broadcasted_iota(i32, (8, row.shape[1]), 0)
+    out = jnp.where(at == 0, hi, jnp.where(at == 1, mid, jnp.where(at == 2, row - hi - mid, 0.0)))
+    return out.astype(bf16)
+
+
+def shape(dims, dtype):
+    return jax.ShapeDtypeStruct(dims, dtype)
+
+
+def cost(gflop, mbytes, mexp=0):
+    return pl.CostEstimate(flops=int(gflop * 1e9), bytes_accessed=int(mbytes * 1e6), transcendentals=int(mexp * 1e6))
 
 
 def rms_factor(values):
-    return lax.rsqrt(jnp.mean(values * values, axis=-1, keepdims=True) + eps)
+    return lax.rsqrt(jnp.mean(values * values, axis=-1, keepdims=True) + EPS)
 
 
 def norm_back(grad, values, factor, gain):
@@ -103,7 +1142,7 @@
     return (grad_query, grad_keys, grad_values)
 
 
-def on_device(
+def plain_on_device(
     tokens,
     prior_logits,
     expert_ids,
@@ -347,42 +1386,195 @@
     )
 
 
+def on_device(
+    dp,
+    tensor,
+    tokens,
+    prior_logits,
+    expert_ids,
+    expert_ranks,
+    piece_starts,
+    norm_attn,
+    qkv_weight,
+    out_weight,
+    norm_moe,
+    router_weight,
+    residual_weight,
+    const_vectors,
+    const_gates,
+    w_gate_up,
+    w_down,
+    out_grad,
+):
+    rows, d = tokens.shape
+    ne = router_weight.shape[1]
+    packs = dp // NF
+    groups = None if packs == 1 else [list(range(NF * r, NF * (r + 1))) for r in range(packs)]
+    across = None if packs == 1 else [list(range(j, dp, NF)) for j in range(NF)]
+    here = lax.axis_index("tensor")
+    ids = lax.dynamic_slice_in_dim(expert_ids, here * rows, rows, 0)
+    ranks = lax.dynamic_slice_in_dim(expert_ranks, here * rows, rows, 0)
+    starts = lax.dynamic_slice_in_dim(piece_starts, here, 1, 0)
+    ga, gm = norm_attn.astype(f32).reshape(1, d), norm_moe.astype(f32).reshape(1, d)
+    cosine, sine = (jnp.asarray(t) for t in rotary_tables())
+    prior = jnp.pad(prior_logits, ((0, 0), (0, LANES - ne)))
+    wr = jnp.concatenate(
+        [router_weight, jnp.zeros((d, Z0 - ne), bf16), const_gates.reshape(2 * NC, d).T,
+         jnp.zeros((d, LANES - Z0 - 2 * NC), bf16)], axis=1)
+    wres = jnp.pad(residual_weight, ((0, LANES - ne), (0, LANES - ne)))
+    cv = const_vectors.astype(f32)
+
+    w_attn = jnp.concatenate([qkv_weight, out_weight.T[None]], axis=0)
+    w_down_t = w_down.transpose(0, 2, 1)[None]
+    shard = w_down.shape[1]
+    w_first, slab = prologue(w_gate_up, w_down_t, w_attn, tensor, 1)
+    if packs > 1:
+        w_attn = lax.all_gather(slab, "dp", axis=1, tiled=True)
+        w_second = exchange_half(w_gate_up, w_down_t, 2)
+    else:
+        w_attn, w_second = gather_weights(slab, w_gate_up, w_down_t, 2)
+
+    def whole(w):
+        w = w.reshape(3, -1, w.shape[3])
+        if packs > 1:
+            w = lax.all_gather(w, "dp", axis=1, tiled=True, axis_index_groups=across)
+        return lax.all_gather(w, "tensor", axis=0, tiled=False)
+
+    w_first, w_second = whole(w_first), whole(w_second)
+
+    heads = 16
+    blocks = shape((NF, ROOM, d), bf16)
+    q, k, v, mixed, lse, nattn, resid, nmoe, base, aux, pos, count, x_b, y_b, pay = pl.pallas_call(
+        fwd_kernel,
+        in_specs=[SM] + [VM] * 13,
+        out_specs=[VM] * 12 + [ANY] * 3,
+        out_shape=(
+            shape((rows, d), bf16), shape((rows, d), bf16), shape((rows, d), bf16), shape((rows, d), bf16),
+            shape((heads, rows), f32), shape((rows, d), bf16), shape((rows, d), f32), shape((rows, d), bf16),
+            shape((rows, d), f32), shape((rows, LANES), f32), shape((NF, 1, rows), f32), shape((1, LANES), f32),
+            blocks, blocks, shape((2 * NF, 1, ROOM), f32),
+        ),
+        scratch_shapes=[
+            pltpu.VMEM((QT, 2 * QT), f32),
+            pltpu.VMEM((NF, 1, rows), f32),
+            pltpu.VMEM((NF, ROOM, d), bf16),
+            pltpu.VMEM((NF, ROOM, d), bf16),
+            pltpu.VMEM((2 * NF, 1, ROOM), f32),
+            *send_scratch(),
+            *send_scratch(),
+            pltpu.SemaphoreType.DMA((2, 2 * (NF - 1))),
+            pltpu.SemaphoreType.DMA((2,)),
+        ],
+        compiler_params=pltpu.CompilerParams(collective_id=3, has_side_effects=True, vmem_limit_bytes=60 << 20),
+        cost_estimate=cost(40, 30, 10),
+    )(starts, tokens, prior, ids, ranks, ga, gm, cosine, sine, w_attn, wr, wres, cv, out_grad)
+
+    xc, yc, gc, eo, dx, dw_a, meta = experts_first(pay, x_b, y_b, w_first)
+    out_b, dx_b, gg_b, dw_b = experts_second(meta, xc, yc, gc, eo, dx, w_second)
+
+    def owned(dw):
+        dw = lax.psum_scatter(dw, "tensor", scatter_dimension=0, tiled=False)
+        if packs > 1:
+            dw = lax.psum_scatter(dw, "dp", scatter_dimension=1, tiled=True, axis_index_groups=across)
+        return dw.reshape(3, NF, -1, dw.shape[-1])
+
+    dw_a = owned(dw_a)
+
+    gmo, gres, pgrad, nmg, wrg, resg, cvg = pl.pallas_call(
+        mid_kernel,
+        in_specs=[ANY] * 2 + [VM] * 11,
+        out_specs=[VM] * 7,
+        out_shape=(
+            shape((rows, d), bf16), shape((rows, d), f32), shape((rows, LANES), f32), shape((1, d), f32),
+            shape((LANES, d), f32), shape((LANES, LANES), f32), shape((LANES, d), f32),
+        ),
+        scratch_shapes=[
+            pltpu.VMEM((NF, ROOM, d), bf16),
+            pltpu.VMEM((NF, 1, ROOM), f32),
+            pltpu.VMEM((rows, d), f32),
+            pltpu.VMEM((NF, rows), f32),
+            *send_scratch(),
+            pltpu.SemaphoreType.DMA((2, NF - 1)),
+            pltpu.SemaphoreType.DMA((1,)),
+        ],
+        compiler_params=pltpu.CompilerParams(collective_id=4, has_side_effects=True, vmem_limit_bytes=60 << 20),
+        cost_estimate=cost(4, 4),
+    )(dx_b, gg_b, pos, out_grad, nmoe, resid, ids, aux, prior, wr, wres, cv, gm)
+    dw_a, dw_b, gmo = lax.optimization_barrier((dw_a, dw_b, gmo))
+    dw_b = owned(dw_b)
+    igrad, wg, nag, layer_out = pl.pallas_call(
+        bwd_kernel,
+        in_specs=[SM] + [VM] * 13 + [ANY] + [VM] * 2,
+        out_specs=[VM] * 4,
+        out_shape=(shape((rows, d), f32), shape((4, d, d), bf16), shape((1, d), f32), shape((rows, d), bf16)),
+        scratch_shapes=[
+            pltpu.VMEM((rows, d), bf16),
+            pltpu.VMEM((heads, rows), f32),
+            pltpu.VMEM((rows // QT, 2 * QT, QT), f32),
+            pltpu.VMEM((3, rows, d), bf16),
+            pltpu.VMEM((rows, LANES), f32),
+            pltpu.VMEM((rows, LANES), f32),
+            pltpu.VMEM((rows, LANES), f32),
+            pltpu.VMEM((NF, ROOM, d), bf16),
+            *send_scratch(),
+        ],
+        compiler_params=pltpu.CompilerParams(collective_id=5, has_side_effects=True, vmem_limit_bytes=60 << 20),
+        cost_estimate=cost(8, 4),
+    )(starts, gmo, gres, mixed, q, k, v, lse, nattn, tokens, ga, cosine, sine, w_attn, out_b, pos, base)
+
+    if packs > 1:
+        wg = lax.psum_scatter(wg, "dp", scatter_dimension=1, tiled=True)
+        wg = lax.psum_scatter(wg, "tensor", scatter_dimension=2, tiled=True).astype(f32)
+        over = jnp.where(count > ROOM, 1.0, 0.0)
+        wrg, cvg, resg, nmg, nag, over = lax.psum((wrg, cvg, resg, nmg, nag, over), ("dp", "tensor"))
+        dw_a, dw_b = exchange8(dw_a, dw_b, 6)
+    else:
+        wg, small, dw_a, dw_b = finish(wg, dw_a, dw_b, wrg, cvg, resg, nmg, nag, count, tensor, 7)
+        wrg, cvg, resg, nmg, nag = small[0:24], small[24:26], small[32:48, 0:LANES], small[26], small[27]
+        over = small[28:29, 0:LANES]
+    overflow = jnp.sum(over) > 0
+
+    def roomy(args):
+        return plain_on_device(*args)
+
+    def packed(args):
+        dw = jnp.concatenate([dw_a, dw_b], axis=-1).astype(f32)
+        return (
+            layer_out,
+            igrad,
+            pgrad[:, 0:ne],
+            nag.reshape(d),
+            wg[0:3],
+            wg[3].T,
+            nmg.reshape(d),
+            wrg[0:ne].T,
+            resg[0:ne, 0:ne],
+            cvg[0:NC],
+            wrg[Z0 : Z0 + 2 * NC].reshape(NC, 2, d),
+            dw[0:2],
+            dw[2].transpose(0, 2, 1),
+        )
+
+    args = (
+        tokens, prior_logits, expert_ids, expert_ranks, piece_starts, norm_attn, qkv_weight, out_weight, norm_moe,
+        router_weight, residual_weight, const_vectors, const_gates, w_gate_up, w_down, out_grad,
+    )
+    return lax.cond(overflow, roomy, packed, args)
+
+
 def solution(mesh):
+    body = functools.partial(on_device, mesh.shape["dp"], mesh.shape["tensor"])
+    rows = P(("dp", "tensor"), None)
     return jax.shard_map(
-        on_device,
+        body,
         mesh=mesh,
         in_specs=(
-            P(("dp", "tensor"), None),
-            P(("dp", "tensor"), None),
-            P("dp", None),
-            P("dp", None),
-            P("dp", None),
-            P(),
-            P(None, "dp", "tensor"),
-            P("tensor", "dp"),
-            P(),
-            P(),
-            P(),
-            P(),
-            P(),
-            P(None, None, "dp", "tensor"),
-            P(None, "tensor", "dp"),
-            P(("dp", "tensor"), None),
+            rows, rows, P("dp", None), P("dp", None), P("dp", None), P(), P(None, "dp", "tensor"), P("tensor", "dp"),
+            P(), P(), P(), P(), P(), P(None, None, "dp", "tensor"), P(None, "tensor", "dp"), rows,
         ),
         out_specs=(
-            P(("dp", "tensor"), None),
-            P(("dp", "tensor"), None),
-            P(("dp", "tensor"), None),
-            P(),
-            P(None, "dp", "tensor"),
-            P("tensor", "dp"),
-            P(),
-            P(),
-            P(),
-            P(),
-            P(),
-            P(None, None, "dp", "tensor"),
-            P(None, "tensor", "dp"),
+            rows, rows, rows, P(), P(None, "dp", "tensor"), P("tensor", "dp"), P(), P(), P(), P(), P(),
+            P(None, None, "dp", "tensor"), P(None, "tensor", "dp"),
         ),
         check_vma=False,
     )

time: 2320 us -> 513 us (0.22)
  waiting for transfers between devices: 980 us -> 24.3 us
  local copies, waits for them, and re-layouts: 674 us -> 22.7 us
  Pallas kernels: 0 us -> 435 us
  matrix products: 310 us -> 0 us
  other arithmetic: 226 us -> 9.49 us
  blocking collectives: 95.2 us -> 0 us
    reduce_scatter x6 -> x2, waiting for transfers between devices: 683 us -> 22.3 us  [owned(): dw = lax.psum_scatter(dw, 'tensor', scatter_dimension=0, tiled=False)]
    pallas_call x0 -> x8, Pallas kernels: none -> 435 us  [the longest x1 95.5 us: on_device(): pl.pallas_call(fwd_kernel, in_specs=[SM] + [VM] * 13, out_specs=[VM] * 12...]
    gather x14 -> x0, local copies, waits for them, and re-layouts: 333 us -> none  [the longest x2 75.8 us: on_device(): combined = jnp.sum(retained_gates[:, :, None] * expert_out[picker], axis=1)]
    dot_general x49 -> x0, matrix products: 297 us -> none  [the longest x4 35.6 us: attend_back(): jnp.einsum('hqk,qhd->khd', shares.astype(jnp.bfloat16), grad_out, preferr...]
    all_gather x6 -> x2, waiting for transfers between devices: 295 us -> 1.91 us  [whole(): return lax.all_gather(w, 'tensor', axis=0, tiled=False)]
    dynamic_update_slice x16 -> x0, local copies, waits for them, and re-layouts: 129 us -> none  [on_device(): lax.map(attend_back, (query, keys, values, piece_starts, log_total, grad_...]
    reduce_sum x17 -> x1, other arithmetic: 114 us -> 0.6 us  [on_device(): overflow = jnp.sum(over) > 0]
    scatter x3 -> x0, local copies, waits for them, and re-layouts: 91.8 us -> none  [the longest x1 30.9 us: dispatch(): slot_token = jnp.zeros((NF * CAP + 1,), jnp.int32).at[target.reshape(-1)]...]
  transfers between devices with their start and end apart: 15 -> 4, of which waited for: 9 -> 2; matrix products, arithmetic and copies ran while one was open for 27% -> 2% of each run, Pallas kernels for 0% -> 65%
where the time goes in v3:
time: 513 us; the launch traced here: 508 us
  Pallas kernels  435 us (85%)
  waiting for transfers between devices  24.3 us (5%)
  local copies, waits for them, and re-layouts  22.7 us (4%)
  between operations  15 us (3%)
  other arithmetic  9.49 us (2%)
    pallas_call x1, Pallas kernels, on_device(): pl.pallas_call(fwd_kernel, in_specs=[SM] + [VM] * 13, out_specs=[VM] * 12...  95.5 us
    pallas_call x1, Pallas kernels, finish(): pl.pallas_call(functools.partial(final_kernel, tensor), in_specs=[ANY] *...  79.5 us
    pallas_call x1, Pallas kernels, on_device(): pl.pallas_call(bwd_kernel, in_specs=[SM] + [VM] * 13 + [ANY] + [VM] * 2,...  65.8 us
    pallas_call x1, Pallas kernels, on_device(): pl.pallas_call(mid_kernel, in_specs=[ANY] * 2 + [VM] * 11, out_specs=[VM]...  63.8 us
    pallas_call x1, Pallas kernels, gather_weights(): pl.pallas_call(weights_kernel, in_specs=[ANY] * 3, out_specs=[ANY] * 2, o...  37.7 us
    pallas_call x1, Pallas kernels, experts_second(): pl.pallas_call(second_kernel, in_specs=[SM] + [VM] * 6, out_specs=[VM] *...  35.5 us
    pallas_call x1, Pallas kernels, experts_first(): pl.pallas_call(first_kernel, in_specs=[VM] * 4, out_specs=[VM] * 6 + [SM]...  34.5 us
    pallas_call x1, Pallas kernels, prologue(): pl.pallas_call(functools.partial(prologue_kernel, tensor), in_specs=[ANY,...  23.2 us
  transfers between devices with their start and end apart: 4, of which 2 were waited for; matrix products, arithmetic and copies ran while one was open for 2% of the time, Pallas kernels for 65%

profile of v3, /device:TPU:0, one launch (start us, length us, event | category | flops | bytes accessed | tf_op | source)
XLA Modules:
  0.0 508.3 jit_solution(718183407647855510)
XLA Ops:
  7.2 0.9 copy.206
  8.1 1.6 pad_maximum_fusion.14.w_ref
  9.7 23.2 %shard_map.295 = (bf16[3,8,96,256]{3,2,1,0:T(8,128)(2,1)}, bf16[4,96,768]{2,1,0:T(8,128)(2,1)}) custom-call(bf16[2,8,96,512]{3,2,1,0:T(8,128)(2,1)} %gu_ref.3, bf16[1,8,96,512]{3,2,1,0:T(8,128)(2,1)} %bitcast.310, bf16[4,96,192]{2,1,0:T(8,128)(2,1)} %pad_maximum_fusion.14.w_ref), custom_call_target="tpu_custom_call" | custom-call | flops 24999999488 | bytes 10000000 | tf_op jit(solution)/shard_map/pallas_call | solution.py:465
  32.9 0.0 all-gather.23.cloned.1.call-start
  33.1 37.7 %shard_map.296 = (bf16[4,768,768]{2,1,0:T(8,128)(2,1)}, bf16[3,8,96,256]{3,2,1,0:T(8,128)(2,1)}) custom-call(bf16[4,96,768]{2,1,0:T(8,128)(2,1)} %get-tuple-element.233.slab, bf16[2,8,96,512]{3,2,1,0:T(8,128)(2,1)S(1)} %copy-done.37, bf16[1,8,96,512]{3,2,1,0:T(8,128)(2,1)S(1)} %bitcast.311), custom_call_target="tpu_custom_call" | custom-call | flops 35000000512 | bytes 10000000 | tf_op jit(solution)/shard_map/pallas_call | solution.py:244
  70.9 0.9 constant_dynamic-slice_fusion.4
  71.7 1.0 copy.267.ids_ref
  72.8 0.7 constant_dynamic-slice_fusion.3
  73.5 1.0 copy.268.ranks_ref
  74.5 0.1 constant_dynamic-slice_fusion.5
  74.6 0.6 copy.266.starts_ref
  75.2 0.8 copy.207
  76.0 0.8 copy.208
  76.9 0.1 pad.30.clone
  76.9 0.1 pad.32.clone
  77.0 0.2 copy.203
  77.2 0.8 pad.8.prior_ref
  78.0 0.6 pad.9.wres_ref
  78.6 0.6 convert_element_type.188.cv_ref
  79.2 0.6 reshape.508.ga_ref
  79.8 0.6 reshape.510.gm_ref
  80.4 1.8 maximum_maximum_fusion.wr_ref
  82.2 95.5 %shard_map.297 = (bf16[1024,768]{1,0:T(8,128)(2,1)}, bf16[1024,768]{1,0:T(8,128)(2,1)}, bf16[1024,768]{1,0:T(8,128)(2,1)}, bf16[1024,768]{1,0:T(8,128)(2,1)}, f3...) custom-call(s32[1,2]{1,0:T(1,128)} %copy.266.starts_ref, ...), custom_call_target="tpu_custom_call" | custom-call | flops 40000000000 | bytes 30000000 | tf_op jit(solution)/shard_map/pallas_call | solution.py:1447
  177.8 34.5 %shard_map.298 = (bf16[2304,768]{1,0:T(8,128)(2,1)}, bf16[2304,768]{1,0:T(8,128)(2,1)}, f32[2304,128]{1,0:T(8,128)}, f32[2304,768]{1,0:T(8,128)}, f32[2304,768]{...) custom-call(f32[16,1,256]{2,1,0:T(1,128)} %get-tuple-element.235.pay_ref, ...), custom_call_target="tpu_custom_call" | custom-call | flops 22000001024 | bytes 25000000 | tf_op jit(solution)/shard_map/pallas_call | solution.py:1000
  212.3 1.9 all-gather.23.cloned.1.call-done.w_ref
  214.2 35.5 %shard_map.299 = (bf16[8,256,768]{2,1,0:T(8,128)(2,1)}, bf16[8,256,768]{2,1,0:T(8,128)(2,1)}, f32[8,1,256]{2,1,0:T(1,128)}, bf16[4,3,768,256]{3,2,1,0:T(8,128)(2,1)}) custom-call(s32[9]{0:T(128)} %get-tuple-element.240.meta_ref, bf16[2304,768]{1,0:T(8,128)(2,1)} %get-tuple-element.241.xc_ref, bf16[2304,768]{1,0:T(8,128)(2,1)} %get-tuple-element.242.yc_ref, ...), custom_call_target="tpu_custom_call" | custom-call | flops 22000001024 | bytes 25000000 | tf_op jit(solution)/shard_map/pallas_call | solution.py:1018
  249.7 63.8 %shard_map.300 = (bf16[1024,768]{1,0:T(8,128)(2,1)}, f32[1024,768]{1,0:T(8,128)}, f32[1024,128]{1,0:T(8,128)}, f32[1,768]{1,0:T(1,128)}, f32[128,768]{1,0:T(8,12...) custom-call(bf16[8,256,768]{2,1,0:T(8,128)(2,1)} %get-tuple-element.248.dxb_ref, f32[8,1,256]{2,1,0:T(1,128)} %get-tuple-element.249.ggb_ref, ...), custom_call_target="tpu_custom_call" | custom-call | flops 4000000000 | bytes 4000000 | tf_op jit(solution)/shard_map/pallas_call | solution.py:1483
  313.6 65.8 %shard_map.301 = (f32[1024,768]{1,0:T(8,128)}, bf16[4,768,768]{2,1,0:T(8,128)(2,1)}, f32[1,768]{1,0:T(1,128)}, bf16[1024,768]{1,0:T(8,128)(2,1)}) custom-call(s32[1,2]{1,0:T(1,128)} %copy.266.starts_ref, bf16[1024,768]{1,0:T(8,128)(2,1)} %get-tuple-element.255.gmo_ref, f32[1024,768]{1,0:T(8,128)} %get-tuple-element.256.gres_ref, ...), custom_call_target="tpu_custom_call" | custom-call | flops 8000000000 | bytes 4000000 | tf_op jit(solution)/shard_map/pallas_call | solution.py:1505
  379.4 22.3 %reduce-scatter.36.cloned.1.call-done = bf16[1,3,768,256]{3,2,1,0:T(8,128)(2,1)} async-done(((bf16[4,3,768,256]{3,2,1,0:T(8,128)(2,1)}), bf16[1,3,768,256]{3,2,1,0:T(8,128)(2,1)}) %reduce-scatter.36.cloned.1.call-update) | async-done | bytes 1179664 | tf_op jit(solution)/shard_map/reduce_scatter | solution.py:1476
  401.8 79.5 %shard_map.302 = (f32[4,96,192]{2,1,0:T(8,128)}, f32[48,768]{1,0:T(8,128)S(1)}, bf16[3,8,96,256]{3,2,1,0:T(8,128)(2,1)}, bf16[3,8,96,256]{3,2,1,0:T(8,128)(2,1)}) custom-call(bf16[4,768,768]{2,1,0:T(8,128)(2,1)} %get-tuple-element.265.g_ref, bf16[3,8,96,256]{3,2,1,0:T(8,128)(2,1)} %bitcast.326, bf16[3,8,96,256]{3,2,1,0:T(8,128)(2,1)} %bitcast.327, ...), custom_call_target="tpu_custom_call" | custom-call | flops 30000001024 | bytes 10000000 | tf_op jit(solution)/shard_map/pallas_call | solution.py:581
  481.3 0.7 copy-done.93
  482.0 0.6 slice_reduce_fusion.2
  483.2 13.7 %conditional.1 = (bf16[1024,768]{1,0:T(8,128)(2,1)}, f32[1024,768]{1,0:T(8,128)}, f32[1024,12]{0,1:T(8,128)}, f32[768]{0:T(1024)S(1)}, f32[192,96]{1,0:T(8,128)}...) conditional(s32[]{:T(128)} %convert_element_type.189, ...), branch_computations={%region_3.4_spmd, %region_4.53_spmd} | conditional | flops 61550759936 | bytes 1739831808 | solution.py:1562
  483.3 0.9 slice_reduce_fusion
  484.2 0.8 slice_bitcast_fusion.3
  485.0 0.7 slice.104
  485.7 0.6 reshape.483
  486.4 0.7 slice.102
  487.1 1.3 slice.103
  488.4 3.5 fusion.130
  491.9 1.4 convert_bitcast_fusion
  493.3 0.2 copy.210
  493.5 0.9 copy.231
  494.3 0.6 slice_bitcast_fusion.2
  495.0 0.2 copy.209
  495.2 0.6 slice.165
  497.0 2.8 copy.341
  499.8 1.7 copy.342
  (62 shorter events, 0.4 us)
Async XLA Ops:
  7.2 170.6 %all-gather.21.cloned.1.call-start = ((), (), s32[]{:S(2)}) async-start(), calls=%async_computation.26 | async-start | bytes 5898240 | tf_op jit(solution)/shard_map/all_gather | solution.py:1441
  9.7 23.3 %copy-start.37 = (bf16[2,8,96,512]{3,2,1,0:T(8,128)(2,1)S(1)}, bf16[2,8,96,512]{3,2,1,0:T(8,128)(2,1)}, u32[]{:S(2)}) copy-start(bf16[2,8,96,512]{3,2,1,0:T(8,128)(2,1)} %gu_ref.3) | copy-start | bytes 4718596
  9.7 23.3 %copy-start.45 = (bf16[8,512,96]{1,2,0:T(8,128)(2,1)S(1)}, bf16[8,512,96]{1,2,0:T(8,128)(2,1)}, u32[]{:S(2)}) copy-start(bf16[8,512,96]{1,2,0:T(8,128)(2,1)} %param.38) | copy-start | bytes 2359300
  32.9 181.3 %all-gather.23.cloned.1.call-start = ((), (), s32[]{:S(2)}) async-start(), calls=%async_computation.28 | async-start | bytes 5898240 | tf_op jit(solution)/shard_map/all_gather | solution.py:1441
  33.0 41.5 %copy-start.66 = (s32[4,2]{0,1:T(2,128)S(1)}, s32[4,2]{0,1:T(2,128)}, u32[]{:S(2)}) copy-start(s32[4,2]{0,1:T(2,128)} %param.28) | copy-start | bytes 100
  33.0 42.1 %copy-start.88 = (bf16[2,2,768]{2,1,0:T(2,128)(2,1)S(1)}, bf16[2,2,768]{2,1,0:T(2,128)(2,1)}, u32[]{:S(2)}) copy-start(bf16[2,2,768]{2,1,0:T(2,128)(2,1)} %param.36) | copy-start | bytes 18436
  33.0 43.0 %copy-start.55 = (bf16[768,12]{0,1:T(8,128)(2,1)S(1)}, bf16[768,12]{0,1:T(8,128)(2,1)}, u32[]{:S(2)}) copy-start(bf16[768,12]{0,1:T(8,128)(2,1)} %param.33) | copy-start | bytes 55300
  33.1 44.0 %copy-start.49 = (bf16[1024,12]{0,1:T(8,128)(2,1)S(1)}, bf16[1024,12]{0,1:T(8,128)(2,1)}, u32[]{:S(2)}) copy-start(bf16[1024,12]{0,1:T(8,128)(2,1)} %param.25) | copy-start | bytes 73732
  70.7 7.3 %copy-start.98 = (bf16[12,12]{1,0:T(8,128)(2,1)S(1)}, bf16[12,12]{1,0:T(8,128)(2,1)}, u32[]{:S(2)}) copy-start(bf16[12,12]{1,0:T(8,128)(2,1)} %param.34) | copy-start | bytes 868
  70.7 7.9 %copy-start.104 = (bf16[2,768]{1,0:T(2,128)(2,1)S(1)}, bf16[2,768]{1,0:T(2,128)(2,1)}, u32[]{:S(2)}) copy-start(bf16[2,768]{1,0:T(2,128)(2,1)} %param.35) | copy-start | bytes 9220
  70.7 8.5 %copy-start.112 = (bf16[768]{0:T(1024)(128)(2,1)S(1)}, bf16[768]{0:T(1024)(128)(2,1)}, u32[]{:S(2)}) copy-start(bf16[768]{0:T(1024)(128)(2,1)} %param.29) | copy-start | bytes 4612
  70.8 9.0 %copy-start.113 = (bf16[768]{0:T(1024)(128)(2,1)S(1)}, bf16[768]{0:T(1024)(128)(2,1)}, u32[]{:S(2)}) copy-start(bf16[768]{0:T(1024)(128)(2,1)} %param.32) | copy-start | bytes 4612
  70.8 11.4 %copy-start.7 = (bf16[1024,768]{1,0:T(8,128)(2,1)S(1)}, bf16[1024,768]{1,0:T(8,128)(2,1)}, u32[]{:S(2)}) copy-start(bf16[1024,768]{1,0:T(8,128)(2,1)} %og_ref.3) | copy-start | bytes 4718596
  70.8 11.4 %copy-start.15 = (bf16[1024,768]{1,0:T(8,128)(2,1)S(1)}, bf16[1024,768]{1,0:T(8,128)(2,1)}, u32[]{:S(2)}) copy-start(bf16[1024,768]{1,0:T(8,128)(2,1)} %tok_ref.3) | copy-start | bytes 4718596
  70.8 242.7 %reduce-scatter.34.cloned.1.call-start = ((), (), s32[]{:S(2)}) async-start(), calls=%async_computation.27 | async-start | bytes 5898240 | tf_op jit(solution)/shard_map/reduce_scatter | solution.py:1476
  212.3 189.5 %reduce-scatter.36.cloned.1.call-start = ((), (), s32[]{:S(2)}) async-start(), calls=%async_computation.29 | async-start | bytes 5898240 | tf_op jit(solution)/shard_map/reduce_scatter | solution.py:1476
  401.8 81.5 %copy-start.46 = (bf16[3,96,192]{2,1,0:T(8,128)(2,1)S(1)}, bf16[3,96,192]{2,1,0:T(8,128)(2,1)}, u32[]{:S(2)}) copy-start(bf16[3,96,192]{2,1,0:T(8,128)(2,1)} %param.30) | copy-start | bytes 331780
  401.8 81.5 %copy-start.61 = (bf16[192,96]{1,0:T(8,128)(2,1)S(1)}, bf16[192,96]{1,0:T(8,128)(2,1)}, u32[]{:S(2)}) copy-start(bf16[192,96]{1,0:T(8,128)(2,1)} %param.31) | copy-start | bytes 110596
  401.8 81.5 %copy-start.67 = (s32[4,2]{0,1:T(2,128)S(1)}, s32[4,2]{0,1:T(2,128)}, u32[]{:S(2)}) copy-start(s32[4,2]{0,1:T(2,128)} %param.28) | copy-start | bytes 100
  481.3 0.7 copy-start.93
  483.3 8.6 %copy-start.29 = (bf16[3,8,96,256]{3,2,1,0:T(8,128)(2,1)S(1)}, bf16[3,8,96,256]{3,2,1,0:T(8,128)(2,1)}, u32[]{:S(2)}) copy-start(bf16[3,8,96,256]{3,2,1,0:T(8,128)(2,1)} %get-tuple-element.130) | copy-start | bytes 3538948 | tf_op jit(solution)/shard_map/cond
  483.3 8.6 %copy-start.30 = (bf16[3,8,96,256]{3,2,1,0:T(8,128)(2,1)S(1)}, bf16[3,8,96,256]{3,2,1,0:T(8,128)(2,1)}, u32[]{:S(2)}) copy-start(bf16[3,8,96,256]{3,2,1,0:T(8,128)(2,1)} %get-tuple-element.131) | copy-start | bytes 3538948 | tf_op jit(solution)/shard_map/cond
  491.9 1.4 copy-start.48
  491.9 3.1 copy-start.47
  497.0 4.5 copy-start.92
  497.0 4.5 copy-start.116
  497.0 4.5 copy-start.117
  497.0 4.5 copy-start.118
  497.0 2.8 copy-start.33
Sparse Core Ops, SparseCore 0:
  33.1 91.6 all-gather.20
  126.3 87.8 all-gather.22
  216.5 87.7 reduce-scatter.33
  313.7 88.0 reduce-scatter.35

commit v4 on v3

--- a/solution.py
+++ b/solution.py
@@ -21,6 +21,8 @@
 TM = 256
 ROOM = 256
 Z0 = 16
+CHOSEN = 32
+RES = 6
 
 bf16 = jnp.bfloat16
 f32 = jnp.float32
@@ -79,7 +81,7 @@
     kpos = lax.broadcasted_iota(i32, shape, 0 if transposed else 1) + tile * QT
     seen = jnp.where(kpos <= qpos, 1, 0)
     for piece in range(PIECES):
-        s = starts_ref[0, piece]
+        s = starts_ref[lax.axis_index("tensor"), piece]
         both = jnp.where(qpos >= s, 1, 0) * jnp.where(qpos < s + PIECE, 1, 0)
         both = both * jnp.where(kpos >= s, 1, 0) * jnp.where(kpos < s + PIECE, 1, 0)
         seen = jnp.maximum(seen, both)
@@ -219,60 +221,81 @@
             c.wait()
 
 
-def weights_kernel(slab, gu_ref, dn_ref, out_ref, wx_ref, sems, own_sem, *scratch):
+def routes(ids_ref, ranks_ref, i):
+    start = lax.axis_index("tensor") * SEQ + i * QT
+    cols = pl.ds(pl.multiple_of(start, QT), QT)
+    at = lax.broadcasted_iota(i32, (16, QT), 0)
+    hit0, hit1 = (jnp.where(at == ids_ref[n : n + 1, cols], 1.0, 0.0) for n in range(2))
+    keep0, keep1 = (jnp.where(ranks_ref[n : n + 1, cols] < CAP, 1.0, 0.0) for n in range(2))
+    return hit0 + hit1, (hit0 * keep0 + hit1 * keep1) * jnp.where(at < NF, 1.0, 0.0)
+
+
+def weights_kernel(
+    gather, slab, gu_ref, dn_ref, ids_ref, ranks_ref, og_ref, out_ref, wx_ref, pos_ref, count_ref, ys_ref, sems, own_sem,
+    *scratch,
+):
     k, r, _ = slab.shape
     greet(all_peers())
     part = lambda h: pl.ds(0, k) if h is None else pl.ds(h * (k // 2), k // 2)
-    g = Gather8(
-        lambda h: slab.at[part(h)],
-        lambda s, h: out_ref.at[part(h), pl.ds(pl.multiple_of(s * r, r), r), :],
-        sems,
-        own_sem,
-    )
+    if gather:
+        g = Gather8(
+            lambda h: slab.at[part(h)],
+            lambda s, h: out_ref.at[part(h), pl.ds(pl.multiple_of(s * r, r), r), :],
+            sems,
+            own_sem,
+        )
+        g.begin()
     swap = Exchange8([gu_ref, dn_ref], wx_ref, 1, *scratch)
-    g.begin()
     swap.begin()
-    g.forward()
-    g.share()
-    g.last()
-    g.end()
+    upper = jnp.where(
+        lax.broadcasted_iota(i32, (QT, QT), 0) < lax.broadcasted_iota(i32, (QT, QT), 1), 1.0, 0.0
+    ).astype(bf16)
+    taken = jnp.zeros((16, 1), f32)
+    for i in range(SEQ // QT):
+        _, kept = routes(ids_ref, ranks_ref, i)
+        pos = jnp.where(kept > 0, nn(kept.astype(bf16), upper) + taken, -1.0)
+        pos_ref[:, 0, i * QT : (i + 1) * QT] = pos[0:NF, :]
+        taken = taken + jnp.sum(kept, axis=1, keepdims=True)
+    count_ref[...] = jnp.broadcast_to(taken, (16, LANES))
+    slot = lax.axis_index("dp") % NF
+
+    def pack(*blocks):
+        for m in blocks:
+            ys_ref[m] = nn(hot_rows(pos_ref[flip(slot, m)]), og_ref[...]).astype(bf16)
+
+    pack(0, 1)
+    if gather:
+        g.forward()
+    pack(2, 3)
+    if gather:
+        g.share()
+    pack(4, 5)
+    if gather:
+        g.last()
+    pack(6, 7)
+    if gather:
+        g.end()
     swap.end()
 
 
-def gather_weights(w, gate_up, down, cid):
+def gather_weights(w, gate_up, down, ids, ranks, og, gather, cid):
     k, r, f = w.shape
     return pl.pallas_call(
-        weights_kernel,
-        in_specs=[ANY] * 3,
-        out_specs=[ANY] * 2,
-        out_shape=(shape((k, NF * r, f), w.dtype), half_shape(gate_up)),
+        functools.partial(weights_kernel, gather),
+        in_specs=[ANY] * 3 + [VM] * 3,
+        out_specs=[ANY] * 2 + [VM] * 3,
+        out_shape=(
+            shape((k, NF * r, f), w.dtype), half_shape(gate_up), shape((NF, 1, og.shape[0]), f32),
+            shape((16, LANES), f32), shape((NF, ROOM, og.shape[1]), bf16),
+        ),
         scratch_shapes=[
             pltpu.SemaphoreType.DMA((2, GATHER_COPIES)),
             pltpu.SemaphoreType.DMA,
             *exchange_scratch(2),
         ],
-        compiler_params=pltpu.CompilerParams(collective_id=cid, has_side_effects=True),
+        compiler_params=pltpu.CompilerParams(collective_id=cid, has_side_effects=True, vmem_limit_bytes=40 << 20),
         cost_estimate=cost(35, 10),
-    )(w, gate_up, down)
-
-
-def half_kernel(gu_ref, dn_ref, wx_ref, *scratch):
-    greet(all_peers())
-    swap = Exchange8([gu_ref, dn_ref], wx_ref, 1, *scratch)
-    swap.begin()
-    swap.end()
-
-
-def exchange_half(gate_up, down, cid):
-    return pl.pallas_call(
-        half_kernel,
-        in_specs=[ANY] * 2,
-        out_specs=ANY,
-        out_shape=half_shape(gate_up),
-        scratch_shapes=exchange_scratch(2),
-        compiler_params=pltpu.CompilerParams(collective_id=cid, has_side_effects=True),
-        cost_estimate=cost(25, 10),
-    )(gate_up, down)
+    )(w, gate_up, down, ids, ranks, og)
 
 
 class Reduce8:
@@ -477,90 +500,162 @@
     )(gate_up, down, w)
 
 
-def exchange_kernel(a_ref, b_ref, a_out, b_out, *scratch):
+def exchange_kernel(src, dst, *scratch):
     greet(all_peers())
-    swaps = [Exchange8([a_ref], a_out, None, *scratch[0:2]), Exchange8([b_ref], b_out, None, *scratch[2:4])]
-    for swap in swaps:
-        swap.begin()
-    for swap in swaps:
-        swap.end()
-
-
-def exchange8(a, b, cid):
+    swap = Exchange8([src], dst, None, *scratch)
+    swap.begin()
+    swap.end()
+
+
+def exchange8(x, cid):
     return pl.pallas_call(
         exchange_kernel,
-        in_specs=[ANY] * 2,
-        out_specs=[ANY] * 2,
-        out_shape=(shape(a.shape, a.dtype), shape(b.shape, b.dtype)),
-        scratch_shapes=exchange_scratch(1) + exchange_scratch(1),
+        in_specs=[ANY],
+        out_specs=ANY,
+        out_shape=shape(x.shape, x.dtype),
+        scratch_shapes=exchange_scratch(1),
         compiler_params=pltpu.CompilerParams(collective_id=cid, has_side_effects=True),
-        cost_estimate=cost(25, 10),
-    )(a, b)
+        cost_estimate=cost(18, 10),
+    )(x)
+
+
+class Near:
+    def __init__(self, have, got, sems):
+        me = lax.axis_index("dp")
+        self.have, self.got = have, got
+        self.c = [remote(have.at[n], got.at[n], sems, n, "dp", flip(me, m)) for n, m in enumerate((1, 2, 4))]
+
+    def begin(self):
+        self.c[0].start()
+
+    def step(self, n):
+        self.c[n].wait_recv()
+        self.have[n + 1] = self.have[n] + self.got[n]
+        if n < 2:
+            self.c[n + 1].start()
+
+    def close(self):
+        for c in self.c:
+            c.wait_send()
+
+
+def near_scratch(dims):
+    return [pltpu.VMEM((4, *dims), f32), pltpu.VMEM((3, *dims), f32), pltpu.SemaphoreType.DMA((2, 3))]
+
+
+class Far:
+    def __init__(self, tensor, have, got, sems):
+        self.tensor, self.have, self.got, self.here = tensor, have, got, lax.axis_index("tensor")
+        self.c = [
+            remote(have, got.at[self.here], sems, n, axis, peer) for n, (axis, peer) in enumerate(far_peers(tensor))
+        ]
+
+    def begin(self):
+        for c in self.c:
+            c.start()
+        self.got[self.here] = self.have[...]
+
+    def end(self):
+        for c in self.c:
+            c.wait_recv()
+        total = self.got[0]
+        for t in range(1, self.tensor):
+            total = total + self.got[t]
+        for c in self.c:
+            c.wait_send()
+        return total
+
+
+def far_scratch(tensor, dims):
+    return [pltpu.VMEM((tensor, *dims), f32), pltpu.SemaphoreType.DMA((2, tensor - 1))]
 
 
 def final_kernel(
-    tensor, g_ref, dwa_ref, dwb_ref, wrg_ref, cvg_ref, resg_ref, nmg_ref, nag_ref, count_ref, out_ref, small_ref, dwax_ref,
-    dwbx_ref, zf, zs, zr, sbuf, srecv, *scratch,
+    tensor, comm, g_ref, gp_any, gres_any, tok_any, w_any, yr_any, base_any, pos_ref, par_ref, small_ref,
+    out_ref, nag_ref, igrad_ref, layer_ref, total_ref,
+    gp_ref, gres_ref, tok_ref, w_ref, yr_ref, base_ref, lsems, zf, zs, zr, *scratch,
 ):
-    here = lax.axis_index("tensor")
-    me = lax.axis_index("dp")
     k, d, _ = g_ref.shape
-    r, f = out_ref.shape[1:]
-    zsems, ssems = scratch[7], scratch[8]
-    red = Reduce8(lambda s: g_ref.at[:, pl.ds(pl.multiple_of(s * r, r), r), :], scratch[:5], *scratch[5:7])
-    swaps = [
-        Exchange8([dwa_ref], dwax_ref, None, *scratch[9:11]), Exchange8([dwb_ref], dwbx_ref, None, *scratch[11:13])
-    ]
-    red.load()
-    sbuf[0] = jnp.zeros_like(sbuf[0])
-    sbuf[0, 0:24, :] = wrg_ref[0:24, :]
-    sbuf[0, 24:26, :] = cvg_ref[0:2, :]
-    sbuf[0, 26:27, :] = nmg_ref[...]
-    sbuf[0, 27:28, :] = nag_ref[...]
-    sbuf[0, 28:29, 0:LANES] = jnp.where(count_ref[...] > ROOM, 1.0, 0.0)
-    sbuf[0, 32:48, 0:LANES] = resg_ref[0:16, :]
-    greet(all_peers() + far_peers(tensor))
-    red.begin()
-    rounds = [remote(sbuf.at[n], srecv.at[n], ssems, n, "dp", flip(me, m)) for n, m in enumerate((1, 2, 4))]
-    rounds[0].start()
-    red.first()
-    for swap in swaps:
-        swap.begin()
-    rounds[0].wait_recv()
-    sbuf[1] = sbuf[0] + srecv[0]
-    rounds[1].start()
-    red.second()
-    rounds[1].wait_recv()
-    sbuf[2] = sbuf[1] + srecv[1]
-    rounds[2].start()
-    red.third()
-    rounds[2].wait_recv()
-    sbuf[3] = sbuf[2] + srecv[2]
-    far = [
-        remote(sbuf.at[3], srecv.at[3 + here], ssems, 3 + n, axis, peer)
-        for n, (axis, peer) in enumerate(far_peers(tensor))
-    ]
-    for c in far:
+    ntile = SEQ // QT
+    pairs = (
+        (gp_any, gp_ref), (w_any.at[pl.ds(0, 3)], w_ref), (tok_any, tok_ref), (gres_any, gres_ref), (yr_any, yr_ref),
+        (base_any, base_ref),
+    )
+    loads = [pltpu.make_async_copy(src, dst, lsems.at[n]) for n, (src, dst) in enumerate(pairs)]
+    if comm:
+        here = lax.axis_index("tensor")
+        r, f = out_ref.shape[1:]
+        red = Reduce8(lambda s: g_ref.at[:, pl.ds(pl.multiple_of(s * r, r), r), :], scratch[:5], *scratch[5:7])
+        zsems = scratch[7]
+        sums = Near(*scratch[8:11])
+        gains, smalls = Far(tensor, sums.have.at[3], *scratch[11:13]), Far(tensor, small_ref, *scratch[13:15])
+        red.load()
+        greet(near_peers() + far_peers(tensor))
+        red.begin()
+        smalls.begin()
+    for c in loads:
         c.start()
+    ga = par_ref[24:25, :].astype(f32)
+    if comm:
+        red.first()
+        red.second()
+    for c in loads[:4]:
+        c.wait()
+    nag = jnp.zeros((1, d), f32)
+    for i in range(ntile):
+        rows = pl.ds(i * QT, QT)
+        gai = nt(gp_ref[0, rows, :], w_ref[0]) + nt(gp_ref[1, rows, :], w_ref[1])
+        gai = gai + nt(gp_ref[2, rows, :], w_ref[2])
+        x = tok_ref[rows, :].astype(f32)
+        r1 = lax.rsqrt(jnp.mean(x * x, axis=-1, keepdims=True) + EPS)
+        nag = nag + jnp.sum(gai * x * r1, axis=0, keepdims=True)
+        scaled = gai * ga
+        avg = jnp.mean(scaled * x, axis=-1, keepdims=True)
+        igrad_ref[rows, :] = gres_ref[rows, :] + r1 * scaled - x * (r1 * r1 * r1 * avg)
+        if comm and i == 0:
+            red.third()
+    if comm:
+        sums.have[0] = nag
+        sums.begin()
+    else:
+        nag_ref[...] = nag
+        total_ref[...] = small_ref[...]
+    for c in loads[4:]:
+        c.wait()
+
+    def layer(i):
+        rows = pl.ds(i * QT, QT)
+        total = base_ref[rows, :]
+        for e in range(NF):
+            total = total + tn(hot_rows(pos_ref[e, :, rows]), yr_ref[e])
+        layer_ref[rows, :] = total.astype(bf16)
 
     def write(part, total):
         for t in range(tensor):
             zf[t, part] = total[:, :, t * f : (t + 1) * f]
             zs[t, part] = total[:, :, t * f : (t + 1) * f].astype(bf16)
 
+    if not comm:
+        for i in range(ntile):
+            layer(i)
+        return
+    layer(0)
+    sums.step(0)
     red.end(write)
     out_copies = [
         remote(zs.at[peer], zr.at[here], zsems, n, axis, peer) for n, (axis, peer) in enumerate(far_peers(tensor))
     ]
     for c in out_copies:
         c.start()
-    srecv[3 + here] = sbuf[3]
-    for c in far:
-        c.wait_recv()
-    total = srecv[3]
-    for t in range(1, tensor):
-        total = total + srecv[3 + t]
-    small_ref[...] = total
+    sums.step(1)
+    for i in range(1, ntile - 1):
+        layer(i)
+    sums.step(2)
+    gains.begin()
+    layer(ntile - 1)
+    nag_ref[...] = gains.end()
+    total_ref[...] = smalls.end()
+    sums.close()
     zr[here] = jnp.zeros(zr.shape[1:], bf16)
     for c in out_copies:
         c.wait_recv()
@@ -569,74 +664,64 @@
         total = total + zr[t].astype(f32)
     out_ref[...] = total
     red.close()
-    for c in rounds + far + out_copies:
+    for c in out_copies:
         c.wait_send()
-    for swap in swaps:
-        swap.end()
-
-
-def finish(g, dwa, dwb, wrg, cvg, resg, nmg, nag, count, tensor, cid):
+
+
+def finish(g, gp, gres, tokens, w, yr, base, pos, params, small, tensor, comm, cid):
     k, d, columns = g.shape
-    r, f = d // NF, columns // tensor
+    rows = tokens.shape[0]
+    r, f = (d // NF if comm else 8), columns // tensor
+    once = pltpu.CompilerParams(vmem_limit_bytes=60 << 20)
+    if comm:
+        once = pltpu.CompilerParams(collective_id=cid, has_side_effects=True, vmem_limit_bytes=60 << 20)
     return pl.pallas_call(
-        functools.partial(final_kernel, tensor),
-        in_specs=[ANY] * 3 + [VM] * 6,
-        out_specs=[VM] * 2 + [ANY] * 2,
-        out_shape=(shape((k, r, f), f32), shape((48, d), f32), shape(dwa.shape, bf16), shape(dwb.shape, bf16)),
+        functools.partial(final_kernel, tensor, comm),
+        in_specs=[ANY] * 7 + [VM] * 3,
+        out_specs=[VM] * 5,
+        out_shape=(
+            shape((k, r, f), f32), shape((1, d), f32), shape((rows, d), f32), shape((rows, d), bf16),
+            shape(small.shape, f32),
+        ),
         scratch_shapes=[
+            pltpu.VMEM(gp.shape, bf16),
+            pltpu.VMEM((rows, d), f32),
+            pltpu.VMEM((rows, d), bf16),
+            pltpu.VMEM((3, d, columns), bf16),
+            pltpu.VMEM(yr.shape, bf16),
+            pltpu.VMEM((rows, d), f32),
+            pltpu.SemaphoreType.DMA((6,)),
             pltpu.VMEM((tensor, k, r, f), f32),
             pltpu.VMEM((tensor, k, r, f), bf16),
             pltpu.VMEM((tensor, k, r, f), bf16),
-            pltpu.VMEM((4, 48, d), f32),
-            pltpu.VMEM((3 + tensor, 48, d), f32),
             *reduce_scratch((k, r, columns)),
             pltpu.SemaphoreType.DMA((2, tensor - 1)),
-            pltpu.SemaphoreType.DMA((2, 2 + tensor)),
-            *exchange_scratch(1),
-            *exchange_scratch(1),
+            *near_scratch((1, d)),
+            *far_scratch(tensor, (1, d)),
+            *far_scratch(tensor, small.shape),
         ],
-        compiler_params=pltpu.CompilerParams(collective_id=cid, has_side_effects=True, vmem_limit_bytes=60 << 20),
-        cost_estimate=cost(30, 10),
-    )(g, dwa, dwb, wrg, cvg, resg, nmg, nag, count)
+        compiler_params=once,
+        cost_estimate=cost(8, 4),
+    )(g, gp, gres, tokens, w, yr, base, pos, params, small)
 
 
 def fwd_kernel(
-    starts_ref, tok_ref, prior_ref, ids_ref, ranks_ref, ga_ref, gm_ref, cos_ref, sin_ref, w_ref, wr_ref, wres_ref, cv_ref,
-    og_ref,
-    q_ref, k_ref, v_ref, mixed_ref, lse_ref, nattn_ref, resid_ref, nmoe_ref, base_ref, aux_ref, pos_ref, count_ref, xr_ref,
-    yr_ref, payr_ref,
-    bias_ref, gate_ref, xs, ys, pay, *scratch,
+    starts_ref, tok_ref, prior_ref, ids_ref, ranks_ref, par_ref, cos_ref, sin_ref, w_ref, pos_ref, ys,
+    q_ref, k_ref, v_ref, mixed_ref, lse_ref, nattn_ref, resid_ref, nmoe_ref, base_ref, aux_ref, xr_ref, yr_ref, payr_ref,
+    bias_ref, gate_ref, xs, pay, wr_ref, *scratch,
 ):
     greet(all_peers())
     send_x, send_y = Send8(xs, xr_ref, *scratch[0:2], True), Send8(ys, yr_ref, *scratch[2:4], True)
     swap = Swap8(pay, payr_ref, *scratch[4:6])
+    send_y.begin()
     lane = lanes(QT)
-    lower = jnp.where(
-        lax.broadcasted_iota(i32, (QT, QT), 1) < lax.broadcasted_iota(i32, (QT, QT), 0), 1.0, 0.0
-    ).astype(bf16)
-
-    def hits(rows):
-        id0, id1 = ids_ref[rows, 0:1], ids_ref[rows, 1:2]
-        rk0, rk1 = ranks_ref[rows, 0:1], ranks_ref[rows, 1:2]
-        hit0, hit1 = jnp.where(lane == id0, 1.0, 0.0), jnp.where(lane == id1, 1.0, 0.0)
-        keep0, keep1 = jnp.where(rk0 < CAP, 1.0, 0.0), jnp.where(rk1 < CAP, 1.0, 0.0)
-        return hit0 + hit1, (hit0 * keep0 + hit1 * keep1) * jnp.where(lane < NF, 1.0, 0.0)
-
-    def places(i, taken):
-        rows = pl.ds(pl.multiple_of(i * QT, QT), QT)
-        _, kept = hits(rows)
-        pos = nn(lower, kept.astype(bf16)) + taken
-        pos_ref[:, 0, rows] = jnp.where(kept > 0, pos, -1.0).T[0:NF, :]
-        return taken + jnp.sum(kept, axis=0, keepdims=True)
-
-    count_ref[...] = lax.fori_loop(0, SEQ // QT, places, jnp.zeros((1, LANES), f32))
-    for m in (*Send8.order, 0):
-        ys[m] = nn(hot_rows(pos_ref[flip(send_y.slot, m)]), og_ref[...]).astype(bf16)
-        send_y.start(m)
+    router_rows(par_ref, wr_ref)
+    wres = par_ref[32:48, 0:LANES]
     d = tok_ref.shape[1]
     pairs = d // LANES
     ntile = SEQ // QT
-    ga, gm = ga_ref[...], gm_ref[...]
+    ga, gm = par_ref[24:25, :].astype(f32), par_ref[25:26, :].astype(f32)
+    cv = par_ref[26:28, :].astype(f32)
     mask_a, mask_b = head_masks()
     mask16 = (mask_a.astype(bf16), mask_b.astype(bf16))
 
@@ -699,16 +784,17 @@
         r2 = lax.rsqrt(jnp.mean(resid * resid, axis=-1, keepdims=True) + EPS)
         nm = (resid * r2 * gm).astype(bf16)
         nmoe_ref[rows, :] = nm
-        raw = nn(nm, wr_ref[...])
-        logits = raw + nn(prior_ref[rows, :], wres_ref[...])
+        raw = nt(nm, wr_ref[...])
+        logits = raw + tn(prior_ref[:, rows], wres)
         logits = jnp.where(lane < NF + 2 + NC, logits, -1e30)
         e = jnp.exp(logits - jnp.max(logits, axis=-1, keepdims=True))
         shares = e / jnp.sum(e, axis=-1, keepdims=True)
-        chosen, kept = hits(rows)
+        chosen, kept = routes(ids_ref, ranks_ref, i)
+        gate_ref[:, 0, rows] = shares.T[0:NF, :] * kept[0:NF, :]
+        chosen = jnp.concatenate([chosen, jnp.zeros((LANES - 16, QT), f32)], axis=0).T
         gates = shares * chosen
-        gate_ref[:, 0, rows] = (shares * kept).T[0:NF, :]
         nv = nm.astype(f32)
-        aux = jnp.where(lane < NF + 2 + NC, shares, 0.0)
+        aux = jnp.where(lane < NF + 2 + NC, shares, 0.0) + pltpu.roll(chosen, CHOSEN, 1)
         direct = gates[:, NF + 1 : NF + 2]
         others = None
         for c in range(NC):
@@ -718,7 +804,7 @@
             aux = jnp.where(lane == Z0 + 2 * c + 1, m1, aux)
             w = gates[:, NF + 2 + c : NF + 3 + c]
             direct = direct + w * m0
-            term = (w * m1) * cv_ref[c : c + 1, :]
+            term = (w * m1) * cv[c : c + 1, :]
             others = term if others is None else others + term
         aux_ref[rows, :] = aux
         base_ref[rows, :] = resid + direct * nv + others
@@ -741,14 +827,52 @@
 
 
 def mid_kernel(
-    dxb_ref, ggb_ref, pos_ref, og_ref, nmoe_ref, resid_ref, ids_ref, aux_ref, prior_ref, wr_ref, wres_ref, cv_ref, gm_ref,
-    gmo_ref, gres_ref, pgrad_ref, nmg_ref, wrg_ref, resg_ref, cvg_ref,
-    dxr, ggr, dx_ref, gg_ref, *scratch,
+    dxb_ref, ggb_ref, pos_ref, og_ref, nmoe_ref, resid_ref, aux_ref, prior_ref, par_ref, count_ref,
+    gmo_ref, gres_ref, pgrad_ref, small_ref,
+    dxr, ggr, dx_ref, gg_ref, inner_ref, extra_ref, wr_ref, resg_ref, *scratch,
 ):
     greet(all_peers())
     send, swap = Send8(dxb_ref, dxr, *scratch[0:2], False), Swap8(ggb_ref, ggr, *scratch[2:4])
     swap.begin()
     send.begin()
+    gm, cv = par_ref[25:26, :].astype(f32), par_ref[26:28, :].astype(f32)
+    wres = par_ref[32:48, 0:LANES]
+    router_rows(par_ref, wr_ref)
+    lane = lanes(QT)
+    small_ref[...] = jnp.zeros_like(small_ref)
+    resg_ref[...] = jnp.zeros_like(resg_ref)
+    small_ref[28:29, 0:LANES] = jnp.max(jnp.where(count_ref[...] > ROOM, 1.0, 0.0), axis=0, keepdims=True)
+
+    def ahead(i, carry):
+        rows = pl.ds(pl.multiple_of(i * QT, QT), QT)
+        g16 = og_ref[rows, :]
+        g, nv = g16.astype(f32), nmoe_ref[rows, :].astype(f32)
+        x = resid_ref[rows, :]
+        aux = aux_ref[rows, :]
+        chosen = jnp.where(lane < 16, pltpu.roll(aux, LANES - CHOSEN, 1), 0.0)
+        gates = jnp.where(lane < NF + 2 + NC, aux, 0.0) * chosen
+        copy_inner = jnp.sum(g * nv, axis=-1, keepdims=True)
+        inner = jnp.where(lane == NF + 1, copy_inner, 0.0)
+        direct = gates[:, NF + 1 : NF + 2]
+        extra = jnp.where(lane == 1, lax.rsqrt(jnp.mean(x * x, axis=-1, keepdims=True) + EPS), 0.0)
+        cvw = jnp.zeros((QT, LANES), f32)
+        for c in range(NC):
+            m0, m1 = aux[:, Z0 + 2 * c : Z0 + 2 * c + 1], aux[:, Z0 + 2 * c + 1 : Z0 + 2 * c + 2]
+            v_inner = jnp.sum(g * cv[c : c + 1, :], axis=-1, keepdims=True)
+            mean = m0 * copy_inner + m1 * v_inner
+            inner = jnp.where(lane == NF + 2 + c, mean, inner)
+            w = gates[:, NF + 2 + c : NF + 3 + c]
+            direct = direct + w * m0
+            extra = jnp.where(lane == Z0 + 2 * c, m0 * (w * copy_inner - w * mean), extra)
+            extra = jnp.where(lane == Z0 + 2 * c + 1, m1 * (w * v_inner - w * mean), extra)
+            cvw = jnp.where(lane == c, w * m1, cvw)
+        inner_ref[rows, :] = inner
+        extra_ref[rows, :] = jnp.where(lane == 0, direct, extra)
+        cv_hi, cv_lo = split(cvw)
+        small_ref[24:26, :] += tn(cv_hi, g16)[0:NC] + tn(cv_lo, g16)[0:NC]
+        return carry
+
+    lax.fori_loop(0, SEQ // QT, ahead, 0)
     swap.end()
     for n, m in enumerate((0, 1, 2, 3, 4, 5, 6, 7)):
         send.got(m)
@@ -761,51 +885,25 @@
         else:
             dx_ref[...] = part
     send.close()
-    gm = gm_ref[...]
-    lane = lanes(QT)
-    nmg_ref[...] = jnp.zeros_like(nmg_ref)
-    wrg_ref[...] = jnp.zeros_like(wrg_ref)
-    resg_ref[...] = jnp.zeros_like(resg_ref)
-    cvg_ref[...] = jnp.zeros_like(cvg_ref)
 
     def tile(i, carry):
         rows = pl.ds(pl.multiple_of(i * QT, QT), QT)
-        g16, n16 = og_ref[rows, :], nmoe_ref[rows, :]
-        g, nv = g16.astype(f32), n16.astype(f32)
+        g, n16 = og_ref[rows, :].astype(f32), nmoe_ref[rows, :]
         x = resid_ref[rows, :]
-        r2 = lax.rsqrt(jnp.mean(x * x, axis=-1, keepdims=True) + EPS)
-        aux = aux_ref[rows, :]
+        aux, extra = aux_ref[rows, :], extra_ref[rows, :]
+        direct, r2 = extra[:, 0:1], extra[:, 1:2]
         shares = jnp.where(lane < NF + 2 + NC, aux, 0.0)
-        id0, id1 = ids_ref[rows, 0:1], ids_ref[rows, 1:2]
-        chosen = jnp.where(lane == id0, 1.0, 0.0) + jnp.where(lane == id1, 1.0, 0.0)
-        gates = shares * chosen
-        copy_inner = jnp.sum(g * nv, axis=-1, keepdims=True)
+        chosen = jnp.where(lane < 16, pltpu.roll(aux, LANES - CHOSEN, 1), 0.0)
         inner = jnp.concatenate([gg_ref[:, rows], jnp.zeros((LANES - NF, QT), f32)], axis=0).T
-        inner = jnp.where(lane == NF + 1, copy_inner, inner)
-        direct = gates[:, NF + 1 : NF + 2]
-        blend = jnp.zeros((QT, LANES), f32)
-        cvw = jnp.zeros((QT, LANES), f32)
-        for c in range(NC):
-            m0, m1 = aux[:, Z0 + 2 * c : Z0 + 2 * c + 1], aux[:, Z0 + 2 * c + 1 : Z0 + 2 * c + 2]
-            v_inner = jnp.sum(g * cv_ref[c : c + 1, :], axis=-1, keepdims=True)
-            mean = m0 * copy_inner + m1 * v_inner
-            inner = jnp.where(lane == NF + 2 + c, mean, inner)
-            w = gates[:, NF + 2 + c : NF + 3 + c]
-            direct = direct + w * m0
-            blend = jnp.where(lane == Z0 + 2 * c, m0 * (w * copy_inner - w * mean), blend)
-            blend = jnp.where(lane == Z0 + 2 * c + 1, m1 * (w * v_inner - w * mean), blend)
-            cvw = jnp.where(lane == c, w * m1, cvw)
-        grad_router = inner * chosen
+        grad_router = (inner + inner_ref[rows, :]) * chosen
         glog = shares * (grad_router - jnp.sum(shares * grad_router, axis=-1, keepdims=True))
-        both_hi, both_lo = split(glog + blend)
+        both_hi, both_lo = split(glog + jnp.where(lane >= Z0, extra, 0.0))
         log_hi, log_lo = split(glog)
-        cv_hi, cv_lo = split(cvw)
-        pgrad_ref[rows, :] = nt(log_hi, wres_ref[...]) + nt(log_lo, wres_ref[...])
-        wrg_ref[...] += tn(both_hi, n16) + tn(both_lo, n16)
-        resg_ref[...] += tn(prior_ref[rows, :], log_hi) + tn(prior_ref[rows, :], log_lo)
-        cvg_ref[...] += tn(cv_hi, g16) + tn(cv_lo, g16)
-        gmi = dx_ref[rows, :] + direct * g + nt(both_hi, wr_ref[...]) + nt(both_lo, wr_ref[...])
-        nmg_ref[...] += jnp.sum(gmi * x * r2, axis=0, keepdims=True)
+        pgrad_ref[:, rows] = nt(wres, log_hi) + nt(wres, log_lo)
+        small_ref[0:24, :] += tn(both_hi, n16)[0:24] + tn(both_lo, n16)[0:24]
+        resg_ref[...] += nn(prior_ref[:, rows], log_hi) + nn(prior_ref[:, rows], log_lo)
+        gmi = dx_ref[rows, :] + direct * g + nn(both_hi, wr_ref[...]) + nn(both_lo, wr_ref[...])
+        small_ref[26:27, :] += jnp.sum(gmi * x * r2, axis=0, keepdims=True)
         scaled = gmi * gm
         avg = jnp.mean(scaled * x, axis=-1, keepdims=True)
         gres = g + r2 * scaled - x * (r2 * r2 * r2 * avg)
@@ -814,21 +912,28 @@
         return carry
 
     lax.fori_loop(0, SEQ // QT, tile, 0)
+    for n in range(NF + 2 + NC):
+        at = n % RES * LANES
+        small_ref[29 + n // RES : 30 + n // RES, at : at + LANES] = resg_ref[n : n + 1, :]
 
 
 def bwd_kernel(
-    starts_ref, gmo_ref, gres_ref, mixed_ref, q_ref, k_ref, v_ref, lse_ref, nattn_ref, tok_ref, ga_ref, cos_ref,
-    sin_ref, w_ref, outb_ref, pos_ref, base_ref,
-    igrad_ref, wg_ref, nag_ref, layer_ref,
-    do_ref, delta_ref, bias_ref, gp_ref, dk_ref, dv_ref, dq_ref, outr, *scratch,
+    starts_ref, gmo_ref, mixed_ref, q_ref, k_ref, v_ref, lse_ref, nattn_ref, cos_ref, sin_ref, wo_ref, small_ref,
+    outb_ref, dw_ref,
+    wg_ref, gp_ref, outr_ref, total_ref, dwx_ref,
+    do_ref, delta_ref, bias_ref, dk_ref, dv_ref, dq_ref, *scratch,
 ):
+    send = Send8(outb_ref, outr_ref, *scratch[0:2], False)
+    sums = Near(*scratch[2:5])
+    sums.have[0] = small_ref[...]
     greet(all_peers())
-    send = Send8(outb_ref, outr, *scratch, False)
+    sums.begin()
     send.begin()
-    d = tok_ref.shape[1]
+    swap = Exchange8([dw_ref], dwx_ref, None, *scratch[5:7])
+    swap.begin()
+    d = mixed_ref.shape[1]
     pairs = d // LANES
     ntile = SEQ // QT
-    ga = ga_ref[...]
     mask_a, mask_b = head_masks()
     mask16 = (mask_a.astype(bf16), mask_b.astype(bf16))
     maskf = (mask_a, mask_b)
@@ -839,13 +944,14 @@
 
     def start(i, carry):
         rows = pl.ds(pl.multiple_of(i * QT, QT), QT)
-        do = nn(gmo_ref[rows, :], w_ref[3]).astype(bf16)
+        do = nn(gmo_ref[rows, :], wo_ref[0]).astype(bf16)
         do_ref[rows, :] = do
         hi, lo = split(do.astype(f32) * mixed_ref[rows, :].astype(f32))
         delta_ref[:, rows] = nt(pick, hi) + nt(pick, lo)
         return carry
 
     lax.fori_loop(0, ntile, start, 0)
+    sums.step(0)
     wg_ref[3] = tn(gmo_ref[...], mixed_ref[...]).astype(wg_ref.dtype)
     for i in range(ntile):
         width = min(SEQ, (i + 2) * QT) - i * QT
@@ -882,31 +988,17 @@
         gp_ref[2, :, cols] = dv_ref[...].astype(bf16)
         return carry
 
+    sums.step(1)
     lax.fori_loop(0, pairs, pair, 0)
+    sums.step(2)
     for c in range(3):
         wg_ref[c] = tn(nattn_ref[...], gp_ref[c]).astype(wg_ref.dtype)
-    nag_ref[...] = jnp.zeros_like(nag_ref)
     for m in range(NF):
         send.got(m)
-
-    def finish(i, carry):
-        rows = pl.ds(pl.multiple_of(i * QT, QT), QT)
-        layer = base_ref[rows, :]
-        for e in range(NF):
-            layer = layer + tn(hot_rows(pos_ref[e, :, rows]), outr[e])
-        layer_ref[rows, :] = layer.astype(bf16)
-        gai = nt(gp_ref[0, rows, :], w_ref[0]) + nt(gp_ref[1, rows, :], w_ref[1])
-        gai = gai + nt(gp_ref[2, rows, :], w_ref[2])
-        x = tok_ref[rows, :].astype(f32)
-        r1 = lax.rsqrt(jnp.mean(x * x, axis=-1, keepdims=True) + EPS)
-        nag_ref[...] += jnp.sum(gai * x * r1, axis=0, keepdims=True)
-        scaled = gai * ga
-        avg = jnp.mean(scaled * x, axis=-1, keepdims=True)
-        igrad_ref[rows, :] = gres_ref[rows, :] + r1 * scaled - x * (r1 * r1 * r1 * avg)
-        return carry
-
-    lax.fori_loop(0, ntile, finish, 0)
     send.close()
+    swap.end()
+    total_ref[...] = sums.have[3]
+    sums.close()
 
 
 def ffn_tile(x, gate, y, w_ref, acc, eo, dx):
@@ -963,18 +1055,36 @@
 
 
 def second_kernel(
-    meta_ref, xc_ref, yc_ref, gc_ref, eo_ref, dx_ref, w_ref, outb_ref, dxb_ref, ggb_ref, dw_ref, outs, dxs, ggs, acc
+    meta_ref, xc_any, yc_any, gc_any, eo_any, dx_any, w_any, outb_ref, dxb_ref, ggb_ref, dw_ref,
+    xc_ref, yc_ref, gc_ref, eo_ref, dx_ref, w_ref, outs, dxs, ggs, acc, sems, wsem,
 ):
     d = xc_ref.shape[1]
     tiles = meta_ref[NF]
+    weights = pltpu.make_async_copy(w_any, w_ref, wsem)
+    weights.start()
+
+    def copies(t):
+        rows = pl.ds(pl.multiple_of(t * TM, TM), TM)
+        pairs = ((xc_any, xc_ref), (yc_any, yc_ref), (gc_any, gc_ref), (eo_any, eo_ref), (dx_any, dx_ref))
+        return [pltpu.make_async_copy(a.at[rows, :], b.at[rows, :], sems.at[n, t]) for n, (a, b) in enumerate(pairs)]
+
+    def begin(t, carry):
+        for c in copies(t):
+            c.start()
+        return carry
+
+    lax.fori_loop(0, tiles, begin, 0)
     acc[...] = jnp.zeros_like(acc)
     rows = pl.ds(pl.multiple_of(tiles * TM, TM), ROOM)
     outs[rows, :] = jnp.zeros((ROOM, d), bf16)
     dxs[rows, :] = jnp.zeros((ROOM, d), bf16)
     ggs[rows, :] = jnp.zeros((ROOM, LANES), f32)
+    weights.wait()
 
     def tile(t, carry):
         rows = pl.ds(pl.multiple_of(t * TM, TM), TM)
+        for c in copies(t):
+            c.wait()
         gate, y = gc_ref[rows, 0:1], yc_ref[rows, :]
         eo, dx = ffn_tile(xc_ref[rows, :], gate, y, w_ref, acc, eo_ref[rows, :], dx_ref[rows, :])
         outs[rows, :] = (gate * eo).astype(bf16)
@@ -1017,18 +1127,34 @@
     room = total + ROOM
     return pl.pallas_call(
         second_kernel,
-        in_specs=[SM] + [VM] * 6,
+        in_specs=[SM] + [ANY] * 6,
         out_specs=[VM] * 4,
         out_shape=(blocks, blocks, shape((NF, 1, ROOM), f32), shape(w.shape, bf16)),
         scratch_shapes=[
+            pltpu.VMEM((total, d), bf16),
+            pltpu.VMEM((total, d), bf16),
+            pltpu.VMEM((total, LANES), f32),
+            pltpu.VMEM((total, d), f32),
+            pltpu.VMEM((total, d), f32),
+            pltpu.VMEM(w.shape, bf16),
             pltpu.VMEM((room, d), bf16),
             pltpu.VMEM((room, d), bf16),
             pltpu.VMEM((room, LANES), f32),
             pltpu.VMEM(w.shape, f32),
+            pltpu.SemaphoreType.DMA((5, total // TM)),
+            pltpu.SemaphoreType.DMA,
         ],
         compiler_params=pltpu.CompilerParams(vmem_limit_bytes=60 << 20),
         cost_estimate=cost(22, 25),
     )(meta, xc, yc, gc, eo, dx, w)
+
+
+def router_rows(par_ref, wr_ref):
+    wr_ref[...] = jnp.zeros_like(wr_ref)
+    wr_ref[0:16, :] = par_ref[0:16, :]
+    wr_ref[16:32, :] = jnp.where(
+        lax.broadcasted_iota(i32, (16, par_ref.shape[1]), 0) < 2 * NC, par_ref[16:32, :].astype(f32), 0.0
+    ).astype(bf16)
 
 
 def hot_rows(pos):
@@ -1411,28 +1537,26 @@
     packs = dp // NF
     groups = None if packs == 1 else [list(range(NF * r, NF * (r + 1))) for r in range(packs)]
     across = None if packs == 1 else [list(range(j, dp, NF)) for j in range(NF)]
-    here = lax.axis_index("tensor")
-    ids = lax.dynamic_slice_in_dim(expert_ids, here * rows, rows, 0)
-    ranks = lax.dynamic_slice_in_dim(expert_ranks, here * rows, rows, 0)
-    starts = lax.dynamic_slice_in_dim(piece_starts, here, 1, 0)
-    ga, gm = norm_attn.astype(f32).reshape(1, d), norm_moe.astype(f32).reshape(1, d)
+    ids, ranks = expert_ids.T, expert_ranks.T
     cosine, sine = (jnp.asarray(t) for t in rotary_tables())
-    prior = jnp.pad(prior_logits, ((0, 0), (0, LANES - ne)))
-    wr = jnp.concatenate(
-        [router_weight, jnp.zeros((d, Z0 - ne), bf16), const_gates.reshape(2 * NC, d).T,
-         jnp.zeros((d, LANES - Z0 - 2 * NC), bf16)], axis=1)
-    wres = jnp.pad(residual_weight, ((0, LANES - ne), (0, LANES - ne)))
-    cv = const_vectors.astype(f32)
+    prior = jnp.pad(prior_logits.T, ((0, 16 - ne), (0, 0)))
+    zeros = lambda n: jnp.zeros((n, d), bf16)
+    params = jnp.concatenate(
+        [
+            router_weight.T, zeros(Z0 - ne), const_gates.reshape(2 * NC, d), zeros(8 - 2 * NC), norm_attn[None],
+            norm_moe[None], const_vectors, zeros(6 - NC), jnp.pad(residual_weight, ((0, 16 - ne), (0, d - ne))),
+        ],
+        axis=0,
+    )
 
     w_attn = jnp.concatenate([qkv_weight, out_weight.T[None]], axis=0)
     w_down_t = w_down.transpose(0, 2, 1)[None]
     shard = w_down.shape[1]
     w_first, slab = prologue(w_gate_up, w_down_t, w_attn, tensor, 1)
-    if packs > 1:
-        w_attn = lax.all_gather(slab, "dp", axis=1, tiled=True)
-        w_second = exchange_half(w_gate_up, w_down_t, 2)
-    else:
-        w_attn, w_second = gather_weights(slab, w_gate_up, w_down_t, 2)
+    w_full, w_second, pos, count, ys = gather_weights(
+        slab, w_gate_up, w_down_t, ids, ranks, out_grad, packs == 1, 2
+    )
+    w_attn = lax.all_gather(slab, "dp", axis=1, tiled=True) if packs > 1 else w_full
 
     def whole(w):
         w = w.reshape(3, -1, w.shape[3])
@@ -1444,22 +1568,21 @@
 
     heads = 16
     blocks = shape((NF, ROOM, d), bf16)
-    q, k, v, mixed, lse, nattn, resid, nmoe, base, aux, pos, count, x_b, y_b, pay = pl.pallas_call(
+    q, k, v, mixed, lse, nattn, resid, nmoe, base, aux, x_b, y_b, pay = pl.pallas_call(
         fwd_kernel,
-        in_specs=[SM] + [VM] * 13,
-        out_specs=[VM] * 12 + [ANY] * 3,
+        in_specs=[SM] + [VM] * 9 + [ANY],
+        out_specs=[VM] * 10 + [ANY] * 3,
         out_shape=(
             shape((rows, d), bf16), shape((rows, d), bf16), shape((rows, d), bf16), shape((rows, d), bf16),
             shape((heads, rows), f32), shape((rows, d), bf16), shape((rows, d), f32), shape((rows, d), bf16),
-            shape((rows, d), f32), shape((rows, LANES), f32), shape((NF, 1, rows), f32), shape((1, LANES), f32),
-            blocks, blocks, shape((2 * NF, 1, ROOM), f32),
+            shape((rows, d), f32), shape((rows, LANES), f32), blocks, blocks, shape((2 * NF, 1, ROOM), f32),
         ),
         scratch_shapes=[
             pltpu.VMEM((QT, 2 * QT), f32),
             pltpu.VMEM((NF, 1, rows), f32),
             pltpu.VMEM((NF, ROOM, d), bf16),
-            pltpu.VMEM((NF, ROOM, d), bf16),
             pltpu.VMEM((2 * NF, 1, ROOM), f32),
+            pltpu.VMEM((LANES, d), bf16),
             *send_scratch(),
             *send_scratch(),
             pltpu.SemaphoreType.DMA((2, 2 * (NF - 1))),
@@ -1467,7 +1590,7 @@
         ],
         compiler_params=pltpu.CompilerParams(collective_id=3, has_side_effects=True, vmem_limit_bytes=60 << 20),
         cost_estimate=cost(40, 30, 10),
-    )(starts, tokens, prior, ids, ranks, ga, gm, cosine, sine, w_attn, wr, wres, cv, out_grad)
+    )(piece_starts, tokens, prior, ids, ranks, params, cosine, sine, w_attn, pos, ys)
 
     xc, yc, gc, eo, dx, dw_a, meta = experts_first(pay, x_b, y_b, w_first)
     out_b, dx_b, gg_b, dw_b = experts_second(meta, xc, yc, gc, eo, dx, w_second)
@@ -1480,59 +1603,64 @@
 
     dw_a = owned(dw_a)
 
-    gmo, gres, pgrad, nmg, wrg, resg, cvg = pl.pallas_call(
+    gmo, gres, pgrad, small = pl.pallas_call(
         mid_kernel,
-        in_specs=[ANY] * 2 + [VM] * 11,
-        out_specs=[VM] * 7,
-        out_shape=(
-            shape((rows, d), bf16), shape((rows, d), f32), shape((rows, LANES), f32), shape((1, d), f32),
-            shape((LANES, d), f32), shape((LANES, LANES), f32), shape((LANES, d), f32),
-        ),
+        in_specs=[ANY] * 2 + [VM] * 8,
+        out_specs=[VM] * 4,
+        out_shape=(shape((rows, d), bf16), shape((rows, d), f32), shape((16, rows), f32), shape((32, d), f32)),
         scratch_shapes=[
             pltpu.VMEM((NF, ROOM, d), bf16),
             pltpu.VMEM((NF, 1, ROOM), f32),
             pltpu.VMEM((rows, d), f32),
             pltpu.VMEM((NF, rows), f32),
+            pltpu.VMEM((rows, LANES), f32),
+            pltpu.VMEM((rows, LANES), f32),
+            pltpu.VMEM((LANES, d), bf16),
+            pltpu.VMEM((16, LANES), f32),
             *send_scratch(),
             pltpu.SemaphoreType.DMA((2, NF - 1)),
             pltpu.SemaphoreType.DMA((1,)),
         ],
         compiler_params=pltpu.CompilerParams(collective_id=4, has_side_effects=True, vmem_limit_bytes=60 << 20),
         cost_estimate=cost(4, 4),
-    )(dx_b, gg_b, pos, out_grad, nmoe, resid, ids, aux, prior, wr, wres, cv, gm)
+    )(dx_b, gg_b, pos, out_grad, nmoe, resid, aux, prior, params, count)
     dw_a, dw_b, gmo = lax.optimization_barrier((dw_a, dw_b, gmo))
     dw_b = owned(dw_b)
-    igrad, wg, nag, layer_out = pl.pallas_call(
+    wg, gp, yr, small, dw_a = pl.pallas_call(
         bwd_kernel,
-        in_specs=[SM] + [VM] * 13 + [ANY] + [VM] * 2,
-        out_specs=[VM] * 4,
-        out_shape=(shape((rows, d), f32), shape((4, d, d), bf16), shape((1, d), f32), shape((rows, d), bf16)),
+        grid=(1,),
+        in_specs=[SM] + [VM] * 9 + [pl.BlockSpec((1, d, d), lambda i: (3, 0, 0)), VM, ANY, ANY],
+        out_specs=[VM] * 2 + [ANY, VM, ANY],
+        out_shape=(shape((4, d, d), bf16), shape((3, rows, d), bf16), blocks, shape((32, d), f32), shape(dw_a.shape, bf16)),
         scratch_shapes=[
             pltpu.VMEM((rows, d), bf16),
             pltpu.VMEM((heads, rows), f32),
             pltpu.VMEM((rows // QT, 2 * QT, QT), f32),
-            pltpu.VMEM((3, rows, d), bf16),
             pltpu.VMEM((rows, LANES), f32),
             pltpu.VMEM((rows, LANES), f32),
             pltpu.VMEM((rows, LANES), f32),
-            pltpu.VMEM((NF, ROOM, d), bf16),
             *send_scratch(),
+            *near_scratch((32, d)),
+            *exchange_scratch(1),
         ],
         compiler_params=pltpu.CompilerParams(collective_id=5, has_side_effects=True, vmem_limit_bytes=60 << 20),
         cost_estimate=cost(8, 4),
-    )(starts, gmo, gres, mixed, q, k, v, lse, nattn, tokens, ga, cosine, sine, w_attn, out_b, pos, base)
-
-    if packs > 1:
+    )(piece_starts, gmo, mixed, q, k, v, lse, nattn, cosine, sine, w_attn, small, out_b, dw_a)
+    alone = packs == 1
+    mine, nag, igrad, layer_out, small = finish(
+        wg, gp, gres, tokens, w_attn, yr, base, pos, params, small, tensor, alone, 6
+    )
+    if alone:
+        wg = mine
+    else:
         wg = lax.psum_scatter(wg, "dp", scatter_dimension=1, tiled=True)
         wg = lax.psum_scatter(wg, "tensor", scatter_dimension=2, tiled=True).astype(f32)
-        over = jnp.where(count > ROOM, 1.0, 0.0)
-        wrg, cvg, resg, nmg, nag, over = lax.psum((wrg, cvg, resg, nmg, nag, over), ("dp", "tensor"))
-        dw_a, dw_b = exchange8(dw_a, dw_b, 6)
-    else:
-        wg, small, dw_a, dw_b = finish(wg, dw_a, dw_b, wrg, cvg, resg, nmg, nag, count, tensor, 7)
-        wrg, cvg, resg, nmg, nag = small[0:24], small[24:26], small[32:48, 0:LANES], small[26], small[27]
-        over = small[28:29, 0:LANES]
-    overflow = jnp.sum(over) > 0
+        nag = lax.psum(nag, ("dp", "tensor"))
+        small = lax.psum(lax.psum(small, "tensor"), "dp", axis_index_groups=across)
+    dw_b = exchange8(dw_b, 7)
+    wrg, cvg, nmg = small[0:24], small[24:26], small[26]
+    resg = small[29:31].reshape(2 * RES, LANES)
+    overflow = jnp.sum(small[28:29, 0:LANES]) > 0
 
     def roomy(args):
         return plain_on_device(*args)
@@ -1542,7 +1670,7 @@
         return (
             layer_out,
             igrad,
-            pgrad[:, 0:ne],
+            pgrad[0:ne].T,
             nag.reshape(d),
             wg[0:3],
             wg[3].T,

time: 513 us -> 494 us (0.963)
  waiting for transfers between devices: 24.3 us -> 9.92 us
    reduce_scatter x2, waiting for transfers between devices: 22.3 us -> 2.15 us  [owned(): dw = lax.psum_scatter(dw, 'tensor', scatter_dimension=0, tiled=False)]
    pallas_call x6 -> x7, Pallas kernels: 378 us -> 372 us  [the longest x1 98.6 us: on_device(): pl.pallas_call(bwd_kernel, grid=(1,), in_specs=[SM] + [VM] * 9 + [pl.Bloc...]
    all_gather x2, waiting for transfers between devices: 1.91 us -> 7.71 us  [whole(): return lax.all_gather(w, 'tensor', axis=0, tiled=False)]
  transfers between devices with their start and end apart: 4 -> 4, of which waited for: 2 -> 2; matrix products, arithmetic and copies ran while one was open for 2% -> 1% of each run, Pallas kernels for 65% -> 80%
where the time goes in v4:
time: 494 us; the launch traced here: 490 us
  Pallas kernels  433 us (88%)
  local copies, waits for them, and re-layouts  22 us (4%)
  between operations  15 us (3%)
  waiting for transfers between devices  9.92 us (2%)
  other arithmetic  7.66 us (2%)
    pallas_call x1, Pallas kernels, on_device(): pl.pallas_call(bwd_kernel, grid=(1,), in_specs=[SM] + [VM] * 9 + [pl.Bloc...  98.6 us
    pallas_call x1, Pallas kernels, on_device(): pl.pallas_call(fwd_kernel, in_specs=[SM] + [VM] * 9 + [ANY], out_specs=[V...  86.2 us
    pallas_call x1, Pallas kernels, on_device(): pl.pallas_call(mid_kernel, in_specs=[ANY] * 2 + [VM] * 8, out_specs=[VM]...  49.6 us
    pallas_call x1, Pallas kernels, finish(): pl.pallas_call(functools.partial(final_kernel, tensor, comm), in_specs=[A...  49.4 us
    pallas_call x1, Pallas kernels, experts_first(): pl.pallas_call(first_kernel, in_specs=[VM] * 4, out_specs=[VM] * 6 + [SM]...  38.4 us
    pallas_call x1, Pallas kernels, gather_weights(): pl.pallas_call(functools.partial(weights_kernel, gather), in_specs=[ANY]...  37.1 us
    pallas_call x1, Pallas kernels, experts_second(): pl.pallas_call(second_kernel, in_specs=[SM] + [ANY] * 6, out_specs=[VM] *...  34.3 us
    pallas_call x1, Pallas kernels, prologue(): pl.pallas_call(functools.partial(prologue_kernel, tensor), in_specs=[ANY,...  23.1 us
  transfers between devices with their start and end apart: 4, of which 2 were waited for; matrix products, arithmetic and copies ran while one was open for 1% of the time, Pallas kernels for 80%

profile of v4, /device:TPU:0, one launch (start us, length us, event | category | flops | bytes accessed | tf_op | source)
XLA Modules:
  0.0 489.5 jit_solution(13263373300147248050)
XLA Ops:
  7.2 0.0 all-gather.21.cloned.1.call-start
  7.2 0.9 copy.187
  8.1 1.6 pad_maximum_fusion.14.w_ref
  9.8 23.1 %shard_map.295 = (bf16[3,8,96,256]{3,2,1,0:T(8,128)(2,1)}, bf16[4,96,768]{2,1,0:T(8,128)(2,1)}) custom-call(bf16[2,8,96,512]{3,2,1,0:T(8,128)(2,1)} %gu_ref.3, bf16[1,8,96,512]{3,2,1,0:T(8,128)(2,1)} %bitcast.315, bf16[4,96,192]{2,1,0:T(8,128)(2,1)} %pad_maximum_fusion.14.w_ref), custom_call_target="tpu_custom_call" | custom-call | flops 24999999488 | bytes 10000000 | tf_op jit(solution)/shard_map/pallas_call | solution.py:488
  32.9 0.0 all-gather.21.cloned.1.call-update
  32.9 0.0 all-gather.23.cloned.1.call-start
  33.0 1.1 copy-done.4
  34.1 0.0 copy-start.56
  34.1 37.1 %shard_map.296 = (bf16[4,768,768]{2,1,0:T(8,128)(2,1)S(1)}, bf16[3,8,96,256]{3,2,1,0:T(8,128)(2,1)}, f32[8,1,1024]{2,1,0:T(1,128)S(1)}, f32[16,128]{1,0:T(8,128)S(1)}, bf16[8,256,768]{2,1,0:T(8,128)(2,1)S(1)}) custom-call(bf16[4,96,768]{2,1,0:T(8,128)(2,1)S(1)} %copy-done.4, bf16[2,8,96,512]{3,2,1,0:T(8,128)(2,1)} %gu_ref.3, ...), custom_call_target="tpu_custom_call" | custom-call | flops 35000000512 | bytes 10000000 | tf_op jit(solution)/shard_map/pallas_call | solution.py:283
  71.2 2.1 copy-done
  73.3 0.6 copy-done.1
  73.9 0.6 copy-done.2
  74.5 1.7 copy-done.3
  76.2 0.0 all-gather.23.cloned.1.call-update
  76.2 0.3 reduce-scatter.34.cloned.1.call-start
  76.7 0.6 pad.8.prior_ref
  77.3 0.7 copy.189.starts_ref
  78.0 3.8 concatenate.35.par_ref
  81.8 86.2 %shard_map.297 = (bf16[1024,768]{1,0:T(8,128)(2,1)}, bf16[1024,768]{1,0:T(8,128)(2,1)}, bf16[1024,768]{1,0:T(8,128)(2,1)}, bf16[1024,768]{1,0:T(8,128)(2,1)}, f3...) custom-call(s32[4,2]{1,0:T(4,128)} %copy.189.starts_ref, ...), custom_call_target="tpu_custom_call" | custom-call | flops 40000000000 | bytes 30000000 | tf_op jit(solution)/shard_map/pallas_call | solution.py:1571
  167.9 0.0 all-gather.21.cloned.1.call-done.w_ref
  168.0 38.4 %shard_map.298 = (bf16[2304,768]{1,0:T(8,128)(2,1)}, bf16[2304,768]{1,0:T(8,128)(2,1)}, f32[2304,128]{1,0:T(8,128)}, f32[2304,768]{1,0:T(8,128)}, f32[2304,768]{...) custom-call(f32[16,1,256]{2,1,0:T(1,128)} %get-tuple-element.238.pay_ref, ...), custom_call_target="tpu_custom_call" | custom-call | flops 22000001024 | bytes 25000000 | tf_op jit(solution)/shard_map/pallas_call | solution.py:1110
  206.4 0.0 reduce-scatter.34.cloned.1.call-update
  206.4 0.0 reduce-scatter.36.cloned.1.call-start
  206.5 7.7 %all-gather.23.cloned.1.call-done.w_any = bf16[4,3,768,256]{3,2,1,0:T(8,128)(2,1)} async-done(((bf16[1,3,768,256]{3,2,1,0:T(8,128)(2,1)}), bf16[4,3,768,256]{3,2,1,0:T(8,128)(2,1)}) %all-gather.23.cloned.1.call-update) | async-done | bytes 4718608 | tf_op jit(solution)/shard_map/all_gather | solution.py:1565
  214.2 34.3 %shard_map.299 = (bf16[8,256,768]{2,1,0:T(8,128)(2,1)}, bf16[8,256,768]{2,1,0:T(8,128)(2,1)}, f32[8,1,256]{2,1,0:T(1,128)}, bf16[4,3,768,256]{3,2,1,0:T(8,128)(2,1)}) custom-call(s32[9]{0:T(128)} %get-tuple-element.243.meta_ref, bf16[2304,768]{1,0:T(8,128)(2,1)} %get-tuple-element.244.xc_any, bf16[2304,768]{1,0:T(8,128)(2,1)} %get-tuple-element.245.yc_any, ...), custom_call_target="tpu_custom_call" | custom-call | flops 22000001024 | bytes 25000000 | tf_op jit(solution)/shard_map/pallas_call | solution.py:1128
  248.5 49.6 %shard_map.300 = (bf16[1024,768]{1,0:T(8,128)(2,1)}, f32[1024,768]{1,0:T(8,128)}, f32[16,1024]{1,0:T(8,128)S(1)}, f32[32,768]{1,0:T(8,128)}) custom-call(bf16[8,256,768]{2,1,0:T(8,128)(2,1)} %get-tuple-element.251.dxb_ref, f32[8,1,256]{2,1,0:T(1,128)} %get-tuple-element.252.ggb_ref, f32[8,1,1024]{2,1,0:T(1,128)} %copy-done.1, ...), custom_call_target="tpu_custom_call" | custom-call | flops 4000000000 | bytes 4000000 | tf_op jit(solution)/shard_map/pallas_call | solution.py:1606
  298.1 2.1 reduce-scatter.34.cloned.1.call-done
  300.2 0.0 reduce-scatter.36.cloned.1.call-update
  300.2 98.6 %shard_map.301 = (bf16[4,768,768]{2,1,0:T(8,128)(2,1)}, bf16[3,1024,768]{2,1,0:T(8,128)(2,1)}, bf16[8,256,768]{2,1,0:T(8,128)(2,1)}, f32[32,768]{1,0:T(8,128)}, bf16[3,8,96,256]{3,2,1,0:T(8,128)(2,1)}) custom-call(s32[4,2]{1,0:T(4,128)} %copy.189.starts_ref, bf16[1024,768]{1,0:T(8,128)(2,1)} %get-tuple-element.258.gmo_ref, ...), custom_call_target="tpu_custom_call" | custom-call | flops 8000000000 | bytes 4000000 | tf_op jit(solution)/shard_map/pallas_call | solution.py:1629
  398.9 49.4 %shard_map.302 = (f32[4,96,192]{2,1,0:T(8,128)}, f32[1,768]{1,0:T(1,128)S(1)}, f32[1024,768]{1,0:T(8,128)}, bf16[1024,768]{1,0:T(8,128)(2,1)}, f32[32,768]{1,0:T(8,128)S(1)}) custom-call(bf16[4,768,768]{2,1,0:T(8,128)(2,1)} %get-tuple-element.268.g_ref, bf16[3,1024,768]{2,1,0:T(8,128)(2,1)} %get-tuple-element.269.gp_any, ...), custom_call_target="tpu_custom_call" | custom-call | flops 8000000000 | bytes 4000000 | tf_op jit(solution)/shard_map/pallas_call | solution.py:678
  448.3 0.6 slice_reduce_fusion.1
  449.5 0.0 reduce-scatter.36.cloned.1.call-done
  449.6 16.6 %shard_map.303 = bf16[3,8,96,256]{3,2,1,0:T(8,128)(2,1)} custom-call(bf16[3,8,96,256]{3,2,1,0:T(8,128)(2,1)} %bitcast.337), custom_call_target="tpu_custom_call" | custom-call | flops 17999998976 | bytes 10000000 | tf_op jit(solution)/shard_map/pallas_call | solution.py:511
  466.3 12.0 %conditional.1 = (bf16[1024,768]{1,0:T(8,128)(2,1)}, f32[1024,768]{1,0:T(8,128)}, f32[1024,12]{0,1:T(8,128)}, f32[768]{0:T(1024)}, f32[192,96]{1,0:T(8,128)}, /*...) conditional(s32[]{:T(128)} %convert_element_type.183, ...), branch_computations={%region_3.4_spmd, %region_4.53_spmd} | conditional | flops 61550759936 | bytes 1739719936 | solution.py:1690
  466.3 0.6 fusion.132
  466.9 0.6 reshape.483
  467.5 0.6 slice_bitcast_fusion.4
  468.1 0.6 reshape.484
  468.7 0.6 slice_reduce_fusion
  469.3 3.5 fusion.130
  472.8 1.4 convert_bitcast_fusion
  474.2 0.2 copy.190
  474.4 0.9 copy.211
  475.3 0.6 slice_bitcast_fusion.2
  475.9 0.6 slice_bitcast_fusion.3
  476.6 0.6 reduce.1
  478.3 2.8 copy.319
  481.1 1.7 copy.320
  (53 shorter events, 0.2 us)
Async XLA Ops:
  7.2 160.8 %all-gather.21.cloned.1.call-start = ((), (), s32[]{:S(2)}) async-start(), calls=%async_computation.26 | async-start | bytes 5898240 | tf_op jit(solution)/shard_map/all_gather | solution.py:1565
  9.7 23.2 %copy-start.12 = (bf16[1024,768]{1,0:T(8,128)(2,1)S(1)}, bf16[1024,768]{1,0:T(8,128)(2,1)}, u32[]{:S(2)}) copy-start(bf16[1024,768]{1,0:T(8,128)(2,1)} %og_ref.3) | copy-start | bytes 4718596
  9.7 23.2 %copy-start.100 = (s32[4096,2]{0,1:T(2,128)S(1)}, s32[4096,2]{0,1:T(2,128)}, u32[]{:S(2)}) copy-start(s32[4096,2]{0,1:T(2,128)} %param.26) | copy-start | bytes 98308
  9.7 23.2 %copy-start.102 = (s32[4096,2]{0,1:T(2,128)S(1)}, s32[4096,2]{0,1:T(2,128)}, u32[]{:S(2)}) copy-start(s32[4096,2]{0,1:T(2,128)} %param.27) | copy-start | bytes 98308
  32.9 181.3 %all-gather.23.cloned.1.call-start = ((), (), s32[]{:S(2)}) async-start(), calls=%async_computation.28 | async-start | bytes 5898240 | tf_op jit(solution)/shard_map/all_gather | solution.py:1565
  33.0 1.1 copy-start.4
  34.0 42.5 %copy-start.89 = (bf16[2,2,768]{2,1,0:T(2,128)(2,1)S(1)}, bf16[2,2,768]{2,1,0:T(2,128)(2,1)}, u32[]{:S(2)}) copy-start(bf16[2,2,768]{2,1,0:T(2,128)(2,1)} %param.36) | copy-start | bytes 18436
  34.0 42.5 %copy-start.113 = (bf16[768]{0:T(1024)(128)(2,1)S(1)}, bf16[768]{0:T(1024)(128)(2,1)}, u32[]{:S(2)}) copy-start(bf16[768]{0:T(1024)(128)(2,1)} %param.29) | copy-start | bytes 4612
  34.1 42.6 %copy-start.114 = (bf16[768]{0:T(1024)(128)(2,1)S(1)}, bf16[768]{0:T(1024)(128)(2,1)}, u32[]{:S(2)}) copy-start(bf16[768]{0:T(1024)(128)(2,1)} %param.32) | copy-start | bytes 4612
  34.1 42.6 %copy-start.95 = (bf16[12,12]{1,0:T(8,128)(2,1)S(1)}, bf16[12,12]{1,0:T(8,128)(2,1)}, u32[]{:S(2)}) copy-start(bf16[12,12]{1,0:T(8,128)(2,1)} %param.34) | copy-start | bytes 868
  34.1 42.6 %copy-start.51 = (bf16[1024,12]{0,1:T(8,128)(2,1)S(1)}, bf16[1024,12]{0,1:T(8,128)(2,1)}, u32[]{:S(2)}) copy-start(bf16[1024,12]{0,1:T(8,128)(2,1)} %param.25) | copy-start | bytes 73732
  34.1 43.2 %copy-start.67 = (s32[4,2]{0,1:T(2,128)S(1)}, s32[4,2]{0,1:T(2,128)}, u32[]{:S(2)}) copy-start(s32[4,2]{0,1:T(2,128)} %param.28) | copy-start | bytes 100
  34.1 43.9 %copy-start.56 = (bf16[768,12]{0,1:T(8,128)(2,1)S(1)}, bf16[768,12]{0,1:T(8,128)(2,1)}, u32[]{:S(2)}) copy-start(bf16[768,12]{0,1:T(8,128)(2,1)} %param.33) | copy-start | bytes 55300
  34.1 43.9 %copy-start.105 = (bf16[2,768]{1,0:T(2,128)(2,1)S(1)}, bf16[2,768]{1,0:T(2,128)(2,1)}, u32[]{:S(2)}) copy-start(bf16[2,768]{1,0:T(2,128)(2,1)} %param.35) | copy-start | bytes 9220
  34.1 47.7 %copy-start.20 = (bf16[1024,768]{1,0:T(8,128)(2,1)S(1)}, bf16[1024,768]{1,0:T(8,128)(2,1)}, u32[]{:S(2)}) copy-start(bf16[1024,768]{1,0:T(8,128)(2,1)} %tok_any.1) | copy-start | bytes 4718596
  71.2 2.1 copy-start
  73.3 0.6 copy-start.1
  73.9 0.6 copy-start.2
  74.5 1.7 copy-start.3
  76.2 224.0 %reduce-scatter.34.cloned.1.call-start = ((), (), s32[]{:S(2)}) async-start(), calls=%async_computation.27 | async-start | bytes 5898240 | tf_op jit(solution)/shard_map/reduce_scatter | solution.py:1599
  206.4 243.1 %reduce-scatter.36.cloned.1.call-start = ((), (), s32[]{:S(2)}) async-start(), calls=%async_computation.29 | async-start | bytes 5898240 | tf_op jit(solution)/shard_map/reduce_scatter | solution.py:1599
  449.5 16.7 %copy-start.49 = (bf16[3,96,192]{2,1,0:T(8,128)(2,1)S(1)}, bf16[3,96,192]{2,1,0:T(8,128)(2,1)}, u32[]{:S(2)}) copy-start(bf16[3,96,192]{2,1,0:T(8,128)(2,1)} %param.30) | copy-start | bytes 331780
  449.6 16.7 %copy-start.62 = (bf16[192,96]{1,0:T(8,128)(2,1)S(1)}, bf16[192,96]{1,0:T(8,128)(2,1)}, u32[]{:S(2)}) copy-start(bf16[192,96]{1,0:T(8,128)(2,1)} %param.31) | copy-start | bytes 110596
  449.6 16.7 %copy-start.68 = (s32[4,2]{0,1:T(2,128)S(1)}, s32[4,2]{0,1:T(2,128)}, u32[]{:S(2)}) copy-start(s32[4,2]{0,1:T(2,128)} %param.28) | copy-start | bytes 100
  449.6 16.7 %copy-start.96 = (bf16[12,12]{1,0:T(8,128)(2,1)S(1)}, bf16[12,12]{1,0:T(8,128)(2,1)}, u32[]{:S(2)}) copy-start(bf16[12,12]{1,0:T(8,128)(2,1)} %param.34) | copy-start | bytes 868
  449.6 16.7 %copy-start.115 = (bf16[768]{0:T(1024)(128)(2,1)S(1)}, bf16[768]{0:T(1024)(128)(2,1)}, u32[]{:S(2)}) copy-start(bf16[768]{0:T(1024)(128)(2,1)} %param.32) | copy-start | bytes 4612
  466.3 6.6 %copy-start.34 = (bf16[3,8,96,256]{3,2,1,0:T(8,128)(2,1)S(1)}, bf16[3,8,96,256]{3,2,1,0:T(8,128)(2,1)}, u32[]{:S(2)}) copy-start(bf16[3,8,96,256]{3,2,1,0:T(8,128)(2,1)} %get-tuple-element.131) | copy-start | bytes 3538948 | tf_op jit(solution)/shard_map/cond
  466.3 6.5 %copy-start.35 = (bf16[3,8,96,256]{3,2,1,0:T(8,128)(2,1)S(1)}, bf16[3,8,96,256]{3,2,1,0:T(8,128)(2,1)}, u32[]{:S(2)}) copy-start(bf16[3,8,96,256]{3,2,1,0:T(8,128)(2,1)} %get-tuple-element.132) | copy-start | bytes 3538948 | tf_op jit(solution)/shard_map/cond
  472.8 1.4 copy-start.50
  478.3 2.8 copy-start.38
Sparse Core Ops, SparseCore 0:
  33.0 91.6 all-gather.20
  126.3 87.8 all-gather.22
  216.5 83.6 reduce-scatter.33
  302.4 85.7 reduce-scatter.35

commit v5 on v4

--- a/solution.py
+++ b/solution.py
@@ -293,7 +293,7 @@
             pltpu.SemaphoreType.DMA,
             *exchange_scratch(2),
         ],
-        compiler_params=pltpu.CompilerParams(collective_id=cid, has_side_effects=True, vmem_limit_bytes=40 << 20),
+        compiler_params=pltpu.CompilerParams(collective_id=cid, has_side_effects=True, vmem_limit_bytes=60 << 20),
         cost_estimate=cost(35, 10),
     )(w, gate_up, down, ids, ranks, og)
 
@@ -460,18 +460,20 @@
     return [pltpu.SemaphoreType.DMA((2, (NF - 1) * n)), pltpu.SemaphoreType.DMA((n,))]
 
 
-def prologue_kernel(tensor, gu_ref, dn_ref, w_ref, out_ref, slab_ref, zbuf, zsems, *scratch):
+def prologue_kernel(tensor, gu_ref, dn_ref, w_ref, wo_ref, out_ref, slab_ref, zbuf, zsems, *scratch):
     here = lax.axis_index("tensor")
-    k, _, f = w_ref.shape
+    k, f = slab_ref.shape[0], w_ref.shape[2]
     greet(all_peers() + far_peers(tensor))
-    copies = [
-        remote(w_ref, zbuf.at[here], zsems, n, axis, peer) for n, (axis, peer) in enumerate(far_peers(tensor))
-    ]
+    copies = []
+    for n, (axis, peer) in enumerate(far_peers(tensor)):
+        copies.append(remote(w_ref, zbuf.at[here, pl.ds(0, k - 1)], zsems, 2 * n, axis, peer))
+        copies.append(remote(wo_ref, zbuf.at[here, k - 1], zsems, 2 * n + 1, axis, peer))
     for c in copies:
         c.start()
     swap = Exchange8([gu_ref, dn_ref], out_ref, 0, *scratch)
     swap.begin()
-    zbuf[here] = w_ref[...]
+    zbuf[here, 0 : k - 1] = w_ref[...]
+    zbuf[here, k - 1] = wo_ref[...]
     for c in copies:
         c.wait_recv()
     for c in range(k):
@@ -483,21 +485,22 @@
         c.wait_send()
 
 
-def prologue(gate_up, down, w, tensor, cid):
+def prologue(gate_up, down, w, wo, tensor, cid):
     k, r, f = w.shape
+    k = k + 1
     return pl.pallas_call(
         functools.partial(prologue_kernel, tensor),
-        in_specs=[ANY, ANY, VM],
+        in_specs=[ANY, ANY, VM, VM],
         out_specs=[ANY, VM],
         out_shape=(half_shape(gate_up), shape((k, r, tensor * f), bf16)),
         scratch_shapes=[
             pltpu.VMEM((tensor, k, r, f), bf16),
-            pltpu.SemaphoreType.DMA((2, tensor - 1)),
+            pltpu.SemaphoreType.DMA((2, 2 * (tensor - 1))),
             *exchange_scratch(2),
         ],
         compiler_params=pltpu.CompilerParams(collective_id=cid, has_side_effects=True),
         cost_estimate=cost(25, 10),
-    )(gate_up, down, w)
+    )(gate_up, down, w, wo)
 
 
 def exchange_kernel(src, dst, *scratch):
@@ -544,13 +547,14 @@
 
 
 class Far:
-    def __init__(self, tensor, have, got, sems):
-        self.tensor, self.have, self.got, self.here = tensor, have, got, lax.axis_index("tensor")
+    def __init__(self, tensor, value, have, got, sems):
+        self.tensor, self.value, self.have, self.got, self.here = tensor, value, have, got, lax.axis_index("tensor")
         self.c = [
             remote(have, got.at[self.here], sems, n, axis, peer) for n, (axis, peer) in enumerate(far_peers(tensor))
         ]
 
     def begin(self):
+        self.have[...] = self.value[...].astype(bf16)
         for c in self.c:
             c.start()
         self.got[self.here] = self.have[...]
@@ -558,22 +562,22 @@
     def end(self):
         for c in self.c:
             c.wait_recv()
-        total = self.got[0]
+        total = self.got[0].astype(f32)
         for t in range(1, self.tensor):
-            total = total + self.got[t]
+            total = total + self.got[t].astype(f32)
         for c in self.c:
             c.wait_send()
         return total
 
 
 def far_scratch(tensor, dims):
-    return [pltpu.VMEM((tensor, *dims), f32), pltpu.SemaphoreType.DMA((2, tensor - 1))]
+    return [pltpu.VMEM(dims, bf16), pltpu.VMEM((tensor, *dims), bf16), pltpu.SemaphoreType.DMA((2, tensor - 1))]
 
 
 def final_kernel(
     tensor, comm, g_ref, gp_any, gres_any, tok_any, w_any, yr_any, base_any, pos_ref, par_ref, small_ref,
-    out_ref, nag_ref, igrad_ref, layer_ref, total_ref,
-    gp_ref, gres_ref, tok_ref, w_ref, yr_ref, base_ref, lsems, zf, zs, zr, *scratch,
+    zs_ref, igrad_ref, layer_ref, total_ref, nag_ref,
+    gp_ref, gres_ref, tok_ref, w_ref, yr_ref, base_ref, lsems, *scratch,
 ):
     k, d, _ = g_ref.shape
     ntile = SEQ // QT
@@ -583,12 +587,9 @@
     )
     loads = [pltpu.make_async_copy(src, dst, lsems.at[n]) for n, (src, dst) in enumerate(pairs)]
     if comm:
-        here = lax.axis_index("tensor")
-        r, f = out_ref.shape[1:]
+        r, f = zs_ref.shape[2:]
         red = Reduce8(lambda s: g_ref.at[:, pl.ds(pl.multiple_of(s * r, r), r), :], scratch[:5], *scratch[5:7])
-        zsems = scratch[7]
-        sums = Near(*scratch[8:11])
-        gains, smalls = Far(tensor, sums.have.at[3], *scratch[11:13]), Far(tensor, small_ref, *scratch[13:15])
+        sums, smalls = Near(*scratch[7:10]), Far(tensor, small_ref, *scratch[10:13])
         red.load()
         greet(near_peers() + far_peers(tensor))
         red.begin()
@@ -632,40 +633,63 @@
 
     def write(part, total):
         for t in range(tensor):
-            zf[t, part] = total[:, :, t * f : (t + 1) * f]
-            zs[t, part] = total[:, :, t * f : (t + 1) * f].astype(bf16)
-
+            zs_ref[t, part] = total[:, :, t * f : (t + 1) * f].astype(bf16)
+
+    for i in range(ntile):
+        layer(i)
+        if comm and i < 3:
+            sums.step(i)
     if not comm:
-        for i in range(ntile):
-            layer(i)
         return
-    layer(0)
-    sums.step(0)
+    for i in range(ntile, 3):
+        sums.step(i)
+    nag_ref[...] = sums.have[3]
     red.end(write)
-    out_copies = [
-        remote(zs.at[peer], zr.at[here], zsems, n, axis, peer) for n, (axis, peer) in enumerate(far_peers(tensor))
+    total_ref[...] = smalls.end()
+    red.close()
+    sums.close()
+
+
+def last_kernel(tensor, zs_ref, small_ref, dw_ref, out_ref, total_ref, dwx_ref, zr, zsems, *scratch):
+    here = lax.axis_index("tensor")
+    smalls = Far(tensor, small_ref, *scratch[0:3])
+    swap = Exchange8([dw_ref], dwx_ref, None, *scratch[3:5])
+    greet(all_peers() + far_peers(tensor))
+    copies = [
+        remote(zs_ref.at[peer], zr.at[here], zsems, n, axis, peer) for n, (axis, peer) in enumerate(far_peers(tensor))
     ]
-    for c in out_copies:
+    for c in copies:
         c.start()
-    sums.step(1)
-    for i in range(1, ntile - 1):
-        layer(i)
-    sums.step(2)
-    gains.begin()
-    layer(ntile - 1)
-    nag_ref[...] = gains.end()
-    total_ref[...] = smalls.end()
-    sums.close()
-    zr[here] = jnp.zeros(zr.shape[1:], bf16)
-    for c in out_copies:
+    smalls.begin()
+    swap.begin()
+    zr[here] = zs_ref[here]
+    for c in copies:
         c.wait_recv()
-    total = zf[here]
-    for t in range(tensor):
+    total = zr[0].astype(f32)
+    for t in range(1, tensor):
         total = total + zr[t].astype(f32)
     out_ref[...] = total
-    red.close()
-    for c in out_copies:
+    total_ref[...] = smalls.end()
+    for c in copies:
         c.wait_send()
+    swap.end()
+
+
+def last(zs, small, dw, tensor, cid):
+    return pl.pallas_call(
+        functools.partial(last_kernel, tensor),
+        in_specs=[VM] * 2 + [ANY],
+        out_specs=[VM] * 2 + [ANY],
+        out_shape=(shape(zs.shape[1:], f32), shape(small.shape, f32), shape(dw.shape, dw.dtype)),
+        scratch_shapes=[
+            pltpu.VMEM(zs.shape, bf16),
+            pltpu.SemaphoreType.DMA((2, tensor - 1)),
+            *far_scratch(tensor, small.shape),
+            *exchange_scratch(1),
+        ],
+        compiler_params=pltpu.CompilerParams(collective_id=cid, has_side_effects=True, vmem_limit_bytes=60 << 20),
+        cost_estimate=cost(18, 10),
+    )(zs, small, dw)
 
 
 def finish(g, gp, gres, tokens, w, yr, base, pos, params, small, tensor, comm, cid):
@@ -680,8 +704,8 @@
         in_specs=[ANY] * 7 + [VM] * 3,
         out_specs=[VM] * 5,
         out_shape=(
-            shape((k, r, f), f32), shape((1, d), f32), shape((rows, d), f32), shape((rows, d), bf16),
-            shape(small.shape, f32),
+            shape((tensor, k, r, f), bf16), shape((rows, d), f32), shape((rows, d), bf16), shape(small.shape, f32),
+            shape((1, d), f32),
         ),
         scratch_shapes=[
             pltpu.VMEM(gp.shape, bf16),
@@ -691,13 +715,8 @@
             pltpu.VMEM(yr.shape, bf16),
             pltpu.VMEM((rows, d), f32),
             pltpu.SemaphoreType.DMA((6,)),
-            pltpu.VMEM((tensor, k, r, f), f32),
-            pltpu.VMEM((tensor, k, r, f), bf16),
-            pltpu.VMEM((tensor, k, r, f), bf16),
             *reduce_scratch((k, r, columns)),
-            pltpu.SemaphoreType.DMA((2, tensor - 1)),
             *near_scratch((1, d)),
-            *far_scratch(tensor, (1, d)),
             *far_scratch(tensor, small.shape),
         ],
         compiler_params=once,
@@ -827,10 +846,14 @@
 
 
 def mid_kernel(
-    dxb_ref, ggb_ref, pos_ref, og_ref, nmoe_ref, resid_ref, aux_ref, prior_ref, par_ref, count_ref,
+    dxb_ref, ggb_ref, og_any, nmoe_any, resid_any, aux_any, pos_ref, prior_ref, par_ref, count_ref,
     gmo_ref, gres_ref, pgrad_ref, small_ref,
-    dxr, ggr, dx_ref, gg_ref, inner_ref, extra_ref, wr_ref, resg_ref, *scratch,
+    dxr, ggr, dx_ref, gg_ref, inner_ref, extra_ref, wr_ref, resg_ref, og_ref, nmoe_ref, resid_ref, aux_ref, lsems, *scratch,
 ):
+    pairs = ((og_any, og_ref), (nmoe_any, nmoe_ref), (resid_any, resid_ref), (aux_any, aux_ref))
+    loads = [pltpu.make_async_copy(a, b, lsems.at[n]) for n, (a, b) in enumerate(pairs)]
+    for c in loads:
+        c.start()
     greet(all_peers())
     send, swap = Send8(dxb_ref, dxr, *scratch[0:2], False), Swap8(ggb_ref, ggr, *scratch[2:4])
     swap.begin()
@@ -872,6 +895,8 @@
         small_ref[24:26, :] += tn(cv_hi, g16)[0:NC] + tn(cv_lo, g16)[0:NC]
         return carry
 
+    for c in loads:
+        c.wait()
     lax.fori_loop(0, SEQ // QT, ahead, 0)
     swap.end()
     for n, m in enumerate((0, 1, 2, 3, 4, 5, 6, 7)):
@@ -918,11 +943,16 @@
 
 
 def bwd_kernel(
-    starts_ref, gmo_ref, mixed_ref, q_ref, k_ref, v_ref, lse_ref, nattn_ref, cos_ref, sin_ref, wo_ref, small_ref,
+    starts_ref, gmo_ref, mixed_ref, q_any, k_any, v_any, lse_ref, nattn_any, cos_any, sin_any, w_any, small_ref,
     outb_ref, dw_ref,
     wg_ref, gp_ref, outr_ref, total_ref, dwx_ref,
-    do_ref, delta_ref, bias_ref, dk_ref, dv_ref, dq_ref, *scratch,
+    do_ref, delta_ref, bias_ref, dk_ref, dv_ref, dq_ref, wo_ref, wsem, q_ref, k_ref, v_ref, nattn_ref, cos_ref, sin_ref, lsems,
+    *scratch,
 ):
+    late = ((q_any, q_ref), (k_any, k_ref), (v_any, v_ref), (cos_any, cos_ref), (sin_any, sin_ref), (nattn_any, nattn_ref))
+    loads = [pltpu.make_async_copy(a, b, lsems.at[n]) for n, (a, b) in enumerate(late)]
+    load = pltpu.make_async_copy(w_any.at[pl.ds(3, 1)], wo_ref, wsem)
+    load.start()
     send = Send8(outb_ref, outr_ref, *scratch[0:2], False)
     sums = Near(*scratch[2:5])
     sums.have[0] = small_ref[...]
@@ -931,6 +961,8 @@
     send.begin()
     swap = Exchange8([dw_ref], dwx_ref, None, *scratch[5:7])
     swap.begin()
+    for c in loads:
+        c.start()
     d = mixed_ref.shape[1]
     pairs = d // LANES
     ntile = SEQ // QT
@@ -941,6 +973,8 @@
     pick = jnp.where(
         lax.broadcasted_iota(i32, (heads, d), 1) // HD == lax.broadcasted_iota(i32, (heads, d), 0), 1.0, 0.0
     ).astype(bf16)
+
+    load.wait()
 
     def start(i, carry):
         rows = pl.ds(pl.multiple_of(i * QT, QT), QT)
@@ -988,15 +1022,17 @@
         gp_ref[2, :, cols] = dv_ref[...].astype(bf16)
         return carry
 
+    for c in loads:
+        c.wait()
+    lax.fori_loop(0, pairs, pair, 0)
     sums.step(1)
-    lax.fori_loop(0, pairs, pair, 0)
-    sums.step(2)
     for c in range(3):
         wg_ref[c] = tn(nattn_ref[...], gp_ref[c]).astype(wg_ref.dtype)
     for m in range(NF):
         send.got(m)
     send.close()
     swap.end()
+    sums.step(2)
     total_ref[...] = sums.have[3]
     sums.close()
 
@@ -1147,6 +1183,52 @@
         compiler_params=pltpu.CompilerParams(vmem_limit_bytes=60 << 20),
         cost_estimate=cost(22, 25),
     )(meta, xc, yc, gc, eo, dx, w)
+
+
+def emit_kernel(a_ref, b_ref, wg_ref, small_ref, nag_ref, gu_ref, dn_ref, qkv_ref, wo_ref, rt_ref, rg_ref, cv_ref, cg_ref, na_ref, nm_ref):
+    half = a_ref.shape[3]
+    for n, ref in ((0, a_ref), (1, b_ref)):
+        at = slice(n * half, (n + 1) * half)
+        gu_ref[:, 0, :, at] = ref[0:2, 0].astype(f32)
+        dn_ref[0, :, at] = ref[2, 0].astype(f32)
+
+    @pl.when(pl.program_id(0) == 0)
+    def _():
+        qkv_ref[...] = wg_ref[0:3]
+        r, f = wg_ref.shape[1:]
+        wide = jnp.concatenate([wg_ref[3], jnp.zeros((r, -f % LANES), f32)], axis=1)
+        wo_ref[...] = jnp.concatenate([wide, jnp.zeros((-r % LANES, wide.shape[1]), f32)], axis=0).T[0:f, 0:r]
+        ne = rg_ref.shape[0]
+        rt_ref[...] = small_ref[0:ne, :]
+        for c in range(NC):
+            cg_ref[c] = small_ref[Z0 + 2 * c : Z0 + 2 * c + 2, :]
+        cv_ref[...] = small_ref[24 : 24 + NC, :]
+        nm_ref[...] = small_ref[26, :]
+        na_ref[...] = nag_ref[0, :]
+        for n in range(ne):
+            at = n % RES * LANES
+            rg_ref[n : n + 1, :] = small_ref[29 + n // RES : 30 + n // RES, at : at + LANES][:, 0:ne]
+
+
+def emit(dw_a, dw_b, wg, small, nag, ne):
+    _, groups, r, half = dw_a.shape
+    d = small.shape[1]
+    piece = pl.BlockSpec((3, 1, r, half), lambda e: (0, e, 0, 0))
+    whole = lambda *dims: pl.BlockSpec(dims, lambda e: (0,) * len(dims))
+    rest = [(3, *wg.shape[1:]), wg.shape[:0:-1], (ne, d), (ne, ne), (NC, d), (NC, 2, d), (d,), (d,)]
+    return pl.pallas_call(
+        emit_kernel,
+        grid=(groups,),
+        in_specs=[piece, piece, whole(*wg.shape), whole(*small.shape), whole(1, d)],
+        out_specs=[
+            pl.BlockSpec((2, 1, r, 2 * half), lambda e: (0, e, 0, 0)), pl.BlockSpec((1, r, 2 * half), lambda e: (e, 0, 0)),
+            *(whole(*dims) for dims in rest),
+        ],
+        out_shape=(
+            shape((2, groups, r, 2 * half), f32), shape((groups, r, 2 * half), f32), *(shape(dims, f32) for dims in rest),
+        ),
+        cost_estimate=cost(1, 8),
+    )(dw_a, dw_b, wg, small, nag)
 
 
 def router_rows(par_ref, wr_ref):
@@ -1549,10 +1631,9 @@
         axis=0,
     )
 
-    w_attn = jnp.concatenate([qkv_weight, out_weight.T[None]], axis=0)
     w_down_t = w_down.transpose(0, 2, 1)[None]
     shard = w_down.shape[1]
-    w_first, slab = prologue(w_gate_up, w_down_t, w_attn, tensor, 1)
+    w_first, slab = prologue(w_gate_up, w_down_t, qkv_weight, out_weight.T, tensor, 1)
     w_full, w_second, pos, count, ys = gather_weights(
         slab, w_gate_up, w_down_t, ids, ranks, out_grad, packs == 1, 2
     )
@@ -1605,7 +1686,7 @@
 
     gmo, gres, pgrad, small = pl.pallas_call(
         mid_kernel,
-        in_specs=[ANY] * 2 + [VM] * 8,
+        in_specs=[ANY] * 6 + [VM] * 4,
         out_specs=[VM] * 4,
         out_shape=(shape((rows, d), bf16), shape((rows, d), f32), shape((16, rows), f32), shape((32, d), f32)),
         scratch_shapes=[
@@ -1617,19 +1698,23 @@
             pltpu.VMEM((rows, LANES), f32),
             pltpu.VMEM((LANES, d), bf16),
             pltpu.VMEM((16, LANES), f32),
+            pltpu.VMEM((rows, d), bf16),
+            pltpu.VMEM((rows, d), bf16),
+            pltpu.VMEM((rows, d), f32),
+            pltpu.VMEM((rows, LANES), f32),
+            pltpu.SemaphoreType.DMA((4,)),
             *send_scratch(),
             pltpu.SemaphoreType.DMA((2, NF - 1)),
             pltpu.SemaphoreType.DMA((1,)),
         ],
         compiler_params=pltpu.CompilerParams(collective_id=4, has_side_effects=True, vmem_limit_bytes=60 << 20),
         cost_estimate=cost(4, 4),
-    )(dx_b, gg_b, pos, out_grad, nmoe, resid, aux, prior, params, count)
+    )(dx_b, gg_b, out_grad, nmoe, resid, aux, pos, prior, params, count)
     dw_a, dw_b, gmo = lax.optimization_barrier((dw_a, dw_b, gmo))
     dw_b = owned(dw_b)
     wg, gp, yr, small, dw_a = pl.pallas_call(
         bwd_kernel,
-        grid=(1,),
-        in_specs=[SM] + [VM] * 9 + [pl.BlockSpec((1, d, d), lambda i: (3, 0, 0)), VM, ANY, ANY],
+        in_specs=[SM, VM, VM, ANY, ANY, ANY, VM] + [ANY] * 4 + [VM, ANY, ANY],
         out_specs=[VM] * 2 + [ANY, VM, ANY],
         out_shape=(shape((4, d, d), bf16), shape((3, rows, d), bf16), blocks, shape((32, d), f32), shape(dw_a.shape, bf16)),
         scratch_shapes=[
@@ -1639,6 +1724,12 @@
             pltpu.VMEM((rows, LANES), f32),
             pltpu.VMEM((rows, LANES), f32),
             pltpu.VMEM((rows, LANES), f32),
+            pltpu.VMEM((1, d, d), bf16),
+            pltpu.SemaphoreType.DMA,
+            *[pltpu.VMEM((rows, d), bf16)] * 3,
+            pltpu.VMEM((rows, d), bf16),
+            *[pltpu.VMEM((rows, LANES), f32)] * 2,
+            pltpu.SemaphoreType.DMA((6,)),
             *send_scratch(),
             *near_scratch((32, d)),
             *exchange_scratch(1),
@@ -1647,40 +1738,38 @@
         cost_estimate=cost(8, 4),
     )(piece_starts, gmo, mixed, q, k, v, lse, nattn, cosine, sine, w_attn, small, out_b, dw_a)
     alone = packs == 1
-    mine, nag, igrad, layer_out, small = finish(
+    zs, igrad, layer_out, small, nag = finish(
         wg, gp, gres, tokens, w_attn, yr, base, pos, params, small, tensor, alone, 6
     )
     if alone:
-        wg = mine
+        wg, nag, dw_b = last(zs, nag, dw_b, tensor, 7)
     else:
         wg = lax.psum_scatter(wg, "dp", scatter_dimension=1, tiled=True)
         wg = lax.psum_scatter(wg, "tensor", scatter_dimension=2, tiled=True).astype(f32)
         nag = lax.psum(nag, ("dp", "tensor"))
         small = lax.psum(lax.psum(small, "tensor"), "dp", axis_index_groups=across)
-    dw_b = exchange8(dw_b, 7)
-    wrg, cvg, nmg = small[0:24], small[24:26], small[26]
-    resg = small[29:31].reshape(2 * RES, LANES)
+        dw_b = exchange8(dw_b, 7)
     overflow = jnp.sum(small[28:29, 0:LANES]) > 0
 
     def roomy(args):
         return plain_on_device(*args)
 
     def packed(args):
-        dw = jnp.concatenate([dw_a, dw_b], axis=-1).astype(f32)
+        gate_up, down, qkv, wo, router, residual, vectors, blends, gain_attn, gain_moe = emit(dw_a, dw_b, wg, small, nag, ne)
         return (
             layer_out,
             igrad,
             pgrad[0:ne].T,
-            nag.reshape(d),
-            wg[0:3],
-            wg[3].T,
-            nmg.reshape(d),
-            wrg[0:ne].T,
-            resg[0:ne, 0:ne],
-            cvg[0:NC],
-            wrg[Z0 : Z0 + 2 * NC].reshape(NC, 2, d),
-            dw[0:2],
-            dw[2].transpose(0, 2, 1),
+            gain_attn,
+            qkv,
+            wo,
+            gain_moe,
+            router.T,
+            residual,
+            vectors,
+            blends,
+            gate_up,
+            down.transpose(0, 2, 1),
         )
 
     args = (

time: 494 us -> 445 us (0.901)
  Pallas kernels: 433 us -> 393 us
  local copies, waits for them, and re-layouts: 22 us -> 11.8 us
  waiting for transfers between devices: 9.92 us -> 18.7 us
  other arithmetic: 7.66 us -> 0.6 us
    pallas_call x3 -> x4, Pallas kernels: 165 us -> 147 us  [the longest x1 62.9 us: on_device(): pl.pallas_call(bwd_kernel, in_specs=[SM, VM, VM, ANY, ANY, ANY, VM] + [AN...]
    pallas_call x1, Pallas kernels: 49.4 us -> 33.9 us  [finish(): pl.pallas_call(functools.partial(final_kernel, tensor, comm), in_specs=[A...]
    all_gather x2, waiting for transfers between devices: 7.71 us -> 16 us  [whole(): return lax.all_gather(w, 'tensor', axis=0, tiled=False)]
    unnamed x50 -> x42, local copies, waits for them, and re-layouts: 12.2 us -> 6.75 us
  transfers between devices with their start and end apart: 4 -> 4, of which waited for: 2 -> 2; matrix products, arithmetic and copies ran while one was open for 1% -> 1% of each run, Pallas kernels for 80% -> 77%
where the time goes in v5:
time: 445 us; the launch traced here: 441 us
  Pallas kernels  393 us (88%)
  waiting for transfers between devices  18.7 us (4%)
  between operations  15.1 us (3%)
  local copies, waits for them, and re-layouts  11.8 us (3%)
    pallas_call x1, Pallas kernels, on_device(): pl.pallas_call(fwd_kernel, in_specs=[SM] + [VM] * 9 + [ANY], out_specs=[V...  86.1 us
    pallas_call x1, Pallas kernels, on_device(): pl.pallas_call(bwd_kernel, in_specs=[SM, VM, VM, ANY, ANY, ANY, VM] + [AN...  62.9 us
    pallas_call x1, Pallas kernels, on_device(): pl.pallas_call(mid_kernel, in_specs=[ANY] * 6 + [VM] * 4, out_specs=[VM]...  53.3 us
    pallas_call x1, Pallas kernels, gather_weights(): pl.pallas_call(functools.partial(weights_kernel, gather), in_specs=[ANY]...  39.3 us
    pallas_call x1, Pallas kernels, experts_first(): pl.pallas_call(first_kernel, in_specs=[VM] * 4, out_specs=[VM] * 6 + [SM]...  34.1 us
    pallas_call x1, Pallas kernels, finish(): pl.pallas_call(functools.partial(final_kernel, tensor, comm), in_specs=[A...  33.9 us
    pallas_call x1, Pallas kernels, experts_second(): pl.pallas_call(second_kernel, in_specs=[SM] + [ANY] * 6, out_specs=[VM] *...  30 us
    pallas_call x1, Pallas kernels, last(): pl.pallas_call(functools.partial(last_kernel, tensor), in_specs=[VM] * 2...  23.6 us
  transfers between devices with their start and end apart: 4, of which 2 were waited for; matrix products, arithmetic and copies ran while one was open for 1% of the time, Pallas kernels for 77%

profile of v5, /device:TPU:0, one launch (start us, length us, event | category | flops | bytes accessed | tf_op | source)
XLA Modules:
  0.0 441.0 jit_solution(3129547842878112893)
XLA Ops:
  7.2 0.0 all-gather.21.cloned.1.call-start
  7.2 1.5 copy.172
  8.7 23.2 %shard_map.279 = (bf16[3,8,96,256]{3,2,1,0:T(8,128)(2,1)}, bf16[4,96,768]{2,1,0:T(8,128)(2,1)}) custom-call(bf16[2,8,96,512]{3,2,1,0:T(8,128)(2,1)} %gu_ref.3, bf16[1,8,96,512]{3,2,1,0:T(8,128)(2,1)} %bitcast.305, bf16[3,96,192]{2,1,0:T(8,128)(2,1)} %w_ref.1, bf16[96,192]{1,0:T(8,128)(2,1)} %bitcast.316), custom_call_target="tpu_custom_call" | custom-call | flops 24999999488 | bytes 10000000 | tf_op jit(solution)/shard_map/pallas_call | solution.py:491
  31.9 0.0 all-gather.21.cloned.1.call-update
  31.9 0.0 all-gather.23.cloned.1.call-start
  32.0 0.0 copy-start.83
  32.0 0.0 copy-start.107
  32.0 0.0 copy-start.108
  32.1 0.0 copy-start.89
  32.1 0.0 copy-start.42
  32.1 0.0 copy-start.61
  32.1 0.0 copy-start.48
  32.1 0.0 copy-start.99
  32.1 0.0 copy-start.15
  32.1 39.3 %shard_map.280 = (bf16[4,768,768]{2,1,0:T(8,128)(2,1)}, bf16[3,8,96,256]{3,2,1,0:T(8,128)(2,1)}, f32[8,1,1024]{2,1,0:T(1,128)}, f32[16,128]{1,0:T(8,128)}, bf16[8,256,768]{2,1,0:T(8,128)(2,1)}) custom-call(bf16[4,96,768]{2,1,0:T(8,128)(2,1)} %get-tuple-element.238.slab, bf16[2,8,96,512]{3,2,1,0:T(8,128)(2,1)} %gu_ref.3, bf16[1,8,96,512]{3,2,1,0:T(8,128)(2,1)} %bitcast.306, ...), custom_call_target="tpu_custom_call" | custom-call | flops 35000000512 | bytes 10000000 | tf_op jit(solution)/shard_map/pallas_call | solution.py:283
  71.5 0.0 all-gather.23.cloned.1.call-update
  71.5 0.2 reduce-scatter.34.cloned.1.call-start
  71.7 0.0 copy-done.83
  71.8 0.6 pad.8.prior_ref
  72.5 0.0 copy-done.61
  72.5 0.7 copy.174.starts_ref
  73.1 0.0 copy-done.99
  73.1 3.8 concatenate.29.par_ref
  76.9 86.1 %shard_map.281 = (bf16[1024,768]{1,0:T(8,128)(2,1)}, bf16[1024,768]{1,0:T(8,128)(2,1)}, bf16[1024,768]{1,0:T(8,128)(2,1)}, bf16[1024,768]{1,0:T(8,128)(2,1)}, f3...) custom-call(s32[4,2]{1,0:T(4,128)} %copy.174.starts_ref, ...), custom_call_target="tpu_custom_call" | custom-call | flops 40000000000 | bytes 30000000 | tf_op jit(solution)/shard_map/pallas_call | solution.py:1652
  163.1 0.0 all-gather.21.cloned.1.call-done.w_ref
  163.1 34.1 %shard_map.282 = (bf16[2304,768]{1,0:T(8,128)(2,1)}, bf16[2304,768]{1,0:T(8,128)(2,1)}, f32[2304,128]{1,0:T(8,128)}, f32[2304,768]{1,0:T(8,128)}, f32[2304,768]{...) custom-call(f32[16,1,256]{2,1,0:T(1,128)} %get-tuple-element.242.pay_ref, ...), custom_call_target="tpu_custom_call" | custom-call | flops 22000001024 | bytes 25000000 | tf_op jit(solution)/shard_map/pallas_call | solution.py:1146
  197.2 0.0 reduce-scatter.34.cloned.1.call-update
  197.2 0.0 reduce-scatter.36.cloned.1.call-start
  197.3 15.9 %all-gather.23.cloned.1.call-done.w_any = bf16[4,3,768,256]{3,2,1,0:T(8,128)(2,1)} async-done(((bf16[1,3,768,256]{3,2,1,0:T(8,128)(2,1)}), bf16[4,3,768,256]{3,2,1,0:T(8,128)(2,1)}) %all-gather.23.cloned.1.call-update) | async-done | bytes 4718608 | tf_op jit(solution)/shard_map/all_gather | solution.py:1646
  213.2 30.0 %shard_map.283 = (bf16[8,256,768]{2,1,0:T(8,128)(2,1)}, bf16[8,256,768]{2,1,0:T(8,128)(2,1)}, f32[8,1,256]{2,1,0:T(1,128)}, bf16[4,3,768,256]{3,2,1,0:T(8,128)(2,1)}) custom-call(s32[9]{0:T(128)} %get-tuple-element.247.meta_ref, bf16[2304,768]{1,0:T(8,128)(2,1)} %get-tuple-element.248.xc_any, bf16[2304,768]{1,0:T(8,128)(2,1)} %get-tuple-element.249.yc_any, ...), custom_call_target="tpu_custom_call" | custom-call | flops 22000001024 | bytes 25000000 | tf_op jit(solution)/shard_map/pallas_call | solution.py:1164
  243.2 53.3 %shard_map.284 = (bf16[1024,768]{1,0:T(8,128)(2,1)}, f32[1024,768]{1,0:T(8,128)}, f32[16,1024]{1,0:T(8,128)S(1)}, f32[32,768]{1,0:T(8,128)}) custom-call(bf16[8,256,768]{2,1,0:T(8,128)(2,1)} %get-tuple-element.255.dxb_ref, f32[8,1,256]{2,1,0:T(1,128)} %get-tuple-element.256.ggb_ref, bf16[1024,768]{1,0:T(8,128)(2,1)S(1)} %copy-done.7, ...), custom_call_target="tpu_custom_call" | custom-call | flops 4000000000 | bytes 4000000 | tf_op jit(solution)/shard_map/pallas_call | solution.py:1687
  296.6 2.7 reduce-scatter.34.cloned.1.call-done
  299.3 0.0 reduce-scatter.36.cloned.1.call-update
  299.3 62.9 %shard_map.285 = (bf16[4,768,768]{2,1,0:T(8,128)(2,1)}, bf16[3,1024,768]{2,1,0:T(8,128)(2,1)}, bf16[8,256,768]{2,1,0:T(8,128)(2,1)}, f32[32,768]{1,0:T(8,128)}, bf16[3,8,96,256]{3,2,1,0:T(8,128)(2,1)}) custom-call(s32[4,2]{1,0:T(4,128)} %copy.174.starts_ref, bf16[1024,768]{1,0:T(8,128)(2,1)} %get-tuple-element.262.gmo_ref, ...), custom_call_target="tpu_custom_call" | custom-call | flops 8000000000 | bytes 4000000 | tf_op jit(solution)/shard_map/pallas_call | solution.py:1715
  362.2 33.9 %shard_map.286 = (bf16[4,4,96,192]{3,2,1,0:T(8,128)(2,1)}, f32[1024,768]{1,0:T(8,128)}, bf16[1024,768]{1,0:T(8,128)(2,1)}, f32[32,768]{1,0:T(8,128)S(1)}, f32[1,768]{1,0:T(1,128)}) custom-call(bf16[4,768,768]{2,1,0:T(8,128)(2,1)} %get-tuple-element.272.g_ref, bf16[3,1024,768]{2,1,0:T(8,128)(2,1)} %get-tuple-element.273.gp_any, ...), custom_call_target="tpu_custom_call" | custom-call | flops 8000000000 | bytes 4000000 | tf_op jit(solution)/shard_map/pallas_call | solution.py:702
  396.0 0.6 slice_reduce_fusion
  397.3 0.0 reduce-scatter.36.cloned.1.call-done
  397.3 0.0 copy-start.55
  397.4 0.0 copy-start.56
  397.4 0.0 copy-start.62
  397.4 0.0 copy-start.90
  397.4 0.0 copy-start.109
  397.4 23.6 %shard_map.287 = (f32[4,96,192]{2,1,0:T(8,128)}, f32[1,768]{1,0:T(1,128)S(1)}, bf16[3,8,96,256]{3,2,1,0:T(8,128)(2,1)}) custom-call(bf16[4,4,96,192]{3,2,1,0:T(8,128)(2,1)} %get-tuple-element.281.zs_ref, f32[1,768]{1,0:T(1,128)} %get-tuple-element.282.small_ref, bf16[3,8,96,256]{3,2,1,0:T(8,128)(2,1)} %bitcast.327), custom_call_target="tpu_custom_call" | custom-call | flops 17999998976 | bytes 10000000 | tf_op jit(solution)/shard_map/pallas_call | solution.py:679
  421.0 8.7 %conditional.1 = (bf16[1024,768]{1,0:T(8,128)(2,1)}, f32[1024,768]{1,0:T(8,128)}, f32[768]{0:T(1024)}, f32[192,96]{1,0:T(8,128)}, f32[768]{0:T(1024)}, /*index=5...) conditional(s32[]{:T(128)} %convert_element_type.180, ...), branch_computations={%region_3.4_spmd, %region_4.53_spmd} | conditional | flops 61550759936 | bytes 1739891968 | solution.py:1779
  421.1 6.9 %branch_0_fun.1 = (f32[2,8,96,512]{3,2,1,0:T(8,128)}, f32[8,96,512]{2,1,0:T(8,128)}, f32[3,96,192]{2,1,0:T(8,128)}, f32[192,96]{1,0:T(8,128)}, f32[12,768]{1,0:T...) custom-call(bf16[3,8,96,256]{3,2,1,0:T(8,128)(2,1)} %get-tuple-element.1, ...), custom_call_target="tpu_custom_call" | custom-call | flops 1000000000 | bytes 8000000 | tf_op jit(solution)/shard_map/cond/branch_0_fun/pallas_call | solution.py:1219
  428.0 0.6 slice_bitcast_fusion
  429.8 2.8 copy.302
  432.6 1.7 copy.303
  (26 shorter events, 0.1 us)
Async XLA Ops:
  7.2 155.9 %all-gather.21.cloned.1.call-start = ((), (), s32[]{:S(2)}) async-start(), calls=%async_computation.26 | async-start | bytes 5898240 | tf_op jit(solution)/shard_map/all_gather | solution.py:1646
  8.7 23.3 %copy-start.7 = (bf16[1024,768]{1,0:T(8,128)(2,1)S(1)}, bf16[1024,768]{1,0:T(8,128)(2,1)}, u32[]{:S(2)}) copy-start(bf16[1024,768]{1,0:T(8,128)(2,1)} %og_any.1) | copy-start | bytes 4718596
  8.7 23.3 %copy-start.94 = (s32[4096,2]{0,1:T(2,128)S(1)}, s32[4096,2]{0,1:T(2,128)}, u32[]{:S(2)}) copy-start(s32[4096,2]{0,1:T(2,128)} %param.26) | copy-start | bytes 98308
  8.7 23.3 %copy-start.96 = (s32[4096,2]{0,1:T(2,128)S(1)}, s32[4096,2]{0,1:T(2,128)}, u32[]{:S(2)}) copy-start(s32[4096,2]{0,1:T(2,128)} %param.27) | copy-start | bytes 98308
  31.9 181.3 %all-gather.23.cloned.1.call-start = ((), (), s32[]{:S(2)}) async-start(), calls=%async_computation.28 | async-start | bytes 5898240 | tf_op jit(solution)/shard_map/all_gather | solution.py:1646
  32.0 39.7 %copy-start.83 = (bf16[2,2,768]{2,1,0:T(2,128)(2,1)S(1)}, bf16[2,2,768]{2,1,0:T(2,128)(2,1)}, u32[]{:S(2)}) copy-start(bf16[2,2,768]{2,1,0:T(2,128)(2,1)} %param.36) | copy-start | bytes 18436
  32.0 39.7 %copy-start.107 = (bf16[768]{0:T(1024)(128)(2,1)S(1)}, bf16[768]{0:T(1024)(128)(2,1)}, u32[]{:S(2)}) copy-start(bf16[768]{0:T(1024)(128)(2,1)} %param.29) | copy-start | bytes 4612
  32.0 39.7 %copy-start.108 = (bf16[768]{0:T(1024)(128)(2,1)S(1)}, bf16[768]{0:T(1024)(128)(2,1)}, u32[]{:S(2)}) copy-start(bf16[768]{0:T(1024)(128)(2,1)} %param.32) | copy-start | bytes 4612
  32.1 39.7 %copy-start.89 = (bf16[12,12]{1,0:T(8,128)(2,1)S(1)}, bf16[12,12]{1,0:T(8,128)(2,1)}, u32[]{:S(2)}) copy-start(bf16[12,12]{1,0:T(8,128)(2,1)} %param.34) | copy-start | bytes 868
  32.1 39.7 %copy-start.42 = (bf16[1024,12]{0,1:T(8,128)(2,1)S(1)}, bf16[1024,12]{0,1:T(8,128)(2,1)}, u32[]{:S(2)}) copy-start(bf16[1024,12]{0,1:T(8,128)(2,1)} %param.25) | copy-start | bytes 73732
  32.1 40.4 %copy-start.61 = (s32[4,2]{0,1:T(2,128)S(1)}, s32[4,2]{0,1:T(2,128)}, u32[]{:S(2)}) copy-start(s32[4,2]{0,1:T(2,128)} %param.28) | copy-start | bytes 100
  32.1 41.0 %copy-start.48 = (bf16[768,12]{0,1:T(8,128)(2,1)S(1)}, bf16[768,12]{0,1:T(8,128)(2,1)}, u32[]{:S(2)}) copy-start(bf16[768,12]{0,1:T(8,128)(2,1)} %param.33) | copy-start | bytes 55300
  32.1 41.0 %copy-start.99 = (bf16[2,768]{1,0:T(2,128)(2,1)S(1)}, bf16[2,768]{1,0:T(2,128)(2,1)}, u32[]{:S(2)}) copy-start(bf16[2,768]{1,0:T(2,128)(2,1)} %param.35) | copy-start | bytes 9220
  32.1 44.8 %copy-start.15 = (bf16[1024,768]{1,0:T(8,128)(2,1)S(1)}, bf16[1024,768]{1,0:T(8,128)(2,1)}, u32[]{:S(2)}) copy-start(bf16[1024,768]{1,0:T(8,128)(2,1)} %tok_any.1) | copy-start | bytes 4718596
  71.5 227.8 %reduce-scatter.34.cloned.1.call-start = ((), (), s32[]{:S(2)}) async-start(), calls=%async_computation.27 | async-start | bytes 5898240 | tf_op jit(solution)/shard_map/reduce_scatter | solution.py:1680
  197.2 200.1 %reduce-scatter.36.cloned.1.call-start = ((), (), s32[]{:S(2)}) async-start(), calls=%async_computation.29 | async-start | bytes 5898240 | tf_op jit(solution)/shard_map/reduce_scatter | solution.py:1680
  396.0 1.3 copy-start.110
  397.3 23.7 %copy-start.55 = (bf16[192,96]{1,0:T(8,128)(2,1)S(1)}, bf16[192,96]{1,0:T(8,128)(2,1)}, u32[]{:S(2)}) copy-start(bf16[192,96]{1,0:T(8,128)(2,1)} %param.31) | copy-start | bytes 110596
  397.4 23.7 %copy-start.56 = (bf16[3,96,192]{2,1,0:T(8,128)(2,1)S(1)}, bf16[3,96,192]{2,1,0:T(8,128)(2,1)}, u32[]{:S(2)}) copy-start(bf16[3,96,192]{2,1,0:T(8,128)(2,1)} %w_ref.1) | copy-start | bytes 331780
  397.4 23.7 %copy-start.62 = (s32[4,2]{0,1:T(2,128)S(1)}, s32[4,2]{0,1:T(2,128)}, u32[]{:S(2)}) copy-start(s32[4,2]{0,1:T(2,128)} %param.28) | copy-start | bytes 100
  397.4 23.7 %copy-start.90 = (bf16[12,12]{1,0:T(8,128)(2,1)S(1)}, bf16[12,12]{1,0:T(8,128)(2,1)}, u32[]{:S(2)}) copy-start(bf16[12,12]{1,0:T(8,128)(2,1)} %param.34) | copy-start | bytes 868
  397.4 23.6 %copy-start.109 = (bf16[768]{0:T(1024)(128)(2,1)S(1)}, bf16[768]{0:T(1024)(128)(2,1)}, u32[]{:S(2)}) copy-start(bf16[768]{0:T(1024)(128)(2,1)} %param.32) | copy-start | bytes 4612
  429.7 2.8 copy-start.31
Sparse Core Ops, SparseCore 0:
  32.1 91.6 all-gather.20
  125.3 87.8 all-gather.22
  215.5 83.6 reduce-scatter.33
  301.4 88.9 reduce-scatter.35

commit v6 on v5

--- a/solution.py
+++ b/solution.py
@@ -231,10 +231,18 @@
 
 
 def weights_kernel(
-    gather, slab, gu_ref, dn_ref, ids_ref, ranks_ref, og_ref, out_ref, wx_ref, pos_ref, count_ref, ys_ref, sems, own_sem,
-    *scratch,
+    gather, zq_ref, zo_ref, gu_ref, dn_ref, ids_ref, ranks_ref, og_ref, out_ref, wx_ref, pos_ref, count_ref, ys_ref, slab, sems,
+    own_sem, *scratch,
 ):
     k, r, _ = slab.shape
+    tensor, _, _, f = zq_ref.shape
+    for t in range(0, tensor, 2):
+        at = slice(t * f, (t + 2) * f)
+        for c in range(k - 1):
+            slab[c, :, at] = jnp.concatenate([zq_ref[n, c].astype(f32) for n in (t, t + 1)], axis=1).astype(bf16)
+        both = jnp.concatenate([zo_ref[n].astype(f32) for n in (t, t + 1)], axis=0)
+        wide = jnp.concatenate([both, jnp.zeros((2 * f, -r % LANES), f32)], axis=1)
+        slab[k - 1, :, at] = wide.T[0:r, :].astype(bf16)
     greet(all_peers())
     part = lambda h: pl.ds(0, k) if h is None else pl.ds(h * (k // 2), k // 2)
     if gather:
@@ -278,15 +286,17 @@
     swap.end()
 
 
-def gather_weights(w, gate_up, down, ids, ranks, og, gather, cid):
-    k, r, f = w.shape
+def gather_weights(zq, zo, gate_up, down, ids, ranks, og, gather, cid):
+    tensor, k, r, f = zq.shape
+    k, f = k + 1, tensor * f
     return pl.pallas_call(
         functools.partial(weights_kernel, gather),
-        in_specs=[ANY] * 3 + [VM] * 3,
-        out_specs=[ANY] * 2 + [VM] * 3,
+        in_specs=[VM] * 2 + [ANY] * 2 + [VM] * 3,
+        out_specs=[ANY] * 2 + [VM] * 4,
         out_shape=(
-            shape((k, NF * r, f), w.dtype), half_shape(gate_up), shape((NF, 1, og.shape[0]), f32),
+            shape((k, NF * r, f), bf16), half_shape(gate_up), shape((NF, 1, og.shape[0]), f32),
             shape((16, LANES), f32), shape((NF, ROOM, og.shape[1]), bf16),
+            shape((k, r, f), bf16),
         ),
         scratch_shapes=[
             pltpu.SemaphoreType.DMA((2, GATHER_COPIES)),
@@ -295,7 +305,7 @@
         ],
         compiler_params=pltpu.CompilerParams(collective_id=cid, has_side_effects=True, vmem_limit_bytes=60 << 20),
         cost_estimate=cost(35, 10),
-    )(w, gate_up, down, ids, ranks, og)
+    )(zq, zo, gate_up, down, ids, ranks, og)
 
 
 class Reduce8:
@@ -460,45 +470,43 @@
     return [pltpu.SemaphoreType.DMA((2, (NF - 1) * n)), pltpu.SemaphoreType.DMA((n,))]
 
 
-def prologue_kernel(tensor, gu_ref, dn_ref, w_ref, wo_ref, out_ref, slab_ref, zbuf, zsems, *scratch):
+def prologue_kernel(tensor, gu_ref, dn_ref, w_ref, wo_ref, out_ref, zq_ref, zo_ref, zsems, own_sems, *scratch):
     here = lax.axis_index("tensor")
-    k, f = slab_ref.shape[0], w_ref.shape[2]
+    pairs = ((w_ref, zq_ref.at[here]), (wo_ref, zo_ref.at[here]))
+    own = [pltpu.make_async_copy(src, dst, own_sems.at[i]) for i, (src, dst) in enumerate(pairs)]
+    for c in own:
+        c.start()
     greet(all_peers() + far_peers(tensor))
-    copies = []
-    for n, (axis, peer) in enumerate(far_peers(tensor)):
-        copies.append(remote(w_ref, zbuf.at[here, pl.ds(0, k - 1)], zsems, 2 * n, axis, peer))
-        copies.append(remote(wo_ref, zbuf.at[here, k - 1], zsems, 2 * n + 1, axis, peer))
+    copies = [
+        remote(src, dst, zsems, 2 * n + i, axis, peer)
+        for n, (axis, peer) in enumerate(far_peers(tensor))
+        for i, (src, dst) in enumerate(pairs)
+    ]
     for c in copies:
         c.start()
     swap = Exchange8([gu_ref, dn_ref], out_ref, 0, *scratch)
     swap.begin()
-    zbuf[here, 0 : k - 1] = w_ref[...]
-    zbuf[here, k - 1] = wo_ref[...]
     for c in copies:
         c.wait_recv()
-    for c in range(k):
-        for t in range(0, tensor, 2):
-            both = jnp.concatenate([zbuf[t, c].astype(f32), zbuf[t + 1, c].astype(f32)], axis=-1)
-            slab_ref[c, :, t * f : (t + 2) * f] = both.astype(bf16)
     swap.end()
     for c in copies:
         c.wait_send()
+    for c in own:
+        c.wait()
 
 
 def prologue(gate_up, down, w, wo, tensor, cid):
-    k, r, f = w.shape
-    k = k + 1
     return pl.pallas_call(
         functools.partial(prologue_kernel, tensor),
-        in_specs=[ANY, ANY, VM, VM],
-        out_specs=[ANY, VM],
-        out_shape=(half_shape(gate_up), shape((k, r, tensor * f), bf16)),
+        in_specs=[ANY] * 4,
+        out_specs=[ANY] * 3,
+        out_shape=(half_shape(gate_up), shape((tensor, *w.shape), bf16), shape((tensor, *wo.shape), bf16)),
         scratch_shapes=[
-            pltpu.VMEM((tensor, k, r, f), bf16),
             pltpu.SemaphoreType.DMA((2, 2 * (tensor - 1))),
+            pltpu.SemaphoreType.DMA((2,)),
             *exchange_scratch(2),
         ],
-        compiler_params=pltpu.CompilerParams(collective_id=cid, has_side_effects=True),
+        compiler_params=pltpu.CompilerParams(collective_id=cid, has_side_effects=True, vmem_limit_bytes=60 << 20),
         cost_estimate=cost(25, 10),
     )(gate_up, down, w, wo)
 
@@ -1633,9 +1641,9 @@
 
     w_down_t = w_down.transpose(0, 2, 1)[None]
     shard = w_down.shape[1]
-    w_first, slab = prologue(w_gate_up, w_down_t, qkv_weight, out_weight.T, tensor, 1)
-    w_full, w_second, pos, count, ys = gather_weights(
-        slab, w_gate_up, w_down_t, ids, ranks, out_grad, packs == 1, 2
+    w_first, zq, zo = prologue(w_gate_up, w_down_t, qkv_weight, out_weight, tensor, 1)
+    w_full, w_second, pos, count, ys, slab = gather_weights(
+        zq, zo, w_gate_up, w_down_t, ids, ranks, out_grad, packs == 1, 2
     )
     w_attn = lax.all_gather(slab, "dp", axis=1, tiled=True) if packs > 1 else w_full
 

time: 445 us -> 442 us (level)
  transfers between devices with their start and end apart: 4 -> 4, of which waited for: 2 -> 2; matrix products, arithmetic and copies ran while one was open for 1% -> 1% of each run, Pallas kernels for 77% -> 78%
where the time goes in v6:
time: 442 us; the launch traced here: 438 us
  Pallas kernels  393 us (89%)
  waiting for transfers between devices  17.3 us (4%)
  between operations  15.1 us (3%)
  local copies, waits for them, and re-layouts  10.3 us (2%)
    pallas_call x1, Pallas kernels, on_device(): pl.pallas_call(fwd_kernel, in_specs=[SM] + [VM] * 9 + [ANY], out_specs=[V...  86.1 us
    pallas_call x1, Pallas kernels, on_device(): pl.pallas_call(bwd_kernel, in_specs=[SM, VM, VM, ANY, ANY, ANY, VM] + [AN...  62.8 us
    pallas_call x1, Pallas kernels, on_device(): pl.pallas_call(mid_kernel, in_specs=[ANY] * 6 + [VM] * 4, out_specs=[VM]...  53.3 us
    pallas_call x1, Pallas kernels, gather_weights(): pl.pallas_call(functools.partial(weights_kernel, gather), in_specs=[VM] *...  40.8 us
    pallas_call x1, Pallas kernels, experts_first(): pl.pallas_call(first_kernel, in_specs=[VM] * 4, out_specs=[VM] * 6 + [SM]...  34.1 us
    pallas_call x1, Pallas kernels, finish(): pl.pallas_call(functools.partial(final_kernel, tensor, comm), in_specs=[A...  33.9 us
    pallas_call x1, Pallas kernels, experts_second(): pl.pallas_call(second_kernel, in_specs=[SM] + [ANY] * 6, out_specs=[VM] *...  30 us
    pallas_call x1, Pallas kernels, last(): pl.pallas_call(functools.partial(last_kernel, tensor), in_specs=[VM] * 2...  23.6 us
  transfers between devices with their start and end apart: 4, of which 2 were waited for; matrix products, arithmetic and copies ran while one was open for 1% of the time, Pallas kernels for 78%

profile of v6, /device:TPU:0, one launch (start us, length us, event | category | flops | bytes accessed | tf_op | source)
XLA Modules:
  0.0 437.9 jit_solution(10519602191357039531)
XLA Ops:
  7.2 0.0 all-gather.21.cloned.1.call-start
  7.2 0.0 copy-start.94
  7.2 0.0 copy-start.96
  7.3 21.6 %shard_map.279 = (bf16[3,8,96,256]{3,2,1,0:T(8,128)(2,1)}, bf16[4,3,96,192]{3,2,1,0:T(8,128)(2,1)}, bf16[4,192,96]{2,1,0:T(8,128)(2,1)}) custom-call(bf16[2,8,96,512]{3,2,1,0:T(8,128)(2,1)} %gu_ref.3, bf16[1,8,96,512]{3,2,1,0:T(8,128)(2,1)} %bitcast.304, bf16[3,96,192]{2,1,0:T(8,128)(2,1)} %w_ref.1, bf16[192,96]{1,0:T(8,128)(2,1)} %wo_ref.1), custom_call_target="tpu_custom_call" | custom-call | flops 24999999488 | bytes 10000000 | tf_op jit(solution)/shard_map/pallas_call | solution.py:499
  28.8 0.0 all-gather.21.cloned.1.call-update
  28.9 0.0 all-gather.23.cloned.1.call-start
  28.9 0.0 copy-start.82
  29.0 0.0 copy-start.107
  29.0 0.0 copy-start.108
  29.0 0.0 copy-start.89
  29.0 0.0 copy-start.42
  29.0 0.0 copy-start.60
  29.0 0.0 copy-start.48
  29.0 0.0 copy-start.99
  29.0 0.0 copy-start.15
  29.1 40.8 %shard_map.280 = (bf16[4,768,768]{2,1,0:T(8,128)(2,1)}, bf16[3,8,96,256]{3,2,1,0:T(8,128)(2,1)}, f32[8,1,1024]{2,1,0:T(1,128)}, f32[16,128]{1,0:T(8,128)}, bf16[...) custom-call(bf16[4,3,96,192]{3,2,1,0:T(8,128)(2,1)} %get-tuple-element.239.zq_ref, ...), custom_call_target="tpu_custom_call" | custom-call | flops 35000000512 | bytes 10000000 | tf_op jit(solution)/shard_map/pallas_call | solution.py:292
  69.8 0.0 all-gather.23.cloned.1.call-update
  69.9 0.2 reduce-scatter.34.cloned.1.call-start
  70.1 0.0 copy-done.107
  70.2 0.0 copy-done.42
  70.2 0.6 pad.8.prior_ref
  70.8 0.7 copy.170.starts_ref
  71.5 3.8 concatenate.29.par_ref
  75.3 86.1 %shard_map.281 = (bf16[1024,768]{1,0:T(8,128)(2,1)}, bf16[1024,768]{1,0:T(8,128)(2,1)}, bf16[1024,768]{1,0:T(8,128)(2,1)}, bf16[1024,768]{1,0:T(8,128)(2,1)}, f3...) custom-call(s32[4,2]{1,0:T(4,128)} %copy.170.starts_ref, ...), custom_call_target="tpu_custom_call" | custom-call | flops 40000000000 | bytes 30000000 | tf_op jit(solution)/shard_map/pallas_call | solution.py:1660
  161.5 0.0 all-gather.21.cloned.1.call-done.w_ref
  161.5 34.1 %shard_map.282 = (bf16[2304,768]{1,0:T(8,128)(2,1)}, bf16[2304,768]{1,0:T(8,128)(2,1)}, f32[2304,128]{1,0:T(8,128)}, f32[2304,768]{1,0:T(8,128)}, f32[2304,768]{...) custom-call(f32[16,1,256]{2,1,0:T(1,128)} %get-tuple-element.244.pay_ref, ...), custom_call_target="tpu_custom_call" | custom-call | flops 22000001024 | bytes 25000000 | tf_op jit(solution)/shard_map/pallas_call | solution.py:1154
  195.5 0.0 reduce-scatter.34.cloned.1.call-update
  195.6 0.0 reduce-scatter.36.cloned.1.call-start
  195.6 14.5 %all-gather.23.cloned.1.call-done.w_any = bf16[4,3,768,256]{3,2,1,0:T(8,128)(2,1)} async-done(((bf16[1,3,768,256]{3,2,1,0:T(8,128)(2,1)}), bf16[4,3,768,256]{3,2,1,0:T(8,128)(2,1)}) %all-gather.23.cloned.1.call-update) | async-done | bytes 4718608 | tf_op jit(solution)/shard_map/all_gather | solution.py:1654
  210.1 30.0 %shard_map.283 = (bf16[8,256,768]{2,1,0:T(8,128)(2,1)}, bf16[8,256,768]{2,1,0:T(8,128)(2,1)}, f32[8,1,256]{2,1,0:T(1,128)}, bf16[4,3,768,256]{3,2,1,0:T(8,128)(2,1)}) custom-call(s32[9]{0:T(128)} %get-tuple-element.249.meta_ref, bf16[2304,768]{1,0:T(8,128)(2,1)} %get-tuple-element.250.xc_any, bf16[2304,768]{1,0:T(8,128)(2,1)} %get-tuple-element.251.yc_any, ...), custom_call_target="tpu_custom_call" | custom-call | flops 22000001024 | bytes 25000000 | tf_op jit(solution)/shard_map/pallas_call | solution.py:1172
  240.1 53.3 %shard_map.284 = (bf16[1024,768]{1,0:T(8,128)(2,1)}, f32[1024,768]{1,0:T(8,128)}, f32[16,1024]{1,0:T(8,128)S(1)}, f32[32,768]{1,0:T(8,128)}) custom-call(bf16[8,256,768]{2,1,0:T(8,128)(2,1)} %get-tuple-element.257.dxb_ref, f32[8,1,256]{2,1,0:T(1,128)} %get-tuple-element.258.ggb_ref, bf16[1024,768]{1,0:T(8,128)(2,1)S(1)} %copy-done.7, ...), custom_call_target="tpu_custom_call" | custom-call | flops 4000000000 | bytes 4000000 | tf_op jit(solution)/shard_map/pallas_call | solution.py:1695
  293.5 2.7 reduce-scatter.34.cloned.1.call-done
  296.2 0.0 reduce-scatter.36.cloned.1.call-update
  296.2 62.8 %shard_map.285 = (bf16[4,768,768]{2,1,0:T(8,128)(2,1)}, bf16[3,1024,768]{2,1,0:T(8,128)(2,1)}, bf16[8,256,768]{2,1,0:T(8,128)(2,1)}, f32[32,768]{1,0:T(8,128)}, bf16[3,8,96,256]{3,2,1,0:T(8,128)(2,1)}) custom-call(s32[4,2]{1,0:T(4,128)} %copy.170.starts_ref, bf16[1024,768]{1,0:T(8,128)(2,1)} %get-tuple-element.264.gmo_ref, ...), custom_call_target="tpu_custom_call" | custom-call | flops 8000000000 | bytes 4000000 | tf_op jit(solution)/shard_map/pallas_call | solution.py:1723
  359.1 33.9 %shard_map.286 = (bf16[4,4,96,192]{3,2,1,0:T(8,128)(2,1)}, f32[1024,768]{1,0:T(8,128)}, bf16[1024,768]{1,0:T(8,128)(2,1)}, f32[32,768]{1,0:T(8,128)S(1)}, f32[1,768]{1,0:T(1,128)}) custom-call(bf16[4,768,768]{2,1,0:T(8,128)(2,1)} %get-tuple-element.274.g_ref, bf16[3,1024,768]{2,1,0:T(8,128)(2,1)} %get-tuple-element.275.gp_any, ...), custom_call_target="tpu_custom_call" | custom-call | flops 8000000000 | bytes 4000000 | tf_op jit(solution)/shard_map/pallas_call | solution.py:710
  392.9 0.6 slice_reduce_fusion
  394.2 0.0 reduce-scatter.36.cloned.1.call-done
  394.2 0.0 copy-start.55
  394.2 0.0 copy-start.61
  394.3 0.0 copy-start.84
  394.3 0.0 copy-start.90
  394.3 0.0 copy-start.109
  394.3 23.6 %shard_map.287 = (f32[4,96,192]{2,1,0:T(8,128)}, f32[1,768]{1,0:T(1,128)S(1)}, bf16[3,8,96,256]{3,2,1,0:T(8,128)(2,1)}) custom-call(bf16[4,4,96,192]{3,2,1,0:T(8,128)(2,1)} %get-tuple-element.283.zs_ref, f32[1,768]{1,0:T(1,128)} %get-tuple-element.284.small_ref, bf16[3,8,96,256]{3,2,1,0:T(8,128)(2,1)} %bitcast.325), custom_call_target="tpu_custom_call" | custom-call | flops 17999998976 | bytes 10000000 | tf_op jit(solution)/shard_map/pallas_call | solution.py:687
  418.0 8.7 %conditional.1 = (bf16[1024,768]{1,0:T(8,128)(2,1)}, f32[1024,768]{1,0:T(8,128)}, f32[768]{0:T(1024)}, f32[192,96]{1,0:T(8,128)}, f32[768]{0:T(1024)}, /*index=5...) conditional(s32[]{:T(128)} %convert_element_type.180, ...), branch_computations={%region_3.4_spmd, %region_4.53_spmd} | conditional | flops 61550759936 | bytes 1739891968 | solution.py:1787
  418.0 6.9 %branch_0_fun.1 = (f32[2,8,96,512]{3,2,1,0:T(8,128)}, f32[8,96,512]{2,1,0:T(8,128)}, f32[3,96,192]{2,1,0:T(8,128)}, f32[192,96]{1,0:T(8,128)}, f32[12,768]{1,0:T...) custom-call(bf16[3,8,96,256]{3,2,1,0:T(8,128)(2,1)} %get-tuple-element.1, ...), custom_call_target="tpu_custom_call" | custom-call | flops 1000000000 | bytes 8000000 | tf_op jit(solution)/shard_map/cond/branch_0_fun/pallas_call | solution.py:1227
  424.9 0.6 slice_bitcast_fusion
  426.7 2.8 copy.298
  429.5 1.7 copy.299
  (25 shorter events, 0.1 us)
Async XLA Ops:
  7.2 154.3 %all-gather.21.cloned.1.call-start = ((), (), s32[]{:S(2)}) async-start(), calls=%async_computation.26 | async-start | bytes 5898240 | tf_op jit(solution)/shard_map/all_gather | solution.py:1654
  7.2 21.7 %copy-start.7 = (bf16[1024,768]{1,0:T(8,128)(2,1)S(1)}, bf16[1024,768]{1,0:T(8,128)(2,1)}, u32[]{:S(2)}) copy-start(bf16[1024,768]{1,0:T(8,128)(2,1)} %og_any.1) | copy-start | bytes 4718596
  7.2 21.7 %copy-start.94 = (s32[4096,2]{0,1:T(2,128)S(1)}, s32[4096,2]{0,1:T(2,128)}, u32[]{:S(2)}) copy-start(s32[4096,2]{0,1:T(2,128)} %param.26) | copy-start | bytes 98308
  7.2 21.7 %copy-start.96 = (s32[4096,2]{0,1:T(2,128)S(1)}, s32[4096,2]{0,1:T(2,128)}, u32[]{:S(2)}) copy-start(s32[4096,2]{0,1:T(2,128)} %param.27) | copy-start | bytes 98308
  28.9 181.3 %all-gather.23.cloned.1.call-start = ((), (), s32[]{:S(2)}) async-start(), calls=%async_computation.28 | async-start | bytes 5898240 | tf_op jit(solution)/shard_map/all_gather | solution.py:1654
  28.9 41.1 %copy-start.82 = (bf16[2,2,768]{2,1,0:T(2,128)(2,1)S(1)}, bf16[2,2,768]{2,1,0:T(2,128)(2,1)}, u32[]{:S(2)}) copy-start(bf16[2,2,768]{2,1,0:T(2,128)(2,1)} %param.36) | copy-start | bytes 18436
  29.0 41.2 %copy-start.107 = (bf16[768]{0:T(1024)(128)(2,1)S(1)}, bf16[768]{0:T(1024)(128)(2,1)}, u32[]{:S(2)}) copy-start(bf16[768]{0:T(1024)(128)(2,1)} %param.29) | copy-start | bytes 4612
  29.0 41.2 %copy-start.108 = (bf16[768]{0:T(1024)(128)(2,1)S(1)}, bf16[768]{0:T(1024)(128)(2,1)}, u32[]{:S(2)}) copy-start(bf16[768]{0:T(1024)(128)(2,1)} %param.32) | copy-start | bytes 4612
  29.0 41.2 %copy-start.89 = (bf16[12,12]{1,0:T(8,128)(2,1)S(1)}, bf16[12,12]{1,0:T(8,128)(2,1)}, u32[]{:S(2)}) copy-start(bf16[12,12]{1,0:T(8,128)(2,1)} %param.34) | copy-start | bytes 868
  29.0 41.2 %copy-start.42 = (bf16[1024,12]{0,1:T(8,128)(2,1)S(1)}, bf16[1024,12]{0,1:T(8,128)(2,1)}, u32[]{:S(2)}) copy-start(bf16[1024,12]{0,1:T(8,128)(2,1)} %param.25) | copy-start | bytes 73732
  29.0 41.8 %copy-start.60 = (s32[4,2]{0,1:T(2,128)S(1)}, s32[4,2]{0,1:T(2,128)}, u32[]{:S(2)}) copy-start(s32[4,2]{0,1:T(2,128)} %param.28) | copy-start | bytes 100
  29.0 42.5 %copy-start.48 = (bf16[768,12]{0,1:T(8,128)(2,1)S(1)}, bf16[768,12]{0,1:T(8,128)(2,1)}, u32[]{:S(2)}) copy-start(bf16[768,12]{0,1:T(8,128)(2,1)} %param.33) | copy-start | bytes 55300
  29.0 42.5 %copy-start.99 = (bf16[2,768]{1,0:T(2,128)(2,1)S(1)}, bf16[2,768]{1,0:T(2,128)(2,1)}, u32[]{:S(2)}) copy-start(bf16[2,768]{1,0:T(2,128)(2,1)} %param.35) | copy-start | bytes 9220
  29.0 46.3 %copy-start.15 = (bf16[1024,768]{1,0:T(8,128)(2,1)S(1)}, bf16[1024,768]{1,0:T(8,128)(2,1)}, u32[]{:S(2)}) copy-start(bf16[1024,768]{1,0:T(8,128)(2,1)} %tok_any.1) | copy-start | bytes 4718596
  69.9 226.3 %reduce-scatter.34.cloned.1.call-start = ((), (), s32[]{:S(2)}) async-start(), calls=%async_computation.27 | async-start | bytes 5898240 | tf_op jit(solution)/shard_map/reduce_scatter | solution.py:1688
  195.6 198.6 %reduce-scatter.36.cloned.1.call-start = ((), (), s32[]{:S(2)}) async-start(), calls=%async_computation.29 | async-start | bytes 5898240 | tf_op jit(solution)/shard_map/reduce_scatter | solution.py:1688
  392.9 1.3 copy-start.110
  394.2 23.7 %copy-start.55 = (bf16[3,96,192]{2,1,0:T(8,128)(2,1)S(1)}, bf16[3,96,192]{2,1,0:T(8,128)(2,1)}, u32[]{:S(2)}) copy-start(bf16[3,96,192]{2,1,0:T(8,128)(2,1)} %w_ref.1) | copy-start | bytes 331780
  394.2 23.7 %copy-start.61 = (s32[4,2]{0,1:T(2,128)S(1)}, s32[4,2]{0,1:T(2,128)}, u32[]{:S(2)}) copy-start(s32[4,2]{0,1:T(2,128)} %param.28) | copy-start | bytes 100
  394.3 23.7 %copy-start.84 = (bf16[192,96]{1,0:T(8,128)(2,1)S(1)}, bf16[192,96]{1,0:T(8,128)(2,1)}, u32[]{:S(2)}) copy-start(bf16[192,96]{1,0:T(8,128)(2,1)} %wo_ref.1) | copy-start | bytes 110596
  394.3 23.7 %copy-start.90 = (bf16[12,12]{1,0:T(8,128)(2,1)S(1)}, bf16[12,12]{1,0:T(8,128)(2,1)}, u32[]{:S(2)}) copy-start(bf16[12,12]{1,0:T(8,128)(2,1)} %param.34) | copy-start | bytes 868
  394.3 23.7 %copy-start.109 = (bf16[768]{0:T(1024)(128)(2,1)S(1)}, bf16[768]{0:T(1024)(128)(2,1)}, u32[]{:S(2)}) copy-start(bf16[768]{0:T(1024)(128)(2,1)} %param.32) | copy-start | bytes 4612
  426.7 2.8 copy-start.31
Sparse Core Ops, SparseCore 0:
  29.0 91.6 all-gather.20
  122.2 87.8 all-gather.22
  212.4 83.7 reduce-scatter.33
  298.4 88.9 reduce-scatter.35

commit v7 on v6

--- a/solution.py
+++ b/solution.py
@@ -533,25 +533,31 @@
 class Near:
     def __init__(self, have, got, sems):
         me = lax.axis_index("dp")
+        self.slot = me % NF
         self.have, self.got = have, got
-        self.c = [remote(have.at[n], got.at[n], sems, n, "dp", flip(me, m)) for n, m in enumerate((1, 2, 4))]
-
-    def begin(self):
-        self.c[0].start()
-
-    def step(self, n):
-        self.c[n].wait_recv()
-        self.have[n + 1] = self.have[n] + self.got[n]
-        if n < 2:
-            self.c[n + 1].start()
-
-    def close(self):
+        self.c = [
+            remote(have, got.at[self.slot], sems, m - 1, "dp", flip(me, m)) for m in (6, 7, 2, 3, 4, 5, 1)
+        ]
+
+    def begin(self, value):
+        self.have[...] = value.astype(bf16)
+        for c in self.c:
+            c.start()
+        self.got[self.slot] = self.have[...]
+
+    def end(self):
+        for c in self.c:
+            c.wait_recv()
+        total = self.got[0].astype(f32)
+        for n in range(1, NF):
+            total = total + self.got[n].astype(f32)
         for c in self.c:
             c.wait_send()
+        return total
 
 
 def near_scratch(dims):
-    return [pltpu.VMEM((4, *dims), f32), pltpu.VMEM((3, *dims), f32), pltpu.SemaphoreType.DMA((2, 3))]
+    return [pltpu.VMEM(dims, bf16), pltpu.VMEM((NF, *dims), bf16), pltpu.SemaphoreType.DMA((2, NF - 1))]
 
 
 class Far:
@@ -599,7 +605,7 @@
         red = Reduce8(lambda s: g_ref.at[:, pl.ds(pl.multiple_of(s * r, r), r), :], scratch[:5], *scratch[5:7])
         sums, smalls = Near(*scratch[7:10]), Far(tensor, small_ref, *scratch[10:13])
         red.load()
-        greet(near_peers() + far_peers(tensor))
+        greet(all_peers() + far_peers(tensor))
         red.begin()
         smalls.begin()
     for c in loads:
@@ -624,8 +630,7 @@
         if comm and i == 0:
             red.third()
     if comm:
-        sums.have[0] = nag
-        sums.begin()
+        sums.begin(nag)
     else:
         nag_ref[...] = nag
         total_ref[...] = small_ref[...]
@@ -645,17 +650,12 @@
 
     for i in range(ntile):
         layer(i)
-        if comm and i < 3:
-            sums.step(i)
     if not comm:
         return
-    for i in range(ntile, 3):
-        sums.step(i)
-    nag_ref[...] = sums.have[3]
+    nag_ref[...] = sums.end()
     red.end(write)
     total_ref[...] = smalls.end()
     red.close()
-    sums.close()
 
 
 def last_kernel(tensor, zs_ref, small_ref, dw_ref, out_ref, total_ref, dwx_ref, zr, zsems, *scratch):
@@ -963,9 +963,8 @@
     load.start()
     send = Send8(outb_ref, outr_ref, *scratch[0:2], False)
     sums = Near(*scratch[2:5])
-    sums.have[0] = small_ref[...]
     greet(all_peers())
-    sums.begin()
+    sums.begin(small_ref[...])
     send.begin()
     swap = Exchange8([dw_ref], dwx_ref, None, *scratch[5:7])
     swap.begin()
@@ -993,7 +992,6 @@
         return carry
 
     lax.fori_loop(0, ntile, start, 0)
-    sums.step(0)
     wg_ref[3] = tn(gmo_ref[...], mixed_ref[...]).astype(wg_ref.dtype)
     for i in range(ntile):
         width = min(SEQ, (i + 2) * QT) - i * QT
@@ -1033,16 +1031,13 @@
     for c in loads:
         c.wait()
     lax.fori_loop(0, pairs, pair, 0)
-    sums.step(1)
     for c in range(3):
         wg_ref[c] = tn(nattn_ref[...], gp_ref[c]).astype(wg_ref.dtype)
     for m in range(NF):
         send.got(m)
     send.close()
     swap.end()
-    sums.step(2)
-    total_ref[...] = sums.have[3]
-    sums.close()
+    total_ref[...] = sums.end()
 
 
 def ffn_tile(x, gate, y, w_ref, acc, eo, dx):

time: 442 us -> 437 us (0.989)
    pallas_call x1, Pallas kernels: 53.3 us -> 48.4 us  [on_device(): pl.pallas_call(mid_kernel, in_specs=[ANY] * 6 + [VM] * 4, out_specs=[VM]...]
  transfers between devices with their start and end apart: 4 -> 4, of which waited for: 2 -> 2; matrix products, arithmetic and copies ran while one was open for 1% -> 1% of each run, Pallas kernels for 78% -> 79%
where the time goes in v7:
time: 437 us; the launch traced here: 433 us
  Pallas kernels  392 us (90%)
  between operations  15.1 us (3%)
  waiting for transfers between devices  13.6 us (3%)
  local copies, waits for them, and re-layouts  10.3 us (2%)
    pallas_call x1, Pallas kernels, on_device(): pl.pallas_call(fwd_kernel, in_specs=[SM] + [VM] * 9 + [ANY], out_specs=[V...  86.1 us
    pallas_call x1, Pallas kernels, on_device(): pl.pallas_call(bwd_kernel, in_specs=[SM, VM, VM, ANY, ANY, ANY, VM] + [AN...  60.8 us
    pallas_call x1, Pallas kernels, on_device(): pl.pallas_call(mid_kernel, in_specs=[ANY] * 6 + [VM] * 4, out_specs=[VM]...  48.4 us
    pallas_call x1, Pallas kernels, gather_weights(): pl.pallas_call(functools.partial(weights_kernel, gather), in_specs=[VM] *...  40.8 us
    pallas_call x1, Pallas kernels, experts_first(): pl.pallas_call(first_kernel, in_specs=[VM] * 4, out_specs=[VM] * 6 + [SM]...  38.4 us
    pallas_call x1, Pallas kernels, experts_second(): pl.pallas_call(second_kernel, in_specs=[SM] + [ANY] * 6, out_specs=[VM] *...  34.3 us
    pallas_call x1, Pallas kernels, finish(): pl.pallas_call(functools.partial(final_kernel, tensor, comm), in_specs=[A...  31.3 us
    pallas_call x1, Pallas kernels, last(): pl.pallas_call(functools.partial(last_kernel, tensor), in_specs=[VM] * 2...  23.4 us
  transfers between devices with their start and end apart: 4, of which 2 were waited for; matrix products, arithmetic and copies ran while one was open for 1% of the time, Pallas kernels for 79%

profile of v7, /device:TPU:0, one launch (start us, length us, event | category | flops | bytes accessed | tf_op | source)
XLA Modules:
  0.0 433.2 jit_solution(1365020728118809875)
XLA Ops:
  7.2 0.0 all-gather.21.cloned.1.call-start
  7.2 0.0 copy-start.94
  7.2 0.0 copy-start.96
  7.3 21.6 %shard_map.279 = (bf16[3,8,96,256]{3,2,1,0:T(8,128)(2,1)}, bf16[4,3,96,192]{3,2,1,0:T(8,128)(2,1)}, bf16[4,192,96]{2,1,0:T(8,128)(2,1)}) custom-call(bf16[2,8,96,512]{3,2,1,0:T(8,128)(2,1)} %gu_ref.3, bf16[1,8,96,512]{3,2,1,0:T(8,128)(2,1)} %bitcast.304, bf16[3,96,192]{2,1,0:T(8,128)(2,1)} %w_ref.1, bf16[192,96]{1,0:T(8,128)(2,1)} %wo_ref.1), custom_call_target="tpu_custom_call" | custom-call | flops 24999999488 | bytes 10000000 | tf_op jit(solution)/shard_map/pallas_call | solution.py:499
  28.8 0.0 all-gather.21.cloned.1.call-update
  28.9 0.0 all-gather.23.cloned.1.call-start
  28.9 0.0 copy-start.82
  29.0 0.0 copy-start.107
  29.0 0.0 copy-start.108
  29.0 0.0 copy-start.89
  29.0 0.0 copy-start.42
  29.0 0.0 copy-start.60
  29.0 0.0 copy-start.48
  29.0 0.0 copy-start.99
  29.0 0.0 copy-start.15
  29.1 40.8 %shard_map.280 = (bf16[4,768,768]{2,1,0:T(8,128)(2,1)}, bf16[3,8,96,256]{3,2,1,0:T(8,128)(2,1)}, f32[8,1,1024]{2,1,0:T(1,128)}, f32[16,128]{1,0:T(8,128)}, bf16[...) custom-call(bf16[4,3,96,192]{3,2,1,0:T(8,128)(2,1)} %get-tuple-element.239.zq_ref, ...), custom_call_target="tpu_custom_call" | custom-call | flops 35000000512 | bytes 10000000 | tf_op jit(solution)/shard_map/pallas_call | solution.py:292
  69.8 0.0 all-gather.23.cloned.1.call-update
  69.9 0.2 reduce-scatter.34.cloned.1.call-start
  70.1 0.0 copy-done.107
  70.1 0.0 copy-done.108
  70.2 0.6 pad.8.prior_ref
  70.8 0.7 copy.170.starts_ref
  71.5 3.8 concatenate.29.par_ref
  75.3 86.1 %shard_map.281 = (bf16[1024,768]{1,0:T(8,128)(2,1)}, bf16[1024,768]{1,0:T(8,128)(2,1)}, bf16[1024,768]{1,0:T(8,128)(2,1)}, bf16[1024,768]{1,0:T(8,128)(2,1)}, f3...) custom-call(s32[4,2]{1,0:T(4,128)} %copy.170.starts_ref, ...), custom_call_target="tpu_custom_call" | custom-call | flops 40000000000 | bytes 30000000 | tf_op jit(solution)/shard_map/pallas_call | solution.py:1655
  161.5 0.0 all-gather.21.cloned.1.call-done.w_ref
  161.5 38.4 %shard_map.282 = (bf16[2304,768]{1,0:T(8,128)(2,1)}, bf16[2304,768]{1,0:T(8,128)(2,1)}, f32[2304,128]{1,0:T(8,128)}, f32[2304,768]{1,0:T(8,128)}, f32[2304,768]{...) custom-call(f32[16,1,256]{2,1,0:T(1,128)} %get-tuple-element.244.pay_ref, ...), custom_call_target="tpu_custom_call" | custom-call | flops 22000001024 | bytes 25000000 | tf_op jit(solution)/shard_map/pallas_call | solution.py:1149
  199.9 0.0 reduce-scatter.34.cloned.1.call-update
  199.9 0.0 reduce-scatter.36.cloned.1.call-start
  200.0 10.1 %all-gather.23.cloned.1.call-done.w_any = bf16[4,3,768,256]{3,2,1,0:T(8,128)(2,1)} async-done(((bf16[1,3,768,256]{3,2,1,0:T(8,128)(2,1)}), bf16[4,3,768,256]{3,2,1,0:T(8,128)(2,1)}) %all-gather.23.cloned.1.call-update) | async-done | bytes 4718608 | tf_op jit(solution)/shard_map/all_gather | solution.py:1649
  210.1 34.3 %shard_map.283 = (bf16[8,256,768]{2,1,0:T(8,128)(2,1)}, bf16[8,256,768]{2,1,0:T(8,128)(2,1)}, f32[8,1,256]{2,1,0:T(1,128)}, bf16[4,3,768,256]{3,2,1,0:T(8,128)(2,1)}) custom-call(s32[9]{0:T(128)} %get-tuple-element.249.meta_ref, bf16[2304,768]{1,0:T(8,128)(2,1)} %get-tuple-element.250.xc_any, bf16[2304,768]{1,0:T(8,128)(2,1)} %get-tuple-element.251.yc_any, ...), custom_call_target="tpu_custom_call" | custom-call | flops 22000001024 | bytes 25000000 | tf_op jit(solution)/shard_map/pallas_call | solution.py:1167
  244.4 48.4 %shard_map.284 = (bf16[1024,768]{1,0:T(8,128)(2,1)}, f32[1024,768]{1,0:T(8,128)}, f32[16,1024]{1,0:T(8,128)S(1)}, f32[32,768]{1,0:T(8,128)}) custom-call(bf16[8,256,768]{2,1,0:T(8,128)(2,1)} %get-tuple-element.257.dxb_ref, f32[8,1,256]{2,1,0:T(1,128)} %get-tuple-element.258.ggb_ref, bf16[1024,768]{1,0:T(8,128)(2,1)S(1)} %copy-done.7, ...), custom_call_target="tpu_custom_call" | custom-call | flops 4000000000 | bytes 4000000 | tf_op jit(solution)/shard_map/pallas_call | solution.py:1690
  292.9 3.3 reduce-scatter.34.cloned.1.call-done
  296.2 0.0 reduce-scatter.36.cloned.1.call-update
  296.2 60.8 %shard_map.285 = (bf16[4,768,768]{2,1,0:T(8,128)(2,1)}, bf16[3,1024,768]{2,1,0:T(8,128)(2,1)}, bf16[8,256,768]{2,1,0:T(8,128)(2,1)}, f32[32,768]{1,0:T(8,128)}, bf16[3,8,96,256]{3,2,1,0:T(8,128)(2,1)}) custom-call(s32[4,2]{1,0:T(4,128)} %copy.170.starts_ref, bf16[1024,768]{1,0:T(8,128)(2,1)} %get-tuple-element.264.gmo_ref, ...), custom_call_target="tpu_custom_call" | custom-call | flops 8000000000 | bytes 4000000 | tf_op jit(solution)/shard_map/pallas_call | solution.py:1718
  357.1 31.3 %shard_map.286 = (bf16[4,4,96,192]{3,2,1,0:T(8,128)(2,1)}, f32[1024,768]{1,0:T(8,128)}, bf16[1024,768]{1,0:T(8,128)(2,1)}, f32[32,768]{1,0:T(8,128)S(1)}, f32[1,768]{1,0:T(1,128)}) custom-call(bf16[4,768,768]{2,1,0:T(8,128)(2,1)} %get-tuple-element.274.g_ref, bf16[3,1024,768]{2,1,0:T(8,128)(2,1)} %get-tuple-element.275.gp_any, ...), custom_call_target="tpu_custom_call" | custom-call | flops 8000000000 | bytes 4000000 | tf_op jit(solution)/shard_map/pallas_call | solution.py:710
  388.4 0.6 slice_reduce_fusion
  389.6 0.0 reduce-scatter.36.cloned.1.call-done
  389.7 0.0 copy-start.55
  389.7 0.0 copy-start.61
  389.7 0.0 copy-start.84
  389.7 0.0 copy-start.90
  389.7 0.0 copy-start.109
  389.7 23.4 %shard_map.287 = (f32[4,96,192]{2,1,0:T(8,128)}, f32[1,768]{1,0:T(1,128)S(1)}, bf16[3,8,96,256]{3,2,1,0:T(8,128)(2,1)}) custom-call(bf16[4,4,96,192]{3,2,1,0:T(8,128)(2,1)} %get-tuple-element.283.zs_ref, f32[1,768]{1,0:T(1,128)} %get-tuple-element.284.small_ref, bf16[3,8,96,256]{3,2,1,0:T(8,128)(2,1)} %bitcast.325), custom_call_target="tpu_custom_call" | custom-call | flops 17999998976 | bytes 10000000 | tf_op jit(solution)/shard_map/pallas_call | solution.py:687
  413.2 8.7 %conditional.1 = (bf16[1024,768]{1,0:T(8,128)(2,1)}, f32[1024,768]{1,0:T(8,128)}, f32[768]{0:T(1024)}, f32[192,96]{1,0:T(8,128)}, f32[768]{0:T(1024)}, /*index=5...) conditional(s32[]{:T(128)} %convert_element_type.180, ...), branch_computations={%region_3.4_spmd, %region_4.53_spmd} | conditional | flops 61550759936 | bytes 1739891968 | solution.py:1782
  413.2 6.9 %branch_0_fun.1 = (f32[2,8,96,512]{3,2,1,0:T(8,128)}, f32[8,96,512]{2,1,0:T(8,128)}, f32[3,96,192]{2,1,0:T(8,128)}, f32[192,96]{1,0:T(8,128)}, f32[12,768]{1,0:T...) custom-call(bf16[3,8,96,256]{3,2,1,0:T(8,128)(2,1)} %get-tuple-element.1, ...), custom_call_target="tpu_custom_call" | custom-call | flops 1000000000 | bytes 8000000 | tf_op jit(solution)/shard_map/cond/branch_0_fun/pallas_call | solution.py:1222
  420.1 0.6 slice_bitcast_fusion
  421.9 2.8 copy.298
  424.7 1.7 copy.299
  (25 shorter events, 0.1 us)
Async XLA Ops:
  7.2 154.3 %all-gather.21.cloned.1.call-start = ((), (), s32[]{:S(2)}) async-start(), calls=%async_computation.26 | async-start | bytes 5898240 | tf_op jit(solution)/shard_map/all_gather | solution.py:1649
  7.2 21.7 %copy-start.7 = (bf16[1024,768]{1,0:T(8,128)(2,1)S(1)}, bf16[1024,768]{1,0:T(8,128)(2,1)}, u32[]{:S(2)}) copy-start(bf16[1024,768]{1,0:T(8,128)(2,1)} %og_any.1) | copy-start | bytes 4718596
  7.2 21.7 %copy-start.94 = (s32[4096,2]{0,1:T(2,128)S(1)}, s32[4096,2]{0,1:T(2,128)}, u32[]{:S(2)}) copy-start(s32[4096,2]{0,1:T(2,128)} %param.26) | copy-start | bytes 98308
  7.2 21.7 %copy-start.96 = (s32[4096,2]{0,1:T(2,128)S(1)}, s32[4096,2]{0,1:T(2,128)}, u32[]{:S(2)}) copy-start(s32[4096,2]{0,1:T(2,128)} %param.27) | copy-start | bytes 98308
  28.9 181.3 %all-gather.23.cloned.1.call-start = ((), (), s32[]{:S(2)}) async-start(), calls=%async_computation.28 | async-start | bytes 5898240 | tf_op jit(solution)/shard_map/all_gather | solution.py:1649
  28.9 41.1 %copy-start.82 = (bf16[2,2,768]{2,1,0:T(2,128)(2,1)S(1)}, bf16[2,2,768]{2,1,0:T(2,128)(2,1)}, u32[]{:S(2)}) copy-start(bf16[2,2,768]{2,1,0:T(2,128)(2,1)} %param.36) | copy-start | bytes 18436
  29.0 41.2 %copy-start.107 = (bf16[768]{0:T(1024)(128)(2,1)S(1)}, bf16[768]{0:T(1024)(128)(2,1)}, u32[]{:S(2)}) copy-start(bf16[768]{0:T(1024)(128)(2,1)} %param.29) | copy-start | bytes 4612
  29.0 41.2 %copy-start.108 = (bf16[768]{0:T(1024)(128)(2,1)S(1)}, bf16[768]{0:T(1024)(128)(2,1)}, u32[]{:S(2)}) copy-start(bf16[768]{0:T(1024)(128)(2,1)} %param.32) | copy-start | bytes 4612
  29.0 41.2 %copy-start.89 = (bf16[12,12]{1,0:T(8,128)(2,1)S(1)}, bf16[12,12]{1,0:T(8,128)(2,1)}, u32[]{:S(2)}) copy-start(bf16[12,12]{1,0:T(8,128)(2,1)} %param.34) | copy-start | bytes 868
  29.0 41.2 %copy-start.42 = (bf16[1024,12]{0,1:T(8,128)(2,1)S(1)}, bf16[1024,12]{0,1:T(8,128)(2,1)}, u32[]{:S(2)}) copy-start(bf16[1024,12]{0,1:T(8,128)(2,1)} %param.25) | copy-start | bytes 73732
  29.0 41.8 %copy-start.60 = (s32[4,2]{0,1:T(2,128)S(1)}, s32[4,2]{0,1:T(2,128)}, u32[]{:S(2)}) copy-start(s32[4,2]{0,1:T(2,128)} %param.28) | copy-start | bytes 100
  29.0 42.5 %copy-start.48 = (bf16[768,12]{0,1:T(8,128)(2,1)S(1)}, bf16[768,12]{0,1:T(8,128)(2,1)}, u32[]{:S(2)}) copy-start(bf16[768,12]{0,1:T(8,128)(2,1)} %param.33) | copy-start | bytes 55300
  29.0 42.5 %copy-start.99 = (bf16[2,768]{1,0:T(2,128)(2,1)S(1)}, bf16[2,768]{1,0:T(2,128)(2,1)}, u32[]{:S(2)}) copy-start(bf16[2,768]{1,0:T(2,128)(2,1)} %param.35) | copy-start | bytes 9220
  29.0 46.3 %copy-start.15 = (bf16[1024,768]{1,0:T(8,128)(2,1)S(1)}, bf16[1024,768]{1,0:T(8,128)(2,1)}, u32[]{:S(2)}) copy-start(bf16[1024,768]{1,0:T(8,128)(2,1)} %tok_any.1) | copy-start | bytes 4718596
  69.9 226.3 %reduce-scatter.34.cloned.1.call-start = ((), (), s32[]{:S(2)}) async-start(), calls=%async_computation.27 | async-start | bytes 5898240 | tf_op jit(solution)/shard_map/reduce_scatter | solution.py:1683
  199.9 189.7 %reduce-scatter.36.cloned.1.call-start = ((), (), s32[]{:S(2)}) async-start(), calls=%async_computation.29 | async-start | bytes 5898240 | tf_op jit(solution)/shard_map/reduce_scatter | solution.py:1683
  388.4 1.3 copy-start.110
  389.7 23.5 %copy-start.55 = (bf16[3,96,192]{2,1,0:T(8,128)(2,1)S(1)}, bf16[3,96,192]{2,1,0:T(8,128)(2,1)}, u32[]{:S(2)}) copy-start(bf16[3,96,192]{2,1,0:T(8,128)(2,1)} %w_ref.1) | copy-start | bytes 331780
  389.7 23.5 %copy-start.61 = (s32[4,2]{0,1:T(2,128)S(1)}, s32[4,2]{0,1:T(2,128)}, u32[]{:S(2)}) copy-start(s32[4,2]{0,1:T(2,128)} %param.28) | copy-start | bytes 100
  389.7 23.5 %copy-start.84 = (bf16[192,96]{1,0:T(8,128)(2,1)S(1)}, bf16[192,96]{1,0:T(8,128)(2,1)}, u32[]{:S(2)}) copy-start(bf16[192,96]{1,0:T(8,128)(2,1)} %wo_ref.1) | copy-start | bytes 110596
  389.7 23.5 %copy-start.90 = (bf16[12,12]{1,0:T(8,128)(2,1)S(1)}, bf16[12,12]{1,0:T(8,128)(2,1)}, u32[]{:S(2)}) copy-start(bf16[12,12]{1,0:T(8,128)(2,1)} %param.34) | copy-start | bytes 868
  389.7 23.5 %copy-start.109 = (bf16[768]{0:T(1024)(128)(2,1)S(1)}, bf16[768]{0:T(1024)(128)(2,1)}, u32[]{:S(2)}) copy-start(bf16[768]{0:T(1024)(128)(2,1)} %param.32) | copy-start | bytes 4612
  421.9 2.8 copy-start.31
Sparse Core Ops, SparseCore 0:
  29.0 91.6 all-gather.20
  122.2 87.8 all-gather.22
  212.4 83.7 reduce-scatter.33
  298.4 89.0 reduce-scatter.35

commit v8 on v7

--- a/solution.py
+++ b/solution.py
@@ -1192,8 +1192,8 @@
     half = a_ref.shape[3]
     for n, ref in ((0, a_ref), (1, b_ref)):
         at = slice(n * half, (n + 1) * half)
-        gu_ref[:, 0, :, at] = ref[0:2, 0].astype(f32)
-        dn_ref[0, :, at] = ref[2, 0].astype(f32)
+        gu_ref[:, :, :, at] = ref[0:2].astype(f32)
+        dn_ref[:, :, at] = ref[2].astype(f32)
 
     @pl.when(pl.program_id(0) == 0)
     def _():
@@ -1216,15 +1216,17 @@
 def emit(dw_a, dw_b, wg, small, nag, ne):
     _, groups, r, half = dw_a.shape
     d = small.shape[1]
-    piece = pl.BlockSpec((3, 1, r, half), lambda e: (0, e, 0, 0))
+    some = 2
+    piece = pl.BlockSpec((3, some, r, half), lambda e: (0, e, 0, 0))
     whole = lambda *dims: pl.BlockSpec(dims, lambda e: (0,) * len(dims))
     rest = [(3, *wg.shape[1:]), wg.shape[:0:-1], (ne, d), (ne, ne), (NC, d), (NC, 2, d), (d,), (d,)]
     return pl.pallas_call(
         emit_kernel,
-        grid=(groups,),
+        grid=(groups // some,),
         in_specs=[piece, piece, whole(*wg.shape), whole(*small.shape), whole(1, d)],
         out_specs=[
-            pl.BlockSpec((2, 1, r, 2 * half), lambda e: (0, e, 0, 0)), pl.BlockSpec((1, r, 2 * half), lambda e: (e, 0, 0)),
+            pl.BlockSpec((2, some, r, 2 * half), lambda e: (0, e, 0, 0)),
+            pl.BlockSpec((some, r, 2 * half), lambda e: (e, 0, 0)),
             *(whole(*dims) for dims in rest),
         ],
         out_shape=(

time: 437 us -> 435 us (level)
  no operation moved by 1% of the time
where the time goes in v8:
time: 435 us; the launch traced here: 431 us
  Pallas kernels  390 us (90%)
  between operations  15.1 us (3%)
  waiting for transfers between devices  13.9 us (3%)
  local copies, waits for them, and re-layouts  10.3 us (2%)
    pallas_call x1, Pallas kernels, on_device(): pl.pallas_call(fwd_kernel, in_specs=[SM] + [VM] * 9 + [ANY], out_specs=[V...  86.1 us
    pallas_call x1, Pallas kernels, on_device(): pl.pallas_call(bwd_kernel, in_specs=[SM, VM, VM, ANY, ANY, ANY, VM] + [AN...  60.8 us
    pallas_call x1, Pallas kernels, on_device(): pl.pallas_call(mid_kernel, in_specs=[ANY] * 6 + [VM] * 4, out_specs=[VM]...  48.1 us
    pallas_call x1, Pallas kernels, gather_weights(): pl.pallas_call(functools.partial(weights_kernel, gather), in_specs=[VM] *...  40.8 us
    pallas_call x1, Pallas kernels, experts_first(): pl.pallas_call(first_kernel, in_specs=[VM] * 4, out_specs=[VM] * 6 + [SM]...  38.4 us
    pallas_call x1, Pallas kernels, experts_second(): pl.pallas_call(second_kernel, in_specs=[SM] + [ANY] * 6, out_specs=[VM] *...  34.3 us
    pallas_call x1, Pallas kernels, finish(): pl.pallas_call(functools.partial(final_kernel, tensor, comm), in_specs=[A...  31.3 us
    pallas_call x1, Pallas kernels, last(): pl.pallas_call(functools.partial(last_kernel, tensor), in_specs=[VM] * 2...  23.4 us
  transfers between devices with their start and end apart: 4, of which 2 were waited for; matrix products, arithmetic and copies ran while one was open for 1% of the time, Pallas kernels for 79%

profile of v8, /device:TPU:0, one launch (start us, length us, event | category | flops | bytes accessed | tf_op | source)
XLA Modules:
  0.0 431.1 jit_solution(11378510557132479725)
XLA Ops:
  7.2 0.0 all-gather.21.cloned.1.call-start
  7.2 0.0 copy-start.94
  7.2 0.0 copy-start.96
  7.3 21.6 %shard_map.279 = (bf16[3,8,96,256]{3,2,1,0:T(8,128)(2,1)}, bf16[4,3,96,192]{3,2,1,0:T(8,128)(2,1)}, bf16[4,192,96]{2,1,0:T(8,128)(2,1)}) custom-call(bf16[2,8,96,512]{3,2,1,0:T(8,128)(2,1)} %gu_ref.3, bf16[1,8,96,512]{3,2,1,0:T(8,128)(2,1)} %bitcast.304, bf16[3,96,192]{2,1,0:T(8,128)(2,1)} %w_ref.1, bf16[192,96]{1,0:T(8,128)(2,1)} %wo_ref.1), custom_call_target="tpu_custom_call" | custom-call | flops 24999999488 | bytes 10000000 | tf_op jit(solution)/shard_map/pallas_call | solution.py:499
  28.8 0.0 all-gather.21.cloned.1.call-update
  28.9 0.0 all-gather.23.cloned.1.call-start
  28.9 0.0 copy-start.82
  29.0 0.0 copy-start.107
  29.0 0.0 copy-start.108
  29.0 0.0 copy-start.89
  29.0 0.0 copy-start.42
  29.0 0.0 copy-start.60
  29.0 0.0 copy-start.48
  29.0 0.0 copy-start.99
  29.0 0.0 copy-start.15
  29.1 40.8 %shard_map.280 = (bf16[4,768,768]{2,1,0:T(8,128)(2,1)}, bf16[3,8,96,256]{3,2,1,0:T(8,128)(2,1)}, f32[8,1,1024]{2,1,0:T(1,128)}, f32[16,128]{1,0:T(8,128)}, bf16[...) custom-call(bf16[4,3,96,192]{3,2,1,0:T(8,128)(2,1)} %get-tuple-element.239.zq_ref, ...), custom_call_target="tpu_custom_call" | custom-call | flops 35000000512 | bytes 10000000 | tf_op jit(solution)/shard_map/pallas_call | solution.py:292
  69.8 0.0 all-gather.23.cloned.1.call-update
  69.9 0.2 reduce-scatter.34.cloned.1.call-start
  70.1 0.0 copy-done.107
  70.1 0.0 copy-done.108
  70.2 0.6 pad.8.prior_ref
  70.8 0.7 copy.170.starts_ref
  71.5 3.8 concatenate.29.par_ref
  75.3 86.1 %shard_map.281 = (bf16[1024,768]{1,0:T(8,128)(2,1)}, bf16[1024,768]{1,0:T(8,128)(2,1)}, bf16[1024,768]{1,0:T(8,128)(2,1)}, bf16[1024,768]{1,0:T(8,128)(2,1)}, f3...) custom-call(s32[4,2]{1,0:T(4,128)} %copy.170.starts_ref, ...), custom_call_target="tpu_custom_call" | custom-call | flops 40000000000 | bytes 30000000 | tf_op jit(solution)/shard_map/pallas_call | solution.py:1657
  161.5 0.0 all-gather.21.cloned.1.call-done.w_ref
  161.5 38.4 %shard_map.282 = (bf16[2304,768]{1,0:T(8,128)(2,1)}, bf16[2304,768]{1,0:T(8,128)(2,1)}, f32[2304,128]{1,0:T(8,128)}, f32[2304,768]{1,0:T(8,128)}, f32[2304,768]{...) custom-call(f32[16,1,256]{2,1,0:T(1,128)} %get-tuple-element.244.pay_ref, ...), custom_call_target="tpu_custom_call" | custom-call | flops 22000001024 | bytes 25000000 | tf_op jit(solution)/shard_map/pallas_call | solution.py:1149
  199.9 0.0 reduce-scatter.34.cloned.1.call-update
  199.9 0.0 reduce-scatter.36.cloned.1.call-start
  200.0 10.1 %all-gather.23.cloned.1.call-done.w_any = bf16[4,3,768,256]{3,2,1,0:T(8,128)(2,1)} async-done(((bf16[1,3,768,256]{3,2,1,0:T(8,128)(2,1)}), bf16[4,3,768,256]{3,2,1,0:T(8,128)(2,1)}) %all-gather.23.cloned.1.call-update) | async-done | bytes 4718608 | tf_op jit(solution)/shard_map/all_gather | solution.py:1651
  210.1 34.3 %shard_map.283 = (bf16[8,256,768]{2,1,0:T(8,128)(2,1)}, bf16[8,256,768]{2,1,0:T(8,128)(2,1)}, f32[8,1,256]{2,1,0:T(1,128)}, bf16[4,3,768,256]{3,2,1,0:T(8,128)(2,1)}) custom-call(s32[9]{0:T(128)} %get-tuple-element.249.meta_ref, bf16[2304,768]{1,0:T(8,128)(2,1)} %get-tuple-element.250.xc_any, bf16[2304,768]{1,0:T(8,128)(2,1)} %get-tuple-element.251.yc_any, ...), custom_call_target="tpu_custom_call" | custom-call | flops 22000001024 | bytes 25000000 | tf_op jit(solution)/shard_map/pallas_call | solution.py:1167
  244.4 48.1 %shard_map.284 = (bf16[1024,768]{1,0:T(8,128)(2,1)}, f32[1024,768]{1,0:T(8,128)}, f32[16,1024]{1,0:T(8,128)S(1)}, f32[32,768]{1,0:T(8,128)}) custom-call(bf16[8,256,768]{2,1,0:T(8,128)(2,1)} %get-tuple-element.257.dxb_ref, f32[8,1,256]{2,1,0:T(1,128)} %get-tuple-element.258.ggb_ref, bf16[1024,768]{1,0:T(8,128)(2,1)S(1)} %copy-done.7, ...), custom_call_target="tpu_custom_call" | custom-call | flops 4000000000 | bytes 4000000 | tf_op jit(solution)/shard_map/pallas_call | solution.py:1692
  292.5 3.7 reduce-scatter.34.cloned.1.call-done
  296.2 0.0 reduce-scatter.36.cloned.1.call-update
  296.2 60.8 %shard_map.285 = (bf16[4,768,768]{2,1,0:T(8,128)(2,1)}, bf16[3,1024,768]{2,1,0:T(8,128)(2,1)}, bf16[8,256,768]{2,1,0:T(8,128)(2,1)}, f32[32,768]{1,0:T(8,128)}, bf16[3,8,96,256]{3,2,1,0:T(8,128)(2,1)}) custom-call(s32[4,2]{1,0:T(4,128)} %copy.170.starts_ref, bf16[1024,768]{1,0:T(8,128)(2,1)} %get-tuple-element.264.gmo_ref, ...), custom_call_target="tpu_custom_call" | custom-call | flops 8000000000 | bytes 4000000 | tf_op jit(solution)/shard_map/pallas_call | solution.py:1720
  357.1 31.3 %shard_map.286 = (bf16[4,4,96,192]{3,2,1,0:T(8,128)(2,1)}, f32[1024,768]{1,0:T(8,128)}, bf16[1024,768]{1,0:T(8,128)(2,1)}, f32[32,768]{1,0:T(8,128)S(1)}, f32[1,768]{1,0:T(1,128)}) custom-call(bf16[4,768,768]{2,1,0:T(8,128)(2,1)} %get-tuple-element.274.g_ref, bf16[3,1024,768]{2,1,0:T(8,128)(2,1)} %get-tuple-element.275.gp_any, ...), custom_call_target="tpu_custom_call" | custom-call | flops 8000000000 | bytes 4000000 | tf_op jit(solution)/shard_map/pallas_call | solution.py:710
  388.4 0.6 slice_reduce_fusion
  389.6 0.0 reduce-scatter.36.cloned.1.call-done
  389.7 0.0 copy-start.55
  389.7 0.0 copy-start.61
  389.7 0.0 copy-start.84
  389.7 0.0 copy-start.90
  389.7 0.0 copy-start.109
  389.7 23.4 %shard_map.287 = (f32[4,96,192]{2,1,0:T(8,128)}, f32[1,768]{1,0:T(1,128)S(1)}, bf16[3,8,96,256]{3,2,1,0:T(8,128)(2,1)}) custom-call(bf16[4,4,96,192]{3,2,1,0:T(8,128)(2,1)} %get-tuple-element.283.zs_ref, f32[1,768]{1,0:T(1,128)} %get-tuple-element.284.small_ref, bf16[3,8,96,256]{3,2,1,0:T(8,128)(2,1)} %bitcast.325), custom_call_target="tpu_custom_call" | custom-call | flops 17999998976 | bytes 10000000 | tf_op jit(solution)/shard_map/pallas_call | solution.py:687
  413.2 6.6 %conditional.1 = (bf16[1024,768]{1,0:T(8,128)(2,1)}, f32[1024,768]{1,0:T(8,128)}, f32[768]{0:T(1024)}, f32[192,96]{1,0:T(8,128)}, f32[768]{0:T(1024)}, /*index=5...) conditional(s32[]{:T(128)} %convert_element_type.180, ...), branch_computations={%region_3.4_spmd, %region_4.53_spmd} | conditional | flops 61550759936 | bytes 1739891968 | solution.py:1784
  413.2 4.8 %branch_0_fun.1 = (f32[2,8,96,512]{3,2,1,0:T(8,128)}, f32[8,96,512]{2,1,0:T(8,128)}, f32[3,96,192]{2,1,0:T(8,128)}, f32[192,96]{1,0:T(8,128)}, f32[12,768]{1,0:T...) custom-call(bf16[3,8,96,256]{3,2,1,0:T(8,128)(2,1)} %get-tuple-element.1, ...), custom_call_target="tpu_custom_call" | custom-call | flops 1000000000 | bytes 8000000 | tf_op jit(solution)/shard_map/cond/branch_0_fun/pallas_call | solution.py:1223
  418.0 0.6 slice_bitcast_fusion
  419.8 2.8 copy.298
  422.6 1.7 copy.299
  (25 shorter events, 0.1 us)
Async XLA Ops:
  7.2 154.3 %all-gather.21.cloned.1.call-start = ((), (), s32[]{:S(2)}) async-start(), calls=%async_computation.26 | async-start | bytes 5898240 | tf_op jit(solution)/shard_map/all_gather | solution.py:1651
  7.2 21.7 %copy-start.7 = (bf16[1024,768]{1,0:T(8,128)(2,1)S(1)}, bf16[1024,768]{1,0:T(8,128)(2,1)}, u32[]{:S(2)}) copy-start(bf16[1024,768]{1,0:T(8,128)(2,1)} %og_any.1) | copy-start | bytes 4718596
  7.2 21.7 %copy-start.94 = (s32[4096,2]{0,1:T(2,128)S(1)}, s32[4096,2]{0,1:T(2,128)}, u32[]{:S(2)}) copy-start(s32[4096,2]{0,1:T(2,128)} %param.26) | copy-start | bytes 98308
  7.2 21.7 %copy-start.96 = (s32[4096,2]{0,1:T(2,128)S(1)}, s32[4096,2]{0,1:T(2,128)}, u32[]{:S(2)}) copy-start(s32[4096,2]{0,1:T(2,128)} %param.27) | copy-start | bytes 98308
  28.9 181.3 %all-gather.23.cloned.1.call-start = ((), (), s32[]{:S(2)}) async-start(), calls=%async_computation.28 | async-start | bytes 5898240 | tf_op jit(solution)/shard_map/all_gather | solution.py:1651
  28.9 41.1 %copy-start.82 = (bf16[2,2,768]{2,1,0:T(2,128)(2,1)S(1)}, bf16[2,2,768]{2,1,0:T(2,128)(2,1)}, u32[]{:S(2)}) copy-start(bf16[2,2,768]{2,1,0:T(2,128)(2,1)} %param.36) | copy-start | bytes 18436
  29.0 41.2 %copy-start.107 = (bf16[768]{0:T(1024)(128)(2,1)S(1)}, bf16[768]{0:T(1024)(128)(2,1)}, u32[]{:S(2)}) copy-start(bf16[768]{0:T(1024)(128)(2,1)} %param.29) | copy-start | bytes 4612
  29.0 41.2 %copy-start.108 = (bf16[768]{0:T(1024)(128)(2,1)S(1)}, bf16[768]{0:T(1024)(128)(2,1)}, u32[]{:S(2)}) copy-start(bf16[768]{0:T(1024)(128)(2,1)} %param.32) | copy-start | bytes 4612
  29.0 41.2 %copy-start.89 = (bf16[12,12]{1,0:T(8,128)(2,1)S(1)}, bf16[12,12]{1,0:T(8,128)(2,1)}, u32[]{:S(2)}) copy-start(bf16[12,12]{1,0:T(8,128)(2,1)} %param.34) | copy-start | bytes 868
  29.0 41.2 %copy-start.42 = (bf16[1024,12]{0,1:T(8,128)(2,1)S(1)}, bf16[1024,12]{0,1:T(8,128)(2,1)}, u32[]{:S(2)}) copy-start(bf16[1024,12]{0,1:T(8,128)(2,1)} %param.25) | copy-start | bytes 73732
  29.0 41.8 %copy-start.60 = (s32[4,2]{0,1:T(2,128)S(1)}, s32[4,2]{0,1:T(2,128)}, u32[]{:S(2)}) copy-start(s32[4,2]{0,1:T(2,128)} %param.28) | copy-start | bytes 100
  29.0 42.5 %copy-start.48 = (bf16[768,12]{0,1:T(8,128)(2,1)S(1)}, bf16[768,12]{0,1:T(8,128)(2,1)}, u32[]{:S(2)}) copy-start(bf16[768,12]{0,1:T(8,128)(2,1)} %param.33) | copy-start | bytes 55300
  29.0 42.5 %copy-start.99 = (bf16[2,768]{1,0:T(2,128)(2,1)S(1)}, bf16[2,768]{1,0:T(2,128)(2,1)}, u32[]{:S(2)}) copy-start(bf16[2,768]{1,0:T(2,128)(2,1)} %param.35) | copy-start | bytes 9220
  29.0 46.3 %copy-start.15 = (bf16[1024,768]{1,0:T(8,128)(2,1)S(1)}, bf16[1024,768]{1,0:T(8,128)(2,1)}, u32[]{:S(2)}) copy-start(bf16[1024,768]{1,0:T(8,128)(2,1)} %tok_any.1) | copy-start | bytes 4718596
  69.9 226.3 %reduce-scatter.34.cloned.1.call-start = ((), (), s32[]{:S(2)}) async-start(), calls=%async_computation.27 | async-start | bytes 5898240 | tf_op jit(solution)/shard_map/reduce_scatter | solution.py:1685
  199.9 189.7 %reduce-scatter.36.cloned.1.call-start = ((), (), s32[]{:S(2)}) async-start(), calls=%async_computation.29 | async-start | bytes 5898240 | tf_op jit(solution)/shard_map/reduce_scatter | solution.py:1685
  388.4 1.3 copy-start.110
  389.7 23.5 %copy-start.55 = (bf16[3,96,192]{2,1,0:T(8,128)(2,1)S(1)}, bf16[3,96,192]{2,1,0:T(8,128)(2,1)}, u32[]{:S(2)}) copy-start(bf16[3,96,192]{2,1,0:T(8,128)(2,1)} %w_ref.1) | copy-start | bytes 331780
  389.7 23.5 %copy-start.61 = (s32[4,2]{0,1:T(2,128)S(1)}, s32[4,2]{0,1:T(2,128)}, u32[]{:S(2)}) copy-start(s32[4,2]{0,1:T(2,128)} %param.28) | copy-start | bytes 100
  389.7 23.5 %copy-start.84 = (bf16[192,96]{1,0:T(8,128)(2,1)S(1)}, bf16[192,96]{1,0:T(8,128)(2,1)}, u32[]{:S(2)}) copy-start(bf16[192,96]{1,0:T(8,128)(2,1)} %wo_ref.1) | copy-start | bytes 110596
  389.7 23.5 %copy-start.90 = (bf16[12,12]{1,0:T(8,128)(2,1)S(1)}, bf16[12,12]{1,0:T(8,128)(2,1)}, u32[]{:S(2)}) copy-start(bf16[12,12]{1,0:T(8,128)(2,1)} %param.34) | copy-start | bytes 868
  389.7 23.5 %copy-start.109 = (bf16[768]{0:T(1024)(128)(2,1)S(1)}, bf16[768]{0:T(1024)(128)(2,1)}, u32[]{:S(2)}) copy-start(bf16[768]{0:T(1024)(128)(2,1)} %param.32) | copy-start | bytes 4612
  419.8 2.8 copy-start.31
Sparse Core Ops, SparseCore 0:
  29.0 91.6 all-gather.20
  122.2 87.8 all-gather.22
  212.4 83.7 reduce-scatter.33
  298.4 89.0 reduce-scatter.35
